TPU v7x, 512 devices: a whole 4x4x16 slice. The times are simulated.
512 devices in a mesh: curve: 32 (over z, x_lo), head: 16 (over x_hi, y, core).
Axes of the slice: x: 4 (x_hi: 2, x_lo: 2; x = x_hi * 2 + x_lo), y: 4, z: 16, core: 2. Of those that a mesh axis runs over, the one named last changes fastest.
Arguments:
- points: bfloat16 [65536, 1024], P(('curve', 'head')), may hold values from -6 to 6
- order: int32 [512, 128], P(('curve', 'head')), may hold values from 0 to 127, each once within a row
- scan_ids: int32 [65536], P(('curve', 'head')), may hold values from 0 to 3
- ln_gain: float32 [2, 1024], replicated, may hold values from 0.25 to 1.75
- w_qkv: bfloat16 [2, 1024, 3072], P(None, None, 'head'), may hold values from -7 to 7, as said below
- w_out: bfloat16 [2, 1024, 1024], P(None, 'head'), may hold values from -0.1875 to 0.1875
Outputs:
- refined: bfloat16 [65536, 1024], P(('curve', 'head'))
Inputs may be any that keep to these rules, and one draw needn't show every extreme that they name: `order`: row b is a permutation of the 128 rows of block b. `w_qkv`: columns ordered by head, then query, key, value, then entry.
All inputs are finite; a program needn't handle non-finite values.
Results may differ from a plain program's by a relative error of at most 0.01.
Values may be sent and summed in bfloat16 or wider, within the bound.
No kernel may reach another device: no remote copies, remote signals or barrier semaphores. Data moves between devices by JAX's collectives and lax.ppermute only.
A program may use at most 64 MiB of HBM per device.

v0:
```python
import jax
import jax.numpy as jnp
from jax import lax
from jax.sharding import Mesh
from jax.sharding import PartitionSpec as P

HEAD_DIM = 64
PATCH = 1024
HEAD = ("head_0", "head_1", "head_2")
CURVE_HEAD = ("curve", "head_0", "head_1", "head_2")


EPSILON = 1e-05


def copy_for_each(array, axis):
    copies = jnp.broadcast_to(array, (lax.axis_size(axis), *array.shape))
    return lax.all_to_all(copies, axis, split_axis=0, concat_axis=0, tiled=True)


def laid_out(parts, dim):
    dims = list(parts.shape[1:])
    dims[dim] *= parts.shape[0]
    return jnp.moveaxis(parts, 0, dim).reshape(dims)


def gather_directly(array, axis, dim):
    parts = copy_for_each(array, axis)
    return laid_out(parts, dim)


def gathered_by_axis(array, axes, dim):
    far, near = axes
    first = copy_for_each(array, far)
    parts = jnp.swapaxes(copy_for_each(first, near), 0, 1)
    return laid_out(parts.reshape(-1, *array.shape), dim)


def extended(array, sides, width):
    for axis, dim in sides:
        peers, length = (lax.axis_size(axis), array.shape[dim])
        up = [(i, (i + 1) % peers) for i in range(peers)]
        down = [(j, i) for i, j in up]
        last = lax.slice_in_dim(array, length - width, length, axis=dim)
        first = lax.slice_in_dim(array, 0, width, axis=dim)
        before = lax.ppermute(last, axis, up)
        after = lax.ppermute(first, axis, down)
        array = jnp.concatenate([before, array, after], axis=dim)
    return array


def layer_norm(rows, gain):
    values = rows.astype(jnp.float32)
    center = values - jnp.mean(values, axis=-1, keepdims=True)
    spread = jnp.mean(center * center, axis=-1, keepdims=True)
    return (center * lax.rsqrt(spread + EPSILON) * gain).astype(jnp.bfloat16)


def plain_window(first_row):
    return first_row // PATCH * PATCH


def centred_window(first_row):
    return (first_row + PATCH // 2) // PATCH * PATCH


def attend(queries, keys, values, query_tags, key_tags, window_of):
    block_rows = PATCH // 2
    blocks_count = queries.shape[0] // block_rows

    def one_block(block_index):
        first_row = block_index * block_rows
        query_block = lax.dynamic_slice_in_dim(queries, first_row, block_rows, 0)
        tags_block = lax.dynamic_slice_in_dim(query_tags, first_row, block_rows, 0)
        first_key = window_of(first_row)
        key_block = lax.dynamic_slice_in_dim(keys, first_key, PATCH, 0)
        value_block = lax.dynamic_slice_in_dim(values, first_key, PATCH, 0)
        key_block_tags = lax.dynamic_slice_in_dim(key_tags, first_key, PATCH, 0)
        scores = jnp.einsum(
            "qhd,khd->hqk", query_block, key_block, preferred_element_type=jnp.float32
        ) * HEAD_DIM ** (-0.5)
        allowed = tags_block[:, None] == key_block_tags[None, :]
        scores = jnp.where(allowed[None], scores, -jnp.inf)
        row_max = jnp.max(scores, axis=-1, keepdims=True)
        expo = jnp.exp(scores - row_max)
        probs = (expo / jnp.sum(expo, axis=-1, keepdims=True)).astype(jnp.bfloat16)
        result = jnp.einsum("hqk,khd->qhd", probs, value_block, preferred_element_type=jnp.float32)
        return result.astype(jnp.bfloat16)

    outputs = lax.map(one_block, jnp.arange(blocks_count))
    return outputs.reshape(queries.shape[0], -1)


def on_device(points, order, scan_ids, ln_gain, w_qkv, w_out):
    stream = points[order[0]]
    range_ids = gather_directly(scan_ids, HEAD, 0)
    span_rows = range_ids.shape[0]
    heads_local = w_qkv.shape[2] // (3 * HEAD_DIM)
    half_patch = PATCH // 2
    for layer_index in range(2):
        normed = layer_norm(stream, ln_gain[layer_index])
        weights_here = w_qkv[layer_index]
        qkv_span = jnp.dot(
            gathered_by_axis(normed, (("head_0", "head_1"), "head_2"), 0),
            weights_here,
            preferred_element_type=jnp.float32,
        ).astype(jnp.bfloat16)
        pieces = qkv_span.reshape(span_rows, heads_local, 3, HEAD_DIM)
        if layer_index == 0:
            attended = attend(
                pieces[:, :, 0],
                pieces[:, :, 1],
                pieces[:, :, 2],
                range_ids,
                range_ids,
                plain_window,
            )
        else:
            tags_float = range_ids.astype(jnp.bfloat16)
            kv_flat = pieces[:, :, 1:].reshape(span_rows, heads_local * 2 * HEAD_DIM)
            wide_kv, wide_tags = (
                extended(kv_flat, (("curve", 0),), half_patch),
                extended(tags_float, (("curve", 0),), half_patch),
            )
            wide_pieces = wide_kv.reshape(-1, heads_local, 2, HEAD_DIM)
            attended = attend(
                pieces[:, :, 0],
                wide_pieces[:, :, 0],
                wide_pieces[:, :, 1],
                range_ids,
                wide_tags.astype(jnp.int32),
                centred_window,
            )
        heads_rows = lax.all_to_all(attended, HEAD, split_axis=0, concat_axis=1, tiled=True)
        update = jnp.dot(
            heads_rows,
            lax.all_gather(w_out[layer_index], HEAD, axis=0, tiled=True),
            preferred_element_type=jnp.float32,
        )
        stream = (stream.astype(jnp.float32) + update).astype(jnp.bfloat16)
    return stream


def solution(mesh):
    split = Mesh(
        mesh.devices.reshape(mesh.shape["curve"], 2, 4, 2), ("curve", "head_0", "head_1", "head_2")
    )
    in_specs = (
        P(CURVE_HEAD, None),
        P(CURVE_HEAD, None),
        P(CURVE_HEAD),
        P(),
        P(None, None, HEAD),
        P(None, HEAD, None),
    )
    out_specs = P(CURVE_HEAD, None)
    return jax.shard_map(
        on_device, mesh=split, in_specs=in_specs, out_specs=out_specs, check_vma=False
    )
```

profile of v0, /device:TPU:1, one launch (start us, length us, event | category | flops | bytes accessed | tf_op | source)
XLA Modules:
  0.0 192.7 jit_solution(8117099118496120220)
XLA Ops:
  7.5 0.9 gather_fusion
  9.0 1.6 broadcast_in_dim.50
  10.6 7.6 %all-to-all-start = ((bf16[8,128,1024]{2,1,0:T(8,128)(2,1)}), bf16[8,128,1024]{2,1,0:T(8,128)(2,1)S(1)}, u32[]{:S(2)}, u32[]{:S(2)}) async-start(bf16[8,128,1024]{2,1,0:T(8,128)(2,1)} %broadcast_in_dim.50), calls=%async_computation | async-start | bytes 4194304 | tf_op jit(solution)/shard_map/all_to_all | solution.py:18
  18.2 0.7 fusion.54
  19.0 24.2 %all-to-all-done = bf16[8,128,1024]{2,1,0:T(8,128)(2,1)S(1)} async-done(((bf16[8,128,1024]{2,1,0:T(8,128)(2,1)}), bf16[8,128,1024]{2,1,0:T(8,128)(2,1)S(1)}, u32[]{:S(2)}, u32[]{:S(2)}) %all-to-all-start) | async-done | bytes 2097184 | tf_op jit(solution)/shard_map/all_to_all | solution.py:18
  43.7 10.1 %all_to_all.64 = bf16[2,8,128,1024]{3,2,1,0:T(8,128)(2,1)} all-to-all(bf16[2,8,128,1024]{3,2,1,0:T(8,128)(2,1)S(1)} %broadcast_in_dim.51), channel_id=1, replica_groups=mesh['curve'=32,'head_0'=2,'head_1'=4,'head_2'=2] {'head_2'}, dimensions={0} | all-to-all | bytes 8388608 | tf_op jit(solution)/shard_map/all_to_all | solution.py:18
  54.4 5.2 %all-to-all-start.2 = ((s32[16,1,128]{2,1,0:T(1,128)}), s32[16,1,128]{2,1,0:T(1,128)S(1)}, u32[]{:S(2)}, u32[]{:S(2)}) async-start(s32[16,1,128]{2,1,0:T(1,128)} %broadcast_in_dim.52), calls=%async_computation.2 | async-start | bytes 16384 | tf_op jit(solution)/shard_map/all_to_all | solution.py:18
  59.6 2.7 %copy.16 = bf16[2,8,128,1024]{3,2,0,1:T(8,128)(2,1)S(1)} copy(bf16[2,8,128,1024]{3,2,1,0:T(8,128)(2,1)} %all_to_all.64) | data formatting | bytes 8388608 | tf_op jit(solution)/shard_map/all_to_all | solution.py:18
  62.3 1.5 convolution_convert_fusion.3
  63.9 2.7 %all-to-all-done.2 = s32[16,1,128]{2,1,0:T(1,128)S(1)} async-done(((s32[16,1,128]{2,1,0:T(1,128)}), s32[16,1,128]{2,1,0:T(1,128)S(1)}, u32[]{:S(2)}, u32[]{:S(2)}) %all-to-all-start.2) | async-done | bytes 8224 | tf_op jit(solution)/shard_map/all_to_all | solution.py:18
  66.6 12.3 %while.24 = (s32[]{:T(128)}, bf16[4,512,1,64]{1,3,2,0:T(8,128)(2,1)S(1)}, s32[4]{0:T(128)S(1)}, bf16[2048,1,64]{0,2,1:T(8,128)(2,1)S(1)}, s32[2048]{0:T(1024)S(1...) while((s32[]{:T(128)}, ...), condition=%wide.region_5.6_spmd, body=%wide.region_2.5_spmd.sunk | while | flops 138968096 | bytes 6713754 | solution.py:90
  79.4 13.1 %all_to_all.65 = bf16[16,128,64]{1,2,0:T(8,128)(2,1)S(1)} all-to-all(bf16[16,128,64]{1,2,0:T(8,128)(2,1)S(1)} %copy.18), channel_id=1, replica_groups=mesh['curve'=32,'head_0'=2,'head_1'=4,'head_2'=2] {'head_0','head_1','he..., dimensions={0} | all-to-all | bytes 524288 | tf_op jit(solution)/shard_map/all_to_all | solution.py:134
  92.4 2.1 %fusion.57 = (f32[128]{0:T(128)S(1)}, f32[128,1024]{1,0:T(8,128)S(1)}) fusion(bf16[128,1024]{0,1:T(8,128)(2,1)S(1)} %bitcast.139, bf16[1,1024,1024]{2,1,0:T(8,128)(2,1)} %all-gather.5.cloned.1.call-done, bf16[128,1024]{1,0:T(8,128)(2,1)S(1)} %gather_fusion), kind=kOutput, calls=%fused_computation.76 | convolution fusion | flops 269090688 | bytes 3146240 | tf_op jit(solution)/shard_map/dot_general | solution.py:135
  94.9 1.6 broadcast_in_dim.53
  96.5 3.6 %all-to-all-start.4 = ((bf16[8,128,1024]{2,1,0:T(8,128)(2,1)}), bf16[8,128,1024]{2,1,0:T(8,128)(2,1)S(1)}, u32[]{:S(2)}, u32[]{:S(2)}) async-start(bf16[8,128,1024]{2,1,0:T(8,128)(2,1)} %broadcast_in_dim.53), calls=%async_computation.4 | async-start | bytes 4194304 | tf_op jit(solution)/shard_map/all_to_all | solution.py:18
  100.2 2.2 %collective-permute-start.2 = (bf16[512]{0:T(512)(128)(2,1)S(1)}, bf16[512]{0:T(512)(128)(2,1)S(1)}, u32[]{:S(2)}, u32[]{:S(2)}) collective-permute-start(bf16[512]{0:T(512)(128)(2,1)S(1)} %get-tuple-element.244), channel_id=1, source_target_pairs={{0,16},{16,32},{32,48},{48,64},{64,80},{80,96},{96,112},{112,128},... | collective-permute-start | bytes 3080 | tf_op jit(solution)/shard_map/ppermute | solution.py:46
  102.4 11.8 %collective-permute-start.3 = (bf16[512]{0:T(512)(128)(2,1)S(1)}, bf16[512]{0:T(512)(128)(2,1)S(1)}, u32[]{:S(2)}, u32[]{:S(2)}) collective-permute-start(bf16[512]{0:T(512)(128)(2,1)S(1)} %get-tuple-element.245), channel_id=1, source_target_pairs={{16,0},{32,16},{48,32},{64,48},{80,64},{96,80},{112,96},{128,112},... | collective-permute-start | bytes 3080 | tf_op jit(solution)/shard_map/ppermute | solution.py:47
  114.3 8.0 %collective-permute-done.2 = bf16[512]{0:T(512)(128)(2,1)S(1)} collective-permute-done((bf16[512]{0:T(512)(128)(2,1)S(1)}, bf16[512]{0:T(512)(128)(2,1)S(1)}, u32[]{:S(2)}, u32[]{:S(2)}) %collective-permute-start.2) | collective-permute-done | bytes 1056 | tf_op jit(solution)/shard_map/ppermute | solution.py:46
  122.2 1.0 collective-permute-done.3
  123.2 3.0 %all-to-all-done.4 = bf16[8,128,1024]{2,1,0:T(8,128)(2,1)S(1)} async-done(((bf16[8,128,1024]{2,1,0:T(8,128)(2,1)}), bf16[8,128,1024]{2,1,0:T(8,128)(2,1)S(1)}, u32[]{:S(2)}, u32[]{:S(2)}) %all-to-all-start.4) | async-done | bytes 2097184 | tf_op jit(solution)/shard_map/all_to_all | solution.py:18
  126.7 8.0 %all_to_all.66 = bf16[2,8,128,1024]{3,2,1,0:T(8,128)(2,1)S(1)} all-to-all(bf16[2,8,128,1024]{3,2,1,0:T(8,128)(2,1)S(1)} %broadcast_in_dim.54), channel_id=1, replica_groups=mesh['curve'=32,'head_0'=2,'head_1'=4,'head_2'=2] {'head_2'}, dimensions={0} | all-to-all | bytes 8388608 | tf_op jit(solution)/shard_map/all_to_all | solution.py:18
  135.8 1.5 convolution_convert_fusion.2
  137.4 2.2 %collective-permute-start = (bf16[512,128]{0,1:T(8,128)(2,1)S(1)}, bf16[512,128]{0,1:T(8,128)(2,1)S(1)}, u32[]{:S(2)}, u32[]{:S(2)}) collective-permute-start(bf16[512,128]{0,1:T(8,128)(2,1)S(1)} %bitcast.145), channel_id=1, source_target_pairs={{0,16},{16,32},{32,48},{48,64},{64,80},{80,96},{96,112},{112,128},... | collective-permute-start | bytes 393224 | tf_op jit(solution)/shard_map/ppermute | solution.py:46
  139.6 11.8 %collective-permute-start.1 = (bf16[512,128]{0,1:T(8,128)(2,1)S(1)}, bf16[512,128]{0,1:T(8,128)(2,1)S(1)}, u32[]{:S(2)}, u32[]{:S(2)}) collective-permute-start(bf16[512,128]{0,1:T(8,128)(2,1)S(1)} %bitcast.144), channel_id=1, source_target_pairs={{16,0},{32,16},{48,32},{64,48},{80,64},{96,80},{112,96},{128,112},... | collective-permute-start | bytes 393224 | tf_op jit(solution)/shard_map/ppermute | solution.py:47
  151.5 1.5 collective-permute-done
  153.0 0.9 collective-permute-done.1
  154.1 12.7 %while.25 = (s32[]{:T(128)}, bf16[4,512,1,64]{1,3,2,0:T(8,128)(2,1)S(1)}, s32[4]{0:T(128)S(1)}, bf16[3072,1,64]{0,2,1:T(8,128)(2,1)S(1)}, s32[2048]{0:T(1024)S(1...) while((s32[]{:T(128)}, ...), condition=%wide.region_11.12_spmd, body=%wide.region_8.11_spmd.sunk | while | flops 138968096 | bytes 6713799 | solution.py:90
  167.1 0.8 copy.21
  167.9 6.6 %all-to-all-start.6 = ((bf16[16,128,64]{1,2,0:T(8,128)(2,1)}), bf16[16,128,64]{1,2,0:T(8,128)(2,1)S(1)}, u32[]{:S(2)}, u32[]{:S(2)}) async-start(bf16[16,128,64]{1,2,0:T(8,128)(2,1)} %copy.21), calls=%async_computation.6 | async-start | bytes 524288 | tf_op jit(solution)/shard_map/all_to_all | solution.py:134
  174.4 2.1 %all-gather.7.cloned.1.call-done = bf16[1,1024,1024]{2,1,0:T(8,128)(2,1)} async-done(((bf16[1,64,1024]{2,1,0:T(8,128)(2,1)}), bf16[1,1024,1024]{2,1,0:T(8,128)(2,1)}) %all-gather.7.cloned.1.call-update) | async-done | bytes 2097168 | tf_op jit(solution)/shard_map/all_gather | solution.py:137
  176.6 6.5 %all-to-all-done.6 = bf16[16,128,64]{1,2,0:T(8,128)(2,1)S(1)} async-done(((bf16[16,128,64]{1,2,0:T(8,128)(2,1)}), bf16[16,128,64]{1,2,0:T(8,128)(2,1)S(1)}, u32[]{:S(2)}, u32[]{:S(2)}) %all-to-all-start.6) | async-done | bytes 262176 | tf_op jit(solution)/shard_map/all_to_all | solution.py:134
  183.1 2.8 %fusion.32 = bf16[128,1024]{1,0:T(8,128)(2,1)} fusion(f32[128,1024]{1,0:T(8,128)S(1)} %get-tuple-element.247, bf16[128,1024]{0,1:T(8,128)(2,1)S(1)} %bitcast.138, bf16[1,1024,1024]{2,1,0:T(8,128)(2,1)} %all-gather.7.cloned.1.call-done), kind=kOutput, calls=%fused_computation.39 | convolution fusion | flops 268697600 | bytes 3145728 | tf_op jit(solution)/shard_map/dot_general | solution.py:135
  (99 shorter events, 25.1 us)
Async XLA Ops:
  6.5 1.0 copy-start
  6.5 2.2 %copy-start.2 = (f32[2,1024]{1,0:T(2,128)S(1)}, f32[2,1024]{1,0:T(2,128)}, u32[]{:S(2)}) copy-start(f32[2,1024]{1,0:T(2,128)} %param.13) | copy-start | bytes 24580
  10.6 7.7 %copy-start.1 = (bf16[2,64,1024]{2,1,0:T(8,128)(2,1)S(1)}, bf16[2,64,1024]{2,1,0:T(8,128)(2,1)}, u32[]{:S(2)}) copy-start(bf16[2,64,1024]{2,1,0:T(8,128)(2,1)} %param.15) | copy-start | bytes 786436
  10.6 32.6 %all-to-all-start = ((bf16[8,128,1024]{2,1,0:T(8,128)(2,1)}), bf16[8,128,1024]{2,1,0:T(8,128)(2,1)S(1)}, u32[]{:S(2)}, u32[]{:S(2)}) async-start(bf16[8,128,1024]{2,1,0:T(8,128)(2,1)} %broadcast_in_dim.50), calls=%async_computation | async-start | bytes 4194304 | tf_op jit(solution)/shard_map/all_to_all | solution.py:18
  18.2 74.2 %all-gather.5.cloned.1.call-start = ((), (), s32[]{:S(2)}) async-start(), calls=%async_computation.7 | async-start | bytes 2228224 | tf_op jit(solution)/shard_map/all_gather | solution.py:137
  43.7 10.1 %copy-start.3 = (s32[128]{0:T(128)S(1)}, s32[128]{0:T(128)}, u32[]{:S(2)}) copy-start(s32[128]{0:T(128)} %param.12) | copy-start | bytes 1540
  54.4 12.2 %all-to-all-start.2 = ((s32[16,1,128]{2,1,0:T(1,128)}), s32[16,1,128]{2,1,0:T(1,128)S(1)}, u32[]{:S(2)}, u32[]{:S(2)}) async-start(s32[16,1,128]{2,1,0:T(1,128)} %broadcast_in_dim.52), calls=%async_computation.2 | async-start | bytes 16384 | tf_op jit(solution)/shard_map/all_to_all | solution.py:18
  59.6 2.7 %copy-start.4 = (bf16[2,1024,192]{1,2,0:T(8,128)(2,1)S(1)}, bf16[2,1024,192]{1,2,0:T(8,128)(2,1)}, u32[]{:S(2)}) copy-start(bf16[2,1024,192]{1,2,0:T(8,128)(2,1)} %param.14) | copy-start | bytes 2359300
  96.5 29.7 %all-to-all-start.4 = ((bf16[8,128,1024]{2,1,0:T(8,128)(2,1)}), bf16[8,128,1024]{2,1,0:T(8,128)(2,1)S(1)}, u32[]{:S(2)}, u32[]{:S(2)}) async-start(bf16[8,128,1024]{2,1,0:T(8,128)(2,1)} %broadcast_in_dim.53), calls=%async_computation.4 | async-start | bytes 4194304 | tf_op jit(solution)/shard_map/all_to_all | solution.py:18
  100.1 76.4 %all-gather.7.cloned.1.call-start = ((), (), s32[]{:S(2)}) async-start(), calls=%async_computation.8 | async-start | bytes 2228224 | tf_op jit(solution)/shard_map/all_gather | solution.py:137
  100.2 22.0 %collective-permute-start.2 = (bf16[512]{0:T(512)(128)(2,1)S(1)}, bf16[512]{0:T(512)(128)(2,1)S(1)}, u32[]{:S(2)}, u32[]{:S(2)}) collective-permute-start(bf16[512]{0:T(512)(128)(2,1)S(1)} %get-tuple-element.244), channel_id=1, source_target_pairs={{0,16},{16,32},{32,48},{48,64},{64,80},{80,96},{96,112},{112,128},... | collective-permute-start | bytes 3080 | tf_op jit(solution)/shard_map/ppermute | solution.py:46
  102.4 20.8 %collective-permute-start.3 = (bf16[512]{0:T(512)(128)(2,1)S(1)}, bf16[512]{0:T(512)(128)(2,1)S(1)}, u32[]{:S(2)}, u32[]{:S(2)}) collective-permute-start(bf16[512]{0:T(512)(128)(2,1)S(1)} %get-tuple-element.245), channel_id=1, source_target_pairs={{16,0},{32,16},{48,32},{64,48},{80,64},{96,80},{112,96},{128,112},... | collective-permute-start | bytes 3080 | tf_op jit(solution)/shard_map/ppermute | solution.py:47
  134.7 1.1 copy-start.5
  137.4 15.7 %collective-permute-start = (bf16[512,128]{0,1:T(8,128)(2,1)S(1)}, bf16[512,128]{0,1:T(8,128)(2,1)S(1)}, u32[]{:S(2)}, u32[]{:S(2)}) collective-permute-start(bf16[512,128]{0,1:T(8,128)(2,1)S(1)} %bitcast.145), channel_id=1, source_target_pairs={{0,16},{16,32},{32,48},{48,64},{64,80},{80,96},{96,112},{112,128},... | collective-permute-start | bytes 393224 | tf_op jit(solution)/shard_map/ppermute | solution.py:46
  139.6 14.3 %collective-permute-start.1 = (bf16[512,128]{0,1:T(8,128)(2,1)S(1)}, bf16[512,128]{0,1:T(8,128)(2,1)S(1)}, u32[]{:S(2)}, u32[]{:S(2)}) collective-permute-start(bf16[512,128]{0,1:T(8,128)(2,1)S(1)} %bitcast.144), channel_id=1, source_target_pairs={{16,0},{32,16},{48,32},{64,48},{80,64},{96,80},{112,96},{128,112},... | collective-permute-start | bytes 393224 | tf_op jit(solution)/shard_map/ppermute | solution.py:47
  167.9 15.2 %all-to-all-start.6 = ((bf16[16,128,64]{1,2,0:T(8,128)(2,1)}), bf16[16,128,64]{1,2,0:T(8,128)(2,1)S(1)}, u32[]{:S(2)}, u32[]{:S(2)}) async-start(bf16[16,128,64]{1,2,0:T(8,128)(2,1)} %copy.21), calls=%async_computation.6 | async-start | bytes 524288 | tf_op jit(solution)/shard_map/all_to_all | solution.py:134
Sparse Core Ops, SparseCore 0:
  22.4 68.5 all-gather.4
  114.4 62.1 all-gather.6
where the time goes:
time: 194 us; the launch traced here: 193 us
  starting transfers between devices  51.1 us (26%)
  waiting for transfers between devices  49.9 us (26%)
  blocking collectives  31.1 us (16%)
  local copies, waits for them, and re-layouts  17.9 us (9%)
  matrix products  17.4 us (9%)
  between operations  13.7 us (7%)
  other arithmetic  5.82 us (3%)
  loops' own time  5.74 us (3%)
    all_to_all x3, waiting for transfers between devices, copy_for_each(): return lax.all_to_all(copies, axis, split_axis=0, concat_axis=0, tiled=True)  29.9 us
    ppermute x2, starting transfers between devices, extended(): after = lax.ppermute(first, axis, down)  23.6 us
    all_to_all x2, blocking collectives, copy_for_each(): return lax.all_to_all(copies, axis, split_axis=0, concat_axis=0, tiled=True)  18.1 us
    all_to_all x3, starting transfers between devices, copy_for_each(): return lax.all_to_all(copies, axis, split_axis=0, concat_axis=0, tiled=True)  16.4 us
    all_to_all x1, blocking collectives, on_device(): lax.all_to_all(attended, HEAD, split_axis=0, concat_axis=1, tiled=True)  13.1 us
    ppermute x2, waiting for transfers between devices, extended(): before = lax.ppermute(last, axis, up)  9.51 us
    all_to_all x1, starting transfers between devices, on_device(): lax.all_to_all(attended, HEAD, split_axis=0, concat_axis=1, tiled=True)  6.56 us
    all_to_all x1, waiting for transfers between devices, on_device(): lax.all_to_all(attended, HEAD, split_axis=0, concat_axis=1, tiled=True)  6.53 us
  transfers between devices with their start and end apart: 10, of which 9 were waited for; matrix products, arithmetic and copies ran while one was open for 15% of the time, Pallas kernels for 0%

commit v1 on v0

v1 whole, which is shorter than its diff:
```python
import jax
import jax.numpy as jnp
import numpy as np
from jax import lax
from jax.experimental import pallas as pl
from jax.experimental.pallas import tpu as pltpu
from jax.sharding import Mesh
from jax.sharding import PartitionSpec as P

HEAD_DIM = 64
D = 1024
ROWS = 128
PATCH = 1024
HALF = 512
LANES = 128
BLOCKS = D // LANES
EXT = D + 16
EPSILON = 1e-05
FAR = -1e30
AXES = ("z", "xl", "xh", "y", "c")
F32 = jnp.float32
BF16 = jnp.bfloat16


def pairs(shape, move):
    result = []
    for i in range(int(np.prod(shape))):
        place = tuple(int(v) for v in np.unravel_index(i, shape))
        result.append((i, int(np.ravel_multi_index(move(*place), shape))))
    return result


def dot(a, b):
    return lax.dot_general(a, b, (((1,), (0,)), ((), ())), preferred_element_type=F32)


def dot_nt(a, b):
    return lax.dot_general(a, b, (((1,), (1,)), ((), ())), preferred_element_type=F32)


def layer_norm(values, gain):
    center = values - jnp.mean(values, axis=-1, keepdims=True)
    spread = jnp.mean(center * center, axis=-1, keepdims=True)
    return (center * lax.rsqrt(spread + EPSILON) * gain).astype(BF16)


def side_by_side(ref, index):
    return jnp.concatenate([ref[index, b * LANES : (b + 1) * LANES, :] for b in range(BLOCKS)], axis=1)


def tag_columns(rows):
    return jnp.transpose(jnp.concatenate(rows, axis=0))


def one_hot(columns, block):
    lane = lax.broadcasted_iota(jnp.int32, (ROWS, LANES), 1).astype(F32)
    return columns[:, block : block + 1] == lane


def attend(queries, hot, keys_ref, values_ref):
    lane = lax.broadcasted_iota(jnp.int32, queries.shape, 1)
    results = []
    for head in range(2):
        own = jnp.where(lane // HEAD_DIM == head, queries, jnp.zeros_like(queries))
        scores = dot_nt(keys_ref[...], jnp.concatenate([own, hot], axis=1))
        top = jnp.max(scores, axis=0, keepdims=True)
        probs = jnp.exp(scores - top).astype(BF16)
        sums = dot(values_ref[head], probs)
        results.append(sums[:HEAD_DIM] / sums[HEAD_DIM : HEAD_DIM + 1])
    return jnp.transpose(jnp.concatenate(results, axis=0)).astype(BF16)


def put_values(values_ref, values):
    turned = jnp.transpose(values.astype(F32)).astype(BF16)
    for head in range(2):
        values_ref[head, :HEAD_DIM, :] = turned[head * HEAD_DIM : (head + 1) * HEAD_DIM]
        values_ref[head, HEAD_DIM:, :] = jnp.ones((16, PATCH), BF16)


def order_kernel(points, order, tags, out):
    row = lax.broadcasted_iota(jnp.int32, (ROWS, ROWS), 0)
    picks = jnp.transpose((row == order[...]).astype(F32)).astype(BF16)
    ordered = dot(picks, points[...]).astype(BF16)
    tag_rows = jnp.broadcast_to(tags[...].astype(F32), (16, LANES)).astype(BF16)
    for copy in range(4):
        for b in range(BLOCKS):
            out[copy, b * LANES : (b + 1) * LANES, :] = ordered[:, b * LANES : (b + 1) * LANES]
        out[copy, D:, :] = tag_rows


def first_kernel(near, far, gain, weights, out, normed, queries, keys, values, hots):
    rows = []
    for s, ref in enumerate((near, far)):
        for y in range(4):
            block = s * 4 + y
            normed[block * ROWS : (block + 1) * ROWS, :] = layer_norm(
                side_by_side(ref, y).astype(F32), gain[...]
            )
            rows.append(ref[y, D:, :].astype(F32)[:1])
    columns = tag_columns(rows)
    qkv = dot(normed[...], weights[...]).astype(BF16)
    queries[...] = qkv[:, :LANES] * jnp.asarray(HEAD_DIM**-0.5, BF16)
    keys[:, :LANES] = qkv[:, LANES : 2 * LANES]
    put_values(values, qkv[:, 2 * LANES :])
    for block in range(8):
        hot = one_hot(columns, block)
        span = slice(block * ROWS, (block + 1) * ROWS)
        hots[span, :] = jnp.where(hot, 1.0, 0.0).astype(BF16)
        keys[span, LANES:] = jnp.where(hot, 0.0, FAR).astype(BF16)
    for part in range(4):
        span = slice(part * 256, (part + 1) * 256)
        result = attend(queries[span, :], hots[span, :], keys, values)
        for copy in range(4):
            out[copy, span, :] = result


def middle_kernel(
    near, far, o_near, o_far, w_near, w_far, gain, weights,
    q_out, kv_p, kv_q, st_out, heads, update, normed,
):
    xh, my_y = lax.axis_index("xh"), lax.axis_index("y")
    for part, kv in enumerate((kv_p, kv_q)):
        half = 1 - xh if part == 0 else xh
        for s in range(2):
            for yy in range(2):
                y = half * 2 + yy
                span = slice((s * 2 + yy) * ROWS, (s * 2 + yy + 1) * ROWS)
                at_near = pl.ds(pl.multiple_of((s * 4 + y) * ROWS, ROWS), ROWS)
                at_far = pl.ds(pl.multiple_of(((1 - s) * 4 + y) * ROWS, ROWS), ROWS)
                for g in range(4):
                    heads[span, g * LANES : (g + 1) * LANES] = o_near[g, at_near, :]
                    heads[span, (g + 4) * LANES : (g + 5) * LANES] = o_far[g, at_far, :]
        update[...] = dot(heads[:, :HALF], w_near[...]) + dot(heads[:, HALF:], w_far[...])
        rows = []
        for s, ref in enumerate((near, far)):
            for yy in range(2):
                y = half * 2 + yy
                span = slice((s * 2 + yy) * ROWS, (s * 2 + yy + 1) * ROWS)
                stream = (side_by_side(ref, y).astype(F32) + update[span, :]).astype(BF16)
                normed[span, :] = layer_norm(stream.astype(F32), gain[...])
                rows.append(ref[y, D:, :].astype(F32)[:1])
                if s == 0:

                    @pl.when(y == my_y)
                    def _(stream=stream):
                        st_out[...] = stream

        qkv = dot(normed[...], weights[...]).astype(BF16)
        q_out[part] = qkv[:, :LANES] * jnp.asarray(HEAD_DIM**-0.5, BF16)
        kv[:HALF, :] = qkv[:, LANES : 2 * LANES]
        kv[HALF:D, :] = qkv[:, 2 * LANES :]
        kv[D:, :] = jnp.concatenate(rows + [jnp.zeros((12, LANES), F32)], axis=0).astype(BF16)


def second_kernel(queries, kv_p, kv_q, halo_p, halo_q, out, keys, values, hots):
    xh, c = lax.axis_index("xh"), lax.axis_index("c")
    for part, (mine, other) in enumerate(((kv_p, halo_p), (kv_q, halo_q))):
        half = 1 - xh if part == 0 else xh
        keys[:HALF, :LANES] = mine[:HALF, :]
        keys[HALF:, :LANES] = other[:HALF, :]
        put_values(values, jnp.concatenate([mine[HALF:D, :], other[HALF:D, :]], axis=0))
        columns = tag_columns([mine[D:, :].astype(F32)[:4], other[D:, :].astype(F32)[:4]])
        for block in range(8):
            hot = one_hot(columns, block)
            span = slice(block * ROWS, (block + 1) * ROWS)
            if block < 4:
                hots[span, :] = jnp.where(hot, 1.0, 0.0).astype(BF16)
            keys[span, LANES:] = jnp.where(hot, 0.0, FAR).astype(BF16)
        for s in range(2):
            span = slice(s * 256, (s + 1) * 256)
            result = attend(queries[part, span, :], hots[span, :], keys, values)
            core = c if s == 0 else 1 - c
            for yy in range(2):
                out[(half * 2 + yy) * 2 + core] = result[yy * ROWS : (yy + 1) * ROWS]


def last_kernel(parts, w_near, w_far, stream, out, heads):
    c = lax.axis_index("c")
    for s in range(2):
        core = c if s == 0 else 1 - c
        for y in range(4):
            heads[:, (s * 4 + y) * LANES : (s * 4 + y + 1) * LANES] = parts[y * 2 + core]
    update = dot(heads[:, :HALF], w_near[...]) + dot(heads[:, HALF:], w_far[...])
    out[...] = (stream[...].astype(F32) + update).astype(BF16)


def call(kernel, outs, scratch, *args):
    return pl.pallas_call(
        kernel,
        out_shape=[jax.ShapeDtypeStruct(shape, BF16) for shape in outs],
        in_specs=[pl.BlockSpec(memory_space=pltpu.VMEM)] * len(args),
        out_specs=[pl.BlockSpec(memory_space=pltpu.VMEM)] * len(outs),
        scratch_shapes=[pltpu.VMEM(shape, dtype) for shape, dtype in scratch],
        compiler_params=pltpu.CompilerParams(vmem_limit_bytes=32 * 1024 * 1024),
    )(*args)


def after(value, *others):
    return lax.optimization_barrier((value, *others))[0]


def solution(mesh):
    curve, heads = mesh.shape["curve"], mesh.shape["head"]
    shape = (curve // 2, 2, 2, heads // 4, 2)
    deep = shape[0]
    other_core = pairs(shape, lambda z, xl, xh, y, c: (z, xl, xh, y, 1 - c))
    mirror = pairs(shape, lambda z, xl, xh, y, c: (z, 1 - xl, 1 - xh, y, c))
    inner = pairs(shape, lambda z, xl, xh, y, c: (z, xl, 1 - xh, y, c))

    def across(z, xl, xh, y, c):
        here = z * 2 + xl
        there = (here + (1 if xh else -1)) % (2 * deep)
        return there // 2, there % 2, 1 - xh, y, c

    outer = pairs(shape, across)

    def by_head(own, mirrored):
        first = lax.axis_index("xh") == 0
        return jnp.where(first, own, mirrored), jnp.where(first, mirrored, own)

    def over_y(copies):
        return lax.all_to_all(copies, "y", 0, 0, tiled=True)

    def swapped(array):
        return lax.ppermute(array, AXES, other_core)

    def projections(own, mirrored):
        low, high = by_head(own, mirrored)
        picks = []
        for kind in range(3):
            cut = slice(kind * HEAD_DIM, (kind + 1) * HEAD_DIM)
            picks += [low[:, cut], high[:, cut]]
        return jnp.concatenate(picks, axis=1)

    def on_device(points, order, scan_ids, ln_gain, w_qkv, w_out):
        (copies,) = call(
            order_kernel, [(4, EXT, LANES)], [], points, order, scan_ids.reshape(1, ROWS)
        )
        w_qkv_far = [lax.ppermute(w_qkv[l], AXES, mirror) for l in range(2)]
        w_out_far = lax.ppermute(w_out, AXES, mirror)
        x_near = over_y(copies)
        x_far = swapped(x_near)
        weights = [projections(w_qkv[l], w_qkv_far[l]) for l in range(2)]
        outs = jnp.concatenate(by_head(w_out, w_out_far), axis=1)
        out_near, out_far = [], []
        for l in range(2):
            got = over_y(jnp.broadcast_to(outs[l], (4, ROWS, D)))
            out_near.append(got.reshape(HALF, D))
            out_far.append(swapped(got).reshape(HALF, D))
        (o_copies,) = call(
            first_kernel,
            [(4, PATCH, LANES)],
            [
                ((PATCH, D), BF16),
                ((PATCH, LANES), BF16),
                ((PATCH, 2 * LANES), BF16),
                ((2, HEAD_DIM + 16, PATCH), BF16),
                ((PATCH, LANES), BF16),
            ],
            x_near, x_far, ln_gain[0:1], weights[0],
        )
        o_near = over_y(o_copies)
        o_far = swapped(o_near)
        queries, kv_p, kv_q, stream = call(
            middle_kernel,
            [(2, HALF, LANES), (EXT, LANES), (EXT, LANES), (ROWS, D)],
            [((HALF, D), BF16), ((HALF, D), F32), ((HALF, D), BF16)],
            x_near, x_far, o_near, o_far, out_near[0], out_far[0], ln_gain[1:2], weights[1],
        )
        halo_p = lax.ppermute(kv_p, AXES, inner)
        halo_q = lax.ppermute(kv_q, AXES, outer)
        (parts,) = call(
            second_kernel,
            [(8, ROWS, LANES)],
            [
                ((PATCH, 2 * LANES), BF16),
                ((2, HEAD_DIM + 16, PATCH), BF16),
                ((HALF, LANES), BF16),
            ],
            queries, kv_p, kv_q, halo_p, halo_q,
        )
        parts = lax.all_to_all(parts, ("y", "c"), 0, 0, tiled=True)
        (result,) = call(
            last_kernel, [(ROWS, D)], [((ROWS, D), BF16)], parts, out_near[1], out_far[1], stream
        )
        return result

    curve_axes, head_axes = ("z", "xl"), ("xh", "y", "c")
    every = curve_axes + head_axes
    return jax.shard_map(
        on_device,
        mesh=Mesh(mesh.devices.reshape(shape), AXES),
        in_specs=(P(every, None), P(every, None), P(every), P(), P(None, None, head_axes), P(None, head_axes, None)),
        out_specs=P(every, None),
        check_vma=False,
    )
```

time: 194 us -> 159 us (0.82)
  waiting for transfers between devices: 49.9 us -> 24.6 us
  Pallas kernels: 0 us -> 24.8 us
  matrix products: 17.4 us -> 0 us
  starting transfers between devices: 51.1 us -> 67 us
  blocking collectives: 31.1 us -> 15.7 us
  between operations: 13.7 us -> 0.23 us
  loops' own time: 5.74 us -> 0 us
  local copies, waits for them, and re-layouts: 17.9 us -> 22.9 us
  other arithmetic: 5.82 us -> 2.72 us
    all_to_all x4, waiting for transfers between devices: 36.4 us -> 8.27 us  [the longest x1 6.52 us: on_device(): parts = lax.all_to_all(parts, ('y', 'c'), 0, 0, tiled=True)]
    pallas_call x0 -> x5, Pallas kernels: none -> 24.8 us  [call(): pl.pallas_call(kernel, out_shape=[jax.ShapeDtypeStruct(shape, BF16) for s...]
    ppermute x4 -> x9, starting transfers between devices: 28 us -> 48.7 us  [the longest x4 21.8 us: swapped(): return lax.ppermute(array, AXES, other_core)]
    dot_general x20 -> x0, matrix products: 17.4 us -> none  [the longest x8 4.98 us: one_block(): jnp.einsum('hqk,khd->qhd', probs, value_block, preferred_element_type=jnp...]
    all_to_all x3 -> x1, blocking collectives: 31.1 us -> 15.7 us  [over_y(): return lax.all_to_all(copies, 'y', 0, 0, tiled=True)]
    unnamed x12 -> x24, local copies, waits for them, and re-layouts: 0.8 us -> 8.75 us
    concatenate x0 -> x2, local copies, waits for them, and re-layouts: none -> 6.7 us  [projections(): return jnp.concatenate(picks, axis=1)]
    another operation x2 -> x0, loops' own time: 5.74 us -> none  [attend(): outputs = lax.map(one_block, jnp.arange(blocks_count))]
  transfers between devices with their start and end apart: 10 -> 13, of which waited for: 9 -> 4; matrix products, arithmetic and copies ran while one was open for 15% -> 11% of each run, Pallas kernels for 0% -> 13%
where the time goes in v1:
time: 159 us; the launch traced here: 158 us
  starting transfers between devices  67 us (42%)
  Pallas kernels  24.8 us (16%)
  waiting for transfers between devices  24.6 us (15%)
  local copies, waits for them, and re-layouts  22.9 us (14%)
  blocking collectives  15.7 us (10%)
  other arithmetic  2.72 us (2%)
    pallas_call x5, Pallas kernels, call(): pl.pallas_call(kernel, out_shape=[jax.ShapeDtypeStruct(shape, BF16) for s...  24.8 us
    ppermute x4, starting transfers between devices, swapped(): return lax.ppermute(array, AXES, other_core)  21.8 us
    all_to_all x1, blocking collectives, over_y(): return lax.all_to_all(copies, 'y', 0, 0, tiled=True)  15.7 us
    all_to_all x3, starting transfers between devices, over_y(): return lax.all_to_all(copies, 'y', 0, 0, tiled=True)  13.8 us
    ppermute x1, starting transfers between devices, on_device(): halo_q = lax.ppermute(kv_q, AXES, outer)  12.6 us
    ppermute x2, waiting for transfers between devices, on_device(): w_qkv_far = [lax.ppermute(w_qkv[l], AXES, mirror) for l in range(2)]  9.74 us
    unnamed x24, local copies, waits for them, and re-layouts  8.75 us
    concatenate x2, local copies, waits for them, and re-layouts, projections(): return jnp.concatenate(picks, axis=1)  6.7 us
  transfers between devices with their start and end apart: 13, of which 4 were waited for; matrix products, arithmetic and copies ran while one was open for 11% of the time, Pallas kernels for 13%

profile of v1, /device:TPU:1, one launch (start us, length us, event | category | flops | bytes accessed | tf_op | source)
XLA Modules:
  0.0 157.9 jit_solution(18335709398890190739)
XLA Ops:
  2.3 1.2 shard_map.64
  3.5 5.1 %all-to-all-start = ((bf16[4,1040,128]{2,1,0:T(8,128)(2,1)}), bf16[4,1040,128]{2,1,0:T(8,128)(2,1)S(1)}, u32[]{:S(2)}, u32[]{:S(2)}) async-start(bf16[4,1040,128]{2,1,0:T(8,128)(2,1)} %shard_map.64), calls=%async_computation | async-start | bytes 2129920 | tf_op jit(solution)/shard_map/all_to_all | solution.py:222
  8.7 4.4 %collective-permute-start.3 = (bf16[2,64,1024]{2,1,0:T(8,128)(2,1)S(1)}, bf16[2,64,1024]{2,1,0:T(8,128)(2,1)S(1)}, u32[]{:S(2)}, u32[]{:S(2)}) collective-permute-start(bf16[2,64,1024]{2,1,0:T(8,128)(2,1)S(1)} %copy-done.9), channel_id=1, source_target_pairs={{0,24},{1,25},{2,26},{3,27},{4,28},{5,29},{6,30},{7,31},{8,16},{9,... | collective-permute-start | bytes 786440 | tf_op jit(solution)/shard_map/ppermute | solution.py:240
  14.1 2.1 %collective-permute-start.1 = (bf16[1024,192]{1,0:T(8,128)(2,1)}, bf16[1024,192]{1,0:T(8,128)(2,1)}, u32[]{:S(2)}, u32[]{:S(2)}) collective-permute-start(bf16[1024,192]{1,0:T(8,128)(2,1)} %bitcast.1), channel_id=1, source_target_pairs={{0,24},{1,25},{2,26},{3,27},{4,28},{5,29},{6,30},{7,31},{8,16},{9,... | collective-permute-start | bytes 1179656 | tf_op jit(solution)/shard_map/ppermute | solution.py:239
  17.2 4.4 %collective-permute-start.5 = (bf16[1024,192]{1,0:T(8,128)(2,1)}, bf16[1024,192]{1,0:T(8,128)(2,1)}, u32[]{:S(2)}, u32[]{:S(2)}) collective-permute-start(bf16[1024,192]{1,0:T(8,128)(2,1)} %bitcast.5), channel_id=1, source_target_pairs={{0,24},{1,25},{2,26},{3,27},{4,28},{5,29},{6,30},{7,31},{8,16},{9,... | collective-permute-start | bytes 1179656 | tf_op jit(solution)/shard_map/ppermute | solution.py:239
  21.7 5.4 %collective-permute-start = (bf16[4,1040,128]{2,1,0:T(8,128)(2,1)S(1)}, bf16[4,1040,128]{2,1,0:T(8,128)(2,1)S(1)}, u32[]{:S(2)}, u32[]{:S(2)}) collective-permute-start(bf16[4,1040,128]{2,1,0:T(8,128)(2,1)S(1)} %all-to-all-done.near), channel_id=1, source_target_pairs={{0,1},{1,0},{2,3},{3,2},{4,5},{5,4},{6,7},{7,6},{8,9},{9,8},{10,11... | collective-permute-start | bytes 3194888 | tf_op jit(solution)/shard_map/ppermute | solution.py:225
  27.2 1.1 broadcast_in_dim.6
  28.3 4.5 %all-to-all-start.2 = ((bf16[4,128,1024]{2,1,0:T(8,128)(2,1)}), bf16[4,128,1024]{2,1,0:T(8,128)(2,1)S(1)}, u32[]{:S(2)}, u32[]{:S(2)}) async-start(bf16[4,128,1024]{2,1,0:T(8,128)(2,1)} %broadcast_in_dim.6), calls=%async_computation.2 | async-start | bytes 2097152 | tf_op jit(solution)/shard_map/all_to_all | solution.py:222
  32.8 9.7 %collective-permute-done.5 = bf16[1024,192]{1,0:T(8,128)(2,1)} collective-permute-done((bf16[1024,192]{1,0:T(8,128)(2,1)}, bf16[1024,192]{1,0:T(8,128)(2,1)}, u32[]{:S(2)}, u32[]{:S(2)}) %collective-permute-start.5) | collective-permute-done | bytes 393248 | tf_op jit(solution)/shard_map/ppermute | solution.py:239
  42.5 2.6 %broadcast_select_fusion = (bf16[1024,192]{1,0:T(8,128)(2,1)}, bf16[1024,192]{1,0:T(8,128)(2,1)}, bf16[1024,192]{1,0:T(8,128)(2,1)S(1)}, bf16[1024,192]{1,0:T(8,128)(2,1)S(1)}) fusion(bf16[1024,192]{1,0:T(8,128)(2,1)} %collective-permute-done.5, pred[]{:T(512)S(6)} %eq.2, bf16[1,1024,192]{2,1,0:T(8,128)(2,1)} %copy.10, ...), kind=kLoop, calls=%fused_computation.2 | loop fusion | flops 786432 | bytes 3145729 | tf_op jit(solution)/shard_map/jit(_where)/select_n | solution.py:219
  47.2 3.5 %concatenate.9.weights = bf16[1024,384]{1,0:T(8,128)(2,1)} concatenate(bf16[1024,64]{1,0:T(8,128)(2,1)} %get-tuple-element.34, bf16[1024,64]{1,0:T(8,128)(2,1)} %get-tuple-element.31, bf16[1024,64]{1,0:T(8,128)(2,1)} %get-tuple-element.33, bf16[1024,64]{1,0:T(8,128)(2,1)} %get-tuple-element.30, bf16[1024,64]{1,0:T(8,128)(2,1)} %get-tuple-element.32, ...), dimensions={1} | concatenate | bytes 1572864 | tf_op jit(solution)/shard_map/concatenate | solution.py:233
  50.7 1.1 copy-done.3
  51.8 8.0 %shard_map.65 = bf16[4,1024,128]{2,1,0:T(8,128)(2,1)S(1)} custom-call(bf16[4,1040,128]{2,1,0:T(8,128)(2,1)S(1)} %all-to-all-done.near, bf16[4,1040,128]{2,1,0:T(8,128)(2,1)S(1)} %collective-permute-done.far, f32[1,1024]{1,0:T(1,128)S(1)} %get-tuple-element.36.gain, bf16[1024,384]{1,0:T(8,128)(2,1)S(1)} %copy-done.3), custom_call_target="tpu_custom_call" | custom-call | tf_op jit(solution)/shard_map/pallas_call | solution.py:188
  60.8 15.7 %all_to_all.25.o_near = bf16[4,1024,128]{2,1,0:T(8,128)(2,1)} all-to-all(bf16[4,1024,128]{2,1,0:T(8,128)(2,1)} %copy-done.1), channel_id=1, replica_groups=mesh['z'=16,'xl'=2,'xh'=2,'y'=4,'c'=2] {'y'}, dimensions={0} | all-to-all | bytes 2097152 | tf_op jit(solution)/shard_map/all_to_all | solution.py:222
  76.5 1.2 broadcast_in_dim.7
  77.7 4.2 %all-to-all-start.4 = ((bf16[4,128,1024]{2,1,0:T(8,128)(2,1)}), bf16[4,128,1024]{2,1,0:T(8,128)(2,1)}, u32[]{:S(2)}, u32[]{:S(2)}) async-start(bf16[4,128,1024]{2,1,0:T(8,128)(2,1)} %broadcast_in_dim.7), calls=%async_computation.4 | async-start | bytes 2097152 | tf_op jit(solution)/shard_map/all_to_all | solution.py:222
  81.9 6.6 %collective-permute-start.4 = (bf16[4,128,1024]{2,1,0:T(8,128)(2,1)S(1)}, bf16[4,128,1024]{2,1,0:T(8,128)(2,1)}, u32[]{:S(2)}, u32[]{:S(2)}) collective-permute-start(bf16[4,128,1024]{2,1,0:T(8,128)(2,1)S(1)} %all-to-all-done.2), channel_id=1, source_target_pairs={{0,1},{1,0},{2,3},{3,2},{4,5},{5,4},{6,7},{7,6},{8,9},{9,8},{10,11... | collective-permute-start | bytes 3145736 | tf_op jit(solution)/shard_map/ppermute | solution.py:225
  88.5 1.9 %collective-permute-start.2 = (bf16[4,1024,128]{2,1,0:T(8,128)(2,1)}, bf16[4,1024,128]{2,1,0:T(8,128)(2,1)}, u32[]{:S(2)}, u32[]{:S(2)}) collective-permute-start(bf16[4,1024,128]{2,1,0:T(8,128)(2,1)} %all_to_all.25.o_near), channel_id=1, source_target_pairs={{0,1},{1,0},{2,3},{3,2},{4,5},{5,4},{6,7},{7,6},{8,9},{9,8},{10,11... | collective-permute-start | bytes 3145736 | tf_op jit(solution)/shard_map/ppermute | solution.py:225
  90.4 1.7 %all-to-all-done.4 = bf16[4,128,1024]{2,1,0:T(8,128)(2,1)} async-done(((bf16[4,128,1024]{2,1,0:T(8,128)(2,1)}), bf16[4,128,1024]{2,1,0:T(8,128)(2,1)}, u32[]{:S(2)}, u32[]{:S(2)}) %all-to-all-start.4) | async-done | bytes 1048608 | tf_op jit(solution)/shard_map/all_to_all | solution.py:222
  92.2 7.9 %collective-permute-start.8 = (bf16[4,128,1024]{2,1,0:T(8,128)(2,1)}, bf16[4,128,1024]{2,1,0:T(8,128)(2,1)}, u32[]{:S(2)}, u32[]{:S(2)}) collective-permute-start(bf16[4,128,1024]{2,1,0:T(8,128)(2,1)} %all-to-all-done.4), channel_id=1, source_target_pairs={{0,1},{1,0},{2,3},{3,2},{4,5},{5,4},{6,7},{7,6},{8,9},{9,8},{10,11... | collective-permute-start | bytes 3145736 | tf_op jit(solution)/shard_map/ppermute | solution.py:225
  100.1 2.0 %fusion.4 = (bf16[1024,64]{1,0:T(8,128)(2,1)S(1)}, bf16[1024,64]{1,0:T(8,128)(2,1)}, bf16[1024,64]{1,0:T(8,128)(2,1)}) fusion(bf16[1024,192]{1,0:T(8,128)(2,1)} %get-tuple-element.13), kind=kLoop, calls=%fused_computation.13 | loop fusion | bytes 786432 | tf_op jit(solution)/shard_map/slice | solution.py:232
  103.1 3.3 %concatenate.11.weights = bf16[1024,384]{1,0:T(8,128)(2,1)} concatenate(bf16[1024,64]{1,0:T(8,128)(2,1)} %get-tuple-element.26, bf16[1024,64]{1,0:T(8,128)(2,1)} %get-tuple-element.23, bf16[1024,64]{1,0:T(8,128)(2,1)} %get-tuple-element.25, bf16[1024,64]{1,0:T(8,128)(2,1)} %get-tuple-element.22, bf16[1024,64]{1,0:T(8,128)(2,1)} %get-tuple-element.24, ...), dimensions={1} | concatenate | bytes 1572864 | tf_op jit(solution)/shard_map/concatenate | solution.py:233
  106.4 1.2 copy-done
  107.6 1.1 copy-done.2
  108.7 6.9 %shard_map.66 = (bf16[2,512,128]{2,1,0:T(8,128)(2,1)S(1)}, bf16[1040,128]{1,0:T(8,128)(2,1)S(1)}, bf16[1040,128]{1,0:T(8,128)(2,1)S(1)}, bf16[128,1024]{1,0:T(8,128)(2,1)S(1)}) custom-call(bf16[4,1040,128]{2,1,0:T(8,128)(2,1)S(1)} %all-to-all-done.near, bf16[4,1040,128]{2,1,0:T(8,128)(2,1)S(1)} %collective-permute-done.far, ...), custom_call_target="tpu_custom_call" | custom-call | tf_op jit(solution)/shard_map/pallas_call | solution.py:188
  115.6 3.5 %collective-permute-start.6 = (bf16[1040,128]{1,0:T(8,128)(2,1)S(1)}, bf16[1040,128]{1,0:T(8,128)(2,1)S(1)}, u32[]{:S(2)}, u32[]{:S(2)}) collective-permute-start(bf16[1040,128]{1,0:T(8,128)(2,1)S(1)} %get-tuple-element.10.kv_p), channel_id=1, source_target_pairs={{0,8},{1,9},{2,10},{3,11},{4,12},{5,13},{6,14},{7,15},{8,0},{9,1},... | collective-permute-start | bytes 798728 | tf_op jit(solution)/shard_map/ppermute | solution.py:270
  119.1 12.6 %collective-permute-start.7 = (bf16[1040,128]{1,0:T(8,128)(2,1)S(1)}, bf16[1040,128]{1,0:T(8,128)(2,1)S(1)}, u32[]{:S(2)}, u32[]{:S(2)}) collective-permute-start(bf16[1040,128]{1,0:T(8,128)(2,1)S(1)} %get-tuple-element.11.kv_q), channel_id=1, source_target_pairs={{0,504},{1,505},{2,506},{3,507},{4,508},{5,509},{6,510},{7,511},{8... | collective-permute-start | bytes 798728 | tf_op jit(solution)/shard_map/ppermute | solution.py:271
  131.7 6.6 %collective-permute-done.7.halo_q = bf16[1040,128]{1,0:T(8,128)(2,1)S(1)} collective-permute-done((bf16[1040,128]{1,0:T(8,128)(2,1)S(1)}, bf16[1040,128]{1,0:T(8,128)(2,1)S(1)}, u32[]{:S(2)}, u32[]{:S(2)}) %collective-permute-start.7) | collective-permute-done | bytes 266272 | tf_op jit(solution)/shard_map/ppermute | solution.py:271
  138.3 5.9 %shard_map.67 = bf16[8,128,128]{2,1,0:T(8,128)(2,1)} custom-call(bf16[2,512,128]{2,1,0:T(8,128)(2,1)S(1)} %get-tuple-element.9.queries, bf16[1040,128]{1,0:T(8,128)(2,1)S(1)} %get-tuple-element.10.kv_p, bf16[1040,128]{1,0:T(8,128)(2,1)S(1)} %get-tuple-element.11.kv_q, bf16[1040,128]{1,0:T(8,128)(2,1)S(1)} %collective-permute-done.6.halo_p, ...), custom_call_target="tpu_custom_call" | custom-call | tf_op jit(solution)/shard_map/pallas_call | solution.py:188
  144.2 4.4 %all-to-all-start.3 = ((bf16[8,128,128]{2,1,0:T(8,128)(2,1)}), bf16[8,128,128]{2,1,0:T(8,128)(2,1)S(1)}, u32[]{:S(2)}, u32[]{:S(2)}) async-start(bf16[8,128,128]{2,1,0:T(8,128)(2,1)} %shard_map.67), calls=%async_computation.3 | async-start | bytes 524288 | tf_op jit(solution)/shard_map/all_to_all | solution.py:282
  148.7 6.5 %all-to-all-done.3.parts = bf16[8,128,128]{2,1,0:T(8,128)(2,1)S(1)} async-done(((bf16[8,128,128]{2,1,0:T(8,128)(2,1)}), bf16[8,128,128]{2,1,0:T(8,128)(2,1)S(1)}, u32[]{:S(2)}, u32[]{:S(2)}) %all-to-all-start.3) | async-done | bytes 262176 | tf_op jit(solution)/shard_map/all_to_all | solution.py:282
  155.2 2.7 %shard_map.68 = bf16[128,1024]{1,0:T(8,128)(2,1)} custom-call(bf16[8,128,128]{2,1,0:T(8,128)(2,1)S(1)} %all-to-all-done.3.parts, bf16[512,1024]{1,0:T(8,128)(2,1)} %bitcast.7.w_near, bf16[512,1024]{1,0:T(8,128)(2,1)} %bitcast.8.w_far, bf16[128,1024]{1,0:T(8,128)(2,1)S(1)} %get-tuple-element.12.stream), custom_call_target="tpu_custom_call" | custom-call | tf_op jit(solution)/shard_map/pallas_call | solution.py:188
  (37 shorter events, 8.5 us)
Async XLA Ops:
  0.0 0.9 copy-start.4
  1.0 0.7 copy-start.5
  1.6 0.7 copy-start.6
  3.5 5.1 %copy-start.9 = (bf16[2,64,1024]{2,1,0:T(8,128)(2,1)S(1)}, bf16[2,64,1024]{2,1,0:T(8,128)(2,1)}, u32[]{:S(2)}) copy-start(bf16[2,64,1024]{2,1,0:T(8,128)(2,1)} %param.11) | copy-start | bytes 786436
  3.5 9.5 %copy-start.8 = (bf16[2,1024,192]{1,2,0:T(8,128)(2,1)S(1)}, bf16[2,1024,192]{1,2,0:T(8,128)(2,1)}, u32[]{:S(2)}) copy-start(bf16[2,1024,192]{1,2,0:T(8,128)(2,1)} %param.10) | copy-start | bytes 2359300
  3.5 18.1 %all-to-all-start = ((bf16[4,1040,128]{2,1,0:T(8,128)(2,1)}), bf16[4,1040,128]{2,1,0:T(8,128)(2,1)S(1)}, u32[]{:S(2)}, u32[]{:S(2)}) async-start(bf16[4,1040,128]{2,1,0:T(8,128)(2,1)} %shard_map.64), calls=%async_computation | async-start | bytes 2129920 | tf_op jit(solution)/shard_map/all_to_all | solution.py:222
  8.7 18.4 %collective-permute-start.3 = (bf16[2,64,1024]{2,1,0:T(8,128)(2,1)S(1)}, bf16[2,64,1024]{2,1,0:T(8,128)(2,1)S(1)}, u32[]{:S(2)}, u32[]{:S(2)}) collective-permute-start(bf16[2,64,1024]{2,1,0:T(8,128)(2,1)S(1)} %copy-done.9), channel_id=1, source_target_pairs={{0,24},{1,25},{2,26},{3,27},{4,28},{5,29},{6,30},{7,31},{8,16},{9,... | collective-permute-start | bytes 786440 | tf_op jit(solution)/shard_map/ppermute | solution.py:240
  13.1 8.5 %copy-start.10 = (f32[2,1024]{1,0:T(2,128)S(1)}, f32[2,1024]{1,0:T(2,128)}, u32[]{:S(2)}) copy-start(f32[2,1024]{1,0:T(2,128)} %param.9) | copy-start | bytes 24580
  14.1 18.6 %collective-permute-start.1 = (bf16[1024,192]{1,0:T(8,128)(2,1)}, bf16[1024,192]{1,0:T(8,128)(2,1)}, u32[]{:S(2)}, u32[]{:S(2)}) collective-permute-start(bf16[1024,192]{1,0:T(8,128)(2,1)} %bitcast.1), channel_id=1, source_target_pairs={{0,24},{1,25},{2,26},{3,27},{4,28},{5,29},{6,30},{7,31},{8,16},{9,... | collective-permute-start | bytes 1179656 | tf_op jit(solution)/shard_map/ppermute | solution.py:239
  17.2 25.3 %collective-permute-start.5 = (bf16[1024,192]{1,0:T(8,128)(2,1)}, bf16[1024,192]{1,0:T(8,128)(2,1)}, u32[]{:S(2)}, u32[]{:S(2)}) collective-permute-start(bf16[1024,192]{1,0:T(8,128)(2,1)} %bitcast.5), channel_id=1, source_target_pairs={{0,24},{1,25},{2,26},{3,27},{4,28},{5,29},{6,30},{7,31},{8,16},{9,... | collective-permute-start | bytes 1179656 | tf_op jit(solution)/shard_map/ppermute | solution.py:239
  21.7 29.0 %collective-permute-start = (bf16[4,1040,128]{2,1,0:T(8,128)(2,1)S(1)}, bf16[4,1040,128]{2,1,0:T(8,128)(2,1)S(1)}, u32[]{:S(2)}, u32[]{:S(2)}) collective-permute-start(bf16[4,1040,128]{2,1,0:T(8,128)(2,1)S(1)} %all-to-all-done.near), channel_id=1, source_target_pairs={{0,1},{1,0},{2,3},{3,2},{4,5},{5,4},{6,7},{7,6},{8,9},{9,8},{10,11... | collective-permute-start | bytes 3194888 | tf_op jit(solution)/shard_map/ppermute | solution.py:225
  28.3 32.5 %all-to-all-start.2 = ((bf16[4,128,1024]{2,1,0:T(8,128)(2,1)}), bf16[4,128,1024]{2,1,0:T(8,128)(2,1)S(1)}, u32[]{:S(2)}, u32[]{:S(2)}) async-start(bf16[4,128,1024]{2,1,0:T(8,128)(2,1)} %broadcast_in_dim.6), calls=%async_computation.2 | async-start | bytes 2097152 | tf_op jit(solution)/shard_map/all_to_all | solution.py:222
  50.7 1.1 copy-start.3
  59.8 1.0 copy-start.1
  77.7 14.5 %all-to-all-start.4 = ((bf16[4,128,1024]{2,1,0:T(8,128)(2,1)}), bf16[4,128,1024]{2,1,0:T(8,128)(2,1)}, u32[]{:S(2)}, u32[]{:S(2)}) async-start(bf16[4,128,1024]{2,1,0:T(8,128)(2,1)} %broadcast_in_dim.7), calls=%async_computation.4 | async-start | bytes 2097152 | tf_op jit(solution)/shard_map/all_to_all | solution.py:222
  81.9 24.5 %collective-permute-start.4 = (bf16[4,128,1024]{2,1,0:T(8,128)(2,1)S(1)}, bf16[4,128,1024]{2,1,0:T(8,128)(2,1)}, u32[]{:S(2)}, u32[]{:S(2)}) collective-permute-start(bf16[4,128,1024]{2,1,0:T(8,128)(2,1)S(1)} %all-to-all-done.2), channel_id=1, source_target_pairs={{0,1},{1,0},{2,3},{3,2},{4,5},{5,4},{6,7},{7,6},{8,9},{9,8},{10,11... | collective-permute-start | bytes 3145736 | tf_op jit(solution)/shard_map/ppermute | solution.py:225
  88.5 17.9 %collective-permute-start.2 = (bf16[4,1024,128]{2,1,0:T(8,128)(2,1)}, bf16[4,1024,128]{2,1,0:T(8,128)(2,1)}, u32[]{:S(2)}, u32[]{:S(2)}) collective-permute-start(bf16[4,1024,128]{2,1,0:T(8,128)(2,1)} %all_to_all.25.o_near), channel_id=1, source_target_pairs={{0,1},{1,0},{2,3},{3,2},{4,5},{5,4},{6,7},{7,6},{8,9},{9,8},{10,11... | collective-permute-start | bytes 3145736 | tf_op jit(solution)/shard_map/ppermute | solution.py:225
  92.2 9.9 %copy-start.7 = (bf16[1024,192]{1,0:T(8,128)(2,1)S(1)}, bf16[1024,192]{1,0:T(8,128)(2,1)}, u32[]{:S(2)}) copy-start(bf16[1024,192]{1,0:T(8,128)(2,1)} %get-tuple-element.14) | copy-start | bytes 1179652
  92.2 56.5 %collective-permute-start.8 = (bf16[4,128,1024]{2,1,0:T(8,128)(2,1)}, bf16[4,128,1024]{2,1,0:T(8,128)(2,1)}, u32[]{:S(2)}, u32[]{:S(2)}) collective-permute-start(bf16[4,128,1024]{2,1,0:T(8,128)(2,1)} %all-to-all-done.4), channel_id=1, source_target_pairs={{0,1},{1,0},{2,3},{3,2},{4,5},{5,4},{6,7},{7,6},{8,9},{9,8},{10,11... | collective-permute-start | bytes 3145736 | tf_op jit(solution)/shard_map/ppermute | solution.py:225
  106.4 1.2 copy-start
  107.6 1.1 copy-start.2
  115.6 16.1 %collective-permute-start.6 = (bf16[1040,128]{1,0:T(8,128)(2,1)S(1)}, bf16[1040,128]{1,0:T(8,128)(2,1)S(1)}, u32[]{:S(2)}, u32[]{:S(2)}) collective-permute-start(bf16[1040,128]{1,0:T(8,128)(2,1)S(1)} %get-tuple-element.10.kv_p), channel_id=1, source_target_pairs={{0,8},{1,9},{2,10},{3,11},{4,12},{5,13},{6,14},{7,15},{8,0},{9,1},... | collective-permute-start | bytes 798728 | tf_op jit(solution)/shard_map/ppermute | solution.py:270
  119.1 19.2 %collective-permute-start.7 = (bf16[1040,128]{1,0:T(8,128)(2,1)S(1)}, bf16[1040,128]{1,0:T(8,128)(2,1)S(1)}, u32[]{:S(2)}, u32[]{:S(2)}) collective-permute-start(bf16[1040,128]{1,0:T(8,128)(2,1)S(1)} %get-tuple-element.11.kv_q), channel_id=1, source_target_pairs={{0,504},{1,505},{2,506},{3,507},{4,508},{5,509},{6,510},{7,511},{8... | collective-permute-start | bytes 798728 | tf_op jit(solution)/shard_map/ppermute | solution.py:271
  144.2 11.0 %all-to-all-start.3 = ((bf16[8,128,128]{2,1,0:T(8,128)(2,1)}), bf16[8,128,128]{2,1,0:T(8,128)(2,1)S(1)}, u32[]{:S(2)}, u32[]{:S(2)}) async-start(bf16[8,128,128]{2,1,0:T(8,128)(2,1)} %shard_map.67), calls=%async_computation.3 | async-start | bytes 524288 | tf_op jit(solution)/shard_map/all_to_all | solution.py:282

commit v2 on v1

v2 whole, which is shorter than its diff:
```python
import functools

import jax
import jax.numpy as jnp
import numpy as np
from jax import lax
from jax.experimental import pallas as pl
from jax.experimental.pallas import tpu as pltpu
from jax.sharding import Mesh
from jax.sharding import PartitionSpec as P

HEAD_DIM = 64
D = 1024
ROWS = 128
PATCH = 1024
HALF = 512
LANES = 128
BLOCKS = D // LANES
EXT = D + 16
EPSILON = 1e-05
FAR = -1e30
AXES = ("z", "xl", "xh", "y", "c")
F32 = jnp.float32
BF16 = jnp.bfloat16


def pairs(shape, move):
    result = []
    for i in range(int(np.prod(shape))):
        place = tuple(int(v) for v in np.unravel_index(i, shape))
        result.append((i, int(np.ravel_multi_index(move(*place), shape))))
    return result


def dot(a, b):
    return lax.dot_general(a, b, (((1,), (0,)), ((), ())), preferred_element_type=F32)


def dot_nt(a, b):
    return lax.dot_general(a, b, (((1,), (1,)), ((), ())), preferred_element_type=F32)


def layer_norm(values, gain):
    center = values - jnp.mean(values, axis=-1, keepdims=True)
    spread = jnp.mean(center * center, axis=-1, keepdims=True)
    return (center * lax.rsqrt(spread + EPSILON) * gain).astype(BF16)


def side_by_side(ref, index):
    return jnp.concatenate([ref[index, b * LANES : (b + 1) * LANES, :] for b in range(BLOCKS)], axis=1)


def tag_columns(rows):
    return jnp.transpose(jnp.concatenate(rows, axis=0))


def one_hot(columns, block):
    lane = lax.broadcasted_iota(jnp.int32, (ROWS, LANES), 1).astype(F32)
    return columns[:, block : block + 1] == lane


def attend(queries, hot, keys_ref, values_ref):
    lane = lax.broadcasted_iota(jnp.int32, queries.shape, 1)
    results = []
    for head in range(2):
        own = jnp.where(lane // HEAD_DIM == head, queries, jnp.zeros_like(queries))
        scores = dot_nt(keys_ref[...], jnp.concatenate([own, hot], axis=1))
        top = jnp.max(scores, axis=0, keepdims=True)
        probs = jnp.exp(scores - top).astype(BF16)
        sums = dot(values_ref[head], probs)
        results.append(sums[:HEAD_DIM] / sums[HEAD_DIM : HEAD_DIM + 1])
    return jnp.transpose(jnp.concatenate(results, axis=0)).astype(BF16)


def order_kernel(points, order, tags, out):
    row = lax.broadcasted_iota(jnp.int32, (ROWS, ROWS), 0)
    picks = jnp.transpose((row == order[...]).astype(F32)).astype(BF16)
    ordered = dot(picks, points[...]).astype(BF16)
    tag_rows = jnp.broadcast_to(tags[...].astype(F32), (16, LANES)).astype(BF16)
    for copy in range(4):
        for b in range(BLOCKS):
            out[copy, b * LANES : (b + 1) * LANES, :] = ordered[:, b * LANES : (b + 1) * LANES]
        out[copy, D:, :] = tag_rows


def joined(own, mirrored, kind):
    cut = slice(kind * HEAD_DIM, (kind + 1) * HEAD_DIM)
    return jnp.concatenate([own[cut, :], mirrored[cut, :]], axis=0)


def project(normed, own, mirrored, queries, keys, turned):
    both = jnp.concatenate([joined(own, mirrored, 0), joined(own, mirrored, 1)], axis=0)
    found = dot_nt(normed[...], both).astype(BF16)
    queries[...] = found[:, :LANES] * jnp.asarray(HEAD_DIM**-0.5, BF16)
    keys[...] = found[:, LANES:]
    turned[...] = dot_nt(joined(own, mirrored, 2), normed[...]).astype(BF16)


def put_values(values_ref, span, turned, swap):
    for head in range(2):
        from_head = 1 - head if swap else head
        values_ref[head, :HEAD_DIM, span] = turned[from_head * HEAD_DIM : (from_head + 1) * HEAD_DIM]


def first_kernel(near, far, gain, own, mirrored, out, normed, queries, keys, turned, values, hots):
    rows = []
    for s, ref in enumerate((near, far)):
        for y in range(4):
            block = s * 4 + y
            normed[block * ROWS : (block + 1) * ROWS, :] = layer_norm(
                side_by_side(ref, y).astype(F32), gain[...]
            )
            rows.append(ref[y, D:, :].astype(F32)[:1])
    columns = tag_columns(rows)
    project(normed, own, mirrored, queries, keys.at[:, :LANES], turned)
    put_values(values, slice(0, PATCH), turned, False)
    values[:, HEAD_DIM:, :] = jnp.ones((2, 16, PATCH), BF16)
    for block in range(8):
        hot = one_hot(columns, block)
        span = slice(block * ROWS, (block + 1) * ROWS)
        hots[span, :] = jnp.where(hot, 1.0, 0.0).astype(BF16)
        keys[span, LANES:] = jnp.where(hot, 0.0, FAR).astype(BF16)
    for part in range(4):
        span = slice(part * 256, (part + 1) * 256)
        result = attend(queries[span, :], hots[span, :], keys, values)
        for copy in range(4):
            out[copy, span, :] = result


def half_of(part):
    xh = lax.axis_index("xh")
    return xh if part else 1 - xh


def middle_kernel(
    part, near, far, o_near, o_far, w_near, w_far, gain, own, mirrored,
    q_out, kv, st_out, heads, update, normed, turned,
):
    my_y, half = lax.axis_index("y"), half_of(part)
    for s in range(2):
        for yy in range(2):
            y = half * 2 + yy
            span = slice((s * 2 + yy) * ROWS, (s * 2 + yy + 1) * ROWS)
            at_near = pl.ds(pl.multiple_of((s * 4 + y) * ROWS, ROWS), ROWS)
            at_far = pl.ds(pl.multiple_of(((1 - s) * 4 + y) * ROWS, ROWS), ROWS)
            for g in range(4):
                heads[span, g * LANES : (g + 1) * LANES] = o_near[g, at_near, :]
                heads[span, (g + 4) * LANES : (g + 5) * LANES] = o_far[g, at_far, :]
    update[...] = dot(heads[:, :HALF], w_near[...]) + dot(heads[:, HALF:], w_far[...])
    rows = []
    for s, ref in enumerate((near, far)):
        for yy in range(2):
            y = half * 2 + yy
            span = slice((s * 2 + yy) * ROWS, (s * 2 + yy + 1) * ROWS)
            stream = (side_by_side(ref, y).astype(F32) + update[span, :]).astype(BF16)
            normed[span, :] = layer_norm(stream.astype(F32), gain[...])
            rows.append(ref[y, D:, :].astype(F32)[:1])
            if s == 0:

                @pl.when(y == my_y)
                def _(stream=stream):
                    st_out[...] = stream

    project(normed, own, mirrored, q_out, kv.at[:HALF, :], turned)
    for b in range(4):
        kv[HALF + b * LANES : HALF + (b + 1) * LANES, :] = turned[:, b * LANES : (b + 1) * LANES]
    kv[D:, :] = jnp.concatenate(rows + [jnp.zeros((12, LANES), F32)], axis=0).astype(BF16)


def second_kernel(part, *refs):
    if part:
        queries, mine, other, had, out, keys, values, hots = refs
    else:
        queries, mine, other, out, keys, values, hots = refs
    half, c = half_of(part), lax.axis_index("c")
    keys[:HALF, :LANES] = mine[:HALF, :]
    keys[HALF:, :HEAD_DIM] = other[:HALF, HEAD_DIM:]
    keys[HALF:, HEAD_DIM:LANES] = other[:HALF, :HEAD_DIM]
    for b in range(4):
        cut = slice(HALF + b * LANES, HALF + (b + 1) * LANES)
        put_values(values, slice(b * LANES, (b + 1) * LANES), mine[cut, :], False)
        put_values(values, slice(HALF + b * LANES, HALF + (b + 1) * LANES), other[cut, :], True)
    values[:, HEAD_DIM:, :] = jnp.ones((2, 16, PATCH), BF16)
    columns = tag_columns([mine[D:, :].astype(F32)[:4], other[D:, :].astype(F32)[:4]])
    for block in range(8):
        hot = one_hot(columns, block)
        span = slice(block * ROWS, (block + 1) * ROWS)
        if block < 4:
            hots[span, :] = jnp.where(hot, 1.0, 0.0).astype(BF16)
        keys[span, LANES:] = jnp.where(hot, 0.0, FAR).astype(BF16)
    for s in range(2):
        span = slice(s * 256, (s + 1) * 256)
        result = attend(queries[span, :], hots[span, :], keys, values)
        core = c if s == 0 else 1 - c
        for yy in range(2):
            block = result[yy * ROWS : (yy + 1) * ROWS]
            if part:
                out[(half * 2 + yy) * 2 + core] = block
                out[((1 - half) * 2 + yy) * 2 + core] = had[s * 2 + yy]
            else:
                out[s * 2 + yy] = block


def last_kernel(parts, w_near, w_far, stream_p, stream_q, out, heads):
    c, y_half = lax.axis_index("c"), lax.axis_index("y") // 2
    for s in range(2):
        core = c if s == 0 else 1 - c
        for y in range(4):
            heads[:, (s * 4 + y) * LANES : (s * 4 + y + 1) * LANES] = parts[y * 2 + core]
    update = dot(heads[:, :HALF], w_near[...]) + dot(heads[:, HALF:], w_far[...])

    def put(stream):
        out[...] = (stream[...].astype(F32) + update).astype(BF16)

    pl.when(y_half == half_of(0))(lambda: put(stream_p))
    pl.when(y_half == half_of(1))(lambda: put(stream_q))


def relay_kernel(own, far, ready, out):
    for copy in range(out.shape[0]):
        out[copy, : own.shape[0]] = own[...]
        out[copy, own.shape[0] :] = far[...]


def pass_kernel(array, ready, out):
    out[...] = array[...]


def call(kernel, micros, outs, scratch, *args, wait_for=()):
    vmem, anywhere = pl.BlockSpec(memory_space=pltpu.VMEM), pl.BlockSpec(memory_space=pl.ANY)
    return pl.pallas_call(
        kernel,
        out_shape=[jax.ShapeDtypeStruct(shape, BF16) for shape in outs],
        in_specs=[vmem] * len(args) + [anywhere] * len(wait_for),
        out_specs=[vmem] * len(outs),
        scratch_shapes=[pltpu.VMEM(shape, dtype) for shape, dtype in scratch],
        compiler_params=pltpu.CompilerParams(vmem_limit_bytes=16 * 1024 * 1024),
        cost_estimate=pl.CostEstimate(
            flops=int(micros * 1.1e9), bytes_accessed=0, transcendentals=0
        ),
    )(*args, *wait_for)


def solution(mesh):
    curve, heads = mesh.shape["curve"], mesh.shape["head"]
    shape = (curve // 2, 2, 2, heads // 4, 2)
    deep = shape[0]
    other_core = pairs(shape, lambda z, xl, xh, y, c: (z, xl, xh, y, 1 - c))
    mirror = pairs(shape, lambda z, xl, xh, y, c: (z, 1 - xl, 1 - xh, y, c))
    inner = pairs(shape, lambda z, xl, xh, y, c: (z, xl, 1 - xh, y, c))

    def across(z, xl, xh, y, c):
        here = z * 2 + xl
        there = (here + (1 if xh else -1)) % (2 * deep)
        return there // 2, there % 2, 1 - xh, y, c

    outer = pairs(shape, across)

    def over_y(copies):
        return lax.all_to_all(copies, "y", 0, 0, tiled=True)

    def swapped(array):
        return lax.ppermute(array, AXES, other_core)

    def on_device(points, order, scan_ids, ln_gain, w_qkv, w_out):
        w_turned = jnp.swapaxes(w_qkv, 1, 2)
        (copies,) = call(
            order_kernel, 1.2, [(4, EXT, LANES)], [], points, order, scan_ids.reshape(1, ROWS)
        )
        first_far = lax.ppermute(w_turned[0], AXES, mirror)
        w_out_far = lax.ppermute(w_out, AXES, mirror)
        x_near = over_y(copies)
        x_near, first_far, w_out_far = lax.optimization_barrier((x_near, first_far, w_out_far))
        x_far = swapped(x_near)

        def gathered_out(layer, ready):
            (outs,) = call(
                relay_kernel, 1, [(4, ROWS, D)], [], w_out[layer], w_out_far[layer], wait_for=(ready,)
            )
            return over_y(outs)

        out_near = gathered_out(0, x_near)
        (second_own,) = call(
            pass_kernel, 1, [(3 * HEAD_DIM, D)], [], w_turned[1], wait_for=(x_near,)
        )
        second_far = lax.ppermute(second_own, AXES, mirror)
        (o_copies,) = call(
            first_kernel,
            8,
            [(4, PATCH, LANES)],
            [
                ((PATCH, D), BF16),
                ((PATCH, LANES), BF16),
                ((PATCH, 2 * LANES), BF16),
                ((LANES, PATCH), BF16),
                ((2, HEAD_DIM + 16, PATCH), BF16),
                ((PATCH, LANES), BF16),
            ],
            x_near, x_far, ln_gain[0:1], w_turned[0], first_far,
        )
        o_copies, out_near = lax.optimization_barrier((o_copies, out_near))
        out_far = swapped(out_near)
        o_near = over_y(o_copies)
        o_near, second_far, out_far = lax.optimization_barrier((o_near, second_far, out_far))
        o_far = swapped(o_near)
        out_first = out_near.reshape(HALF, D), out_far.reshape(HALF, D)
        last_near = gathered_out(1, o_near)
        middle, halos = [], []
        for part, links in enumerate((inner, outer)):
            middle.append(
                call(
                    functools.partial(middle_kernel, part),
                    4,
                    [(HALF, LANES), (EXT, LANES), (ROWS, D)],
                    [((HALF, D), BF16), ((HALF, D), F32), ((HALF, D), BF16), ((LANES, HALF), BF16)],
                    x_near, x_far, o_near, o_far, *out_first, ln_gain[1:2], second_own, second_far,
                )
            )
            halos.append(lax.ppermute(middle[part][1], AXES, links))
        halos[0], *middle[1] = lax.optimization_barrier((halos[0], *middle[1]))
        parts = None
        for part in range(2):
            queries, kv, _ = middle[part]
            (parts,) = call(
                functools.partial(second_kernel, part),
                3,
                [(8 if part else 4, ROWS, LANES)],
                [
                    ((PATCH, 2 * LANES), BF16),
                    ((2, HEAD_DIM + 16, PATCH), BF16),
                    ((HALF, LANES), BF16),
                ],
                queries, kv, halos[part], *([parts] if part else []),
            )
            if part == 0:
                last_near, parts = lax.optimization_barrier((last_near, parts))
                out_second = last_near.reshape(HALF, D), swapped(last_near).reshape(HALF, D)
        parts = lax.all_to_all(parts, ("y", "c"), 0, 0, tiled=True)
        (result,) = call(
            last_kernel, 1.5, [(ROWS, D)], [((ROWS, D), BF16)],
            parts, *out_second, middle[0][2], middle[1][2],
        )
        return result

    curve_axes, head_axes = ("z", "xl"), ("xh", "y", "c")
    every = curve_axes + head_axes
    return jax.shard_map(
        on_device,
        mesh=Mesh(mesh.devices.reshape(shape), AXES),
        in_specs=(P(every, None), P(every, None), P(every), P(), P(None, None, head_axes), P(None, head_axes, None)),
        out_specs=P(every, None),
        check_vma=False,
    )
```

time: 159 us -> 143 us (0.90)
  local copies, waits for them, and re-layouts: 22.9 us -> 9.17 us
  waiting for transfers between devices: 24.6 us -> 33.6 us
  starting transfers between devices: 67 us -> 59.3 us
  blocking collectives: 15.7 us -> 11.3 us
  Pallas kernels: 24.8 us -> 28.5 us
  other arithmetic: 2.72 us -> 0 us
    ppermute x1, waiting for transfers between devices: 0.01 us -> 9.33 us  [on_device(): w_out_far = lax.ppermute(w_out, AXES, mirror)]
    ppermute x4, starting transfers between devices: 21.8 us -> 15 us  [swapped(): return lax.ppermute(array, AXES, other_core)]
    concatenate x2 -> x0, local copies, waits for them, and re-layouts: 6.7 us -> none  [projections(): return jnp.concatenate(picks, axis=1)]
    all_to_all x1 -> x0, waiting for transfers between devices: 6.52 us -> none  [on_device(): parts = lax.all_to_all(parts, ('y', 'c'), 0, 0, tiled=True)]
    slice x5 -> x0, local copies, waits for them, and re-layouts: 5.17 us -> none  [the longest x4 5.12 us: projections(): picks += [low[:, cut], high[:, cut]]]
    all_to_all x1 -> x0, starting transfers between devices: 4.44 us -> none  [on_device(): parts = lax.all_to_all(parts, ('y', 'c'), 0, 0, tiled=True)]
    all_to_all x1, blocking collectives: 15.7 us -> 11.3 us  [on_device(): parts = lax.all_to_all(parts, ('y', 'c'), 0, 0, tiled=True)]
    all_to_all x3 -> x4, waiting for transfers between devices: 1.75 us -> 6.04 us  [over_y(): return lax.all_to_all(copies, 'y', 0, 0, tiled=True)]
  transfers between devices with their start and end apart: 13 -> 13, of which waited for: 4 -> 6; matrix products, arithmetic and copies ran while one was open for 11% -> 0% of each run, Pallas kernels for 13% -> 18%
where the time goes in v2:
time: 143 us; the launch traced here: 142 us
  starting transfers between devices  59.3 us (41%)
  waiting for transfers between devices  33.6 us (23%)
  Pallas kernels  28.5 us (20%)
  blocking collectives  11.3 us (8%)
  local copies, waits for them, and re-layouts  9.17 us (6%)
    pallas_call x10, Pallas kernels, call(): pl.pallas_call(kernel, out_shape=[jax.ShapeDtypeStruct(shape, BF16) for s...  28.5 us
    all_to_all x4, starting transfers between devices, over_y(): return lax.all_to_all(copies, 'y', 0, 0, tiled=True)  17.1 us
    ppermute x2, starting transfers between devices, on_device(): halos.append(lax.ppermute(middle[part][1], AXES, links))  16.4 us
    ppermute x4, starting transfers between devices, swapped(): return lax.ppermute(array, AXES, other_core)  15 us
    all_to_all x1, blocking collectives, on_device(): parts = lax.all_to_all(parts, ('y', 'c'), 0, 0, tiled=True)  11.3 us
    ppermute x1, waiting for transfers between devices, on_device(): second_far = lax.ppermute(second_own, AXES, mirror)  9.74 us
    ppermute x1, waiting for transfers between devices, on_device(): w_out_far = lax.ppermute(w_out, AXES, mirror)  9.33 us
    unnamed x38, local copies, waits for them, and re-layouts  9.07 us
  transfers between devices with their start and end apart: 13, of which 6 were waited for; matrix products, arithmetic and copies ran while one was open for 0% of the time, Pallas kernels for 18%

profile of v2, /device:TPU:1, one launch (start us, length us, event | category | flops | bytes accessed | tf_op | source)
XLA Modules:
  0.0 142.3 jit_solution(17602046536052916676)
XLA Ops:
  2.3 1.3 shard_map.64
  3.5 5.1 %all-to-all-start = ((bf16[4,1040,128]{2,1,0:T(8,128)(2,1)}), bf16[4,1040,128]{2,1,0:T(8,128)(2,1)S(1)}, u32[]{:S(2)}, u32[]{:S(2)}) async-start(bf16[4,1040,128]{2,1,0:T(8,128)(2,1)} %shard_map.64), calls=%async_computation | async-start | bytes 2129920 | tf_op jit(solution)/shard_map/all_to_all | solution.py:260
  8.8 4.5 %collective-permute-start = (bf16[192,1024]{1,0:T(8,128)(2,1)S(1)}, bf16[192,1024]{1,0:T(8,128)(2,1)S(1)}, u32[]{:S(2)}, u32[]{:S(2)}) collective-permute-start(bf16[192,1024]{1,0:T(8,128)(2,1)S(1)} %get-tuple-element.46.own), channel_id=1, source_target_pairs={{0,24},{1,25},{2,26},{3,27},{4,28},{5,29},{6,30},{7,31},{8,16},{9,... | collective-permute-start | bytes 1179656 | tf_op jit(solution)/shard_map/ppermute | solution.py:270
  13.3 2.1 %collective-permute-start.1 = (bf16[2,64,1024]{2,1,0:T(8,128)(2,1)S(1)}, bf16[2,64,1024]{2,1,0:T(8,128)(2,1)S(1)}, u32[]{:S(2)}, u32[]{:S(2)}) collective-permute-start(bf16[2,64,1024]{2,1,0:T(8,128)(2,1)S(1)} %copy-done.17), channel_id=1, source_target_pairs={{0,24},{1,25},{2,26},{3,27},{4,28},{5,29},{6,30},{7,31},{8,16},{9,... | collective-permute-start | bytes 786440 | tf_op jit(solution)/shard_map/ppermute | solution.py:271
  15.4 9.3 %collective-permute-done.1 = bf16[2,64,1024]{2,1,0:T(8,128)(2,1)S(1)} collective-permute-done((bf16[2,64,1024]{2,1,0:T(8,128)(2,1)S(1)}, bf16[2,64,1024]{2,1,0:T(8,128)(2,1)S(1)}, u32[]{:S(2)}, u32[]{:S(2)}) %collective-permute-start.1) | collective-permute-done | bytes 262176 | tf_op jit(solution)/shard_map/ppermute | solution.py:271
  25.5 6.5 %collective-permute-start.2 = (bf16[4,1040,128]{2,1,0:T(8,128)(2,1)S(1)}, bf16[4,1040,128]{2,1,0:T(8,128)(2,1)}, u32[]{:S(2)}, u32[]{:S(2)}) collective-permute-start(bf16[4,1040,128]{2,1,0:T(8,128)(2,1)S(1)} %all-to-all-done.near.ready), channel_id=1, source_target_pairs={{0,1},{1,0},{2,3},{3,2},{4,5},{5,4},{6,7},{7,6},{8,9},{9,8},{10,11... | collective-permute-start | bytes 3194888 | tf_op jit(solution)/shard_map/ppermute | solution.py:263
  32.1 1.0 shard_map.66
  33.1 4.2 %all-to-all-start.1 = ((bf16[4,128,1024]{2,1,0:T(8,128)(2,1)}), bf16[4,128,1024]{2,1,0:T(8,128)(2,1)S(1)}, u32[]{:S(2)}, u32[]{:S(2)}) async-start(bf16[4,128,1024]{2,1,0:T(8,128)(2,1)} %shard_map.66), calls=%async_computation.1 | async-start | bytes 2097152 | tf_op jit(solution)/shard_map/all_to_all | solution.py:260
  37.4 1.0 copy-done.6
  38.4 9.2 %shard_map.65 = bf16[4,1024,128]{2,1,0:T(8,128)(2,1)} custom-call(bf16[4,1040,128]{2,1,0:T(8,128)(2,1)S(1)} %all-to-all-done.near.ready, bf16[4,1040,128]{2,1,0:T(8,128)(2,1)} %collective-permute-done.2.far, f32[1,1024]{1,0:T(1,128)S(1)} %get-tuple-element.52.gain, bf16[192,1024]{1,0:T(8,128)(2,1)S(1)} %get-tuple-element.46.own, bf16[192,1024]{1,0:T(8,128)(2,1)S(1)} %copy-done.6), custom_call_target="tpu_custom_call" | custom-call | flops 8800000000 | tf_op jit(solution)/shard_map/pallas_call | solution.py:231
  47.6 4.7 %all-to-all-done.1 = bf16[4,128,1024]{2,1,0:T(8,128)(2,1)S(1)} async-done(((bf16[4,128,1024]{2,1,0:T(8,128)(2,1)}), bf16[4,128,1024]{2,1,0:T(8,128)(2,1)S(1)}, u32[]{:S(2)}, u32[]{:S(2)}) %all-to-all-start.1) | async-done | bytes 1048608 | tf_op jit(solution)/shard_map/all_to_all | solution.py:260
  52.3 3.0 %collective-permute-start.4 = (bf16[4,128,1024]{2,1,0:T(8,128)(2,1)S(1)}, bf16[4,128,1024]{2,1,0:T(8,128)(2,1)}, u32[]{:S(2)}, u32[]{:S(2)}) collective-permute-start(bf16[4,128,1024]{2,1,0:T(8,128)(2,1)S(1)} %all-to-all-done.1), channel_id=1, source_target_pairs={{0,1},{1,0},{2,3},{3,2},{4,5},{5,4},{6,7},{7,6},{8,9},{9,8},{10,11... | collective-permute-start | bytes 3145736 | tf_op jit(solution)/shard_map/ppermute | solution.py:263
  55.3 4.3 %all-to-all-start.2 = ((bf16[4,1024,128]{2,1,0:T(8,128)(2,1)}), bf16[4,1024,128]{2,1,0:T(8,128)(2,1)}, u32[]{:S(2)}, u32[]{:S(2)}) async-start(bf16[4,1024,128]{2,1,0:T(8,128)(2,1)} %shard_map.65), calls=%async_computation.2 | async-start | bytes 2097152 | tf_op jit(solution)/shard_map/all_to_all | solution.py:260
  59.6 4.2 %collective-permute-start.3 = (bf16[192,1024]{1,0:T(8,128)(2,1)S(1)}, bf16[192,1024]{1,0:T(8,128)(2,1)S(1)}, u32[]{:S(2)}, u32[]{:S(2)}) collective-permute-start(bf16[192,1024]{1,0:T(8,128)(2,1)S(1)} %shard_map.67.own), channel_id=1, source_target_pairs={{0,24},{1,25},{2,26},{3,27},{4,28},{5,29},{6,30},{7,31},{8,16},{9,... | collective-permute-start | bytes 1179656 | tf_op jit(solution)/shard_map/ppermute | solution.py:286
  63.8 9.7 %collective-permute-done.3.mirrored = bf16[192,1024]{1,0:T(8,128)(2,1)S(1)} collective-permute-done((bf16[192,1024]{1,0:T(8,128)(2,1)S(1)}, bf16[192,1024]{1,0:T(8,128)(2,1)S(1)}, u32[]{:S(2)}, u32[]{:S(2)}) %collective-permute-start.3) | collective-permute-done | bytes 393248 | tf_op jit(solution)/shard_map/ppermute | solution.py:286
  73.6 1.3 all-to-all-done.2.o_near.ready
  74.9 2.7 %collective-permute-start.5 = (bf16[4,1024,128]{2,1,0:T(8,128)(2,1)}, bf16[4,1024,128]{2,1,0:T(8,128)(2,1)}, u32[]{:S(2)}, u32[]{:S(2)}) collective-permute-start(bf16[4,1024,128]{2,1,0:T(8,128)(2,1)} %all-to-all-done.2.o_near.ready), channel_id=1, source_target_pairs={{0,1},{1,0},{2,3},{3,2},{4,5},{5,4},{6,7},{7,6},{8,9},{9,8},{10,11... | collective-permute-start | bytes 3145736 | tf_op jit(solution)/shard_map/ppermute | solution.py:263
  77.7 1.0 copy-done
  78.7 3.5 %all-to-all-start.3 = ((bf16[4,128,1024]{2,1,0:T(8,128)(2,1)}), bf16[4,128,1024]{2,1,0:T(8,128)(2,1)S(1)}, u32[]{:S(2)}, u32[]{:S(2)}) async-start(bf16[4,128,1024]{2,1,0:T(8,128)(2,1)} %copy-done), calls=%async_computation.3 | async-start | bytes 2097152 | tf_op jit(solution)/shard_map/all_to_all | solution.py:260
  82.2 1.0 copy-done.2
  83.2 1.0 copy-done.4
  84.2 4.9 %shard_map.68 = (bf16[512,128]{1,0:T(8,128)(2,1)S(1)}, bf16[1040,128]{1,0:T(8,128)(2,1)S(1)}, bf16[128,1024]{1,0:T(8,128)(2,1)S(1)}) custom-call(bf16[4,1040,128]{2,1,0:T(8,128)(2,1)S(1)} %all-to-all-done.near.ready, bf16[4,1040,128]{2,1,0:T(8,128)(2,1)} %collective-permute-done.2.far, bf16[4,1024,128]{2,1,0:T(8,128)(2,1)} %all-to-all-done.2.o_near.ready, ...), custom_call_target="tpu_custom_call" | custom-call | flops 4400000000 | tf_op jit(solution)/shard_map/pallas_call | solution.py:231
  89.8 3.2 %collective-permute-start.6 = (bf16[1040,128]{1,0:T(8,128)(2,1)S(1)}, bf16[1040,128]{1,0:T(8,128)(2,1)S(1)}, u32[]{:S(2)}, u32[]{:S(2)}) collective-permute-start(bf16[1040,128]{1,0:T(8,128)(2,1)S(1)} %get-tuple-element.33.refs_1_), channel_id=1, source_target_pairs={{0,8},{1,9},{2,10},{3,11},{4,12},{5,13},{6,14},{7,15},{8,0},{9,1},... | collective-permute-start | bytes 798728 | tf_op jit(solution)/shard_map/ppermute | solution.py:319
  93.1 5.0 %shard_map.69 = (bf16[512,128]{1,0:T(8,128)(2,1)S(1)}, bf16[1040,128]{1,0:T(8,128)(2,1)S(1)}, bf16[128,1024]{1,0:T(8,128)(2,1)S(1)}) custom-call(bf16[4,1040,128]{2,1,0:T(8,128)(2,1)S(1)} %all-to-all-done.near.ready, bf16[4,1040,128]{2,1,0:T(8,128)(2,1)} %collective-permute-done.2.far, bf16[4,1024,128]{2,1,0:T(8,128)(2,1)} %all-to-all-done.2.o_near.ready, ...), custom_call_target="tpu_custom_call" | custom-call | flops 4400000000 | tf_op jit(solution)/shard_map/pallas_call | solution.py:231
  99.5 1.7 %collective-permute-done.6.refs_2_ = bf16[1040,128]{1,0:T(8,128)(2,1)S(1)} collective-permute-done((bf16[1040,128]{1,0:T(8,128)(2,1)S(1)}, bf16[1040,128]{1,0:T(8,128)(2,1)S(1)}, u32[]{:S(2)}, u32[]{:S(2)}) %collective-permute-start.6) | collective-permute-done | bytes 266272 | tf_op jit(solution)/shard_map/ppermute | solution.py:319
  101.2 2.9 %shard_map.71.refs_3_ = bf16[4,128,128]{2,1,0:T(8,128)(2,1)S(1)} custom-call(bf16[512,128]{1,0:T(8,128)(2,1)S(1)} %get-tuple-element.39.refs_0_, bf16[1040,128]{1,0:T(8,128)(2,1)S(1)} %get-tuple-element.33.refs_1_, bf16[1040,128]{1,0:T(8,128)(2,1)S(1)} %collective-permute-done.6.refs_2_), custom_call_target="tpu_custom_call" | custom-call | flops 3300000000 | tf_op jit(solution)/shard_map/pallas_call | solution.py:231
  104.1 2.8 %collective-permute-start.8 = (bf16[4,128,1024]{2,1,0:T(8,128)(2,1)S(1)}, bf16[4,128,1024]{2,1,0:T(8,128)(2,1)S(1)}, u32[]{:S(2)}, u32[]{:S(2)}) collective-permute-start(bf16[4,128,1024]{2,1,0:T(8,128)(2,1)S(1)} %all-to-all-done.3), channel_id=1, source_target_pairs={{0,1},{1,0},{2,3},{3,2},{4,5},{5,4},{6,7},{7,6},{8,9},{9,8},{10,11... | collective-permute-start | bytes 3145736 | tf_op jit(solution)/shard_map/ppermute | solution.py:263
  107.0 13.1 %collective-permute-start.7 = (bf16[1040,128]{1,0:T(8,128)(2,1)S(1)}, bf16[1040,128]{1,0:T(8,128)(2,1)S(1)}, u32[]{:S(2)}, u32[]{:S(2)}) collective-permute-start(bf16[1040,128]{1,0:T(8,128)(2,1)S(1)} %get-tuple-element.38.refs_1_), channel_id=1, source_target_pairs={{0,504},{1,505},{2,506},{3,507},{4,508},{5,509},{6,510},{7,511},{8... | collective-permute-start | bytes 798728 | tf_op jit(solution)/shard_map/ppermute | solution.py:319
  120.1 6.7 %collective-permute-done.7.refs_2_ = bf16[1040,128]{1,0:T(8,128)(2,1)S(1)} collective-permute-done((bf16[1040,128]{1,0:T(8,128)(2,1)S(1)}, bf16[1040,128]{1,0:T(8,128)(2,1)S(1)}, u32[]{:S(2)}, u32[]{:S(2)}) %collective-permute-start.7) | collective-permute-done | bytes 266272 | tf_op jit(solution)/shard_map/ppermute | solution.py:319
  126.8 2.9 %shard_map.72 = bf16[8,128,128]{2,1,0:T(8,128)(2,1)S(1)} custom-call(bf16[512,128]{1,0:T(8,128)(2,1)S(1)} %copy-done.15, bf16[1040,128]{1,0:T(8,128)(2,1)S(1)} %get-tuple-element.38.refs_1_, bf16[1040,128]{1,0:T(8,128)(2,1)S(1)} %collective-permute-done.7.refs_2_, bf16[4,128,128]{2,1,0:T(8,128)(2,1)S(1)} %shard_map.71.refs_3_), custom_call_target="tpu_custom_call" | custom-call | flops 3300000000 | tf_op jit(solution)/shard_map/pallas_call | solution.py:231
  129.7 11.3 %all_to_all.25.parts = bf16[8,128,128]{2,1,0:T(8,128)(2,1)S(1)} all-to-all(bf16[8,128,128]{2,1,0:T(8,128)(2,1)S(1)} %shard_map.72), channel_id=1, replica_groups=mesh['z'=16,'xl'=2,'xh'=2,'y'=4,'c'=2] {'y','c'}, dimensions={0} | all-to-all | bytes 524288 | tf_op jit(solution)/shard_map/all_to_all | solution.py:338
  141.1 1.2 shard_map.73
  (47 shorter events, 5.3 us)
Async XLA Ops:
  0.0 0.9 copy-start.7
  1.0 0.7 copy-start.8
  1.6 0.7 copy-start.9
  3.5 5.2 %copy-start.16 = (bf16[2,1024,192]{1,2,0:T(8,128)(2,1)S(1)}, bf16[2,1024,192]{1,2,0:T(8,128)(2,1)}, u32[]{:S(2)}) copy-start(bf16[2,1024,192]{1,2,0:T(8,128)(2,1)} %param.10) | copy-start | bytes 2359300
  3.5 22.0 %all-to-all-start = ((bf16[4,1040,128]{2,1,0:T(8,128)(2,1)}), bf16[4,1040,128]{2,1,0:T(8,128)(2,1)S(1)}, u32[]{:S(2)}, u32[]{:S(2)}) async-start(bf16[4,1040,128]{2,1,0:T(8,128)(2,1)} %shard_map.64), calls=%async_computation | async-start | bytes 2129920 | tf_op jit(solution)/shard_map/all_to_all | solution.py:260
  8.7 4.6 %copy-start.17 = (bf16[2,64,1024]{2,1,0:T(8,128)(2,1)S(1)}, bf16[2,64,1024]{2,1,0:T(8,128)(2,1)}, u32[]{:S(2)}) copy-start(bf16[2,64,1024]{2,1,0:T(8,128)(2,1)} %param.11) | copy-start | bytes 786436
  8.7 23.3 %copy-start.18 = (f32[2,1024]{1,0:T(2,128)S(1)}, f32[2,1024]{1,0:T(2,128)}, u32[]{:S(2)}) copy-start(f32[2,1024]{1,0:T(2,128)} %param.9) | copy-start | bytes 24580
  8.8 16.0 %collective-permute-start = (bf16[192,1024]{1,0:T(8,128)(2,1)S(1)}, bf16[192,1024]{1,0:T(8,128)(2,1)S(1)}, u32[]{:S(2)}, u32[]{:S(2)}) collective-permute-start(bf16[192,1024]{1,0:T(8,128)(2,1)S(1)} %get-tuple-element.46.own), channel_id=1, source_target_pairs={{0,24},{1,25},{2,26},{3,27},{4,28},{5,29},{6,30},{7,31},{8,16},{9,... | collective-permute-start | bytes 1179656 | tf_op jit(solution)/shard_map/ppermute | solution.py:270
  13.3 11.4 %collective-permute-start.1 = (bf16[2,64,1024]{2,1,0:T(8,128)(2,1)S(1)}, bf16[2,64,1024]{2,1,0:T(8,128)(2,1)S(1)}, u32[]{:S(2)}, u32[]{:S(2)}) collective-permute-start(bf16[2,64,1024]{2,1,0:T(8,128)(2,1)S(1)} %copy-done.17), channel_id=1, source_target_pairs={{0,24},{1,25},{2,26},{3,27},{4,28},{5,29},{6,30},{7,31},{8,16},{9,... | collective-permute-start | bytes 786440 | tf_op jit(solution)/shard_map/ppermute | solution.py:271
  24.7 0.8 copy-start.5
  25.5 11.9 %collective-permute-start.2 = (bf16[4,1040,128]{2,1,0:T(8,128)(2,1)S(1)}, bf16[4,1040,128]{2,1,0:T(8,128)(2,1)}, u32[]{:S(2)}, u32[]{:S(2)}) collective-permute-start(bf16[4,1040,128]{2,1,0:T(8,128)(2,1)S(1)} %all-to-all-done.near.ready), channel_id=1, source_target_pairs={{0,1},{1,0},{2,3},{3,2},{4,5},{5,4},{6,7},{7,6},{8,9},{9,8},{10,11... | collective-permute-start | bytes 3194888 | tf_op jit(solution)/shard_map/ppermute | solution.py:263
  33.1 19.2 %all-to-all-start.1 = ((bf16[4,128,1024]{2,1,0:T(8,128)(2,1)}), bf16[4,128,1024]{2,1,0:T(8,128)(2,1)S(1)}, u32[]{:S(2)}, u32[]{:S(2)}) async-start(bf16[4,128,1024]{2,1,0:T(8,128)(2,1)} %shard_map.66), calls=%async_computation.1 | async-start | bytes 2097152 | tf_op jit(solution)/shard_map/all_to_all | solution.py:260
  37.4 1.0 copy-start.6
  52.3 22.6 %collective-permute-start.4 = (bf16[4,128,1024]{2,1,0:T(8,128)(2,1)S(1)}, bf16[4,128,1024]{2,1,0:T(8,128)(2,1)}, u32[]{:S(2)}, u32[]{:S(2)}) collective-permute-start(bf16[4,128,1024]{2,1,0:T(8,128)(2,1)S(1)} %all-to-all-done.1), channel_id=1, source_target_pairs={{0,1},{1,0},{2,3},{3,2},{4,5},{5,4},{6,7},{7,6},{8,9},{9,8},{10,11... | collective-permute-start | bytes 3145736 | tf_op jit(solution)/shard_map/ppermute | solution.py:263
  55.3 19.6 %all-to-all-start.2 = ((bf16[4,1024,128]{2,1,0:T(8,128)(2,1)}), bf16[4,1024,128]{2,1,0:T(8,128)(2,1)}, u32[]{:S(2)}, u32[]{:S(2)}) async-start(bf16[4,1024,128]{2,1,0:T(8,128)(2,1)} %shard_map.65), calls=%async_computation.2 | async-start | bytes 2097152 | tf_op jit(solution)/shard_map/all_to_all | solution.py:260
  59.6 18.1 %copy-start.1 = (bf16[192,1024]{1,0:T(8,128)(2,1)}, bf16[192,1024]{1,0:T(8,128)(2,1)S(1)}, u32[]{:S(2)}) copy-start(bf16[192,1024]{1,0:T(8,128)(2,1)S(1)} %shard_map.67.own) | copy-start | bytes 1179652
  59.6 13.9 %collective-permute-start.3 = (bf16[192,1024]{1,0:T(8,128)(2,1)S(1)}, bf16[192,1024]{1,0:T(8,128)(2,1)S(1)}, u32[]{:S(2)}, u32[]{:S(2)}) collective-permute-start(bf16[192,1024]{1,0:T(8,128)(2,1)S(1)} %shard_map.67.own), channel_id=1, source_target_pairs={{0,24},{1,25},{2,26},{3,27},{4,28},{5,29},{6,30},{7,31},{8,16},{9,... | collective-permute-start | bytes 1179656 | tf_op jit(solution)/shard_map/ppermute | solution.py:286
  73.6 4.1 %copy-start.3 = (bf16[192,1024]{1,0:T(8,128)(2,1)}, bf16[192,1024]{1,0:T(8,128)(2,1)S(1)}, u32[]{:S(2)}) copy-start(bf16[192,1024]{1,0:T(8,128)(2,1)S(1)} %collective-permute-done.3.mirrored) | copy-start | bytes 1179652
  74.9 7.3 %collective-permute-start.5 = (bf16[4,1024,128]{2,1,0:T(8,128)(2,1)}, bf16[4,1024,128]{2,1,0:T(8,128)(2,1)}, u32[]{:S(2)}, u32[]{:S(2)}) collective-permute-start(bf16[4,1024,128]{2,1,0:T(8,128)(2,1)} %all-to-all-done.2.o_near.ready), channel_id=1, source_target_pairs={{0,1},{1,0},{2,3},{3,2},{4,5},{5,4},{6,7},{7,6},{8,9},{9,8},{10,11... | collective-permute-start | bytes 3145736 | tf_op jit(solution)/shard_map/ppermute | solution.py:263
  77.7 1.0 copy-start
  78.7 25.4 %all-to-all-start.3 = ((bf16[4,128,1024]{2,1,0:T(8,128)(2,1)}), bf16[4,128,1024]{2,1,0:T(8,128)(2,1)S(1)}, u32[]{:S(2)}, u32[]{:S(2)}) async-start(bf16[4,128,1024]{2,1,0:T(8,128)(2,1)} %copy-done), calls=%async_computation.3 | async-start | bytes 2097152 | tf_op jit(solution)/shard_map/all_to_all | solution.py:260
  82.2 1.0 copy-start.2
  83.2 1.0 copy-start.4
  89.1 0.7 copy-start.10
  89.8 11.4 %collective-permute-start.6 = (bf16[1040,128]{1,0:T(8,128)(2,1)S(1)}, bf16[1040,128]{1,0:T(8,128)(2,1)S(1)}, u32[]{:S(2)}, u32[]{:S(2)}) collective-permute-start(bf16[1040,128]{1,0:T(8,128)(2,1)S(1)} %get-tuple-element.33.refs_1_), channel_id=1, source_target_pairs={{0,8},{1,9},{2,10},{3,11},{4,12},{5,13},{6,14},{7,15},{8,0},{9,1},... | collective-permute-start | bytes 798728 | tf_op jit(solution)/shard_map/ppermute | solution.py:319
  98.1 0.7 copy-start.12
  98.8 0.7 copy-start.14
  101.2 25.6 %copy-start.15 = (bf16[512,128]{1,0:T(8,128)(2,1)S(1)}, bf16[512,128]{1,0:T(8,128)(2,1)}, u32[]{:S(2)}) copy-start(bf16[512,128]{1,0:T(8,128)(2,1)} %copy-done.14) | copy-start | bytes 393220
  104.1 37.0 %copy-start.11 = (bf16[128,1024]{1,0:T(8,128)(2,1)S(1)}, bf16[128,1024]{1,0:T(8,128)(2,1)}, u32[]{:S(2)}) copy-start(bf16[128,1024]{1,0:T(8,128)(2,1)} %copy-done.10) | copy-start | bytes 786436
  104.1 37.0 %copy-start.13 = (bf16[128,1024]{1,0:T(8,128)(2,1)S(1)}, bf16[128,1024]{1,0:T(8,128)(2,1)}, u32[]{:S(2)}) copy-start(bf16[128,1024]{1,0:T(8,128)(2,1)} %copy-done.12) | copy-start | bytes 786436
  104.1 36.9 %collective-permute-start.8 = (bf16[4,128,1024]{2,1,0:T(8,128)(2,1)S(1)}, bf16[4,128,1024]{2,1,0:T(8,128)(2,1)S(1)}, u32[]{:S(2)}, u32[]{:S(2)}) collective-permute-start(bf16[4,128,1024]{2,1,0:T(8,128)(2,1)S(1)} %all-to-all-done.3), channel_id=1, source_target_pairs={{0,1},{1,0},{2,3},{3,2},{4,5},{5,4},{6,7},{7,6},{8,9},{9,8},{10,11... | collective-permute-start | bytes 3145736 | tf_op jit(solution)/shard_map/ppermute | solution.py:263
  107.0 19.9 %collective-permute-start.7 = (bf16[1040,128]{1,0:T(8,128)(2,1)S(1)}, bf16[1040,128]{1,0:T(8,128)(2,1)S(1)}, u32[]{:S(2)}, u32[]{:S(2)}) collective-permute-start(bf16[1040,128]{1,0:T(8,128)(2,1)S(1)} %get-tuple-element.38.refs_1_), channel_id=1, source_target_pairs={{0,504},{1,505},{2,506},{3,507},{4,508},{5,509},{6,510},{7,511},{8... | collective-permute-start | bytes 798728 | tf_op jit(solution)/shard_map/ppermute | solution.py:319

commit v3 on v2

--- a/solution.py
+++ b/solution.py
@@ -88,6 +88,13 @@
     return jnp.concatenate([own[cut, :], mirrored[cut, :]], axis=0)
 
 
+def fetch(sources, targets, sems):
+    copies = [pltpu.make_async_copy(a, b, sems.at[i]) for i, (a, b) in enumerate(zip(sources, targets))]
+    for copy in copies:
+        copy.start()
+    return copies
+
+
 def project(normed, own, mirrored, queries, keys, turned):
     both = jnp.concatenate([joined(own, mirrored, 0), joined(own, mirrored, 1)], axis=0)
     found = dot_nt(normed[...], both).astype(BF16)
@@ -102,7 +109,11 @@
         values_ref[head, :HEAD_DIM, span] = turned[from_head * HEAD_DIM : (from_head + 1) * HEAD_DIM]
 
 
-def first_kernel(near, far, gain, own, mirrored, out, normed, queries, keys, turned, values, hots):
+def first_kernel(
+    near, far, gain, own_at, mirrored_at, out,
+    normed, queries, keys, turned, values, hots, own, mirrored, sems,
+):
+    copies = fetch((own_at, mirrored_at), (own, mirrored), sems)
     rows = []
     for s, ref in enumerate((near, far)):
         for y in range(4):
@@ -112,6 +123,8 @@
             )
             rows.append(ref[y, D:, :].astype(F32)[:1])
     columns = tag_columns(rows)
+    for copy in copies:
+        copy.wait()
     project(normed, own, mirrored, queries, keys.at[:, :LANES], turned)
     put_values(values, slice(0, PATCH), turned, False)
     values[:, HEAD_DIM:, :] = jnp.ones((2, 16, PATCH), BF16)
@@ -133,20 +146,33 @@
 
 
 def middle_kernel(
-    part, near, far, o_near, o_far, w_near, w_far, gain, own, mirrored,
-    q_out, kv, st_out, heads, update, normed, turned,
+    part, near, far, gain, o_near, o_far, w_mine, w_mine_far, w_next, w_next_far, own_at, mirrored_at,
+    q_out, kv, st_out, heads, update, normed, turned, w, own, mirrored, o_sems, w_sems,
 ):
-    my_y, half = lax.axis_index("y"), half_of(part)
+    my_y, xl, half = lax.axis_index("y"), lax.axis_index("xl"), half_of(part)
+    sources, targets = [], []
     for s in range(2):
-        for yy in range(2):
-            y = half * 2 + yy
-            span = slice((s * 2 + yy) * ROWS, (s * 2 + yy + 1) * ROWS)
-            at_near = pl.ds(pl.multiple_of((s * 4 + y) * ROWS, ROWS), ROWS)
-            at_far = pl.ds(pl.multiple_of(((1 - s) * 4 + y) * ROWS, ROWS), ROWS)
-            for g in range(4):
-                heads[span, g * LANES : (g + 1) * LANES] = o_near[g, at_near, :]
-                heads[span, (g + 4) * LANES : (g + 5) * LANES] = o_far[g, at_far, :]
-    update[...] = dot(heads[:, :HALF], w_near[...]) + dot(heads[:, HALF:], w_far[...])
+        span = slice(s * 256, (s + 1) * 256)
+        at_near = pl.ds(pl.multiple_of(s * HALF + half * 256, 256), 256)
+        at_far = pl.ds(pl.multiple_of((1 - s) * HALF + half * 256, 256), 256)
+        for g in range(4):
+            sources += [o_near.at[g, at_near, :], o_far.at[g, at_far, :]]
+            targets += [
+                heads.at[span, g * LANES : (g + 1) * LANES],
+                heads.at[span, (g + 4) * LANES : (g + 5) * LANES],
+            ]
+    o_copies = fetch(sources, targets, o_sems)
+    w_copies = fetch(
+        (w_mine, w_mine_far, w_next, w_next_far, own_at, mirrored_at),
+        (w.at[0, :HALF], w.at[0, HALF:], w.at[1, :HALF], w.at[1, HALF:], own, mirrored),
+        w_sems,
+    )
+    for copy in o_copies + w_copies[:2]:
+        copy.wait()
+    update[:, pl.ds(pl.multiple_of(xl * HALF, HALF), HALF)] = dot(heads[...], w[0])
+    for copy in w_copies[2:]:
+        copy.wait()
+    update[:, pl.ds(pl.multiple_of((1 - xl) * HALF, HALF), HALF)] = dot(heads[...], w[1])
     rows = []
     for s, ref in enumerate((near, far)):
         for yy in range(2):
@@ -171,7 +197,7 @@
     if part:
         queries, mine, other, had, out, keys, values, hots = refs
     else:
-        queries, mine, other, out, keys, values, hots = refs
+        queries, mine, other, ready, out, keys, values, hots = refs
     half, c = half_of(part), lax.axis_index("c")
     keys[:HALF, :LANES] = mine[:HALF, :]
     keys[HALF:, :HEAD_DIM] = other[:HALF, HEAD_DIM:]
@@ -201,13 +227,19 @@
                 out[s * 2 + yy] = block
 
 
-def last_kernel(parts, w_near, w_far, stream_p, stream_q, out, heads):
-    c, y_half = lax.axis_index("c"), lax.axis_index("y") // 2
-    for s in range(2):
-        core = c if s == 0 else 1 - c
-        for y in range(4):
-            heads[:, (s * 4 + y) * LANES : (s * 4 + y + 1) * LANES] = parts[y * 2 + core]
-    update = dot(heads[:, :HALF], w_near[...]) + dot(heads[:, HALF:], w_far[...])
+def last_kernel(parts, w, stream_p, stream_q, out, heads):
+    xh, y_half = lax.axis_index("xh"), lax.axis_index("y") // 2
+    for b in range(4):
+        pair = []
+        for block in (parts[2 * b], parts[2 * b + 1]):
+            turned = jnp.concatenate([block[:, HEAD_DIM:], block[:, :HEAD_DIM]], axis=1)
+            pair.append(jnp.where(xh == 0, block, turned))
+        for k in range(2):
+            cut = slice(k * HEAD_DIM, (k + 1) * HEAD_DIM)
+            heads[:, (k * 4 + b) * LANES : (k * 4 + b + 1) * LANES] = jnp.concatenate(
+                [pair[0][:, cut], pair[1][:, cut]], axis=1
+            )
+    update = dot(heads[...], w[...])
 
     def put(stream):
         out[...] = (stream[...].astype(F32) + update).astype(BF16)
@@ -217,36 +249,40 @@
 
 
 def relay_kernel(own, far, ready, out):
+    cut = pl.ds(pl.multiple_of(lax.axis_index("xl") * HALF, HALF), HALF)
     for copy in range(out.shape[0]):
-        out[copy, : own.shape[0]] = own[...]
-        out[copy, own.shape[0] :] = far[...]
+        out[copy, : own.shape[0]] = own[:, cut]
+        out[copy, own.shape[0] :] = far[:, cut]
 
 
 def pass_kernel(array, ready, out):
     out[...] = array[...]
 
 
-def call(kernel, micros, outs, scratch, *args, wait_for=()):
+def call(kernel, micros, outs, scratch, *args, late=(), semaphores=(), megabytes=16):
     vmem, anywhere = pl.BlockSpec(memory_space=pltpu.VMEM), pl.BlockSpec(memory_space=pl.ANY)
     return pl.pallas_call(
         kernel,
         out_shape=[jax.ShapeDtypeStruct(shape, BF16) for shape in outs],
-        in_specs=[vmem] * len(args) + [anywhere] * len(wait_for),
+        in_specs=[vmem] * len(args) + [anywhere] * len(late),
         out_specs=[vmem] * len(outs),
-        scratch_shapes=[pltpu.VMEM(shape, dtype) for shape, dtype in scratch],
-        compiler_params=pltpu.CompilerParams(vmem_limit_bytes=16 * 1024 * 1024),
+        scratch_shapes=[pltpu.VMEM(shape, dtype) for shape, dtype in scratch]
+        + [pltpu.SemaphoreType.DMA((count,)) for count in semaphores],
+        compiler_params=pltpu.CompilerParams(vmem_limit_bytes=megabytes * 1024 * 1024),
         cost_estimate=pl.CostEstimate(
             flops=int(micros * 1.1e9), bytes_accessed=0, transcendentals=0
         ),
-    )(*args, *wait_for)
+    )(*args, *late)
 
 
 def solution(mesh):
     curve, heads = mesh.shape["curve"], mesh.shape["head"]
     shape = (curve // 2, 2, 2, heads // 4, 2)
     deep = shape[0]
+    head_axes = ("xh", "y", "c")
     other_core = pairs(shape, lambda z, xl, xh, y, c: (z, xl, xh, y, 1 - c))
     mirror = pairs(shape, lambda z, xl, xh, y, c: (z, 1 - xl, 1 - xh, y, c))
+    beside = pairs(shape, lambda z, xl, xh, y, c: (z, 1 - xl, xh, y, c))
     inner = pairs(shape, lambda z, xl, xh, y, c: (z, xl, 1 - xh, y, c))
 
     def across(z, xl, xh, y, c):
@@ -264,26 +300,24 @@
 
     def on_device(points, order, scan_ids, ln_gain, w_qkv, w_out):
         w_turned = jnp.swapaxes(w_qkv, 1, 2)
+        w_last = lax.all_gather(w_out[1], head_axes, axis=0, tiled=True)
         (copies,) = call(
             order_kernel, 1.2, [(4, EXT, LANES)], [], points, order, scan_ids.reshape(1, ROWS)
         )
         first_far = lax.ppermute(w_turned[0], AXES, mirror)
-        w_out_far = lax.ppermute(w_out, AXES, mirror)
+        out_far = lax.ppermute(w_out[0], AXES, mirror)
         x_near = over_y(copies)
-        x_near, first_far, w_out_far = lax.optimization_barrier((x_near, first_far, w_out_far))
+        x_near, first_far, out_far = lax.optimization_barrier((x_near, first_far, out_far))
         x_far = swapped(x_near)
-
-        def gathered_out(layer, ready):
-            (outs,) = call(
-                relay_kernel, 1, [(4, ROWS, D)], [], w_out[layer], w_out_far[layer], wait_for=(ready,)
-            )
-            return over_y(outs)
-
-        out_near = gathered_out(0, x_near)
+        (shares,) = call(
+            relay_kernel, 1, [(4, ROWS, HALF)], [], w_out[0], out_far, late=(x_near,), megabytes=4
+        )
+        w_mine = over_y(shares)
         (second_own,) = call(
-            pass_kernel, 1, [(3 * HEAD_DIM, D)], [], w_turned[1], wait_for=(x_near,)
+            pass_kernel, 1, [(3 * HEAD_DIM, D)], [], w_turned[1], late=(x_near,), megabytes=4
         )
         second_far = lax.ppermute(second_own, AXES, mirror)
+        projection = [((3 * HEAD_DIM, D), BF16)] * 2
         (o_copies,) = call(
             first_kernel,
             8,
@@ -295,16 +329,21 @@
                 ((LANES, PATCH), BF16),
                 ((2, HEAD_DIM + 16, PATCH), BF16),
                 ((PATCH, LANES), BF16),
+                *projection,
             ],
-            x_near, x_far, ln_gain[0:1], w_turned[0], first_far,
-        )
-        o_copies, out_near = lax.optimization_barrier((o_copies, out_near))
-        out_far = swapped(out_near)
+            x_near, x_far, ln_gain[0:1],
+            late=(w_turned[0], first_far), semaphores=(2,),
+        )
+        o_copies, w_mine = lax.optimization_barrier((o_copies, w_mine))
+        w_next = lax.ppermute(w_mine, AXES, beside)
+        w_mine_far = swapped(w_mine)
         o_near = over_y(o_copies)
-        o_near, second_far, out_far = lax.optimization_barrier((o_near, second_far, out_far))
+        o_near, second_far, w_next, w_mine_far = lax.optimization_barrier(
+            (o_near, second_far, w_next, w_mine_far)
+        )
         o_far = swapped(o_near)
-        out_first = out_near.reshape(HALF, D), out_far.reshape(HALF, D)
-        last_near = gathered_out(1, o_near)
+        w_next_far = swapped(w_next)
+        w_first = [w.reshape(HALF, HALF) for w in (w_mine, w_mine_far, w_next, w_next_far)]
         middle, halos = [], []
         for part, links in enumerate((inner, outer)):
             middle.append(
@@ -312,18 +351,25 @@
                     functools.partial(middle_kernel, part),
                     4,
                     [(HALF, LANES), (EXT, LANES), (ROWS, D)],
-                    [((HALF, D), BF16), ((HALF, D), F32), ((HALF, D), BF16), ((LANES, HALF), BF16)],
-                    x_near, x_far, o_near, o_far, *out_first, ln_gain[1:2], second_own, second_far,
+                    [
+                        ((HALF, D), BF16),
+                        ((HALF, D), F32),
+                        ((HALF, D), BF16),
+                        ((LANES, HALF), BF16),
+                        ((2, D, HALF), BF16),
+                        *projection,
+                    ],
+                    x_near, x_far, ln_gain[1:2],
+                    late=(o_near, o_far, *w_first, second_own, second_far), semaphores=(16, 6),
                 )
             )
             halos.append(lax.ppermute(middle[part][1], AXES, links))
-        halos[0], *middle[1] = lax.optimization_barrier((halos[0], *middle[1]))
         parts = None
         for part in range(2):
             queries, kv, _ = middle[part]
             (parts,) = call(
                 functools.partial(second_kernel, part),
-                3,
+                3 if part else 0,
                 [(8 if part else 4, ROWS, LANES)],
                 [
                     ((PATCH, 2 * LANES), BF16),
@@ -331,19 +377,16 @@
                     ((HALF, LANES), BF16),
                 ],
                 queries, kv, halos[part], *([parts] if part else []),
+                late=() if part else (middle[1][1],), megabytes=8,
             )
-            if part == 0:
-                last_near, parts = lax.optimization_barrier((last_near, parts))
-                out_second = last_near.reshape(HALF, D), swapped(last_near).reshape(HALF, D)
         parts = lax.all_to_all(parts, ("y", "c"), 0, 0, tiled=True)
         (result,) = call(
             last_kernel, 1.5, [(ROWS, D)], [((ROWS, D), BF16)],
-            parts, *out_second, middle[0][2], middle[1][2],
+            parts, w_last, middle[0][2], middle[1][2], megabytes=8,
         )
         return result
 
-    curve_axes, head_axes = ("z", "xl"), ("xh", "y", "c")
-    every = curve_axes + head_axes
+    every = ("z", "xl") + head_axes
     return jax.shard_map(
         on_device,
         mesh=Mesh(mesh.devices.reshape(shape), AXES),

time: 143 us -> 144 us (level)
  between operations: 0.29 us -> 13.6 us
  blocking collectives: 11.3 us -> 0 us
  waiting for transfers between devices: 33.6 us -> 28 us
  starting transfers between devices: 59.3 us -> 61.5 us
  Pallas kernels: 28.5 us -> 30.7 us
    all_to_all x1 -> x0, blocking collectives: 11.3 us -> none  [on_device(): parts = lax.all_to_all(parts, ('y', 'c'), 0, 0, tiled=True)]
    all_to_all x0 -> x1, waiting for transfers between devices: none -> 6.5 us  [on_device(): parts = lax.all_to_all(parts, ('y', 'c'), 0, 0, tiled=True)]
    all_to_all x4 -> x3, waiting for transfers between devices: 6.04 us -> 0.01 us  [over_y(): return lax.all_to_all(copies, 'y', 0, 0, tiled=True)]
    all_to_all x0 -> x1, starting transfers between devices: none -> 5.72 us  [on_device(): parts = lax.all_to_all(parts, ('y', 'c'), 0, 0, tiled=True)]
    ppermute x2, waiting for transfers between devices: 8.48 us -> 3.41 us  [on_device(): halos.append(lax.ppermute(middle[part][1], AXES, links))]
    ppermute x1 -> x2, waiting for transfers between devices: 9.33 us -> 5.7 us  [the longest x1 5.7 us: on_device(): out_far = lax.ppermute(w_out[0], AXES, mirror)]
    all_to_all x4 -> x3, starting transfers between devices: 17.1 us -> 13.6 us  [over_y(): return lax.all_to_all(copies, 'y', 0, 0, tiled=True)]
    pallas_call x10 -> x9, Pallas kernels: 28.5 us -> 30.7 us  [call(): pl.pallas_call(kernel, out_shape=[jax.ShapeDtypeStruct(shape, BF16) for s...]
  transfers between devices with their start and end apart: 13 -> 15, of which waited for: 6 -> 5; matrix products, arithmetic and copies ran while one was open for 0% -> 1% of each run, Pallas kernels for 18% -> 20%
where the time goes in v3:
time: 144 us; the launch traced here: 143 us
  starting transfers between devices  61.5 us (43%)
  Pallas kernels  30.7 us (21%)
  waiting for transfers between devices  28 us (19%)
  between operations  13.6 us (9%)
  local copies, waits for them, and re-layouts  9.03 us (6%)
    pallas_call x9, Pallas kernels, call(): pl.pallas_call(kernel, out_shape=[jax.ShapeDtypeStruct(shape, BF16) for s...  30.7 us
    ppermute x2, starting transfers between devices, on_device(): halos.append(lax.ppermute(middle[part][1], AXES, links))  15.5 us
    ppermute x4, starting transfers between devices, swapped(): return lax.ppermute(array, AXES, other_core)  14.7 us
    all_to_all x3, starting transfers between devices, over_y(): return lax.all_to_all(copies, 'y', 0, 0, tiled=True)  13.6 us
    ppermute x1, waiting for transfers between devices, on_device(): second_far = lax.ppermute(second_own, AXES, mirror)  10.3 us
    unnamed x34, local copies, waits for them, and re-layouts  8.3 us
    all_to_all x1, waiting for transfers between devices, on_device(): parts = lax.all_to_all(parts, ('y', 'c'), 0, 0, tiled=True)  6.5 us
    all_to_all x1, starting transfers between devices, on_device(): parts = lax.all_to_all(parts, ('y', 'c'), 0, 0, tiled=True)  5.72 us
  transfers between devices with their start and end apart: 15, of which 5 were waited for; matrix products, arithmetic and copies ran while one was open for 1% of the time, Pallas kernels for 20%

profile of v3, /device:TPU:1, one launch (start us, length us, event | category | flops | bytes accessed | tf_op | source)
XLA Modules:
  0.0 142.9 jit_solution(3968831765360745879)
XLA Ops:
  6.5 0.9 copy-done.7
  8.8 1.3 shard_map.64
  10.1 5.1 %all-to-all-start = ((bf16[4,1040,128]{2,1,0:T(8,128)(2,1)}), bf16[4,1040,128]{2,1,0:T(8,128)(2,1)S(1)}, u32[]{:S(2)}, u32[]{:S(2)}) async-start(bf16[4,1040,128]{2,1,0:T(8,128)(2,1)} %shard_map.64), calls=%async_computation | async-start | bytes 2129920 | tf_op jit(solution)/shard_map/all_to_all | solution.py:296
  15.3 4.4 %collective-permute-start = (bf16[192,1024]{1,0:T(8,128)(2,1)S(1)}, bf16[192,1024]{1,0:T(8,128)(2,1)S(1)}, u32[]{:S(2)}, u32[]{:S(2)}) collective-permute-start(bf16[192,1024]{1,0:T(8,128)(2,1)S(1)} %get-tuple-element.36.own_at), channel_id=1, source_target_pairs={{0,24},{1,25},{2,26},{3,27},{4,28},{5,29},{6,30},{7,31},{8,16},{9,... | collective-permute-start | bytes 1179656 | tf_op jit(solution)/shard_map/ppermute | solution.py:307
  20.4 2.1 %collective-permute-start.1 = (bf16[64,1024]{1,0:T(8,128)(2,1)S(1)}, bf16[64,1024]{1,0:T(8,128)(2,1)S(1)}, u32[]{:S(2)}, u32[]{:S(2)}) collective-permute-start(bf16[64,1024]{1,0:T(8,128)(2,1)S(1)} %get-tuple-element.38.own), channel_id=1, source_target_pairs={{0,24},{1,25},{2,26},{3,27},{4,28},{5,29},{6,30},{7,31},{8,16},{9,... | collective-permute-start | bytes 393224 | tf_op jit(solution)/shard_map/ppermute | solution.py:308
  22.5 5.7 %collective-permute-done.1.far = bf16[64,1024]{1,0:T(8,128)(2,1)S(1)} collective-permute-done((bf16[64,1024]{1,0:T(8,128)(2,1)S(1)}, bf16[64,1024]{1,0:T(8,128)(2,1)S(1)}, u32[]{:S(2)}, u32[]{:S(2)}) %collective-permute-start.1) | collective-permute-done | bytes 131104 | tf_op jit(solution)/shard_map/ppermute | solution.py:308
  28.2 7.3 %collective-permute-start.2 = (bf16[4,1040,128]{2,1,0:T(8,128)(2,1)S(1)}, bf16[4,1040,128]{2,1,0:T(8,128)(2,1)}, u32[]{:S(2)}, u32[]{:S(2)}) collective-permute-start(bf16[4,1040,128]{2,1,0:T(8,128)(2,1)S(1)} %all-to-all-done.near.ready), channel_id=1, source_target_pairs={{0,1},{1,0},{2,3},{3,2},{4,5},{5,4},{6,7},{7,6},{8,9},{9,8},{10,11... | collective-permute-start | bytes 3194888 | tf_op jit(solution)/shard_map/ppermute | solution.py:299
  35.6 0.8 shard_map.66
  36.4 4.2 %all-to-all-start.1 = ((bf16[4,128,512]{2,1,0:T(8,128)(2,1)}), bf16[4,128,512]{2,1,0:T(8,128)(2,1)S(1)}, u32[]{:S(2)}, u32[]{:S(2)}) async-start(bf16[4,128,512]{2,1,0:T(8,128)(2,1)} %shard_map.66), calls=%async_computation.1 | async-start | bytes 1048576 | tf_op jit(solution)/shard_map/all_to_all | solution.py:296
  40.6 10.1 %shard_map.65 = bf16[4,1024,128]{2,1,0:T(8,128)(2,1)} custom-call(bf16[4,1040,128]{2,1,0:T(8,128)(2,1)S(1)} %all-to-all-done.near.ready, bf16[4,1040,128]{2,1,0:T(8,128)(2,1)} %collective-permute-done.2.far, f32[1,1024]{1,0:T(1,128)S(1)} %get-tuple-element.39.gain, bf16[192,1024]{1,0:T(8,128)(2,1)S(1)} %get-tuple-element.36.own_at, ...), custom_call_target="tpu_custom_call" | custom-call | flops 8800000000 | tf_op jit(solution)/shard_map/pallas_call | solution.py:264
  50.8 4.2 %all-to-all-start.2 = ((bf16[4,1024,128]{2,1,0:T(8,128)(2,1)}), bf16[4,1024,128]{2,1,0:T(8,128)(2,1)S(1)}, u32[]{:S(2)}, u32[]{:S(2)}) async-start(bf16[4,1024,128]{2,1,0:T(8,128)(2,1)} %shard_map.65), calls=%async_computation.2 | async-start | bytes 2097152 | tf_op jit(solution)/shard_map/all_to_all | solution.py:296
  55.1 1.9 %collective-permute-start.4 = (bf16[4,128,512]{2,1,0:T(8,128)(2,1)S(1)}, bf16[4,128,512]{2,1,0:T(8,128)(2,1)S(1)}, u32[]{:S(2)}, u32[]{:S(2)}) collective-permute-start(bf16[4,128,512]{2,1,0:T(8,128)(2,1)S(1)} %all-to-all-done.1), channel_id=1, source_target_pairs={{0,16},{1,17},{2,18},{3,19},{4,20},{5,21},{6,22},{7,23},{8,24},{9,... | collective-permute-start | bytes 1572872 | tf_op jit(solution)/shard_map/ppermute | solution.py:338
  57.0 2.8 %collective-permute-start.5 = (bf16[4,128,512]{2,1,0:T(8,128)(2,1)S(1)}, bf16[4,128,512]{2,1,0:T(8,128)(2,1)S(1)}, u32[]{:S(2)}, u32[]{:S(2)}) collective-permute-start(bf16[4,128,512]{2,1,0:T(8,128)(2,1)S(1)} %all-to-all-done.1), channel_id=1, source_target_pairs={{0,1},{1,0},{2,3},{3,2},{4,5},{5,4},{6,7},{7,6},{8,9},{9,8},{10,11... | collective-permute-start | bytes 1572872 | tf_op jit(solution)/shard_map/ppermute | solution.py:299
  59.8 3.5 %collective-permute-start.3 = (bf16[192,1024]{1,0:T(8,128)(2,1)S(1)}, bf16[192,1024]{1,0:T(8,128)(2,1)S(1)}, u32[]{:S(2)}, u32[]{:S(2)}) collective-permute-start(bf16[192,1024]{1,0:T(8,128)(2,1)S(1)} %shard_map.67.own_at), channel_id=1, source_target_pairs={{0,24},{1,25},{2,26},{3,27},{4,28},{5,29},{6,30},{7,31},{8,16},{9,... | collective-permute-start | bytes 1179656 | tf_op jit(solution)/shard_map/ppermute | solution.py:319
  63.3 10.3 %collective-permute-done.3.mirrored_at = bf16[192,1024]{1,0:T(8,128)(2,1)S(1)} collective-permute-done((bf16[192,1024]{1,0:T(8,128)(2,1)S(1)}, bf16[192,1024]{1,0:T(8,128)(2,1)S(1)}, u32[]{:S(2)}, u32[]{:S(2)}) %collective-permute-start.3) | collective-permute-done | bytes 393248 | tf_op jit(solution)/shard_map/ppermute | solution.py:319
  73.6 0.8 copy-done.1
  75.3 2.7 %collective-permute-start.6 = (bf16[4,1024,128]{2,1,0:T(8,128)(2,1)S(1)}, bf16[4,1024,128]{2,1,0:T(8,128)(2,1)S(1)}, u32[]{:S(2)}, u32[]{:S(2)}) collective-permute-start(bf16[4,1024,128]{2,1,0:T(8,128)(2,1)S(1)} %all-to-all-done.2.o_near), channel_id=1, source_target_pairs={{0,1},{1,0},{2,3},{3,2},{4,5},{5,4},{6,7},{7,6},{8,9},{9,8},{10,11... | collective-permute-start | bytes 3145736 | tf_op jit(solution)/shard_map/ppermute | solution.py:299
  78.0 1.9 %collective-permute-start.7 = (bf16[4,128,512]{2,1,0:T(8,128)(2,1)}, bf16[4,128,512]{2,1,0:T(8,128)(2,1)S(1)}, u32[]{:S(2)}, u32[]{:S(2)}) collective-permute-start(bf16[4,128,512]{2,1,0:T(8,128)(2,1)} %copy-done.1), channel_id=1, source_target_pairs={{0,1},{1,0},{2,3},{3,2},{4,5},{5,4},{6,7},{7,6},{8,9},{9,8},{10,11... | collective-permute-start | bytes 1572872 | tf_op jit(solution)/shard_map/ppermute | solution.py:299
  79.9 2.1 %collective-permute-done.7 = bf16[4,128,512]{2,1,0:T(8,128)(2,1)S(1)} collective-permute-done((bf16[4,128,512]{2,1,0:T(8,128)(2,1)}, bf16[4,128,512]{2,1,0:T(8,128)(2,1)S(1)}, u32[]{:S(2)}, u32[]{:S(2)}) %collective-permute-start.7) | collective-permute-done | bytes 524320 | tf_op jit(solution)/shard_map/ppermute | solution.py:299
  82.0 1.0 copy-done.2
  83.0 1.0 copy-done.5
  84.1 5.3 %shard_map.69 = (bf16[512,128]{1,0:T(8,128)(2,1)S(1)}, bf16[1040,128]{1,0:T(8,128)(2,1)S(1)}, bf16[128,1024]{1,0:T(8,128)(2,1)S(1)}) custom-call(bf16[4,1040,128]{2,1,0:T(8,128)(2,1)S(1)} %all-to-all-done.near.ready, bf16[4,1040,128]{2,1,0:T(8,128)(2,1)} %collective-permute-done.2.far, f32[1,1024]{1,0:T(1,128)S(1)} %get-tuple-element.40.gain, ...), custom_call_target="tpu_custom_call" | custom-call | flops 4400000000 | tf_op jit(solution)/shard_map/pallas_call | solution.py:264
  90.1 3.9 %collective-permute-start.9 = (bf16[1040,128]{1,0:T(8,128)(2,1)S(1)}, bf16[1040,128]{1,0:T(8,128)(2,1)S(1)}, u32[]{:S(2)}, u32[]{:S(2)}) collective-permute-start(bf16[1040,128]{1,0:T(8,128)(2,1)S(1)} %get-tuple-element.32.refs_1_), channel_id=1, source_target_pairs={{0,8},{1,9},{2,10},{3,11},{4,12},{5,13},{6,14},{7,15},{8,0},{9,1},... | collective-permute-start | bytes 798728 | tf_op jit(solution)/shard_map/ppermute | solution.py:366
  94.1 5.2 %shard_map.68 = (bf16[512,128]{1,0:T(8,128)(2,1)S(1)}, bf16[1040,128]{1,0:T(8,128)(2,1)S(1)}, bf16[128,1024]{1,0:T(8,128)(2,1)S(1)}) custom-call(bf16[4,1040,128]{2,1,0:T(8,128)(2,1)S(1)} %all-to-all-done.near.ready, bf16[4,1040,128]{2,1,0:T(8,128)(2,1)} %collective-permute-done.2.far, f32[1,1024]{1,0:T(1,128)S(1)} %get-tuple-element.40.gain, ...), custom_call_target="tpu_custom_call" | custom-call | flops 4400000000 | tf_op jit(solution)/shard_map/pallas_call | solution.py:264
  99.3 11.6 %collective-permute-start.8 = (bf16[1040,128]{1,0:T(8,128)(2,1)S(1)}, bf16[1040,128]{1,0:T(8,128)(2,1)S(1)}, u32[]{:S(2)}, u32[]{:S(2)}) collective-permute-start(bf16[1040,128]{1,0:T(8,128)(2,1)S(1)} %get-tuple-element.30.refs_3_.refs_1_), channel_id=1, source_target_pairs={{0,504},{1,505},{2,506},{3,507},{4,508},{5,509},{6,510},{7,511},{8... | collective-permute-start | bytes 798728 | tf_op jit(solution)/shard_map/ppermute | solution.py:366
  110.9 2.9 %shard_map.70.refs_3_ = bf16[4,128,128]{2,1,0:T(8,128)(2,1)S(1)} custom-call(bf16[512,128]{1,0:T(8,128)(2,1)S(1)} %get-tuple-element.31.refs_0_, bf16[1040,128]{1,0:T(8,128)(2,1)S(1)} %get-tuple-element.32.refs_1_, bf16[1040,128]{1,0:T(8,128)(2,1)S(1)} %collective-permute-done.9.refs_2_, bf16[1040,128]{1,0:T(8,128)(2,1)S(1)} %get-tuple-element.30.refs_3_.refs_1_), custom_call_target="tpu_custom_call" | custom-call | tf_op jit(solution)/shard_map/pallas_call | solution.py:264
  113.8 3.4 %collective-permute-done.8.refs_2_ = bf16[1040,128]{1,0:T(8,128)(2,1)S(1)} collective-permute-done((bf16[1040,128]{1,0:T(8,128)(2,1)S(1)}, bf16[1040,128]{1,0:T(8,128)(2,1)S(1)}, u32[]{:S(2)}, u32[]{:S(2)}) %collective-permute-start.8) | collective-permute-done | bytes 266272 | tf_op jit(solution)/shard_map/ppermute | solution.py:366
  117.2 3.6 %shard_map.71 = bf16[8,128,128]{2,1,0:T(8,128)(2,1)} custom-call(bf16[512,128]{1,0:T(8,128)(2,1)S(1)} %get-tuple-element.29.refs_0_, bf16[1040,128]{1,0:T(8,128)(2,1)S(1)} %get-tuple-element.30.refs_3_.refs_1_, bf16[1040,128]{1,0:T(8,128)(2,1)S(1)} %collective-permute-done.8.refs_2_, bf16[4,128,128]{2,1,0:T(8,128)(2,1)S(1)} %shard_map.70.refs_3_), custom_call_target="tpu_custom_call" | custom-call | flops 3300000000 | tf_op jit(solution)/shard_map/pallas_call | solution.py:264
  120.8 5.7 %all-to-all-start.3 = ((bf16[8,128,128]{2,1,0:T(8,128)(2,1)}), bf16[8,128,128]{2,1,0:T(8,128)(2,1)S(1)}, u32[]{:S(2)}, u32[]{:S(2)}) async-start(bf16[8,128,128]{2,1,0:T(8,128)(2,1)} %shard_map.71), calls=%async_computation.3 | async-start | bytes 524288 | tf_op jit(solution)/shard_map/all_to_all | solution.py:382
  126.5 6.5 %all-to-all-done.3.parts = bf16[8,128,128]{2,1,0:T(8,128)(2,1)S(1)} async-done(((bf16[8,128,128]{2,1,0:T(8,128)(2,1)}), bf16[8,128,128]{2,1,0:T(8,128)(2,1)S(1)}, u32[]{:S(2)}, u32[]{:S(2)}) %all-to-all-start.3) | async-done | bytes 262176 | tf_op jit(solution)/shard_map/all_to_all | solution.py:382
  133.0 1.6 %copy-done = bf16[1,1024,1024]{2,1,0:T(8,128)(2,1)S(1)} copy-done((bf16[1,1024,1024]{2,1,0:T(8,128)(2,1)S(1)}, bf16[1,1024,1024]{2,1,0:T(8,128)(2,1)}, u32[]{:S(2)}) %copy-start) | copy-done | bytes 2097176
  134.6 1.4 shard_map.72
  (45 shorter events, 3.7 us)
Async XLA Ops:
  6.5 0.9 copy-start.7
  7.5 0.7 copy-start.8
  8.1 0.7 copy-start.9
  10.1 5.2 %copy-start.14 = (bf16[2,1024,192]{1,2,0:T(8,128)(2,1)S(1)}, bf16[2,1024,192]{1,2,0:T(8,128)(2,1)}, u32[]{:S(2)}) copy-start(bf16[2,1024,192]{1,2,0:T(8,128)(2,1)} %param.10) | copy-start | bytes 2359300
  10.1 18.1 %all-to-all-start = ((bf16[4,1040,128]{2,1,0:T(8,128)(2,1)}), bf16[4,1040,128]{2,1,0:T(8,128)(2,1)S(1)}, u32[]{:S(2)}, u32[]{:S(2)}) async-start(bf16[4,1040,128]{2,1,0:T(8,128)(2,1)} %shard_map.64), calls=%async_computation | async-start | bytes 2129920 | tf_op jit(solution)/shard_map/all_to_all | solution.py:296
  15.2 4.5 %copy-start.15 = (bf16[2,64,1024]{2,1,0:T(8,128)(2,1)S(1)}, bf16[2,64,1024]{2,1,0:T(8,128)(2,1)}, u32[]{:S(2)}) copy-start(bf16[2,64,1024]{2,1,0:T(8,128)(2,1)} %param.11) | copy-start | bytes 786436
  15.2 111.3 %all-gather.3.cloned.1.call-start = ((), (), s32[]{:S(2)}) async-start(), calls=%async_computation.4 | async-start | bytes 2228224 | tf_op jit(solution)/shard_map/all_gather | solution.py:303
  15.2 20.3 %copy-start.16 = (f32[2,1024]{1,0:T(2,128)S(1)}, f32[2,1024]{1,0:T(2,128)}, u32[]{:S(2)}) copy-start(f32[2,1024]{1,0:T(2,128)} %param.9) | copy-start | bytes 24580
  15.3 12.9 %collective-permute-start = (bf16[192,1024]{1,0:T(8,128)(2,1)S(1)}, bf16[192,1024]{1,0:T(8,128)(2,1)S(1)}, u32[]{:S(2)}, u32[]{:S(2)}) collective-permute-start(bf16[192,1024]{1,0:T(8,128)(2,1)S(1)} %get-tuple-element.36.own_at), channel_id=1, source_target_pairs={{0,24},{1,25},{2,26},{3,27},{4,28},{5,29},{6,30},{7,31},{8,16},{9,... | collective-permute-start | bytes 1179656 | tf_op jit(solution)/shard_map/ppermute | solution.py:307
  20.4 7.8 %collective-permute-start.1 = (bf16[64,1024]{1,0:T(8,128)(2,1)S(1)}, bf16[64,1024]{1,0:T(8,128)(2,1)S(1)}, u32[]{:S(2)}, u32[]{:S(2)}) collective-permute-start(bf16[64,1024]{1,0:T(8,128)(2,1)S(1)} %get-tuple-element.38.own), channel_id=1, source_target_pairs={{0,24},{1,25},{2,26},{3,27},{4,28},{5,29},{6,30},{7,31},{8,16},{9,... | collective-permute-start | bytes 393224 | tf_op jit(solution)/shard_map/ppermute | solution.py:308
  28.2 12.5 %collective-permute-start.2 = (bf16[4,1040,128]{2,1,0:T(8,128)(2,1)S(1)}, bf16[4,1040,128]{2,1,0:T(8,128)(2,1)}, u32[]{:S(2)}, u32[]{:S(2)}) collective-permute-start(bf16[4,1040,128]{2,1,0:T(8,128)(2,1)S(1)} %all-to-all-done.near.ready), channel_id=1, source_target_pairs={{0,1},{1,0},{2,3},{3,2},{4,5},{5,4},{6,7},{7,6},{8,9},{9,8},{10,11... | collective-permute-start | bytes 3194888 | tf_op jit(solution)/shard_map/ppermute | solution.py:299
  36.4 14.4 %all-to-all-start.1 = ((bf16[4,128,512]{2,1,0:T(8,128)(2,1)}), bf16[4,128,512]{2,1,0:T(8,128)(2,1)S(1)}, u32[]{:S(2)}, u32[]{:S(2)}) async-start(bf16[4,128,512]{2,1,0:T(8,128)(2,1)} %shard_map.66), calls=%async_computation.1 | async-start | bytes 1048576 | tf_op jit(solution)/shard_map/all_to_all | solution.py:296
  50.8 24.4 %all-to-all-start.2 = ((bf16[4,1024,128]{2,1,0:T(8,128)(2,1)}), bf16[4,1024,128]{2,1,0:T(8,128)(2,1)S(1)}, u32[]{:S(2)}, u32[]{:S(2)}) async-start(bf16[4,1024,128]{2,1,0:T(8,128)(2,1)} %shard_map.65), calls=%async_computation.2 | async-start | bytes 2097152 | tf_op jit(solution)/shard_map/all_to_all | solution.py:296
  55.1 18.6 %collective-permute-start.4 = (bf16[4,128,512]{2,1,0:T(8,128)(2,1)S(1)}, bf16[4,128,512]{2,1,0:T(8,128)(2,1)S(1)}, u32[]{:S(2)}, u32[]{:S(2)}) collective-permute-start(bf16[4,128,512]{2,1,0:T(8,128)(2,1)S(1)} %all-to-all-done.1), channel_id=1, source_target_pairs={{0,16},{1,17},{2,18},{3,19},{4,20},{5,21},{6,22},{7,23},{8,24},{9,... | collective-permute-start | bytes 1572872 | tf_op jit(solution)/shard_map/ppermute | solution.py:338
  57.0 17.5 %collective-permute-start.5 = (bf16[4,128,512]{2,1,0:T(8,128)(2,1)S(1)}, bf16[4,128,512]{2,1,0:T(8,128)(2,1)S(1)}, u32[]{:S(2)}, u32[]{:S(2)}) collective-permute-start(bf16[4,128,512]{2,1,0:T(8,128)(2,1)S(1)} %all-to-all-done.1), channel_id=1, source_target_pairs={{0,1},{1,0},{2,3},{3,2},{4,5},{5,4},{6,7},{7,6},{8,9},{9,8},{10,11... | collective-permute-start | bytes 1572872 | tf_op jit(solution)/shard_map/ppermute | solution.py:299
  59.8 13.8 %collective-permute-start.3 = (bf16[192,1024]{1,0:T(8,128)(2,1)S(1)}, bf16[192,1024]{1,0:T(8,128)(2,1)S(1)}, u32[]{:S(2)}, u32[]{:S(2)}) collective-permute-start(bf16[192,1024]{1,0:T(8,128)(2,1)S(1)} %shard_map.67.own_at), channel_id=1, source_target_pairs={{0,24},{1,25},{2,26},{3,27},{4,28},{5,29},{6,30},{7,31},{8,16},{9,... | collective-permute-start | bytes 1179656 | tf_op jit(solution)/shard_map/ppermute | solution.py:319
  73.6 0.8 copy-start.1
  74.5 0.8 copy-start.4
  75.3 6.7 %collective-permute-start.6 = (bf16[4,1024,128]{2,1,0:T(8,128)(2,1)S(1)}, bf16[4,1024,128]{2,1,0:T(8,128)(2,1)S(1)}, u32[]{:S(2)}, u32[]{:S(2)}) collective-permute-start(bf16[4,1024,128]{2,1,0:T(8,128)(2,1)S(1)} %all-to-all-done.2.o_near), channel_id=1, source_target_pairs={{0,1},{1,0},{2,3},{3,2},{4,5},{5,4},{6,7},{7,6},{8,9},{9,8},{10,11... | collective-permute-start | bytes 3145736 | tf_op jit(solution)/shard_map/ppermute | solution.py:299
  78.0 4.0 %collective-permute-start.7 = (bf16[4,128,512]{2,1,0:T(8,128)(2,1)}, bf16[4,128,512]{2,1,0:T(8,128)(2,1)S(1)}, u32[]{:S(2)}, u32[]{:S(2)}) collective-permute-start(bf16[4,128,512]{2,1,0:T(8,128)(2,1)} %copy-done.1), channel_id=1, source_target_pairs={{0,1},{1,0},{2,3},{3,2},{4,5},{5,4},{6,7},{7,6},{8,9},{9,8},{10,11... | collective-permute-start | bytes 1572872 | tf_op jit(solution)/shard_map/ppermute | solution.py:299
  82.0 1.0 copy-start.2
  83.0 1.0 copy-start.5
  84.1 10.0 %copy-start.3 = (bf16[4,128,512]{2,1,0:T(8,128)(2,1)S(1)}, bf16[4,128,512]{2,1,0:T(8,128)(2,1)}, u32[]{:S(2)}) copy-start(bf16[4,128,512]{2,1,0:T(8,128)(2,1)} %copy-done.1) | copy-start | bytes 1572868
  84.1 10.0 %copy-start.6 = (bf16[4,128,512]{2,1,0:T(8,128)(2,1)S(1)}, bf16[4,128,512]{2,1,0:T(8,128)(2,1)}, u32[]{:S(2)}) copy-start(bf16[4,128,512]{2,1,0:T(8,128)(2,1)} %copy-done.4) | copy-start | bytes 1572868
  89.4 0.7 copy-start.10
  90.1 20.8 %collective-permute-start.9 = (bf16[1040,128]{1,0:T(8,128)(2,1)S(1)}, bf16[1040,128]{1,0:T(8,128)(2,1)S(1)}, u32[]{:S(2)}, u32[]{:S(2)}) collective-permute-start(bf16[1040,128]{1,0:T(8,128)(2,1)S(1)} %get-tuple-element.32.refs_1_), channel_id=1, source_target_pairs={{0,8},{1,9},{2,10},{3,11},{4,12},{5,13},{6,14},{7,15},{8,0},{9,1},... | collective-permute-start | bytes 798728 | tf_op jit(solution)/shard_map/ppermute | solution.py:366
  99.3 17.9 %copy-start.12 = (bf16[128,1024]{1,0:T(8,128)(2,1)}, bf16[128,1024]{1,0:T(8,128)(2,1)S(1)}, u32[]{:S(2)}) copy-start(bf16[128,1024]{1,0:T(8,128)(2,1)S(1)} %get-tuple-element.34.stream_q) | copy-start | bytes 786436
  99.3 17.9 %collective-permute-start.8 = (bf16[1040,128]{1,0:T(8,128)(2,1)S(1)}, bf16[1040,128]{1,0:T(8,128)(2,1)S(1)}, u32[]{:S(2)}, u32[]{:S(2)}) collective-permute-start(bf16[1040,128]{1,0:T(8,128)(2,1)S(1)} %get-tuple-element.30.refs_3_.refs_1_), channel_id=1, source_target_pairs={{0,504},{1,505},{2,506},{3,507},{4,508},{5,509},{6,510},{7,511},{8... | collective-permute-start | bytes 798728 | tf_op jit(solution)/shard_map/ppermute | solution.py:366
  117.2 15.8 %copy-start.11 = (bf16[128,1024]{1,0:T(8,128)(2,1)S(1)}, bf16[128,1024]{1,0:T(8,128)(2,1)}, u32[]{:S(2)}) copy-start(bf16[128,1024]{1,0:T(8,128)(2,1)} %copy-done.10) | copy-start | bytes 786436
  117.2 15.8 %copy-start.13 = (bf16[128,1024]{1,0:T(8,128)(2,1)S(1)}, bf16[128,1024]{1,0:T(8,128)(2,1)}, u32[]{:S(2)}) copy-start(bf16[128,1024]{1,0:T(8,128)(2,1)} %copy-done.12) | copy-start | bytes 786436
  120.8 12.2 %all-to-all-start.3 = ((bf16[8,128,128]{2,1,0:T(8,128)(2,1)}), bf16[8,128,128]{2,1,0:T(8,128)(2,1)S(1)}, u32[]{:S(2)}, u32[]{:S(2)}) async-start(bf16[8,128,128]{2,1,0:T(8,128)(2,1)} %shard_map.71), calls=%async_computation.3 | async-start | bytes 524288 | tf_op jit(solution)/shard_map/all_to_all | solution.py:382
  133.0 1.6 %copy-start = (bf16[1,1024,1024]{2,1,0:T(8,128)(2,1)S(1)}, bf16[1,1024,1024]{2,1,0:T(8,128)(2,1)}, u32[]{:S(2)}) copy-start(bf16[1,1024,1024]{2,1,0:T(8,128)(2,1)} %all-gather.3.cloned.1.call-done) | copy-start | bytes 6291460
Sparse Core Ops, SparseCore 0:
  35.7 70.6 all-gather.2

commit v4 on v3

--- a/solution.py
+++ b/solution.py
@@ -72,7 +72,17 @@
     return jnp.transpose(jnp.concatenate(results, axis=0)).astype(BF16)
 
 
-def order_kernel(points, order, tags, out):
+def fetch(sources, targets, sems):
+    copies = [pltpu.make_async_copy(a, b, sems.at[i]) for i, (a, b) in enumerate(zip(sources, targets))]
+    for copy in copies:
+        copy.start()
+    return copies
+
+
+def order_kernel(points_at, order_at, tags_at, out, points, order, tags, sems):
+    copies = fetch((order_at, points_at, tags_at), (order, points, tags), sems)
+    for copy in copies:
+        copy.wait()
     row = lax.broadcasted_iota(jnp.int32, (ROWS, ROWS), 0)
     picks = jnp.transpose((row == order[...]).astype(F32)).astype(BF16)
     ordered = dot(picks, points[...]).astype(BF16)
@@ -86,13 +96,6 @@
 def joined(own, mirrored, kind):
     cut = slice(kind * HEAD_DIM, (kind + 1) * HEAD_DIM)
     return jnp.concatenate([own[cut, :], mirrored[cut, :]], axis=0)
-
-
-def fetch(sources, targets, sems):
-    copies = [pltpu.make_async_copy(a, b, sems.at[i]) for i, (a, b) in enumerate(zip(sources, targets))]
-    for copy in copies:
-        copy.start()
-    return copies
 
 
 def project(normed, own, mirrored, queries, keys, turned):
@@ -146,10 +149,10 @@
 
 
 def middle_kernel(
-    part, near, far, gain, o_near, o_far, w_mine, w_mine_far, w_next, w_next_far, own_at, mirrored_at,
-    q_out, kv, st_out, heads, update, normed, turned, w, own, mirrored, o_sems, w_sems,
+    part, near, far, gain, o_near, o_far, w_own, w_own_far, w_mir, w_mir_far, own_at, mirrored_at,
+    ready, q_out, kv, st_out, heads, update, normed, turned, w, own, mirrored, o_sems, w_sems,
 ):
-    my_y, xl, half = lax.axis_index("y"), lax.axis_index("xl"), half_of(part)
+    my_y, half = lax.axis_index("y"), half_of(part)
     sources, targets = [], []
     for s in range(2):
         span = slice(s * 256, (s + 1) * 256)
@@ -162,17 +165,16 @@
                 heads.at[span, (g + 4) * LANES : (g + 5) * LANES],
             ]
     o_copies = fetch(sources, targets, o_sems)
-    w_copies = fetch(
-        (w_mine, w_mine_far, w_next, w_next_far, own_at, mirrored_at),
-        (w.at[0, :HALF], w.at[0, HALF:], w.at[1, :HALF], w.at[1, HALF:], own, mirrored),
-        w_sems,
-    )
-    for copy in o_copies + w_copies[:2]:
+    sources, targets = [own_at, mirrored_at], [own, mirrored]
+    for i, ref in enumerate((w_own, w_mir, w_own_far, w_mir_far)):
+        for g in range(4):
+            row = (i // 2 * 4 + g) * LANES + i % 2 * HEAD_DIM
+            sources.append(ref.at[g])
+            targets.append(w.at[row : row + HEAD_DIM, :])
+    w_copies = fetch(sources, targets, w_sems)
+    for copy in o_copies + w_copies:
         copy.wait()
-    update[:, pl.ds(pl.multiple_of(xl * HALF, HALF), HALF)] = dot(heads[...], w[0])
-    for copy in w_copies[2:]:
-        copy.wait()
-    update[:, pl.ds(pl.multiple_of((1 - xl) * HALF, HALF), HALF)] = dot(heads[...], w[1])
+    update[...] = dot(heads[...], w[...])
     rows = []
     for s, ref in enumerate((near, far)):
         for yy in range(2):
@@ -228,17 +230,9 @@
 
 
 def last_kernel(parts, w, stream_p, stream_q, out, heads):
-    xh, y_half = lax.axis_index("xh"), lax.axis_index("y") // 2
-    for b in range(4):
-        pair = []
-        for block in (parts[2 * b], parts[2 * b + 1]):
-            turned = jnp.concatenate([block[:, HEAD_DIM:], block[:, :HEAD_DIM]], axis=1)
-            pair.append(jnp.where(xh == 0, block, turned))
-        for k in range(2):
-            cut = slice(k * HEAD_DIM, (k + 1) * HEAD_DIM)
-            heads[:, (k * 4 + b) * LANES : (k * 4 + b + 1) * LANES] = jnp.concatenate(
-                [pair[0][:, cut], pair[1][:, cut]], axis=1
-            )
+    y_half = lax.axis_index("y") // 2
+    for g in range(8):
+        heads[:, g * LANES : (g + 1) * LANES] = parts[g]
     update = dot(heads[...], w[...])
 
     def put(stream):
@@ -248,15 +242,11 @@
     pl.when(y_half == half_of(1))(lambda: put(stream_q))
 
 
-def relay_kernel(own, far, ready, out):
-    cut = pl.ds(pl.multiple_of(lax.axis_index("xl") * HALF, HALF), HALF)
+def relay_kernel(count, *refs):
+    out = refs[-1]
     for copy in range(out.shape[0]):
-        out[copy, : own.shape[0]] = own[:, cut]
-        out[copy, own.shape[0] :] = far[:, cut]
-
-
-def pass_kernel(array, ready, out):
-    out[...] = array[...]
+        for i in range(count):
+            out[copy, i * HEAD_DIM : (i + 1) * HEAD_DIM] = refs[i][...]
 
 
 def call(kernel, micros, outs, scratch, *args, late=(), semaphores=(), megabytes=16):
@@ -300,23 +290,21 @@
 
     def on_device(points, order, scan_ids, ln_gain, w_qkv, w_out):
         w_turned = jnp.swapaxes(w_qkv, 1, 2)
-        w_last = lax.all_gather(w_out[1], head_axes, axis=0, tiled=True)
         (copies,) = call(
-            order_kernel, 1.2, [(4, EXT, LANES)], [], points, order, scan_ids.reshape(1, ROWS)
+            order_kernel, 1.2, [(4, EXT, LANES)],
+            [((ROWS, D), BF16), ((1, ROWS), jnp.int32), ((1, ROWS), jnp.int32)],
+            late=(points, order, scan_ids.reshape(1, ROWS)), semaphores=(3,), megabytes=56,
         )
         first_far = lax.ppermute(w_turned[0], AXES, mirror)
-        out_far = lax.ppermute(w_out[0], AXES, mirror)
+        second_far = lax.ppermute(w_turned[1], AXES, mirror)
         x_near = over_y(copies)
-        x_near, first_far, out_far = lax.optimization_barrier((x_near, first_far, out_far))
+        x_near, first_far = lax.optimization_barrier((x_near, first_far))
         x_far = swapped(x_near)
         (shares,) = call(
-            relay_kernel, 1, [(4, ROWS, HALF)], [], w_out[0], out_far, late=(x_near,), megabytes=4
-        )
-        w_mine = over_y(shares)
-        (second_own,) = call(
-            pass_kernel, 1, [(3 * HEAD_DIM, D)], [], w_turned[1], late=(x_near,), megabytes=4
-        )
-        second_far = lax.ppermute(second_own, AXES, mirror)
+            functools.partial(relay_kernel, 1), 1, [(4, HEAD_DIM, D)], [], w_out[0],
+            late=(x_near,), megabytes=4,
+        )
+        w_own = over_y(shares)
         projection = [((3 * HEAD_DIM, D), BF16)] * 2
         (o_copies,) = call(
             first_kernel,
@@ -332,18 +320,23 @@
                 *projection,
             ],
             x_near, x_far, ln_gain[0:1],
-            late=(w_turned[0], first_far), semaphores=(2,),
-        )
-        o_copies, w_mine = lax.optimization_barrier((o_copies, w_mine))
-        w_next = lax.ppermute(w_mine, AXES, beside)
-        w_mine_far = swapped(w_mine)
+            late=(w_turned[0], first_far), semaphores=(2,), megabytes=56,
+        )
+        o_copies, w_own, second_far = lax.optimization_barrier((o_copies, w_own, second_far))
+        w_mir = lax.ppermute(w_own, AXES, mirror)
+        w_own_far = swapped(w_own)
+        last_far = lax.ppermute(w_out[1], AXES, mirror)
         o_near = over_y(o_copies)
-        o_near, second_far, w_next, w_mine_far = lax.optimization_barrier(
-            (o_near, second_far, w_next, w_mine_far)
+        o_near, w_mir, w_own_far, last_far = lax.optimization_barrier(
+            (o_near, w_mir, w_own_far, last_far)
         )
         o_far = swapped(o_near)
-        w_next_far = swapped(w_next)
-        w_first = [w.reshape(HALF, HALF) for w in (w_mine, w_mine_far, w_next, w_next_far)]
+        w_mir_far = swapped(w_mir)
+        (shares,) = call(
+            functools.partial(relay_kernel, 2), 1, [(8, ROWS, D)], [], w_out[1], last_far,
+            late=(o_near,), megabytes=4,
+        )
+        w_last = lax.all_to_all(shares, ("y", "c"), 0, 0, tiled=True).reshape(D, D)
         middle, halos = [], []
         for part, links in enumerate((inner, outer)):
             middle.append(
@@ -356,11 +349,12 @@
                         ((HALF, D), F32),
                         ((HALF, D), BF16),
                         ((LANES, HALF), BF16),
-                        ((2, D, HALF), BF16),
+                        ((D, D), BF16),
                         *projection,
                     ],
                     x_near, x_far, ln_gain[1:2],
-                    late=(o_near, o_far, *w_first, second_own, second_far), semaphores=(16, 6),
+                    late=(o_near, o_far, w_own, w_own_far, w_mir, w_mir_far, w_turned[1], second_far, shares),
+                    semaphores=(16, 18), megabytes=56,
                 )
             )
             halos.append(lax.ppermute(middle[part][1], AXES, links))
@@ -379,6 +373,7 @@
                 queries, kv, halos[part], *([parts] if part else []),
                 late=() if part else (middle[1][1],), megabytes=8,
             )
+        parts, w_last = lax.optimization_barrier((parts, w_last))
         parts = lax.all_to_all(parts, ("y", "c"), 0, 0, tiled=True)
         (result,) = call(
             last_kernel, 1.5, [(ROWS, D)], [((ROWS, D), BF16)],

time: 144 us -> 134 us (0.931)
  between operations: 13.6 us -> 0.36 us
  blocking collectives: 0 us -> 11.6 us
  waiting for transfers between devices: 28 us -> 17.7 us
  Pallas kernels: 30.7 us -> 35.3 us
  local copies, waits for them, and re-layouts: 9.03 us -> 4.66 us
  starting transfers between devices: 61.5 us -> 63.5 us
    all_to_all x0 -> x1, blocking collectives: none -> 11.6 us  [on_device(): parts = lax.all_to_all(parts, ('y', 'c'), 0, 0, tiled=True)]
    ppermute x3, waiting for transfers between devices: 16 us -> 8.96 us  [the longest x1 8.95 us: on_device(): last_far = lax.ppermute(w_out[1], AXES, mirror)]
    all_to_all x1, waiting for transfers between devices: 6.5 us -> 0.01 us  [on_device(): w_last = lax.all_to_all(shares, ('y', 'c'), 0, 0, tiled=True).reshape(D, D)]
    ppermute x1, waiting for transfers between devices: 0.01 us -> 5.84 us  [on_device(): first_far = lax.ppermute(w_turned[0], AXES, mirror)]
    pallas_call x9, Pallas kernels: 30.7 us -> 35.3 us  [call(): pl.pallas_call(kernel, out_shape=[jax.ShapeDtypeStruct(shape, BF16) for s...]
    unnamed x34 -> x36, local copies, waits for them, and re-layouts: 8.3 us -> 3.99 us
    ppermute x3, starting transfers between devices: 7.53 us -> 10.4 us  [the longest x1 4.21 us: on_device(): second_far = lax.ppermute(w_turned[1], AXES, mirror)]
    ppermute x4, waiting for transfers between devices: 2.09 us -> 0.01 us  [swapped(): return lax.ppermute(array, AXES, other_core)]
  transfers between devices with their start and end apart: 15 -> 14, of which waited for: 5 -> 3; matrix products, arithmetic and copies ran while one was open for 1% -> 1% of each run, Pallas kernels for 20% -> 24%
where the time goes in v4:
time: 134 us; the launch traced here: 133 us
  starting transfers between devices  63.5 us (47%)
  Pallas kernels  35.3 us (26%)
  waiting for transfers between devices  17.7 us (13%)
  blocking collectives  11.6 us (9%)
  local copies, waits for them, and re-layouts  4.66 us (3%)
    pallas_call x9, Pallas kernels, call(): pl.pallas_call(kernel, out_shape=[jax.ShapeDtypeStruct(shape, BF16) for s...  35.3 us
    ppermute x4, starting transfers between devices, swapped(): return lax.ppermute(array, AXES, other_core)  16.7 us
    ppermute x2, starting transfers between devices, on_device(): halos.append(lax.ppermute(middle[part][1], AXES, links))  14 us
    all_to_all x3, starting transfers between devices, over_y(): return lax.all_to_all(copies, 'y', 0, 0, tiled=True)  12.8 us
    all_to_all x1, blocking collectives, on_device(): parts = lax.all_to_all(parts, ('y', 'c'), 0, 0, tiled=True)  11.6 us
    ppermute x1, waiting for transfers between devices, on_device(): last_far = lax.ppermute(w_out[1], AXES, mirror)  8.95 us
    ppermute x1, waiting for transfers between devices, on_device(): first_far = lax.ppermute(w_turned[0], AXES, mirror)  5.84 us
    all_to_all x1, starting transfers between devices, on_device(): w_last = lax.all_to_all(shares, ('y', 'c'), 0, 0, tiled=True).reshape(D, D)  5.02 us
  transfers between devices with their start and end apart: 14, of which 3 were waited for; matrix products, arithmetic and copies ran while one was open for 1% of the time, Pallas kernels for 24%

profile of v4, /device:TPU:1, one launch (start us, length us, event | category | flops | bytes accessed | tf_op | source)
XLA Modules:
  0.0 133.1 jit_solution(15858349993827470402)
XLA Ops:
  0.0 2.3 %shard_map.64 = bf16[4,1040,128]{2,1,0:T(8,128)(2,1)} custom-call(bf16[128,1024]{1,0:T(8,128)(2,1)} %points_at.1, s32[1,128]{1,0:T(1,128)} %order_at.1, s32[1,128]{1,0:T(1,128)} %bitcast.13), custom_call_target="tpu_custom_call" | custom-call | flops 1320000000 | tf_op jit(solution)/shard_map/pallas_call | solution.py:254
  2.3 5.2 %all-to-all-start = ((bf16[4,1040,128]{2,1,0:T(8,128)(2,1)}), bf16[4,1040,128]{2,1,0:T(8,128)(2,1)S(1)}, u32[]{:S(2)}, u32[]{:S(2)}) async-start(bf16[4,1040,128]{2,1,0:T(8,128)(2,1)} %shard_map.64), calls=%async_computation | async-start | bytes 2129920 | tf_op jit(solution)/shard_map/all_to_all | solution.py:286
  7.5 4.5 %collective-permute-start = (bf16[192,1024]{1,0:T(8,128)(2,1)S(1)}, bf16[192,1024]{1,0:T(8,128)(2,1)S(1)}, u32[]{:S(2)}, u32[]{:S(2)}) collective-permute-start(bf16[192,1024]{1,0:T(8,128)(2,1)S(1)} %get-tuple-element.40.own_at), channel_id=1, source_target_pairs={{0,24},{1,25},{2,26},{3,27},{4,28},{5,29},{6,30},{7,31},{8,16},{9,... | collective-permute-start | bytes 1179656 | tf_op jit(solution)/shard_map/ppermute | solution.py:298
  12.1 5.8 %collective-permute-done.mirrored_at = bf16[192,1024]{1,0:T(8,128)(2,1)S(1)} collective-permute-done((bf16[192,1024]{1,0:T(8,128)(2,1)S(1)}, bf16[192,1024]{1,0:T(8,128)(2,1)S(1)}, u32[]{:S(2)}, u32[]{:S(2)}) %collective-permute-start) | collective-permute-done | bytes 393248 | tf_op jit(solution)/shard_map/ppermute | solution.py:298
  17.9 7.8 %collective-permute-start.1 = (bf16[4,1040,128]{2,1,0:T(8,128)(2,1)S(1)}, bf16[4,1040,128]{2,1,0:T(8,128)(2,1)}, u32[]{:S(2)}, u32[]{:S(2)}) collective-permute-start(bf16[4,1040,128]{2,1,0:T(8,128)(2,1)S(1)} %all-to-all-done.near.refs_1_), channel_id=1, source_target_pairs={{0,1},{1,0},{2,3},{3,2},{4,5},{5,4},{6,7},{7,6},{8,9},{9,8},{10,11... | collective-permute-start | bytes 3194888 | tf_op jit(solution)/shard_map/ppermute | solution.py:289
  25.8 4.2 %collective-permute-start.2 = (bf16[192,1024]{1,0:T(8,128)(2,1)S(1)}, bf16[192,1024]{1,0:T(8,128)(2,1)S(1)}, u32[]{:S(2)}, u32[]{:S(2)}) collective-permute-start(bf16[192,1024]{1,0:T(8,128)(2,1)S(1)} %get-tuple-element.39.own_at), channel_id=1, source_target_pairs={{0,24},{1,25},{2,26},{3,27},{4,28},{5,29},{6,30},{7,31},{8,16},{9,... | collective-permute-start | bytes 1179656 | tf_op jit(solution)/shard_map/ppermute | solution.py:299
  30.0 0.6 fusion
  30.6 0.8 shard_map.66
  31.4 3.5 %all-to-all-start.1 = ((bf16[4,64,1024]{2,1,0:T(8,128)(2,1)}), bf16[4,64,1024]{2,1,0:T(8,128)(2,1)S(1)}, u32[]{:S(2)}, u32[]{:S(2)}) async-start(bf16[4,64,1024]{2,1,0:T(8,128)(2,1)} %shard_map.66), calls=%async_computation.1 | async-start | bytes 1048576 | tf_op jit(solution)/shard_map/all_to_all | solution.py:286
  34.9 10.1 %shard_map.65 = bf16[4,1024,128]{2,1,0:T(8,128)(2,1)} custom-call(bf16[4,1040,128]{2,1,0:T(8,128)(2,1)} %copy-done.1, bf16[4,1040,128]{2,1,0:T(8,128)(2,1)} %collective-permute-done.1.far, f32[1,1024]{1,0:T(1,128)} %get-tuple-element.43.gain, bf16[192,1024]{1,0:T(8,128)(2,1)} %copy-done.12, bf16[192,1024]{1,0:T(8,128)(2,1)} %copy-done.17), custom_call_target="tpu_custom_call" | custom-call | flops 8800000000 | tf_op jit(solution)/shard_map/pallas_call | solution.py:254
  45.1 0.7 copy-done.16
  45.8 4.2 %all-to-all-start.2 = ((bf16[4,1024,128]{2,1,0:T(8,128)(2,1)}), bf16[4,1024,128]{2,1,0:T(8,128)(2,1)S(1)}, u32[]{:S(2)}, u32[]{:S(2)}) async-start(bf16[4,1024,128]{2,1,0:T(8,128)(2,1)} %shard_map.65), calls=%async_computation.2 | async-start | bytes 2097152 | tf_op jit(solution)/shard_map/all_to_all | solution.py:286
  50.0 3.4 %collective-permute-start.3 = (bf16[4,64,1024]{2,1,0:T(8,128)(2,1)S(1)}, bf16[4,64,1024]{2,1,0:T(8,128)(2,1)}, u32[]{:S(2)}, u32[]{:S(2)}) collective-permute-start(bf16[4,64,1024]{2,1,0:T(8,128)(2,1)S(1)} %all-to-all-done.1.w_own), channel_id=1, source_target_pairs={{0,24},{1,25},{2,26},{3,27},{4,28},{5,29},{6,30},{7,31},{8,16},{9,... | collective-permute-start | bytes 1572872 | tf_op jit(solution)/shard_map/ppermute | solution.py:326
  53.4 3.3 %collective-permute-start.4 = (bf16[4,64,1024]{2,1,0:T(8,128)(2,1)S(1)}, bf16[4,64,1024]{2,1,0:T(8,128)(2,1)S(1)}, u32[]{:S(2)}, u32[]{:S(2)}) collective-permute-start(bf16[4,64,1024]{2,1,0:T(8,128)(2,1)S(1)} %all-to-all-done.1.w_own), channel_id=1, source_target_pairs={{0,1},{1,0},{2,3},{3,2},{4,5},{5,4},{6,7},{7,6},{8,9},{9,8},{10,11... | collective-permute-start | bytes 1572872 | tf_op jit(solution)/shard_map/ppermute | solution.py:289
  56.7 2.8 %collective-permute-start.5 = (bf16[64,1024]{1,0:T(8,128)(2,1)S(1)}, bf16[64,1024]{1,0:T(8,128)(2,1)S(1)}, u32[]{:S(2)}, u32[]{:S(2)}) collective-permute-start(bf16[64,1024]{1,0:T(8,128)(2,1)S(1)} %get-tuple-element.41.refs_0_), channel_id=1, source_target_pairs={{0,24},{1,25},{2,26},{3,27},{4,28},{5,29},{6,30},{7,31},{8,16},{9,... | collective-permute-start | bytes 393224 | tf_op jit(solution)/shard_map/ppermute | solution.py:328
  59.5 9.0 %collective-permute-done.5.refs_1_ = bf16[64,1024]{1,0:T(8,128)(2,1)S(1)} collective-permute-done((bf16[64,1024]{1,0:T(8,128)(2,1)S(1)}, bf16[64,1024]{1,0:T(8,128)(2,1)S(1)}, u32[]{:S(2)}, u32[]{:S(2)}) %collective-permute-start.5) | collective-permute-done | bytes 131104 | tf_op jit(solution)/shard_map/ppermute | solution.py:328
  68.5 3.7 %collective-permute-start.6 = (bf16[4,1024,128]{2,1,0:T(8,128)(2,1)S(1)}, bf16[4,1024,128]{2,1,0:T(8,128)(2,1)}, u32[]{:S(2)}, u32[]{:S(2)}) collective-permute-start(bf16[4,1024,128]{2,1,0:T(8,128)(2,1)S(1)} %all-to-all-done.2.refs_2_.o_near), channel_id=1, source_target_pairs={{0,1},{1,0},{2,3},{3,2},{4,5},{5,4},{6,7},{7,6},{8,9},{9,8},{10,11... | collective-permute-start | bytes 3145736 | tf_op jit(solution)/shard_map/ppermute | solution.py:289
  72.2 1.9 %collective-permute-start.7 = (bf16[4,64,1024]{2,1,0:T(8,128)(2,1)}, bf16[4,64,1024]{2,1,0:T(8,128)(2,1)}, u32[]{:S(2)}, u32[]{:S(2)}) collective-permute-start(bf16[4,64,1024]{2,1,0:T(8,128)(2,1)} %collective-permute-done.3.w_mir), channel_id=1, source_target_pairs={{0,1},{1,0},{2,3},{3,2},{4,5},{5,4},{6,7},{7,6},{8,9},{9,8},{10,11... | collective-permute-start | bytes 1572872 | tf_op jit(solution)/shard_map/ppermute | solution.py:289
  74.1 0.1 shard_map.67.ready
  74.3 1.3 %copy-done = bf16[8,128,1024]{2,1,0:T(8,128)(2,1)} copy-done((bf16[8,128,1024]{2,1,0:T(8,128)(2,1)}, bf16[8,128,1024]{2,1,0:T(8,128)(2,1)S(1)}, u32[]{:S(2)}) %copy-start) | copy-done | bytes 2097176
  75.6 5.0 %all-to-all-start.3 = ((bf16[8,128,1024]{2,1,0:T(8,128)(2,1)}), bf16[8,128,1024]{2,1,0:T(8,128)(2,1)S(1)}, u32[]{:S(2)}, u32[]{:S(2)}) async-start(bf16[8,128,1024]{2,1,0:T(8,128)(2,1)} %copy-done), calls=%async_computation.3 | async-start | bytes 4194304 | tf_op jit(solution)/shard_map/all_to_all | solution.py:339
  80.6 7.4 %shard_map.69 = (bf16[512,128]{1,0:T(8,128)(2,1)}, bf16[1040,128]{1,0:T(8,128)(2,1)}, bf16[128,1024]{1,0:T(8,128)(2,1)}) custom-call(bf16[4,1040,128]{2,1,0:T(8,128)(2,1)} %copy-done.1, bf16[4,1040,128]{2,1,0:T(8,128)(2,1)} %collective-permute-done.1.far, f32[1,1024]{1,0:T(1,128)} %get-tuple-element.44.gain, bf16[4,1024,128]{2,1,0:T(8,128)(2,1)} %copy-done.2, ...), custom_call_target="tpu_custom_call" | custom-call | flops 4400000000 | tf_op jit(solution)/shard_map/pallas_call | solution.py:254
  88.1 2.1 %collective-permute-start.9 = (bf16[1040,128]{1,0:T(8,128)(2,1)}, bf16[1040,128]{1,0:T(8,128)(2,1)S(1)}, u32[]{:S(2)}, u32[]{:S(2)}) collective-permute-start(bf16[1040,128]{1,0:T(8,128)(2,1)} %get-tuple-element.34.refs_1_), channel_id=1, source_target_pairs={{0,8},{1,9},{2,10},{3,11},{4,12},{5,13},{6,14},{7,15},{8,0},{9,1},... | collective-permute-start | bytes 798728 | tf_op jit(solution)/shard_map/ppermute | solution.py:360
  90.2 7.6 %shard_map.68 = (bf16[512,128]{1,0:T(8,128)(2,1)}, bf16[1040,128]{1,0:T(8,128)(2,1)}, bf16[128,1024]{1,0:T(8,128)(2,1)}) custom-call(bf16[4,1040,128]{2,1,0:T(8,128)(2,1)} %copy-done.1, bf16[4,1040,128]{2,1,0:T(8,128)(2,1)} %collective-permute-done.1.far, f32[1,1024]{1,0:T(1,128)} %get-tuple-element.44.gain, bf16[4,1024,128]{2,1,0:T(8,128)(2,1)} %copy-done.2, ...), custom_call_target="tpu_custom_call" | custom-call | flops 4400000000 | tf_op jit(solution)/shard_map/pallas_call | solution.py:254
  97.8 11.9 %collective-permute-start.8 = (bf16[1040,128]{1,0:T(8,128)(2,1)}, bf16[1040,128]{1,0:T(8,128)(2,1)S(1)}, u32[]{:S(2)}, u32[]{:S(2)}) collective-permute-start(bf16[1040,128]{1,0:T(8,128)(2,1)} %get-tuple-element.32.refs_3_.refs_1_), channel_id=1, source_target_pairs={{0,504},{1,505},{2,506},{3,507},{4,508},{5,509},{6,510},{7,511},{8... | collective-permute-start | bytes 798728 | tf_op jit(solution)/shard_map/ppermute | solution.py:360
  109.8 1.0 copy-done.4
  110.7 2.9 %shard_map.70.refs_3_ = bf16[4,128,128]{2,1,0:T(8,128)(2,1)S(1)} custom-call(bf16[512,128]{1,0:T(8,128)(2,1)S(1)} %copy-done.5, bf16[1040,128]{1,0:T(8,128)(2,1)S(1)} %copy-done.3, bf16[1040,128]{1,0:T(8,128)(2,1)S(1)} %collective-permute-done.9.refs_2_, bf16[1040,128]{1,0:T(8,128)(2,1)S(1)} %copy-done.4), custom_call_target="tpu_custom_call" | custom-call | tf_op jit(solution)/shard_map/pallas_call | solution.py:254
  113.6 2.9 %collective-permute-done.8.refs_2_ = bf16[1040,128]{1,0:T(8,128)(2,1)S(1)} collective-permute-done((bf16[1040,128]{1,0:T(8,128)(2,1)}, bf16[1040,128]{1,0:T(8,128)(2,1)S(1)}, u32[]{:S(2)}, u32[]{:S(2)}) %collective-permute-start.8) | collective-permute-done | bytes 266272 | tf_op jit(solution)/shard_map/ppermute | solution.py:360
  116.5 0.9 copy-done.8
  117.4 2.9 %shard_map.71 = bf16[8,128,128]{2,1,0:T(8,128)(2,1)S(1)} custom-call(bf16[512,128]{1,0:T(8,128)(2,1)S(1)} %copy-done.8, bf16[1040,128]{1,0:T(8,128)(2,1)S(1)} %copy-done.4, bf16[1040,128]{1,0:T(8,128)(2,1)S(1)} %collective-permute-done.8.refs_2_, bf16[4,128,128]{2,1,0:T(8,128)(2,1)S(1)} %shard_map.70.refs_3_), custom_call_target="tpu_custom_call" | custom-call | flops 3300000000 | tf_op jit(solution)/shard_map/pallas_call | solution.py:254
  120.3 11.6 %all_to_all.25.parts = bf16[8,128,128]{2,1,0:T(8,128)(2,1)S(1)} all-to-all(bf16[8,128,128]{2,1,0:T(8,128)(2,1)S(1)} %shard_map.71), channel_id=1, replica_groups=mesh['z'=16,'xl'=2,'xh'=2,'y'=4,'c'=2] {'y','c'}, dimensions={0} | all-to-all | bytes 524288 | tf_op jit(solution)/shard_map/all_to_all | solution.py:377
  131.9 1.2 shard_map.72
  (45 shorter events, 0.2 us)
Async XLA Ops:
  2.3 5.2 %copy-start.9 = (bf16[2,1024,192]{1,2,0:T(8,128)(2,1)S(1)}, bf16[2,1024,192]{1,2,0:T(8,128)(2,1)}, u32[]{:S(2)}) copy-start(bf16[2,1024,192]{1,2,0:T(8,128)(2,1)} %param.10) | copy-start | bytes 2359300
  2.3 15.6 %all-to-all-start = ((bf16[4,1040,128]{2,1,0:T(8,128)(2,1)}), bf16[4,1040,128]{2,1,0:T(8,128)(2,1)S(1)}, u32[]{:S(2)}, u32[]{:S(2)}) async-start(bf16[4,1040,128]{2,1,0:T(8,128)(2,1)} %shard_map.64), calls=%async_computation | async-start | bytes 2129920 | tf_op jit(solution)/shard_map/all_to_all | solution.py:286
  7.4 22.5 %copy-start.14 = (f32[2,1024]{1,0:T(2,128)S(1)}, f32[2,1024]{1,0:T(2,128)}, u32[]{:S(2)}) copy-start(f32[2,1024]{1,0:T(2,128)} %param.9) | copy-start | bytes 24580
  7.4 23.1 %copy-start.13 = (bf16[2,64,1024]{2,1,0:T(8,128)(2,1)S(1)}, bf16[2,64,1024]{2,1,0:T(8,128)(2,1)}, u32[]{:S(2)}) copy-start(bf16[2,64,1024]{2,1,0:T(8,128)(2,1)} %param.11) | copy-start | bytes 786436
  7.5 23.9 %copy-start.11 = (bf16[192,1024]{1,0:T(8,128)(2,1)}, bf16[192,1024]{1,0:T(8,128)(2,1)S(1)}, u32[]{:S(2)}) copy-start(bf16[192,1024]{1,0:T(8,128)(2,1)S(1)} %get-tuple-element.39.own_at) | copy-start | bytes 1179652
  7.5 23.9 %copy-start.12 = (bf16[192,1024]{1,0:T(8,128)(2,1)}, bf16[192,1024]{1,0:T(8,128)(2,1)S(1)}, u32[]{:S(2)}) copy-start(bf16[192,1024]{1,0:T(8,128)(2,1)S(1)} %get-tuple-element.40.own_at) | copy-start | bytes 1179652
  7.5 10.4 %collective-permute-start = (bf16[192,1024]{1,0:T(8,128)(2,1)S(1)}, bf16[192,1024]{1,0:T(8,128)(2,1)S(1)}, u32[]{:S(2)}, u32[]{:S(2)}) collective-permute-start(bf16[192,1024]{1,0:T(8,128)(2,1)S(1)} %get-tuple-element.40.own_at), channel_id=1, source_target_pairs={{0,24},{1,25},{2,26},{3,27},{4,28},{5,29},{6,30},{7,31},{8,16},{9,... | collective-permute-start | bytes 1179656 | tf_op jit(solution)/shard_map/ppermute | solution.py:298
  17.9 7.9 %copy-start.17 = (bf16[192,1024]{1,0:T(8,128)(2,1)}, bf16[192,1024]{1,0:T(8,128)(2,1)S(1)}, u32[]{:S(2)}) copy-start(bf16[192,1024]{1,0:T(8,128)(2,1)S(1)} %collective-permute-done.mirrored_at) | copy-start | bytes 1179652
  17.9 13.5 %copy-start.1 = (bf16[4,1040,128]{2,1,0:T(8,128)(2,1)}, bf16[4,1040,128]{2,1,0:T(8,128)(2,1)S(1)}, u32[]{:S(2)}) copy-start(bf16[4,1040,128]{2,1,0:T(8,128)(2,1)S(1)} %all-to-all-done.near.refs_1_) | copy-start | bytes 3194884
  17.9 17.0 %collective-permute-start.1 = (bf16[4,1040,128]{2,1,0:T(8,128)(2,1)S(1)}, bf16[4,1040,128]{2,1,0:T(8,128)(2,1)}, u32[]{:S(2)}, u32[]{:S(2)}) collective-permute-start(bf16[4,1040,128]{2,1,0:T(8,128)(2,1)S(1)} %all-to-all-done.near.refs_1_), channel_id=1, source_target_pairs={{0,1},{1,0},{2,3},{3,2},{4,5},{5,4},{6,7},{7,6},{8,9},{9,8},{10,11... | collective-permute-start | bytes 3194888 | tf_op jit(solution)/shard_map/ppermute | solution.py:289
  25.8 19.3 %collective-permute-start.2 = (bf16[192,1024]{1,0:T(8,128)(2,1)S(1)}, bf16[192,1024]{1,0:T(8,128)(2,1)S(1)}, u32[]{:S(2)}, u32[]{:S(2)}) collective-permute-start(bf16[192,1024]{1,0:T(8,128)(2,1)S(1)} %get-tuple-element.39.own_at), channel_id=1, source_target_pairs={{0,24},{1,25},{2,26},{3,27},{4,28},{5,29},{6,30},{7,31},{8,16},{9,... | collective-permute-start | bytes 1179656 | tf_op jit(solution)/shard_map/ppermute | solution.py:299
  31.4 13.6 %all-to-all-start.1 = ((bf16[4,64,1024]{2,1,0:T(8,128)(2,1)}), bf16[4,64,1024]{2,1,0:T(8,128)(2,1)S(1)}, u32[]{:S(2)}, u32[]{:S(2)}) async-start(bf16[4,64,1024]{2,1,0:T(8,128)(2,1)} %shard_map.66), calls=%async_computation.1 | async-start | bytes 1048576 | tf_op jit(solution)/shard_map/all_to_all | solution.py:286
  45.0 0.7 copy-start.16
  45.0 29.2 %copy-start.10 = (bf16[4,64,1024]{2,1,0:T(8,128)(2,1)}, bf16[4,64,1024]{2,1,0:T(8,128)(2,1)S(1)}, u32[]{:S(2)}) copy-start(bf16[4,64,1024]{2,1,0:T(8,128)(2,1)S(1)} %all-to-all-done.1.w_own) | copy-start | bytes 1572868
  45.8 22.7 %all-to-all-start.2 = ((bf16[4,1024,128]{2,1,0:T(8,128)(2,1)}), bf16[4,1024,128]{2,1,0:T(8,128)(2,1)S(1)}, u32[]{:S(2)}, u32[]{:S(2)}) async-start(bf16[4,1024,128]{2,1,0:T(8,128)(2,1)} %shard_map.65), calls=%async_computation.2 | async-start | bytes 2097152 | tf_op jit(solution)/shard_map/all_to_all | solution.py:286
  50.0 18.5 %collective-permute-start.3 = (bf16[4,64,1024]{2,1,0:T(8,128)(2,1)S(1)}, bf16[4,64,1024]{2,1,0:T(8,128)(2,1)}, u32[]{:S(2)}, u32[]{:S(2)}) collective-permute-start(bf16[4,64,1024]{2,1,0:T(8,128)(2,1)S(1)} %all-to-all-done.1.w_own), channel_id=1, source_target_pairs={{0,24},{1,25},{2,26},{3,27},{4,28},{5,29},{6,30},{7,31},{8,16},{9,... | collective-permute-start | bytes 1572872 | tf_op jit(solution)/shard_map/ppermute | solution.py:326
  53.4 15.1 %collective-permute-start.4 = (bf16[4,64,1024]{2,1,0:T(8,128)(2,1)S(1)}, bf16[4,64,1024]{2,1,0:T(8,128)(2,1)S(1)}, u32[]{:S(2)}, u32[]{:S(2)}) collective-permute-start(bf16[4,64,1024]{2,1,0:T(8,128)(2,1)S(1)} %all-to-all-done.1.w_own), channel_id=1, source_target_pairs={{0,1},{1,0},{2,3},{3,2},{4,5},{5,4},{6,7},{7,6},{8,9},{9,8},{10,11... | collective-permute-start | bytes 1572872 | tf_op jit(solution)/shard_map/ppermute | solution.py:289
  56.7 11.7 %collective-permute-start.5 = (bf16[64,1024]{1,0:T(8,128)(2,1)S(1)}, bf16[64,1024]{1,0:T(8,128)(2,1)S(1)}, u32[]{:S(2)}, u32[]{:S(2)}) collective-permute-start(bf16[64,1024]{1,0:T(8,128)(2,1)S(1)} %get-tuple-element.41.refs_0_), channel_id=1, source_target_pairs={{0,24},{1,25},{2,26},{3,27},{4,28},{5,29},{6,30},{7,31},{8,16},{9,... | collective-permute-start | bytes 393224 | tf_op jit(solution)/shard_map/ppermute | solution.py:328
  68.5 5.8 %copy-start.15 = (bf16[4,64,1024]{2,1,0:T(8,128)(2,1)}, bf16[4,64,1024]{2,1,0:T(8,128)(2,1)S(1)}, u32[]{:S(2)}) copy-start(bf16[4,64,1024]{2,1,0:T(8,128)(2,1)S(1)} %collective-permute-done.4.w_own_far) | copy-start | bytes 1572868
  68.5 5.8 %copy-start.2 = (bf16[4,1024,128]{2,1,0:T(8,128)(2,1)}, bf16[4,1024,128]{2,1,0:T(8,128)(2,1)S(1)}, u32[]{:S(2)}) copy-start(bf16[4,1024,128]{2,1,0:T(8,128)(2,1)S(1)} %all-to-all-done.2.refs_2_.o_near) | copy-start | bytes 3145732
  68.5 12.1 %collective-permute-start.6 = (bf16[4,1024,128]{2,1,0:T(8,128)(2,1)S(1)}, bf16[4,1024,128]{2,1,0:T(8,128)(2,1)}, u32[]{:S(2)}, u32[]{:S(2)}) collective-permute-start(bf16[4,1024,128]{2,1,0:T(8,128)(2,1)S(1)} %all-to-all-done.2.refs_2_.o_near), channel_id=1, source_target_pairs={{0,1},{1,0},{2,3},{3,2},{4,5},{5,4},{6,7},{7,6},{8,9},{9,8},{10,11... | collective-permute-start | bytes 3145736 | tf_op jit(solution)/shard_map/ppermute | solution.py:289
  72.2 8.5 %collective-permute-start.7 = (bf16[4,64,1024]{2,1,0:T(8,128)(2,1)}, bf16[4,64,1024]{2,1,0:T(8,128)(2,1)}, u32[]{:S(2)}, u32[]{:S(2)}) collective-permute-start(bf16[4,64,1024]{2,1,0:T(8,128)(2,1)} %collective-permute-done.3.w_mir), channel_id=1, source_target_pairs={{0,1},{1,0},{2,3},{3,2},{4,5},{5,4},{6,7},{7,6},{8,9},{9,8},{10,11... | collective-permute-start | bytes 1572872 | tf_op jit(solution)/shard_map/ppermute | solution.py:289
  74.3 1.4 %copy-start = (bf16[8,128,1024]{2,1,0:T(8,128)(2,1)}, bf16[8,128,1024]{2,1,0:T(8,128)(2,1)S(1)}, u32[]{:S(2)}) copy-start(bf16[8,128,1024]{2,1,0:T(8,128)(2,1)S(1)} %shard_map.67.ready) | copy-start | bytes 6291460
  75.6 44.6 %all-to-all-start.3 = ((bf16[8,128,1024]{2,1,0:T(8,128)(2,1)}), bf16[8,128,1024]{2,1,0:T(8,128)(2,1)S(1)}, u32[]{:S(2)}, u32[]{:S(2)}) async-start(bf16[8,128,1024]{2,1,0:T(8,128)(2,1)} %copy-done), calls=%async_computation.3 | async-start | bytes 4194304 | tf_op jit(solution)/shard_map/all_to_all | solution.py:339
  88.1 21.6 %copy-start.3 = (bf16[1040,128]{1,0:T(8,128)(2,1)S(1)}, bf16[1040,128]{1,0:T(8,128)(2,1)}, u32[]{:S(2)}) copy-start(bf16[1040,128]{1,0:T(8,128)(2,1)} %get-tuple-element.34.refs_1_) | copy-start | bytes 798724
  88.1 21.6 %copy-start.5 = (bf16[512,128]{1,0:T(8,128)(2,1)S(1)}, bf16[512,128]{1,0:T(8,128)(2,1)}, u32[]{:S(2)}) copy-start(bf16[512,128]{1,0:T(8,128)(2,1)} %get-tuple-element.33.refs_0_) | copy-start | bytes 393220
  88.1 21.6 %collective-permute-start.9 = (bf16[1040,128]{1,0:T(8,128)(2,1)}, bf16[1040,128]{1,0:T(8,128)(2,1)S(1)}, u32[]{:S(2)}, u32[]{:S(2)}) collective-permute-start(bf16[1040,128]{1,0:T(8,128)(2,1)} %get-tuple-element.34.refs_1_), channel_id=1, source_target_pairs={{0,8},{1,9},{2,10},{3,11},{4,12},{5,13},{6,14},{7,15},{8,0},{9,1},... | collective-permute-start | bytes 798728 | tf_op jit(solution)/shard_map/ppermute | solution.py:360
  97.8 18.7 %collective-permute-start.8 = (bf16[1040,128]{1,0:T(8,128)(2,1)}, bf16[1040,128]{1,0:T(8,128)(2,1)S(1)}, u32[]{:S(2)}, u32[]{:S(2)}) collective-permute-start(bf16[1040,128]{1,0:T(8,128)(2,1)} %get-tuple-element.32.refs_3_.refs_1_), channel_id=1, source_target_pairs={{0,504},{1,505},{2,506},{3,507},{4,508},{5,509},{6,510},{7,511},{8... | collective-permute-start | bytes 798728 | tf_op jit(solution)/shard_map/ppermute | solution.py:360
  109.7 1.0 copy-start.4
  116.5 0.9 copy-start.8
  117.4 14.5 %copy-start.6 = (bf16[128,1024]{1,0:T(8,128)(2,1)S(1)}, bf16[128,1024]{1,0:T(8,128)(2,1)}, u32[]{:S(2)}) copy-start(bf16[128,1024]{1,0:T(8,128)(2,1)} %get-tuple-element.37.stream_p) | copy-start | bytes 786436
  117.4 14.5 %copy-start.7 = (bf16[128,1024]{1,0:T(8,128)(2,1)S(1)}, bf16[128,1024]{1,0:T(8,128)(2,1)}, u32[]{:S(2)}) copy-start(bf16[128,1024]{1,0:T(8,128)(2,1)} %get-tuple-element.38.stream_q) | copy-start | bytes 786436

commit v5 on v4

--- a/solution.py
+++ b/solution.py
@@ -17,6 +17,7 @@
 LANES = 128
 BLOCKS = D // LANES
 EXT = D + 16
+FULL = EXT + BLOCKS * HEAD_DIM
 EPSILON = 1e-05
 FAR = -1e30
 AXES = ("z", "xl", "xh", "y", "c")
@@ -79,8 +80,8 @@
     return copies
 
 
-def order_kernel(points_at, order_at, tags_at, out, points, order, tags, sems):
-    copies = fetch((order_at, points_at, tags_at), (order, points, tags), sems)
+def order_kernel(points_at, order_at, tags_at, w_at, out, points, order, tags, w, sems):
+    copies = fetch((order_at, points_at, tags_at, w_at.at[0]), (order, points, tags, w), sems)
     for copy in copies:
         copy.wait()
     row = lax.broadcasted_iota(jnp.int32, (ROWS, ROWS), 0)
@@ -90,7 +91,8 @@
     for copy in range(4):
         for b in range(BLOCKS):
             out[copy, b * LANES : (b + 1) * LANES, :] = ordered[:, b * LANES : (b + 1) * LANES]
-        out[copy, D:, :] = tag_rows
+            out[copy, EXT + b * HEAD_DIM : EXT + (b + 1) * HEAD_DIM, :] = w[:, b * LANES : (b + 1) * LANES]
+        out[copy, D:EXT, :] = tag_rows
 
 
 def joined(own, mirrored, kind):
@@ -113,18 +115,19 @@
 
 
 def first_kernel(
-    near, far, gain, own_at, mirrored_at, out,
-    normed, queries, keys, turned, values, hots, own, mirrored, sems,
+    gain, near, far, own_at, mirrored_at, out,
+    points, normed, queries, keys, turned, values, hots, own, mirrored, sems, w_sems,
 ):
-    copies = fetch((own_at, mirrored_at), (own, mirrored), sems)
+    sources = [ref.at[y, :EXT, :] for ref in (near, far) for y in range(4)]
+    blocks = fetch(sources, [points.at[b] for b in range(8)], sems)
+    copies = fetch((own_at.at[0], mirrored_at.at[0]), (own, mirrored), w_sems)
     rows = []
-    for s, ref in enumerate((near, far)):
-        for y in range(4):
-            block = s * 4 + y
-            normed[block * ROWS : (block + 1) * ROWS, :] = layer_norm(
-                side_by_side(ref, y).astype(F32), gain[...]
-            )
-            rows.append(ref[y, D:, :].astype(F32)[:1])
+    for block in range(8):
+        blocks[block].wait()
+        normed[block * ROWS : (block + 1) * ROWS, :] = layer_norm(
+            side_by_side(points, block).astype(F32), gain[...]
+        )
+        rows.append(points[block, D:, :].astype(F32)[:1])
     columns = tag_columns(rows)
     for copy in copies:
         copy.wait()
@@ -149,8 +152,9 @@
 
 
 def middle_kernel(
-    part, near, far, gain, o_near, o_far, w_own, w_own_far, w_mir, w_mir_far, own_at, mirrored_at,
-    ready, q_out, kv, st_out, heads, update, normed, turned, w, own, mirrored, o_sems, w_sems,
+    part, gain, o_near, o_far, w_own, w_own_far, w_mir, w_mir_far, near, far, own_at, mirrored_at, ready,
+    q_out, kv, st_out,
+    heads, update, normed, turned, w, points, own, mirrored, o_sems, w_sems, sems,
 ):
     my_y, half = lax.axis_index("y"), half_of(part)
     sources, targets = [], []
@@ -164,30 +168,40 @@
                 heads.at[span, g * LANES : (g + 1) * LANES],
                 heads.at[span, (g + 4) * LANES : (g + 5) * LANES],
             ]
-    o_copies = fetch(sources, targets, o_sems)
-    sources, targets = [own_at, mirrored_at], [own, mirrored]
+    copies = fetch(sources, targets, o_sems)
+    sources, targets = [], []
     for i, ref in enumerate((w_own, w_mir, w_own_far, w_mir_far)):
         for g in range(4):
             row = (i // 2 * 4 + g) * LANES + i % 2 * HEAD_DIM
             sources.append(ref.at[g])
-            targets.append(w.at[row : row + HEAD_DIM, :])
-    w_copies = fetch(sources, targets, w_sems)
-    for copy in o_copies + w_copies:
+            targets.append(w.at[:, row : row + HEAD_DIM, :])
+    copies += fetch(sources, targets, w_sems)
+    late = fetch(
+        (
+            near.at[pl.ds(half * 2, 2), :EXT, :], far.at[pl.ds(half * 2, 2), :EXT, :],
+            own_at.at[1], mirrored_at.at[1],
+        ),
+        (points.at[:2], points.at[2:], own, mirrored),
+        sems,
+    )
+    for copy in copies:
         copy.wait()
-    update[...] = dot(heads[...], w[...])
+    for j in range(4):
+        both = jnp.concatenate([w[2 * j], w[2 * j + 1]], axis=1)
+        update[:, j * 256 : (j + 1) * 256] = dot(heads[...], both)
+    for copy in late:
+        copy.wait()
     rows = []
-    for s, ref in enumerate((near, far)):
-        for yy in range(2):
-            y = half * 2 + yy
-            span = slice((s * 2 + yy) * ROWS, (s * 2 + yy + 1) * ROWS)
-            stream = (side_by_side(ref, y).astype(F32) + update[span, :]).astype(BF16)
-            normed[span, :] = layer_norm(stream.astype(F32), gain[...])
-            rows.append(ref[y, D:, :].astype(F32)[:1])
-            if s == 0:
-
-                @pl.when(y == my_y)
-                def _(stream=stream):
-                    st_out[...] = stream
+    for block in range(4):
+        span = slice(block * ROWS, (block + 1) * ROWS)
+        stream = (side_by_side(points, block).astype(F32) + update[span, :]).astype(BF16)
+        normed[span, :] = layer_norm(stream.astype(F32), gain[...])
+        rows.append(points[block, D:, :].astype(F32)[:1])
+        if block < 2:
+
+            @pl.when(half * 2 + block == my_y)
+            def _(stream=stream):
+                st_out[...] = stream
 
     project(normed, own, mirrored, q_out, kv.at[:HALF, :], turned)
     for b in range(4):
@@ -242,11 +256,10 @@
     pl.when(y_half == half_of(1))(lambda: put(stream_q))
 
 
-def relay_kernel(count, *refs):
-    out = refs[-1]
+def relay_kernel(own, mirrored, ready, out):
     for copy in range(out.shape[0]):
-        for i in range(count):
-            out[copy, i * HEAD_DIM : (i + 1) * HEAD_DIM] = refs[i][...]
+        out[copy, :HEAD_DIM] = own[...]
+        out[copy, HEAD_DIM:] = mirrored[...]
 
 
 def call(kernel, micros, outs, scratch, *args, late=(), semaphores=(), megabytes=16):
@@ -291,26 +304,30 @@
     def on_device(points, order, scan_ids, ln_gain, w_qkv, w_out):
         w_turned = jnp.swapaxes(w_qkv, 1, 2)
         (copies,) = call(
-            order_kernel, 1.2, [(4, EXT, LANES)],
-            [((ROWS, D), BF16), ((1, ROWS), jnp.int32), ((1, ROWS), jnp.int32)],
-            late=(points, order, scan_ids.reshape(1, ROWS)), semaphores=(3,), megabytes=56,
-        )
-        first_far = lax.ppermute(w_turned[0], AXES, mirror)
-        second_far = lax.ppermute(w_turned[1], AXES, mirror)
-        x_near = over_y(copies)
-        x_near, first_far = lax.optimization_barrier((x_near, first_far))
-        x_far = swapped(x_near)
-        (shares,) = call(
-            functools.partial(relay_kernel, 1), 1, [(4, HEAD_DIM, D)], [], w_out[0],
-            late=(x_near,), megabytes=4,
-        )
-        w_own = over_y(shares)
+            order_kernel, 1.2, [(4, FULL, LANES)],
+            [
+                ((ROWS, D), BF16), ((1, ROWS), jnp.int32), ((1, ROWS), jnp.int32),
+                ((HEAD_DIM, D), BF16),
+            ],
+            late=(points, order, scan_ids.reshape(1, ROWS), w_out), semaphores=(4,), megabytes=56,
+        )
+        w_far = lax.ppermute(w_turned, AXES, mirror)
+        near = over_y(copies)
+        near, w_far = lax.optimization_barrier((near, w_far))
+        far = swapped(near)
+
+        def out_weights(array):
+            return array[:, EXT:].reshape(4, BLOCKS, HEAD_DIM, LANES)
+
+        w_own = out_weights(near)
+        w_mir = lax.ppermute(w_own, AXES, mirror)
         projection = [((3 * HEAD_DIM, D), BF16)] * 2
         (o_copies,) = call(
             first_kernel,
             8,
             [(4, PATCH, LANES)],
             [
+                ((8, EXT, LANES), BF16),
                 ((PATCH, D), BF16),
                 ((PATCH, LANES), BF16),
                 ((PATCH, 2 * LANES), BF16),
@@ -319,22 +336,20 @@
                 ((PATCH, LANES), BF16),
                 *projection,
             ],
-            x_near, x_far, ln_gain[0:1],
-            late=(w_turned[0], first_far), semaphores=(2,), megabytes=56,
-        )
-        o_copies, w_own, second_far = lax.optimization_barrier((o_copies, w_own, second_far))
-        w_mir = lax.ppermute(w_own, AXES, mirror)
-        w_own_far = swapped(w_own)
+            ln_gain[0:1],
+            late=(near, far, w_turned, w_far), semaphores=(8, 2), megabytes=56,
+        )
+        o_copies, w_mir = lax.optimization_barrier((o_copies, w_mir))
         last_far = lax.ppermute(w_out[1], AXES, mirror)
+        w_mir_far = swapped(w_mir)
+        w_own_far = out_weights(far)
         o_near = over_y(o_copies)
-        o_near, w_mir, w_own_far, last_far = lax.optimization_barrier(
-            (o_near, w_mir, w_own_far, last_far)
+        o_near, w_mir_far, w_own_far, last_far = lax.optimization_barrier(
+            (o_near, w_mir_far, w_own_far, last_far)
         )
         o_far = swapped(o_near)
-        w_mir_far = swapped(w_mir)
         (shares,) = call(
-            functools.partial(relay_kernel, 2), 1, [(8, ROWS, D)], [], w_out[1], last_far,
-            late=(o_near,), megabytes=4,
+            relay_kernel, 1, [(8, ROWS, D)], [], w_out[1], last_far, late=(o_near,), megabytes=4
         )
         w_last = lax.all_to_all(shares, ("y", "c"), 0, 0, tiled=True).reshape(D, D)
         middle, halos = [], []
@@ -349,12 +364,16 @@
                         ((HALF, D), F32),
                         ((HALF, D), BF16),
                         ((LANES, HALF), BF16),
-                        ((D, D), BF16),
+                        ((BLOCKS, D, LANES), BF16),
+                        ((4, EXT, LANES), BF16),
                         *projection,
                     ],
-                    x_near, x_far, ln_gain[1:2],
-                    late=(o_near, o_far, w_own, w_own_far, w_mir, w_mir_far, w_turned[1], second_far, shares),
-                    semaphores=(16, 18), megabytes=56,
+                    ln_gain[1:2],
+                    late=(
+                        o_near, o_far, w_own, w_own_far, w_mir, w_mir_far, near, far,
+                        w_turned, w_far, shares,
+                    ),
+                    semaphores=(16, 16, 4), megabytes=56,
                 )
             )
             halos.append(lax.ppermute(middle[part][1], AXES, links))

time: 134 us -> 131 us (0.978)
  starting transfers between devices: 63.5 us -> 54.8 us
  waiting for transfers between devices: 17.7 us -> 22.1 us
  local copies, waits for them, and re-layouts: 4.66 us -> 6.98 us
    ppermute x2 -> x1, waiting for transfers between devices: 5.84 us -> 14.1 us  [on_device(): w_far = lax.ppermute(w_turned, AXES, mirror)]
    ppermute x1, waiting for transfers between devices: 8.95 us -> 1.94 us  [on_device(): last_far = lax.ppermute(w_out[1], AXES, mirror)]
    ppermute x2 -> x1, starting transfers between devices: 8.73 us -> 4.38 us  [on_device(): w_far = lax.ppermute(w_turned, AXES, mirror)]
    all_to_all x3 -> x2, starting transfers between devices: 12.8 us -> 9.39 us  [over_y(): return lax.all_to_all(copies, 'y', 0, 0, tiled=True)]
    ppermute x4 -> x3, starting transfers between devices: 16.7 us -> 13.3 us  [swapped(): return lax.ppermute(array, AXES, other_core)]
    all_to_all x3 -> x2, waiting for transfers between devices: 0.01 us -> 2.82 us  [over_y(): return lax.all_to_all(copies, 'y', 0, 0, tiled=True)]
    slice x0 -> x2, local copies, waits for them, and re-layouts: none -> 1.92 us  [out_weights(): return array[:, EXT:].reshape(4, BLOCKS, HEAD_DIM, LANES)]
    ppermute x1, starting transfers between devices: 2.78 us -> 4.39 us  [on_device(): last_far = lax.ppermute(w_out[1], AXES, mirror)]
  transfers between devices with their start and end apart: 14 -> 11, of which waited for: 3 -> 5; matrix products, arithmetic and copies ran while one was open for 1% -> 2% of each run, Pallas kernels for 24% -> 24%
where the time goes in v5:
time: 131 us; the launch traced here: 130 us
  starting transfers between devices  54.8 us (42%)
  Pallas kernels  34.7 us (26%)
  waiting for transfers between devices  22.1 us (17%)
  blocking collectives  11.4 us (9%)
  local copies, waits for them, and re-layouts  6.98 us (5%)
    pallas_call x8, Pallas kernels, call(): pl.pallas_call(kernel, out_shape=[jax.ShapeDtypeStruct(shape, BF16) for s...  34.7 us
    ppermute x2, starting transfers between devices, on_device(): halos.append(lax.ppermute(middle[part][1], AXES, links))  15.4 us
    ppermute x1, waiting for transfers between devices, on_device(): w_far = lax.ppermute(w_turned, AXES, mirror)  14.1 us
    ppermute x3, starting transfers between devices, swapped(): return lax.ppermute(array, AXES, other_core)  13.3 us
    all_to_all x1, blocking collectives, on_device(): parts = lax.all_to_all(parts, ('y', 'c'), 0, 0, tiled=True)  11.4 us
    all_to_all x2, starting transfers between devices, over_y(): return lax.all_to_all(copies, 'y', 0, 0, tiled=True)  9.39 us
    unnamed x32, local copies, waits for them, and re-layouts  4.45 us
    ppermute x1, starting transfers between devices, on_device(): w_mir = lax.ppermute(w_own, AXES, mirror)  4.39 us
  transfers between devices with their start and end apart: 11, of which 5 were waited for; matrix products, arithmetic and copies ran while one was open for 2% of the time, Pallas kernels for 24%

profile of v5, /device:TPU:1, one launch (start us, length us, event | category | flops | bytes accessed | tf_op | source)
XLA Modules:
  0.0 130.2 jit_solution(9836653396732987036)
XLA Ops:
  0.0 2.5 %shard_map.64 = bf16[4,1552,128]{2,1,0:T(8,128)(2,1)} custom-call(bf16[128,1024]{1,0:T(8,128)(2,1)} %points_at.1, s32[1,128]{1,0:T(1,128)} %order_at.1, s32[1,128]{1,0:T(1,128)} %bitcast.17, bf16[2,64,1024]{2,1,0:T(8,128)(2,1)} %w_at.1), custom_call_target="tpu_custom_call" | custom-call | flops 1320000000 | tf_op jit(solution)/shard_map/pallas_call | solution.py:267
  2.5 0.0 copy-start.12
  2.5 5.2 %all-to-all-start = ((bf16[4,1552,128]{2,1,0:T(8,128)(2,1)}), bf16[4,1552,128]{2,1,0:T(8,128)(2,1)S(1)}, u32[]{:S(2)}, u32[]{:S(2)}) async-start(bf16[4,1552,128]{2,1,0:T(8,128)(2,1)} %shard_map.64), calls=%async_computation | async-start | bytes 3178496 | tf_op jit(solution)/shard_map/all_to_all | solution.py:299
  7.7 4.4 %collective-permute-start = (bf16[2,192,1024]{2,1,0:T(8,128)(2,1)S(1)}, bf16[2,192,1024]{2,1,0:T(8,128)(2,1)S(1)}, u32[]{:S(2)}, u32[]{:S(2)}) collective-permute-start(bf16[2,192,1024]{2,1,0:T(8,128)(2,1)S(1)} %bitcast.16), channel_id=1, source_target_pairs={{0,24},{1,25},{2,26},{3,27},{4,28},{5,29},{6,30},{7,31},{8,16},{9,... | collective-permute-start | bytes 2359304 | tf_op jit(solution)/shard_map/ppermute | solution.py:314
  12.1 14.1 %collective-permute-done.mirrored_at = bf16[2,192,1024]{2,1,0:T(8,128)(2,1)S(1)} collective-permute-done((bf16[2,192,1024]{2,1,0:T(8,128)(2,1)S(1)}, bf16[2,192,1024]{2,1,0:T(8,128)(2,1)S(1)}, u32[]{:S(2)}, u32[]{:S(2)}) %collective-permute-start) | collective-permute-done | bytes 786464 | tf_op jit(solution)/shard_map/ppermute | solution.py:314
  26.2 6.5 %collective-permute-start.1 = (bf16[4,1552,128]{2,1,0:T(8,128)(2,1)S(1)}, bf16[4,1552,128]{2,1,0:T(8,128)(2,1)S(1)}, u32[]{:S(2)}, u32[]{:S(2)}) collective-permute-start(bf16[4,1552,128]{2,1,0:T(8,128)(2,1)S(1)} %all-to-all-done.near), channel_id=1, source_target_pairs={{0,1},{1,0},{2,3},{3,2},{4,5},{5,4},{6,7},{7,6},{8,9},{9,8},{10,11... | collective-permute-start | bytes 4767752 | tf_op jit(solution)/shard_map/ppermute | solution.py:302
  32.7 0.6 fusion
  33.3 4.4 %collective-permute-start.2 = (bf16[4,8,64,128]{3,2,1,0:T(8,128)(2,1)S(1)}, bf16[4,8,64,128]{3,2,1,0:T(8,128)(2,1)}, u32[]{:S(2)}, u32[]{:S(2)}) collective-permute-start(bf16[4,8,64,128]{3,2,1,0:T(8,128)(2,1)S(1)} %bitcast.8), channel_id=1, source_target_pairs={{0,24},{1,25},{2,26},{3,27},{4,28},{5,29},{6,30},{7,31},{8,16},{9,... | collective-permute-start | bytes 1572872 | tf_op jit(solution)/shard_map/ppermute | solution.py:323
  37.8 1.2 copy-done.10
  38.9 10.9 %shard_map.65 = bf16[4,1024,128]{2,1,0:T(8,128)(2,1)} custom-call(f32[1,1024]{1,0:T(1,128)} %get-tuple-element.37.gain, bf16[4,1552,128]{2,1,0:T(8,128)(2,1)} %copy-done.8, bf16[4,1552,128]{2,1,0:T(8,128)(2,1)} %copy-done.10, bf16[2,192,1024]{2,1,0:T(8,128)(2,1)} %bitcast.13, bf16[2,192,1024]{2,1,0:T(8,128)(2,1)} %copy-done.14), custom_call_target="tpu_custom_call" | custom-call | flops 8800000000 | tf_op jit(solution)/shard_map/pallas_call | solution.py:267
  49.9 0.2 collective-permute-done.2.w_mir
  50.1 4.2 %all-to-all-start.1 = ((bf16[4,1024,128]{2,1,0:T(8,128)(2,1)}), bf16[4,1024,128]{2,1,0:T(8,128)(2,1)S(1)}, u32[]{:S(2)}, u32[]{:S(2)}) async-start(bf16[4,1024,128]{2,1,0:T(8,128)(2,1)} %shard_map.65), calls=%async_computation.1 | async-start | bytes 2097152 | tf_op jit(solution)/shard_map/all_to_all | solution.py:299
  54.3 3.0 %collective-permute-start.3 = (bf16[4,8,64,128]{3,2,1,0:T(8,128)(2,1)}, bf16[4,8,64,128]{3,2,1,0:T(8,128)(2,1)S(1)}, u32[]{:S(2)}, u32[]{:S(2)}) collective-permute-start(bf16[4,8,64,128]{3,2,1,0:T(8,128)(2,1)} %collective-permute-done.2.w_mir), channel_id=1, source_target_pairs={{0,1},{1,0},{2,3},{3,2},{4,5},{5,4},{6,7},{7,6},{8,9},{9,8},{10,11... | collective-permute-start | bytes 1572872 | tf_op jit(solution)/shard_map/ppermute | solution.py:302
  57.3 4.4 %collective-permute-start.4 = (bf16[64,1024]{1,0:T(8,128)(2,1)S(1)}, bf16[64,1024]{1,0:T(8,128)(2,1)S(1)}, u32[]{:S(2)}, u32[]{:S(2)}) collective-permute-start(bf16[64,1024]{1,0:T(8,128)(2,1)S(1)} %slice_bitcast_fusion.own), channel_id=1, source_target_pairs={{0,24},{1,25},{2,26},{3,27},{4,28},{5,29},{6,30},{7,31},{8,16},{9,... | collective-permute-start | bytes 393224 | tf_op jit(solution)/shard_map/ppermute | solution.py:343
  61.7 1.9 %slice.22 = bf16[4,512,128]{2,1,0:T(8,128)(2,1)} slice(bf16[4,1552,128]{2,1,0:T(8,128)(2,1)} %copy-done.10), slice={[0:4], [1040:1552], [0:128]} | slice | bytes 1048576 | tf_op jit(solution)/shard_map/slice | solution.py:320
  63.6 1.9 %collective-permute-done.4.mirrored = bf16[64,1024]{1,0:T(8,128)(2,1)S(1)} collective-permute-done((bf16[64,1024]{1,0:T(8,128)(2,1)S(1)}, bf16[64,1024]{1,0:T(8,128)(2,1)S(1)}, u32[]{:S(2)}, u32[]{:S(2)}) %collective-permute-start.4) | collective-permute-done | bytes 131104 | tf_op jit(solution)/shard_map/ppermute | solution.py:343
  65.6 2.8 %all-to-all-done.1.ready.o_near = bf16[4,1024,128]{2,1,0:T(8,128)(2,1)S(1)} async-done(((bf16[4,1024,128]{2,1,0:T(8,128)(2,1)}), bf16[4,1024,128]{2,1,0:T(8,128)(2,1)S(1)}, u32[]{:S(2)}, u32[]{:S(2)}) %all-to-all-start.1) | async-done | bytes 1048608 | tf_op jit(solution)/shard_map/all_to_all | solution.py:299
  68.4 3.9 %collective-permute-start.5 = (bf16[4,1024,128]{2,1,0:T(8,128)(2,1)S(1)}, bf16[4,1024,128]{2,1,0:T(8,128)(2,1)}, u32[]{:S(2)}, u32[]{:S(2)}) collective-permute-start(bf16[4,1024,128]{2,1,0:T(8,128)(2,1)S(1)} %all-to-all-done.1.ready.o_near), channel_id=1, source_target_pairs={{0,1},{1,0},{2,3},{3,2},{4,5},{5,4},{6,7},{7,6},{8,9},{9,8},{10,11... | collective-permute-start | bytes 3145736 | tf_op jit(solution)/shard_map/ppermute | solution.py:302
  72.3 0.1 shard_map.66.ready
  72.5 1.4 %copy-done = bf16[8,128,1024]{2,1,0:T(8,128)(2,1)} copy-done((bf16[8,128,1024]{2,1,0:T(8,128)(2,1)}, bf16[8,128,1024]{2,1,0:T(8,128)(2,1)S(1)}, u32[]{:S(2)}) %copy-start) | copy-done | bytes 2097176
  73.8 3.6 %all-to-all-start.2 = ((bf16[8,128,1024]{2,1,0:T(8,128)(2,1)}), bf16[8,128,1024]{2,1,0:T(8,128)(2,1)S(1)}, u32[]{:S(2)}, u32[]{:S(2)}) async-start(bf16[8,128,1024]{2,1,0:T(8,128)(2,1)} %copy-done), calls=%async_computation.2 | async-start | bytes 4194304 | tf_op jit(solution)/shard_map/all_to_all | solution.py:354
  77.4 7.0 %shard_map.68 = (bf16[512,128]{1,0:T(8,128)(2,1)}, bf16[1040,128]{1,0:T(8,128)(2,1)}, bf16[128,1024]{1,0:T(8,128)(2,1)}) custom-call(f32[1,1024]{1,0:T(1,128)} %get-tuple-element.38.gain, bf16[4,1024,128]{2,1,0:T(8,128)(2,1)} %copy-done.1, bf16[4,1024,128]{2,1,0:T(8,128)(2,1)} %collective-permute-done.5.o_far, bf16[4,8,64,128]{3,2,1,0:T(8,128)(2,1)} %bitcast.9, ...), custom_call_target="tpu_custom_call" | custom-call | flops 4400000000 | tf_op jit(solution)/shard_map/pallas_call | solution.py:267
  84.4 2.4 %collective-permute-start.7 = (bf16[1040,128]{1,0:T(8,128)(2,1)}, bf16[1040,128]{1,0:T(8,128)(2,1)S(1)}, u32[]{:S(2)}, u32[]{:S(2)}) collective-permute-start(bf16[1040,128]{1,0:T(8,128)(2,1)} %get-tuple-element.32.refs_1_), channel_id=1, source_target_pairs={{0,8},{1,9},{2,10},{3,11},{4,12},{5,13},{6,14},{7,15},{8,0},{9,1},... | collective-permute-start | bytes 798728 | tf_op jit(solution)/shard_map/ppermute | solution.py:379
  86.8 7.2 %shard_map.67 = (bf16[512,128]{1,0:T(8,128)(2,1)}, bf16[1040,128]{1,0:T(8,128)(2,1)}, bf16[128,1024]{1,0:T(8,128)(2,1)}) custom-call(f32[1,1024]{1,0:T(1,128)} %get-tuple-element.38.gain, bf16[4,1024,128]{2,1,0:T(8,128)(2,1)} %copy-done.1, bf16[4,1024,128]{2,1,0:T(8,128)(2,1)} %collective-permute-done.5.o_far, bf16[4,8,64,128]{3,2,1,0:T(8,128)(2,1)} %bitcast.10, ...), custom_call_target="tpu_custom_call" | custom-call | flops 4400000000 | tf_op jit(solution)/shard_map/pallas_call | solution.py:267
  94.0 13.0 %collective-permute-start.6 = (bf16[1040,128]{1,0:T(8,128)(2,1)}, bf16[1040,128]{1,0:T(8,128)(2,1)S(1)}, u32[]{:S(2)}, u32[]{:S(2)}) collective-permute-start(bf16[1040,128]{1,0:T(8,128)(2,1)} %get-tuple-element.30.refs_3_.refs_1_), channel_id=1, source_target_pairs={{0,504},{1,505},{2,506},{3,507},{4,508},{5,509},{6,510},{7,511},{8... | collective-permute-start | bytes 798728 | tf_op jit(solution)/shard_map/ppermute | solution.py:379
  107.0 1.0 copy-done.3
  108.0 2.9 %shard_map.69.refs_3_ = bf16[4,128,128]{2,1,0:T(8,128)(2,1)S(1)} custom-call(bf16[512,128]{1,0:T(8,128)(2,1)S(1)} %copy-done.4, bf16[1040,128]{1,0:T(8,128)(2,1)S(1)} %copy-done.2, bf16[1040,128]{1,0:T(8,128)(2,1)S(1)} %collective-permute-done.7.refs_2_, bf16[1040,128]{1,0:T(8,128)(2,1)S(1)} %copy-done.3), custom_call_target="tpu_custom_call" | custom-call | tf_op jit(solution)/shard_map/pallas_call | solution.py:267
  110.8 3.0 %collective-permute-done.6.refs_2_ = bf16[1040,128]{1,0:T(8,128)(2,1)S(1)} collective-permute-done((bf16[1040,128]{1,0:T(8,128)(2,1)}, bf16[1040,128]{1,0:T(8,128)(2,1)S(1)}, u32[]{:S(2)}, u32[]{:S(2)}) %collective-permute-start.6) | collective-permute-done | bytes 266272 | tf_op jit(solution)/shard_map/ppermute | solution.py:379
  113.9 0.9 copy-done.7
  114.8 2.9 %shard_map.70 = bf16[8,128,128]{2,1,0:T(8,128)(2,1)S(1)} custom-call(bf16[512,128]{1,0:T(8,128)(2,1)S(1)} %copy-done.7, bf16[1040,128]{1,0:T(8,128)(2,1)S(1)} %copy-done.3, bf16[1040,128]{1,0:T(8,128)(2,1)S(1)} %collective-permute-done.6.refs_2_, bf16[4,128,128]{2,1,0:T(8,128)(2,1)S(1)} %shard_map.69.refs_3_), custom_call_target="tpu_custom_call" | custom-call | flops 3300000000 | tf_op jit(solution)/shard_map/pallas_call | solution.py:267
  117.7 11.4 %all_to_all.20.parts = bf16[8,128,128]{2,1,0:T(8,128)(2,1)S(1)} all-to-all(bf16[8,128,128]{2,1,0:T(8,128)(2,1)S(1)} %shard_map.70), channel_id=1, replica_groups=mesh['z'=16,'xl'=2,'xh'=2,'y'=4,'c'=2] {'y','c'}, dimensions={0} | all-to-all | bytes 524288 | tf_op jit(solution)/shard_map/all_to_all | solution.py:396
  129.0 1.2 shard_map.71
  (35 shorter events, 0.1 us)
Async XLA Ops:
  2.5 5.2 %copy-start.13 = (bf16[2,1024,192]{1,2,0:T(8,128)(2,1)S(1)}, bf16[2,1024,192]{1,2,0:T(8,128)(2,1)}, u32[]{:S(2)}) copy-start(bf16[2,1024,192]{1,2,0:T(8,128)(2,1)} %param.10) | copy-start | bytes 2359300
  2.5 30.1 %copy-start.12 = (f32[2,1024]{1,0:T(2,128)S(1)}, f32[2,1024]{1,0:T(2,128)}, u32[]{:S(2)}) copy-start(f32[2,1024]{1,0:T(2,128)} %param.9) | copy-start | bytes 24580
  2.5 23.6 %all-to-all-start = ((bf16[4,1552,128]{2,1,0:T(8,128)(2,1)}), bf16[4,1552,128]{2,1,0:T(8,128)(2,1)S(1)}, u32[]{:S(2)}, u32[]{:S(2)}) async-start(bf16[4,1552,128]{2,1,0:T(8,128)(2,1)} %shard_map.64), calls=%async_computation | async-start | bytes 3178496 | tf_op jit(solution)/shard_map/all_to_all | solution.py:299
  7.7 18.5 %collective-permute-start = (bf16[2,192,1024]{2,1,0:T(8,128)(2,1)S(1)}, bf16[2,192,1024]{2,1,0:T(8,128)(2,1)S(1)}, u32[]{:S(2)}, u32[]{:S(2)}) collective-permute-start(bf16[2,192,1024]{2,1,0:T(8,128)(2,1)S(1)} %bitcast.16), channel_id=1, source_target_pairs={{0,24},{1,25},{2,26},{3,27},{4,28},{5,29},{6,30},{7,31},{8,16},{9,... | collective-permute-start | bytes 2359304 | tf_op jit(solution)/shard_map/ppermute | solution.py:314
  26.2 11.6 %copy-start.14 = (bf16[2,192,1024]{2,1,0:T(8,128)(2,1)}, bf16[2,192,1024]{2,1,0:T(8,128)(2,1)S(1)}, u32[]{:S(2)}) copy-start(bf16[2,192,1024]{2,1,0:T(8,128)(2,1)S(1)} %collective-permute-done.mirrored_at) | copy-start | bytes 2359300
  26.2 11.6 %copy-start.8 = (bf16[4,1552,128]{2,1,0:T(8,128)(2,1)}, bf16[4,1552,128]{2,1,0:T(8,128)(2,1)S(1)}, u32[]{:S(2)}) copy-start(bf16[4,1552,128]{2,1,0:T(8,128)(2,1)S(1)} %all-to-all-done.near) | copy-start | bytes 4767748
  26.2 11.5 %collective-permute-start.1 = (bf16[4,1552,128]{2,1,0:T(8,128)(2,1)S(1)}, bf16[4,1552,128]{2,1,0:T(8,128)(2,1)S(1)}, u32[]{:S(2)}, u32[]{:S(2)}) collective-permute-start(bf16[4,1552,128]{2,1,0:T(8,128)(2,1)S(1)} %all-to-all-done.near), channel_id=1, source_target_pairs={{0,1},{1,0},{2,3},{3,2},{4,5},{5,4},{6,7},{7,6},{8,9},{9,8},{10,11... | collective-permute-start | bytes 4767752 | tf_op jit(solution)/shard_map/ppermute | solution.py:302
  33.3 16.5 %copy-start.9 = (bf16[4,512,128]{2,1,0:T(8,128)(2,1)}, bf16[4,512,128]{2,1,0:T(8,128)(2,1)S(1)}, u32[]{:S(2)}) copy-start(bf16[4,512,128]{2,1,0:T(8,128)(2,1)S(1)} %slice.19) | copy-start | bytes 1572868
  33.3 16.8 %collective-permute-start.2 = (bf16[4,8,64,128]{3,2,1,0:T(8,128)(2,1)S(1)}, bf16[4,8,64,128]{3,2,1,0:T(8,128)(2,1)}, u32[]{:S(2)}, u32[]{:S(2)}) collective-permute-start(bf16[4,8,64,128]{3,2,1,0:T(8,128)(2,1)S(1)} %bitcast.8), channel_id=1, source_target_pairs={{0,24},{1,25},{2,26},{3,27},{4,28},{5,29},{6,30},{7,31},{8,16},{9,... | collective-permute-start | bytes 1572872 | tf_op jit(solution)/shard_map/ppermute | solution.py:323
  37.7 1.2 copy-start.10
  49.9 7.4 %copy-start.11 = (bf16[2,64,1024]{2,1,0:T(8,128)(2,1)S(1)}, bf16[2,64,1024]{2,1,0:T(8,128)(2,1)}, u32[]{:S(2)}) copy-start(bf16[2,64,1024]{2,1,0:T(8,128)(2,1)} %w_at.1) | copy-start | bytes 786436
  50.1 18.3 %all-to-all-start.1 = ((bf16[4,1024,128]{2,1,0:T(8,128)(2,1)}), bf16[4,1024,128]{2,1,0:T(8,128)(2,1)S(1)}, u32[]{:S(2)}, u32[]{:S(2)}) async-start(bf16[4,1024,128]{2,1,0:T(8,128)(2,1)} %shard_map.65), calls=%async_computation.1 | async-start | bytes 2097152 | tf_op jit(solution)/shard_map/all_to_all | solution.py:299
  54.3 11.2 %collective-permute-start.3 = (bf16[4,8,64,128]{3,2,1,0:T(8,128)(2,1)}, bf16[4,8,64,128]{3,2,1,0:T(8,128)(2,1)S(1)}, u32[]{:S(2)}, u32[]{:S(2)}) collective-permute-start(bf16[4,8,64,128]{3,2,1,0:T(8,128)(2,1)} %collective-permute-done.2.w_mir), channel_id=1, source_target_pairs={{0,1},{1,0},{2,3},{3,2},{4,5},{5,4},{6,7},{7,6},{8,9},{9,8},{10,11... | collective-permute-start | bytes 1572872 | tf_op jit(solution)/shard_map/ppermute | solution.py:302
  57.3 8.2 %collective-permute-start.4 = (bf16[64,1024]{1,0:T(8,128)(2,1)S(1)}, bf16[64,1024]{1,0:T(8,128)(2,1)S(1)}, u32[]{:S(2)}, u32[]{:S(2)}) collective-permute-start(bf16[64,1024]{1,0:T(8,128)(2,1)S(1)} %slice_bitcast_fusion.own), channel_id=1, source_target_pairs={{0,24},{1,25},{2,26},{3,27},{4,28},{5,29},{6,30},{7,31},{8,16},{9,... | collective-permute-start | bytes 393224 | tf_op jit(solution)/shard_map/ppermute | solution.py:343
  65.6 6.9 %copy-start.15 = (bf16[4,8,64,128]{3,2,1,0:T(8,128)(2,1)}, bf16[4,8,64,128]{3,2,1,0:T(8,128)(2,1)S(1)}, u32[]{:S(2)}) copy-start(bf16[4,8,64,128]{3,2,1,0:T(8,128)(2,1)S(1)} %collective-permute-done.3.w_mir_far) | copy-start | bytes 1572868
  68.4 4.1 %copy-start.1 = (bf16[4,1024,128]{2,1,0:T(8,128)(2,1)}, bf16[4,1024,128]{2,1,0:T(8,128)(2,1)S(1)}, u32[]{:S(2)}) copy-start(bf16[4,1024,128]{2,1,0:T(8,128)(2,1)S(1)} %all-to-all-done.1.ready.o_near) | copy-start | bytes 3145732
  68.4 9.0 %collective-permute-start.5 = (bf16[4,1024,128]{2,1,0:T(8,128)(2,1)S(1)}, bf16[4,1024,128]{2,1,0:T(8,128)(2,1)}, u32[]{:S(2)}, u32[]{:S(2)}) collective-permute-start(bf16[4,1024,128]{2,1,0:T(8,128)(2,1)S(1)} %all-to-all-done.1.ready.o_near), channel_id=1, source_target_pairs={{0,1},{1,0},{2,3},{3,2},{4,5},{5,4},{6,7},{7,6},{8,9},{9,8},{10,11... | collective-permute-start | bytes 3145736 | tf_op jit(solution)/shard_map/ppermute | solution.py:302
  72.5 1.4 %copy-start = (bf16[8,128,1024]{2,1,0:T(8,128)(2,1)}, bf16[8,128,1024]{2,1,0:T(8,128)(2,1)S(1)}, u32[]{:S(2)}) copy-start(bf16[8,128,1024]{2,1,0:T(8,128)(2,1)S(1)} %shard_map.66.ready) | copy-start | bytes 6291460
  73.8 43.9 %all-to-all-start.2 = ((bf16[8,128,1024]{2,1,0:T(8,128)(2,1)}), bf16[8,128,1024]{2,1,0:T(8,128)(2,1)S(1)}, u32[]{:S(2)}, u32[]{:S(2)}) async-start(bf16[8,128,1024]{2,1,0:T(8,128)(2,1)} %copy-done), calls=%async_computation.2 | async-start | bytes 4194304 | tf_op jit(solution)/shard_map/all_to_all | solution.py:354
  84.4 22.6 %copy-start.2 = (bf16[1040,128]{1,0:T(8,128)(2,1)S(1)}, bf16[1040,128]{1,0:T(8,128)(2,1)}, u32[]{:S(2)}) copy-start(bf16[1040,128]{1,0:T(8,128)(2,1)} %get-tuple-element.32.refs_1_) | copy-start | bytes 798724
  84.4 22.6 %copy-start.4 = (bf16[512,128]{1,0:T(8,128)(2,1)S(1)}, bf16[512,128]{1,0:T(8,128)(2,1)}, u32[]{:S(2)}) copy-start(bf16[512,128]{1,0:T(8,128)(2,1)} %get-tuple-element.31.refs_0_) | copy-start | bytes 393220
  84.4 22.6 %collective-permute-start.7 = (bf16[1040,128]{1,0:T(8,128)(2,1)}, bf16[1040,128]{1,0:T(8,128)(2,1)S(1)}, u32[]{:S(2)}, u32[]{:S(2)}) collective-permute-start(bf16[1040,128]{1,0:T(8,128)(2,1)} %get-tuple-element.32.refs_1_), channel_id=1, source_target_pairs={{0,8},{1,9},{2,10},{3,11},{4,12},{5,13},{6,14},{7,15},{8,0},{9,1},... | collective-permute-start | bytes 798728 | tf_op jit(solution)/shard_map/ppermute | solution.py:379
  94.0 19.9 %collective-permute-start.6 = (bf16[1040,128]{1,0:T(8,128)(2,1)}, bf16[1040,128]{1,0:T(8,128)(2,1)S(1)}, u32[]{:S(2)}, u32[]{:S(2)}) collective-permute-start(bf16[1040,128]{1,0:T(8,128)(2,1)} %get-tuple-element.30.refs_3_.refs_1_), channel_id=1, source_target_pairs={{0,504},{1,505},{2,506},{3,507},{4,508},{5,509},{6,510},{7,511},{8... | collective-permute-start | bytes 798728 | tf_op jit(solution)/shard_map/ppermute | solution.py:379
  107.0 1.0 copy-start.3
  113.9 0.9 copy-start.7
  114.8 14.3 %copy-start.5 = (bf16[128,1024]{1,0:T(8,128)(2,1)S(1)}, bf16[128,1024]{1,0:T(8,128)(2,1)}, u32[]{:S(2)}) copy-start(bf16[128,1024]{1,0:T(8,128)(2,1)} %get-tuple-element.35.stream_p) | copy-start | bytes 786436
  114.8 14.3 %copy-start.6 = (bf16[128,1024]{1,0:T(8,128)(2,1)S(1)}, bf16[128,1024]{1,0:T(8,128)(2,1)}, u32[]{:S(2)}) copy-start(bf16[128,1024]{1,0:T(8,128)(2,1)} %get-tuple-element.36.stream_q) | copy-start | bytes 786436

commit v6 on v5

--- a/solution.py
+++ b/solution.py
@@ -120,12 +120,12 @@
 ):
     sources = [ref.at[y, :EXT, :] for ref in (near, far) for y in range(4)]
     blocks = fetch(sources, [points.at[b] for b in range(8)], sems)
-    copies = fetch((own_at.at[0], mirrored_at.at[0]), (own, mirrored), w_sems)
+    copies = fetch((own_at.at[0], mirrored_at), (own, mirrored), w_sems)
     rows = []
     for block in range(8):
         blocks[block].wait()
         normed[block * ROWS : (block + 1) * ROWS, :] = layer_norm(
-            side_by_side(points, block).astype(F32), gain[...]
+            side_by_side(points, block).astype(F32), gain[0:1, :]
         )
         rows.append(points[block, D:, :].astype(F32)[:1])
     columns = tag_columns(rows)
@@ -152,68 +152,86 @@
 
 
 def middle_kernel(
-    part, gain, o_near, o_far, w_own, w_own_far, w_mir, w_mir_far, near, far, own_at, mirrored_at, ready,
-    q_out, kv, st_out,
-    heads, update, normed, turned, w, points, own, mirrored, o_sems, w_sems, sems,
+    gain, o_near, o_far, near, far, w_mir, w_mir_far, own_at, mirrored_at, ready,
+    q_out, kv_p, kv_q, st_out,
+    heads, update, normed, queries, keys, turned, w, points, own, mirrored,
+    o_sems, w_sems, sems,
 ):
-    my_y, half = lax.axis_index("y"), half_of(part)
+    my_y = lax.axis_index("y")
     sources, targets = [], []
-    for s in range(2):
-        span = slice(s * 256, (s + 1) * 256)
-        at_near = pl.ds(pl.multiple_of(s * HALF + half * 256, 256), 256)
-        at_far = pl.ds(pl.multiple_of((1 - s) * HALF + half * 256, 256), 256)
-        for g in range(4):
-            sources += [o_near.at[g, at_near, :], o_far.at[g, at_far, :]]
-            targets += [
-                heads.at[span, g * LANES : (g + 1) * LANES],
-                heads.at[span, (g + 4) * LANES : (g + 5) * LANES],
-            ]
-    copies = fetch(sources, targets, o_sems)
-    sources, targets = [], []
-    for i, ref in enumerate((w_own, w_mir, w_own_far, w_mir_far)):
+    for i, ref in enumerate((near, w_mir, far, w_mir_far)):
         for g in range(4):
             row = (i // 2 * 4 + g) * LANES + i % 2 * HEAD_DIM
-            sources.append(ref.at[g])
+            if i % 2:
+                sources.append(ref.at[g])
+            else:
+                sources.append(ref.at[g, EXT:FULL, :].reshape(BLOCKS, HEAD_DIM, LANES))
             targets.append(w.at[:, row : row + HEAD_DIM, :])
-    copies += fetch(sources, targets, w_sems)
-    late = fetch(
-        (
-            near.at[pl.ds(half * 2, 2), :EXT, :], far.at[pl.ds(half * 2, 2), :EXT, :],
-            own_at.at[1], mirrored_at.at[1],
-        ),
-        (points.at[:2], points.at[2:], own, mirrored),
-        sems,
+    w_copies = fetch(sources, targets, w_sems)
+
+    def heads_of(s):
+        span, other = slice(s * HALF, (s + 1) * HALF), slice((1 - s) * HALF, (2 - s) * HALF)
+        sources = [o_near.at[:, span, :], o_far.at[:, other, :]]
+        targets = [heads.at[:4, span, :], heads.at[4:, span, :]]
+        return fetch(sources, targets, o_sems.at[s])
+
+    o_copies = [heads_of(0)]
+    late = fetch((near.at[:, :EXT, :],), (points.at[0],), sems.at[0:1])
+    o_copies.append(heads_of(1))
+    late += fetch(
+        (far.at[:, :EXT, :], own_at.at[1], mirrored_at.at[: 3 * HEAD_DIM]),
+        (points.at[1], own, mirrored),
+        sems.at[1:4],
     )
-    for copy in copies:
-        copy.wait()
-    for j in range(4):
-        both = jnp.concatenate([w[2 * j], w[2 * j + 1]], axis=1)
-        update[:, j * 256 : (j + 1) * 256] = dot(heads[...], both)
-    for copy in late:
+    for copy in w_copies:
         copy.wait()
     rows = []
-    for block in range(4):
-        span = slice(block * ROWS, (block + 1) * ROWS)
-        stream = (side_by_side(points, block).astype(F32) + update[span, :]).astype(BF16)
-        normed[span, :] = layer_norm(stream.astype(F32), gain[...])
-        rows.append(points[block, D:, :].astype(F32)[:1])
-        if block < 2:
-
-            @pl.when(half * 2 + block == my_y)
-            def _(stream=stream):
-                st_out[...] = stream
-
-    project(normed, own, mirrored, q_out, kv.at[:HALF, :], turned)
-    for b in range(4):
-        kv[HALF + b * LANES : HALF + (b + 1) * LANES, :] = turned[:, b * LANES : (b + 1) * LANES]
-    kv[D:, :] = jnp.concatenate(rows + [jnp.zeros((12, LANES), F32)], axis=0).astype(BF16)
+    for s in range(2):
+        for copy in o_copies[s]:
+            copy.wait()
+        span = slice(s * HALF, (s + 1) * HALF)
+        left = jnp.concatenate([heads[g, span, :] for g in range(BLOCKS)], axis=1)
+        for j in range(4):
+            both = jnp.concatenate([w[2 * j], w[2 * j + 1]], axis=1)
+            update[:, j * 256 : (j + 1) * 256] = dot(left, both)
+        late[s].wait()
+        for y in range(4):
+            there = slice(y * ROWS, (y + 1) * ROWS)
+            x = jnp.concatenate(
+                [points[s, y, b * LANES : (b + 1) * LANES, :] for b in range(BLOCKS)], axis=1
+            )
+            stream = (x.astype(F32) + update[there, :]).astype(BF16)
+            normed[s * HALF + y * ROWS : s * HALF + (y + 1) * ROWS, :] = layer_norm(
+                stream.astype(F32), gain[1:2, :]
+            )
+            rows.append(points[s, y, D:, :].astype(F32)[:1])
+            if s == 0:
+
+                @pl.when(y == my_y)
+                def _(stream=stream):
+                    st_out[...] = stream
+
+    for copy in late[2:]:
+        copy.wait()
+    project(normed, own, mirrored, queries, keys, turned)
+    for part, kv in enumerate((kv_p, kv_q)):
+        half = half_of(part)
+        for s in range(2):
+            at = pl.multiple_of(s * HALF + half * 256, 256)
+            q_out[part, s * 256 : (s + 1) * 256, :] = queries[pl.ds(at, 256), :]
+            kv[s * 256 : (s + 1) * 256, :] = keys[pl.ds(at, 256), :]
+            for b in range(2):
+                cut = slice(HALF + (s * 2 + b) * LANES, HALF + (s * 2 + b + 1) * LANES)
+                kv[cut, :] = turned[:, pl.ds(pl.multiple_of(at + b * LANES, LANES), LANES)]
+        tags = [jnp.where(half == 0, rows[s * 4 + b], rows[s * 4 + 2 + b]) for s in range(2) for b in range(2)]
+        kv[D:, :] = jnp.concatenate(tags + [jnp.zeros((12, LANES), F32)], axis=0).astype(BF16)
 
 
 def second_kernel(part, *refs):
     if part:
         queries, mine, other, had, out, keys, values, hots = refs
     else:
-        queries, mine, other, ready, out, keys, values, hots = refs
+        queries, mine, other, out, keys, values, hots = refs
     half, c = half_of(part), lax.axis_index("c")
     keys[:HALF, :LANES] = mine[:HALF, :]
     keys[HALF:, :HEAD_DIM] = other[:HALF, HEAD_DIM:]
@@ -232,7 +250,7 @@
         keys[span, LANES:] = jnp.where(hot, 0.0, FAR).astype(BF16)
     for s in range(2):
         span = slice(s * 256, (s + 1) * 256)
-        result = attend(queries[span, :], hots[span, :], keys, values)
+        result = attend(queries[part, span, :], hots[span, :], keys, values)
         core = c if s == 0 else 1 - c
         for yy in range(2):
             block = result[yy * ROWS : (yy + 1) * ROWS]
@@ -243,23 +261,18 @@
                 out[s * 2 + yy] = block
 
 
-def last_kernel(parts, w, stream_p, stream_q, out, heads):
-    y_half = lax.axis_index("y") // 2
+def last_kernel(parts, w, stream, out, heads):
     for g in range(8):
         heads[:, g * LANES : (g + 1) * LANES] = parts[g]
     update = dot(heads[...], w[...])
 
-    def put(stream):
-        out[...] = (stream[...].astype(F32) + update).astype(BF16)
-
-    pl.when(y_half == half_of(0))(lambda: put(stream_p))
-    pl.when(y_half == half_of(1))(lambda: put(stream_q))
-
-
-def relay_kernel(own, mirrored, ready, out):
+    out[...] = (stream[...].astype(F32) + update).astype(BF16)
+
+
+def relay_kernel(own, rest, out):
     for copy in range(out.shape[0]):
         out[copy, :HEAD_DIM] = own[...]
-        out[copy, HEAD_DIM:] = mirrored[...]
+        out[copy, HEAD_DIM:] = rest[3 * HEAD_DIM :]
 
 
 def call(kernel, micros, outs, scratch, *args, late=(), semaphores=(), megabytes=16):
@@ -270,7 +283,10 @@
         in_specs=[vmem] * len(args) + [anywhere] * len(late),
         out_specs=[vmem] * len(outs),
         scratch_shapes=[pltpu.VMEM(shape, dtype) for shape, dtype in scratch]
-        + [pltpu.SemaphoreType.DMA((count,)) for count in semaphores],
+        + [
+            pltpu.SemaphoreType.DMA(count if isinstance(count, tuple) else (count,))
+            for count in semaphores
+        ],
         compiler_params=pltpu.CompilerParams(vmem_limit_bytes=megabytes * 1024 * 1024),
         cost_estimate=pl.CostEstimate(
             flops=int(micros * 1.1e9), bytes_accessed=0, transcendentals=0
@@ -311,9 +327,9 @@
             ],
             late=(points, order, scan_ids.reshape(1, ROWS), w_out), semaphores=(4,), megabytes=56,
         )
-        w_far = lax.ppermute(w_turned, AXES, mirror)
+        first_far = lax.ppermute(w_turned[0], AXES, mirror)
         near = over_y(copies)
-        near, w_far = lax.optimization_barrier((near, w_far))
+        near, first_far = lax.optimization_barrier((near, first_far))
         far = swapped(near)
 
         def out_weights(array):
@@ -336,50 +352,44 @@
                 ((PATCH, LANES), BF16),
                 *projection,
             ],
-            ln_gain[0:1],
-            late=(near, far, w_turned, w_far), semaphores=(8, 2), megabytes=56,
+            ln_gain,
+            late=(near, far, w_turned, first_far), semaphores=(8, 2), megabytes=56,
         )
         o_copies, w_mir = lax.optimization_barrier((o_copies, w_mir))
-        last_far = lax.ppermute(w_out[1], AXES, mirror)
+        rest = jnp.concatenate([w_turned[1], w_out[1]], axis=0)
+        o_copies, rest = lax.optimization_barrier((o_copies, rest))
+        rest_far = lax.ppermute(rest, AXES, mirror)
         w_mir_far = swapped(w_mir)
-        w_own_far = out_weights(far)
         o_near = over_y(o_copies)
-        o_near, w_mir_far, w_own_far, last_far = lax.optimization_barrier(
-            (o_near, w_mir_far, w_own_far, last_far)
+        (shares,) = call(relay_kernel, 1, [(8, ROWS, D)], [], w_out[1], rest_far, megabytes=4)
+        o_near, w_mir_far, rest_far, shares = lax.optimization_barrier(
+            (o_near, w_mir_far, rest_far, shares)
         )
         o_far = swapped(o_near)
-        (shares,) = call(
-            relay_kernel, 1, [(8, ROWS, D)], [], w_out[1], last_far, late=(o_near,), megabytes=4
-        )
         w_last = lax.all_to_all(shares, ("y", "c"), 0, 0, tiled=True).reshape(D, D)
-        middle, halos = [], []
-        for part, links in enumerate((inner, outer)):
-            middle.append(
-                call(
-                    functools.partial(middle_kernel, part),
-                    4,
-                    [(HALF, LANES), (EXT, LANES), (ROWS, D)],
-                    [
-                        ((HALF, D), BF16),
-                        ((HALF, D), F32),
-                        ((HALF, D), BF16),
-                        ((LANES, HALF), BF16),
-                        ((BLOCKS, D, LANES), BF16),
-                        ((4, EXT, LANES), BF16),
-                        *projection,
-                    ],
-                    ln_gain[1:2],
-                    late=(
-                        o_near, o_far, w_own, w_own_far, w_mir, w_mir_far, near, far,
-                        w_turned, w_far, shares,
-                    ),
-                    semaphores=(16, 16, 4), megabytes=56,
-                )
-            )
-            halos.append(lax.ppermute(middle[part][1], AXES, links))
+        queries, *kvs, stream = call(
+            middle_kernel,
+            8,
+            [(2, HALF, LANES), (EXT, LANES), (EXT, LANES), (ROWS, D)],
+            [
+                ((BLOCKS, PATCH, LANES), BF16),
+                ((HALF, D), F32),
+                ((PATCH, D), BF16),
+                ((PATCH, LANES), BF16),
+                ((PATCH, LANES), BF16),
+                ((LANES, PATCH), BF16),
+                ((BLOCKS, D, LANES), BF16),
+                ((2, 4, EXT, LANES), BF16),
+                *projection,
+            ],
+            ln_gain,
+            late=(o_near, o_far, near, far, w_mir, w_mir_far, w_turned, rest_far, shares),
+            semaphores=((2, 2), 16, 4), megabytes=56,
+        )
+        halos = [lax.ppermute(kv, AXES, links) for kv, links in zip(kvs, (inner, outer))]
         parts = None
         for part in range(2):
-            queries, kv, _ = middle[part]
+            kv = kvs[part]
             (parts,) = call(
                 functools.partial(second_kernel, part),
                 3 if part else 0,
@@ -390,13 +400,13 @@
                     ((HALF, LANES), BF16),
                 ],
                 queries, kv, halos[part], *([parts] if part else []),
-                late=() if part else (middle[1][1],), megabytes=8,
+                megabytes=8,
             )
         parts, w_last = lax.optimization_barrier((parts, w_last))
         parts = lax.all_to_all(parts, ("y", "c"), 0, 0, tiled=True)
         (result,) = call(
             last_kernel, 1.5, [(ROWS, D)], [((ROWS, D), BF16)],
-            parts, w_last, middle[0][2], middle[1][2], megabytes=8,
+            parts, w_last, stream, megabytes=8,
         )
         return result
 

time: 131 us -> 129 us (0.985)
  local copies, waits for them, and re-layouts: 6.98 us -> 4.14 us
  Pallas kernels: 34.7 us -> 32.4 us
  starting transfers between devices: 54.8 us -> 56.8 us
    all_to_all x2, waiting for transfers between devices: 2.82 us -> 5.09 us  [over_y(): return lax.all_to_all(copies, 'y', 0, 0, tiled=True)]
    pallas_call x8 -> x7, Pallas kernels: 34.7 us -> 32.4 us  [call(): pl.pallas_call(kernel, out_shape=[jax.ShapeDtypeStruct(shape, BF16) for s...]
    slice x2 -> x1, local copies, waits for them, and re-layouts: 1.92 us -> 0.03 us  [out_weights(): return array[:, EXT:].reshape(4, BLOCKS, HEAD_DIM, LANES)]
    ppermute x4, waiting for transfers between devices: 19.1 us -> 17.3 us  [the longest x1 8.37 us: on_device(): rest_far = lax.ppermute(rest, AXES, mirror)]
    ppermute x3, starting transfers between devices: 13.3 us -> 15.1 us  [swapped(): return lax.ppermute(array, AXES, other_core)]
    unnamed x32 -> x26, local copies, waits for them, and re-layouts: 4.45 us -> 4.04 us
  transfers between devices with their start and end apart: 11 -> 11, of which waited for: 5 -> 5; matrix products, arithmetic and copies ran while one was open for 2% -> 1% of each run, Pallas kernels for 24% -> 22%
where the time goes in v6:
time: 129 us
  starting transfers between devices  56.8 us (44%)
  Pallas kernels  32.4 us (25%)
  waiting for transfers between devices  22.6 us (18%)
  blocking collectives  11.5 us (9%)
  local copies, waits for them, and re-layouts  4.14 us (3%)
    pallas_call x7, Pallas kernels, call(): pl.pallas_call(kernel, out_shape=[jax.ShapeDtypeStruct(shape, BF16) for s...  32.4 us
    ppermute x2, starting transfers between devices, on_device(): lax.ppermute(kv, AXES, links)  15.3 us
    ppermute x3, starting transfers between devices, swapped(): return lax.ppermute(array, AXES, other_core)  15.1 us
    all_to_all x1, blocking collectives, on_device(): parts = lax.all_to_all(parts, ('y', 'c'), 0, 0, tiled=True)  11.5 us
    all_to_all x2, starting transfers between devices, over_y(): return lax.all_to_all(copies, 'y', 0, 0, tiled=True)  8.67 us
    ppermute x1, waiting for transfers between devices, on_device(): rest_far = lax.ppermute(rest, AXES, mirror)  8.37 us
    ppermute x1, waiting for transfers between devices, on_device(): first_far = lax.ppermute(w_turned[0], AXES, mirror)  5.68 us
    all_to_all x2, waiting for transfers between devices, over_y(): return lax.all_to_all(copies, 'y', 0, 0, tiled=True)  5.09 us
  transfers between devices with their start and end apart: 11, of which 5 were waited for; matrix products, arithmetic and copies ran while one was open for 1% of the time, Pallas kernels for 22%

profile of v6, /device:TPU:1, one launch (start us, length us, event | category | flops | bytes accessed | tf_op | source)
XLA Modules:
  0.0 128.6 jit_solution(6146799776873390198)
XLA Ops:
  0.0 2.5 %shard_map.64 = bf16[4,1552,128]{2,1,0:T(8,128)(2,1)} custom-call(bf16[128,1024]{1,0:T(8,128)(2,1)} %points_at.1, s32[1,128]{1,0:T(1,128)} %order_at.1, s32[1,128]{1,0:T(1,128)} %bitcast.15, bf16[2,64,1024]{2,1,0:T(8,128)(2,1)} %w_at.1), custom_call_target="tpu_custom_call" | custom-call | flops 1320000000 | tf_op jit(solution)/shard_map/pallas_call | solution.py:280
  2.5 0.0 copy-start.7
  2.5 0.0 copy-start.9
  2.5 5.2 %all-to-all-start = ((bf16[4,1552,128]{2,1,0:T(8,128)(2,1)}), bf16[4,1552,128]{2,1,0:T(8,128)(2,1)S(1)}, u32[]{:S(2)}, u32[]{:S(2)}) async-start(bf16[4,1552,128]{2,1,0:T(8,128)(2,1)} %shard_map.64), calls=%async_computation | async-start | bytes 3178496 | tf_op jit(solution)/shard_map/all_to_all | solution.py:315
  7.7 0.1 slice_bitcast_fusion
  7.7 4.4 %collective-permute-start = (bf16[192,1024]{1,0:T(8,128)(2,1)S(1)}, bf16[192,1024]{1,0:T(8,128)(2,1)S(1)}, u32[]{:S(2)}, u32[]{:S(2)}) collective-permute-start(bf16[192,1024]{1,0:T(8,128)(2,1)S(1)} %get-tuple-element.38), channel_id=1, source_target_pairs={{0,24},{1,25},{2,26},{3,27},{4,28},{5,29},{6,30},{7,31},{8,16},{9,... | collective-permute-start | bytes 1179656 | tf_op jit(solution)/shard_map/ppermute | solution.py:330
  12.1 5.7 %collective-permute-done.mirrored_at = bf16[192,1024]{1,0:T(8,128)(2,1)S(1)} collective-permute-done((bf16[192,1024]{1,0:T(8,128)(2,1)S(1)}, bf16[192,1024]{1,0:T(8,128)(2,1)S(1)}, u32[]{:S(2)}, u32[]{:S(2)}) %collective-permute-start) | collective-permute-done | bytes 393248 | tf_op jit(solution)/shard_map/ppermute | solution.py:330
  17.8 5.1 %all-to-all-done.near = bf16[4,1552,128]{2,1,0:T(8,128)(2,1)S(1)} async-done(((bf16[4,1552,128]{2,1,0:T(8,128)(2,1)}), bf16[4,1552,128]{2,1,0:T(8,128)(2,1)S(1)}, u32[]{:S(2)}, u32[]{:S(2)}) %all-to-all-start) | async-done | bytes 1589280 | tf_op jit(solution)/shard_map/all_to_all | solution.py:315
  22.9 8.5 %collective-permute-start.1 = (bf16[4,1552,128]{2,1,0:T(8,128)(2,1)S(1)}, bf16[4,1552,128]{2,1,0:T(8,128)(2,1)S(1)}, u32[]{:S(2)}, u32[]{:S(2)}) collective-permute-start(bf16[4,1552,128]{2,1,0:T(8,128)(2,1)S(1)} %all-to-all-done.near), channel_id=1, source_target_pairs={{0,1},{1,0},{2,3},{3,2},{4,5},{5,4},{6,7},{7,6},{8,9},{9,8},{10,11... | collective-permute-start | bytes 4767752 | tf_op jit(solution)/shard_map/ppermute | solution.py:318
  31.5 0.8 pad_maximum_fusion
  32.3 4.4 %collective-permute-start.2 = (bf16[4,8,64,128]{3,2,1,0:T(8,128)(2,1)S(1)}, bf16[4,8,64,128]{3,2,1,0:T(8,128)(2,1)}, u32[]{:S(2)}, u32[]{:S(2)}) collective-permute-start(bf16[4,8,64,128]{3,2,1,0:T(8,128)(2,1)S(1)} %bitcast.14), channel_id=1, source_target_pairs={{0,24},{1,25},{2,26},{3,27},{4,28},{5,29},{6,30},{7,31},{8,16},{9,... | collective-permute-start | bytes 1572872 | tf_op jit(solution)/shard_map/ppermute | solution.py:339
  36.8 1.2 copy-done.10
  37.9 10.9 %shard_map.65 = bf16[4,1024,128]{2,1,0:T(8,128)(2,1)} custom-call(f32[2,1024]{1,0:T(2,128)} %gain.3, bf16[4,1552,128]{2,1,0:T(8,128)(2,1)} %copy-done.5, bf16[4,1552,128]{2,1,0:T(8,128)(2,1)} %copy-done.10, bf16[2,192,1024]{2,1,0:T(8,128)(2,1)} %bitcast.11, bf16[192,1024]{1,0:T(8,128)(2,1)} %copy-done.12), custom_call_target="tpu_custom_call" | custom-call | flops 8800000000 | tf_op jit(solution)/shard_map/pallas_call | solution.py:280
  48.9 0.2 collective-permute-done.2.w_mir
  49.1 3.5 %all-to-all-start.1 = ((bf16[4,1024,128]{2,1,0:T(8,128)(2,1)}), bf16[4,1024,128]{2,1,0:T(8,128)(2,1)S(1)}, u32[]{:S(2)}, u32[]{:S(2)}) async-start(bf16[4,1024,128]{2,1,0:T(8,128)(2,1)} %shard_map.65), calls=%async_computation.1 | async-start | bytes 2097152 | tf_op jit(solution)/shard_map/all_to_all | solution.py:315
  52.6 4.4 %collective-permute-start.4 = (bf16[256,1024]{1,0:T(8,128)(2,1)S(1)}, bf16[256,1024]{1,0:T(8,128)(2,1)S(1)}, u32[]{:S(2)}, u32[]{:S(2)}) collective-permute-start(bf16[256,1024]{1,0:T(8,128)(2,1)S(1)} %copy-done.8), channel_id=1, source_target_pairs={{0,24},{1,25},{2,26},{3,27},{4,28},{5,29},{6,30},{7,31},{8,16},{9,... | collective-permute-start | bytes 1572872 | tf_op jit(solution)/shard_map/ppermute | solution.py:361
  57.0 3.0 %collective-permute-start.3 = (bf16[4,8,64,128]{3,2,1,0:T(8,128)(2,1)}, bf16[4,8,64,128]{3,2,1,0:T(8,128)(2,1)S(1)}, u32[]{:S(2)}, u32[]{:S(2)}) collective-permute-start(bf16[4,8,64,128]{3,2,1,0:T(8,128)(2,1)} %collective-permute-done.2.w_mir), channel_id=1, source_target_pairs={{0,1},{1,0},{2,3},{3,2},{4,5},{5,4},{6,7},{7,6},{8,9},{9,8},{10,11... | collective-permute-start | bytes 1572872 | tf_op jit(solution)/shard_map/ppermute | solution.py:318
  60.0 8.4 %collective-permute-done.4.rest.mirrored_at = bf16[256,1024]{1,0:T(8,128)(2,1)S(1)} collective-permute-done((bf16[256,1024]{1,0:T(8,128)(2,1)S(1)}, bf16[256,1024]{1,0:T(8,128)(2,1)S(1)}, u32[]{:S(2)}, u32[]{:S(2)}) %collective-permute-start.4) | collective-permute-done | bytes 524320 | tf_op jit(solution)/shard_map/ppermute | solution.py:361
  68.4 1.5 %shard_map.66.ready = bf16[8,128,1024]{2,1,0:T(8,128)(2,1)} custom-call(bf16[64,1024]{1,0:T(8,128)(2,1)S(1)} %slice_bitcast_fusion.2.own, bf16[256,1024]{1,0:T(8,128)(2,1)S(1)} %collective-permute-done.4.rest.mirrored_at), custom_call_target="tpu_custom_call" | custom-call | flops 1100000000 | tf_op jit(solution)/shard_map/pallas_call | solution.py:280
  69.9 3.6 %collective-permute-start.5 = (bf16[4,1024,128]{2,1,0:T(8,128)(2,1)S(1)}, bf16[4,1024,128]{2,1,0:T(8,128)(2,1)}, u32[]{:S(2)}, u32[]{:S(2)}) collective-permute-start(bf16[4,1024,128]{2,1,0:T(8,128)(2,1)S(1)} %all-to-all-done.1.o_near), channel_id=1, source_target_pairs={{0,1},{1,0},{2,3},{3,2},{4,5},{5,4},{6,7},{7,6},{8,9},{9,8},{10,11... | collective-permute-start | bytes 3145736 | tf_op jit(solution)/shard_map/ppermute | solution.py:318
  73.5 4.6 %all-to-all-start.2 = ((bf16[8,128,1024]{2,1,0:T(8,128)(2,1)}), bf16[8,128,1024]{2,1,0:T(8,128)(2,1)S(1)}, u32[]{:S(2)}, u32[]{:S(2)}) async-start(bf16[8,128,1024]{2,1,0:T(8,128)(2,1)} %shard_map.66.ready), calls=%async_computation.2 | async-start | bytes 4194304 | tf_op jit(solution)/shard_map/all_to_all | solution.py:369
  78.1 10.6 %shard_map.67 = (bf16[2,512,128]{2,1,0:T(8,128)(2,1)}, bf16[1040,128]{1,0:T(8,128)(2,1)}, bf16[1040,128]{1,0:T(8,128)(2,1)}, bf16[128,1024]{1,0:T(8,128)(2,1)}) custom-call(f32[2,1024]{1,0:T(2,128)} %gain.3, bf16[4,1024,128]{2,1,0:T(8,128)(2,1)} %copy-done.6, bf16[4,1024,128]{2,1,0:T(8,128)(2,1)} %collective-permute-done.5.o_far, ...), custom_call_target="tpu_custom_call" | custom-call | flops 8800000000 | tf_op jit(solution)/shard_map/pallas_call | solution.py:280
  88.8 2.3 %collective-permute-start.7 = (bf16[1040,128]{1,0:T(8,128)(2,1)}, bf16[1040,128]{1,0:T(8,128)(2,1)S(1)}, u32[]{:S(2)}, u32[]{:S(2)}) collective-permute-start(bf16[1040,128]{1,0:T(8,128)(2,1)} %get-tuple-element.33.refs_1_), channel_id=1, source_target_pairs={{0,8},{1,9},{2,10},{3,11},{4,12},{5,13},{6,14},{7,15},{8,0},{9,1},... | collective-permute-start | bytes 798728 | tf_op jit(solution)/shard_map/ppermute | solution.py:389
  91.0 13.0 %collective-permute-start.6 = (bf16[1040,128]{1,0:T(8,128)(2,1)}, bf16[1040,128]{1,0:T(8,128)(2,1)S(1)}, u32[]{:S(2)}, u32[]{:S(2)}) collective-permute-start(bf16[1040,128]{1,0:T(8,128)(2,1)} %get-tuple-element.32.refs_1_), channel_id=1, source_target_pairs={{0,504},{1,505},{2,506},{3,507},{4,508},{5,509},{6,510},{7,511},{8... | collective-permute-start | bytes 798728 | tf_op jit(solution)/shard_map/ppermute | solution.py:389
  104.1 0.9 copy-done
  105.0 0.9 copy-done.1
  106.0 2.9 %shard_map.68.refs_3_ = bf16[4,128,128]{2,1,0:T(8,128)(2,1)S(1)} custom-call(bf16[2,512,128]{2,1,0:T(8,128)(2,1)S(1)} %copy-done.1, bf16[1040,128]{1,0:T(8,128)(2,1)S(1)} %copy-done, bf16[1040,128]{1,0:T(8,128)(2,1)S(1)} %collective-permute-done.7.refs_2_), custom_call_target="tpu_custom_call" | custom-call | tf_op jit(solution)/shard_map/pallas_call | solution.py:280
  108.8 3.2 %collective-permute-done.6.refs_2_ = bf16[1040,128]{1,0:T(8,128)(2,1)S(1)} collective-permute-done((bf16[1040,128]{1,0:T(8,128)(2,1)}, bf16[1040,128]{1,0:T(8,128)(2,1)S(1)}, u32[]{:S(2)}, u32[]{:S(2)}) %collective-permute-start.6) | collective-permute-done | bytes 266272 | tf_op jit(solution)/shard_map/ppermute | solution.py:389
  112.1 0.9 copy-done.3
  113.0 2.9 %shard_map.69 = bf16[8,128,128]{2,1,0:T(8,128)(2,1)S(1)} custom-call(bf16[2,512,128]{2,1,0:T(8,128)(2,1)S(1)} %copy-done.1, bf16[1040,128]{1,0:T(8,128)(2,1)S(1)} %copy-done.3, bf16[1040,128]{1,0:T(8,128)(2,1)S(1)} %collective-permute-done.6.refs_2_, bf16[4,128,128]{2,1,0:T(8,128)(2,1)S(1)} %shard_map.68.refs_3_), custom_call_target="tpu_custom_call" | custom-call | flops 3300000000 | tf_op jit(solution)/shard_map/pallas_call | solution.py:280
  115.9 11.5 %all_to_all.20.parts = bf16[8,128,128]{2,1,0:T(8,128)(2,1)S(1)} all-to-all(bf16[8,128,128]{2,1,0:T(8,128)(2,1)S(1)} %shard_map.69), channel_id=1, replica_groups=mesh['z'=16,'xl'=2,'xh'=2,'y'=4,'c'=2] {'y','c'}, dimensions={0} | all-to-all | bytes 524288 | tf_op jit(solution)/shard_map/all_to_all | solution.py:406
  127.4 1.2 shard_map.70
  (28 shorter events, 0.1 us)
Async XLA Ops:
  2.5 5.2 %copy-start.7 = (bf16[2,1024,192]{1,2,0:T(8,128)(2,1)S(1)}, bf16[2,1024,192]{1,2,0:T(8,128)(2,1)}, u32[]{:S(2)}) copy-start(bf16[2,1024,192]{1,2,0:T(8,128)(2,1)} %param.10) | copy-start | bytes 2359300
  2.5 28.9 %copy-start.9 = (bf16[2,64,1024]{2,1,0:T(8,128)(2,1)S(1)}, bf16[2,64,1024]{2,1,0:T(8,128)(2,1)}, u32[]{:S(2)}) copy-start(bf16[2,64,1024]{2,1,0:T(8,128)(2,1)} %w_at.1) | copy-start | bytes 786436
  2.5 20.4 %all-to-all-start = ((bf16[4,1552,128]{2,1,0:T(8,128)(2,1)}), bf16[4,1552,128]{2,1,0:T(8,128)(2,1)S(1)}, u32[]{:S(2)}, u32[]{:S(2)}) async-start(bf16[4,1552,128]{2,1,0:T(8,128)(2,1)} %shard_map.64), calls=%async_computation | async-start | bytes 3178496 | tf_op jit(solution)/shard_map/all_to_all | solution.py:315
  7.7 10.1 %collective-permute-start = (bf16[192,1024]{1,0:T(8,128)(2,1)S(1)}, bf16[192,1024]{1,0:T(8,128)(2,1)S(1)}, u32[]{:S(2)}, u32[]{:S(2)}) collective-permute-start(bf16[192,1024]{1,0:T(8,128)(2,1)S(1)} %get-tuple-element.38), channel_id=1, source_target_pairs={{0,24},{1,25},{2,26},{3,27},{4,28},{5,29},{6,30},{7,31},{8,16},{9,... | collective-permute-start | bytes 1179656 | tf_op jit(solution)/shard_map/ppermute | solution.py:330
  17.8 18.9 %copy-start.12 = (bf16[192,1024]{1,0:T(8,128)(2,1)}, bf16[192,1024]{1,0:T(8,128)(2,1)S(1)}, u32[]{:S(2)}) copy-start(bf16[192,1024]{1,0:T(8,128)(2,1)S(1)} %collective-permute-done.mirrored_at) | copy-start | bytes 1179652
  22.9 13.9 %copy-start.5 = (bf16[4,1552,128]{2,1,0:T(8,128)(2,1)}, bf16[4,1552,128]{2,1,0:T(8,128)(2,1)S(1)}, u32[]{:S(2)}) copy-start(bf16[4,1552,128]{2,1,0:T(8,128)(2,1)S(1)} %all-to-all-done.near) | copy-start | bytes 4767748
  22.9 13.8 %collective-permute-start.1 = (bf16[4,1552,128]{2,1,0:T(8,128)(2,1)S(1)}, bf16[4,1552,128]{2,1,0:T(8,128)(2,1)S(1)}, u32[]{:S(2)}, u32[]{:S(2)}) collective-permute-start(bf16[4,1552,128]{2,1,0:T(8,128)(2,1)S(1)} %all-to-all-done.near), channel_id=1, source_target_pairs={{0,1},{1,0},{2,3},{3,2},{4,5},{5,4},{6,7},{7,6},{8,9},{9,8},{10,11... | collective-permute-start | bytes 4767752 | tf_op jit(solution)/shard_map/ppermute | solution.py:318
  32.3 16.8 %collective-permute-start.2 = (bf16[4,8,64,128]{3,2,1,0:T(8,128)(2,1)S(1)}, bf16[4,8,64,128]{3,2,1,0:T(8,128)(2,1)}, u32[]{:S(2)}, u32[]{:S(2)}) collective-permute-start(bf16[4,8,64,128]{3,2,1,0:T(8,128)(2,1)S(1)} %bitcast.14), channel_id=1, source_target_pairs={{0,24},{1,25},{2,26},{3,27},{4,28},{5,29},{6,30},{7,31},{8,16},{9,... | collective-permute-start | bytes 1572872 | tf_op jit(solution)/shard_map/ppermute | solution.py:339
  36.8 1.2 copy-start.10
  48.9 3.8 %copy-start.8 = (bf16[256,1024]{1,0:T(8,128)(2,1)S(1)}, bf16[256,1024]{1,0:T(8,128)(2,1)}, u32[]{:S(2)}) copy-start(bf16[256,1024]{1,0:T(8,128)(2,1)} %pad_maximum_fusion) | copy-start | bytes 1572868
  49.1 20.8 %all-to-all-start.1 = ((bf16[4,1024,128]{2,1,0:T(8,128)(2,1)}), bf16[4,1024,128]{2,1,0:T(8,128)(2,1)S(1)}, u32[]{:S(2)}, u32[]{:S(2)}) async-start(bf16[4,1024,128]{2,1,0:T(8,128)(2,1)} %shard_map.65), calls=%async_computation.1 | async-start | bytes 2097152 | tf_op jit(solution)/shard_map/all_to_all | solution.py:315
  52.6 15.8 %collective-permute-start.4 = (bf16[256,1024]{1,0:T(8,128)(2,1)S(1)}, bf16[256,1024]{1,0:T(8,128)(2,1)S(1)}, u32[]{:S(2)}, u32[]{:S(2)}) collective-permute-start(bf16[256,1024]{1,0:T(8,128)(2,1)S(1)} %copy-done.8), channel_id=1, source_target_pairs={{0,24},{1,25},{2,26},{3,27},{4,28},{5,29},{6,30},{7,31},{8,16},{9,... | collective-permute-start | bytes 1572872 | tf_op jit(solution)/shard_map/ppermute | solution.py:361
  57.0 12.9 %collective-permute-start.3 = (bf16[4,8,64,128]{3,2,1,0:T(8,128)(2,1)}, bf16[4,8,64,128]{3,2,1,0:T(8,128)(2,1)S(1)}, u32[]{:S(2)}, u32[]{:S(2)}) collective-permute-start(bf16[4,8,64,128]{3,2,1,0:T(8,128)(2,1)} %collective-permute-done.2.w_mir), channel_id=1, source_target_pairs={{0,1},{1,0},{2,3},{3,2},{4,5},{5,4},{6,7},{7,6},{8,9},{9,8},{10,11... | collective-permute-start | bytes 1572872 | tf_op jit(solution)/shard_map/ppermute | solution.py:318
  68.4 1.5 %copy-start.2 = (bf16[256,1024]{1,0:T(8,128)(2,1)}, bf16[256,1024]{1,0:T(8,128)(2,1)S(1)}, u32[]{:S(2)}) copy-start(bf16[256,1024]{1,0:T(8,128)(2,1)S(1)} %collective-permute-done.4.rest.mirrored_at) | copy-start | bytes 1572868
  69.9 3.6 %copy-start.11 = (bf16[4,8,64,128]{3,2,1,0:T(8,128)(2,1)}, bf16[4,8,64,128]{3,2,1,0:T(8,128)(2,1)S(1)}, u32[]{:S(2)}) copy-start(bf16[4,8,64,128]{3,2,1,0:T(8,128)(2,1)S(1)} %collective-permute-done.3.w_mir_far) | copy-start | bytes 1572868
  69.9 3.6 %copy-start.6 = (bf16[4,1024,128]{2,1,0:T(8,128)(2,1)}, bf16[4,1024,128]{2,1,0:T(8,128)(2,1)S(1)}, u32[]{:S(2)}) copy-start(bf16[4,1024,128]{2,1,0:T(8,128)(2,1)S(1)} %all-to-all-done.1.o_near) | copy-start | bytes 3145732
  69.9 8.2 %collective-permute-start.5 = (bf16[4,1024,128]{2,1,0:T(8,128)(2,1)S(1)}, bf16[4,1024,128]{2,1,0:T(8,128)(2,1)}, u32[]{:S(2)}, u32[]{:S(2)}) collective-permute-start(bf16[4,1024,128]{2,1,0:T(8,128)(2,1)S(1)} %all-to-all-done.1.o_near), channel_id=1, source_target_pairs={{0,1},{1,0},{2,3},{3,2},{4,5},{5,4},{6,7},{7,6},{8,9},{9,8},{10,11... | collective-permute-start | bytes 3145736 | tf_op jit(solution)/shard_map/ppermute | solution.py:318
  73.5 42.3 %all-to-all-start.2 = ((bf16[8,128,1024]{2,1,0:T(8,128)(2,1)}), bf16[8,128,1024]{2,1,0:T(8,128)(2,1)S(1)}, u32[]{:S(2)}, u32[]{:S(2)}) async-start(bf16[8,128,1024]{2,1,0:T(8,128)(2,1)} %shard_map.66.ready), calls=%async_computation.2 | async-start | bytes 4194304 | tf_op jit(solution)/shard_map/all_to_all | solution.py:369
  88.8 15.3 %collective-permute-start.7 = (bf16[1040,128]{1,0:T(8,128)(2,1)}, bf16[1040,128]{1,0:T(8,128)(2,1)S(1)}, u32[]{:S(2)}, u32[]{:S(2)}) collective-permute-start(bf16[1040,128]{1,0:T(8,128)(2,1)} %get-tuple-element.33.refs_1_), channel_id=1, source_target_pairs={{0,8},{1,9},{2,10},{3,11},{4,12},{5,13},{6,14},{7,15},{8,0},{9,1},... | collective-permute-start | bytes 798728 | tf_op jit(solution)/shard_map/ppermute | solution.py:389
  91.0 21.0 %collective-permute-start.6 = (bf16[1040,128]{1,0:T(8,128)(2,1)}, bf16[1040,128]{1,0:T(8,128)(2,1)S(1)}, u32[]{:S(2)}, u32[]{:S(2)}) collective-permute-start(bf16[1040,128]{1,0:T(8,128)(2,1)} %get-tuple-element.32.refs_1_), channel_id=1, source_target_pairs={{0,504},{1,505},{2,506},{3,507},{4,508},{5,509},{6,510},{7,511},{8... | collective-permute-start | bytes 798728 | tf_op jit(solution)/shard_map/ppermute | solution.py:389
  104.1 1.0 copy-start
  105.0 0.9 copy-start.1
  112.1 1.0 copy-start.3
  113.0 14.4 %copy-start.4 = (bf16[128,1024]{1,0:T(8,128)(2,1)S(1)}, bf16[128,1024]{1,0:T(8,128)(2,1)}, u32[]{:S(2)}) copy-start(bf16[128,1024]{1,0:T(8,128)(2,1)} %get-tuple-element.36.stream) | copy-start | bytes 786436

commit v7 on v6

--- a/solution.py
+++ b/solution.py
@@ -62,13 +62,20 @@
 
 def attend(queries, hot, keys_ref, values_ref):
     lane = lax.broadcasted_iota(jnp.int32, queries.shape, 1)
+    pieces = [slice(k * 256, (k + 1) * 256) for k in range(4)]
+    scores = []
+    for head in range(2):
+        own = jnp.where(lane // HEAD_DIM == head, queries, jnp.zeros_like(queries))
+        both = jnp.concatenate([own, hot], axis=1)
+        scores.append([dot_nt(keys_ref[piece, :], both) for piece in pieces])
     results = []
     for head in range(2):
-        own = jnp.where(lane // HEAD_DIM == head, queries, jnp.zeros_like(queries))
-        scores = dot_nt(keys_ref[...], jnp.concatenate([own, hot], axis=1))
-        top = jnp.max(scores, axis=0, keepdims=True)
-        probs = jnp.exp(scores - top).astype(BF16)
-        sums = dot(values_ref[head], probs)
+        tops = [jnp.max(part, axis=0, keepdims=True) for part in scores[head]]
+        top = functools.reduce(jnp.maximum, tops)
+        sums = sum(
+            dot(values_ref[head, :, piece], jnp.exp(part - top).astype(BF16))
+            for part, piece in zip(scores[head], pieces)
+        )
         results.append(sums[:HEAD_DIM] / sums[HEAD_DIM : HEAD_DIM + 1])
     return jnp.transpose(jnp.concatenate(results, axis=0)).astype(BF16)
 
@@ -101,11 +108,11 @@
 
 
 def project(normed, own, mirrored, queries, keys, turned):
-    both = jnp.concatenate([joined(own, mirrored, 0), joined(own, mirrored, 1)], axis=0)
-    found = dot_nt(normed[...], both).astype(BF16)
-    queries[...] = found[:, :LANES] * jnp.asarray(HEAD_DIM**-0.5, BF16)
-    keys[...] = found[:, LANES:]
-    turned[...] = dot_nt(joined(own, mirrored, 2), normed[...]).astype(BF16)
+    every = jnp.concatenate([joined(own, mirrored, kind) for kind in range(3)], axis=0)
+    found = dot_nt(normed, every)
+    queries[...] = found[:, :LANES].astype(BF16) * jnp.asarray(HEAD_DIM**-0.5, BF16)
+    keys[...] = found[:, LANES : 2 * LANES].astype(BF16)
+    turned[...] = jnp.transpose(found[:, 2 * LANES :]).astype(BF16)
 
 
 def put_values(values_ref, span, turned, swap):
@@ -115,23 +122,17 @@
 
 
 def first_kernel(
-    gain, near, far, own_at, mirrored_at, out,
-    points, normed, queries, keys, turned, values, hots, own, mirrored, sems, w_sems,
+    gain, near, far, own, mirrored, out, normed, queries, keys, turned, values, hots
 ):
-    sources = [ref.at[y, :EXT, :] for ref in (near, far) for y in range(4)]
-    blocks = fetch(sources, [points.at[b] for b in range(8)], sems)
-    copies = fetch((own_at.at[0], mirrored_at), (own, mirrored), w_sems)
     rows = []
     for block in range(8):
-        blocks[block].wait()
+        ref, y = (near, far)[block // 4], block % 4
         normed[block * ROWS : (block + 1) * ROWS, :] = layer_norm(
-            side_by_side(points, block).astype(F32), gain[0:1, :]
-        )
-        rows.append(points[block, D:, :].astype(F32)[:1])
+            side_by_side(ref, y).astype(F32), gain[0:1, :]
+        )
+        rows.append(ref[y, D:EXT, :].astype(F32)[:1])
     columns = tag_columns(rows)
-    for copy in copies:
-        copy.wait()
-    project(normed, own, mirrored, queries, keys.at[:, :LANES], turned)
+    project(normed[...], own.at[0], mirrored, queries, keys.at[:, :LANES], turned)
     put_values(values, slice(0, PATCH), turned, False)
     values[:, HEAD_DIM:, :] = jnp.ones((2, 16, PATCH), BF16)
     for block in range(8):
@@ -169,41 +170,30 @@
             targets.append(w.at[:, row : row + HEAD_DIM, :])
     w_copies = fetch(sources, targets, w_sems)
 
-    def heads_of(s):
-        span, other = slice(s * HALF, (s + 1) * HALF), slice((1 - s) * HALF, (2 - s) * HALF)
-        sources = [o_near.at[:, span, :], o_far.at[:, other, :]]
-        targets = [heads.at[:4, span, :], heads.at[4:, span, :]]
-        return fetch(sources, targets, o_sems.at[s])
-
-    o_copies = [heads_of(0)]
-    late = fetch((near.at[:, :EXT, :],), (points.at[0],), sems.at[0:1])
-    o_copies.append(heads_of(1))
-    late += fetch(
-        (far.at[:, :EXT, :], own_at.at[1], mirrored_at.at[: 3 * HEAD_DIM]),
-        (points.at[1], own, mirrored),
-        sems.at[1:4],
+    late = fetch((own_at.at[1], mirrored_at), (own, mirrored), sems.at[2:4])
+    top, end = slice(0, HALF), slice(HALF, PATCH)
+    o_copies = fetch(
+        (o_near, o_far.at[:, end, :], o_far.at[:, top, :]),
+        (heads.at[:4], heads.at[4:, top, :], heads.at[4:, end, :]),
+        o_sems,
     )
-    for copy in w_copies:
+    x_copies = fetch((near.at[:, :EXT, :], far.at[:, :EXT, :]), (points.at[0], points.at[1]), sems)
+    for copy in w_copies + o_copies:
         copy.wait()
+    left = jnp.concatenate([heads[g] for g in range(BLOCKS)], axis=1)
+    for j in range(2):
+        both = jnp.concatenate([w[4 * j + i] for i in range(4)], axis=1)
+        update[:, j * 512 : (j + 1) * 512] = dot(left, both)
     rows = []
     for s in range(2):
-        for copy in o_copies[s]:
-            copy.wait()
-        span = slice(s * HALF, (s + 1) * HALF)
-        left = jnp.concatenate([heads[g, span, :] for g in range(BLOCKS)], axis=1)
-        for j in range(4):
-            both = jnp.concatenate([w[2 * j], w[2 * j + 1]], axis=1)
-            update[:, j * 256 : (j + 1) * 256] = dot(left, both)
-        late[s].wait()
+        x_copies[s].wait()
         for y in range(4):
-            there = slice(y * ROWS, (y + 1) * ROWS)
+            there = slice(s * HALF + y * ROWS, s * HALF + (y + 1) * ROWS)
             x = jnp.concatenate(
                 [points[s, y, b * LANES : (b + 1) * LANES, :] for b in range(BLOCKS)], axis=1
             )
             stream = (x.astype(F32) + update[there, :]).astype(BF16)
-            normed[s * HALF + y * ROWS : s * HALF + (y + 1) * ROWS, :] = layer_norm(
-                stream.astype(F32), gain[1:2, :]
-            )
+            normed[there, :] = layer_norm(stream.astype(F32), gain[1:2, :])
             rows.append(points[s, y, D:, :].astype(F32)[:1])
             if s == 0:
 
@@ -211,9 +201,9 @@
                 def _(stream=stream):
                     st_out[...] = stream
 
-    for copy in late[2:]:
+    for copy in late:
         copy.wait()
-    project(normed, own, mirrored, queries, keys, turned)
+    project(normed[...], own, mirrored, queries, keys, turned)
     for part, kv in enumerate((kv_p, kv_q)):
         half = half_of(part)
         for s in range(2):
@@ -269,7 +259,7 @@
     out[...] = (stream[...].astype(F32) + update).astype(BF16)
 
 
-def relay_kernel(own, rest, out):
+def relay_kernel(own, rest, ready, out):
     for copy in range(out.shape[0]):
         out[copy, :HEAD_DIM] = own[...]
         out[copy, HEAD_DIM:] = rest[3 * HEAD_DIM :]
@@ -327,7 +317,8 @@
             ],
             late=(points, order, scan_ids.reshape(1, ROWS), w_out), semaphores=(4,), megabytes=56,
         )
-        first_far = lax.ppermute(w_turned[0], AXES, mirror)
+        first = jnp.concatenate([w_turned[0], w_out[1]], axis=0)
+        first_far = lax.ppermute(first, AXES, mirror)
         near = over_y(copies)
         near, first_far = lax.optimization_barrier((near, first_far))
         far = swapped(near)
@@ -343,25 +334,23 @@
             8,
             [(4, PATCH, LANES)],
             [
-                ((8, EXT, LANES), BF16),
                 ((PATCH, D), BF16),
                 ((PATCH, LANES), BF16),
                 ((PATCH, 2 * LANES), BF16),
                 ((LANES, PATCH), BF16),
                 ((2, HEAD_DIM + 16, PATCH), BF16),
                 ((PATCH, LANES), BF16),
-                *projection,
             ],
-            ln_gain,
-            late=(near, far, w_turned, first_far), semaphores=(8, 2), megabytes=56,
+            ln_gain, near, far, w_turned, first_far, megabytes=16,
         )
         o_copies, w_mir = lax.optimization_barrier((o_copies, w_mir))
-        rest = jnp.concatenate([w_turned[1], w_out[1]], axis=0)
-        o_copies, rest = lax.optimization_barrier((o_copies, rest))
+        o_copies, rest = lax.optimization_barrier((o_copies, w_turned[1]))
         rest_far = lax.ppermute(rest, AXES, mirror)
         w_mir_far = swapped(w_mir)
         o_near = over_y(o_copies)
-        (shares,) = call(relay_kernel, 1, [(8, ROWS, D)], [], w_out[1], rest_far, megabytes=4)
+        (shares,) = call(
+            relay_kernel, 1, [(8, ROWS, D)], [], w_out[1], first_far, late=(w_mir_far,), megabytes=4
+        )
         o_near, w_mir_far, rest_far, shares = lax.optimization_barrier(
             (o_near, w_mir_far, rest_far, shares)
         )
@@ -373,7 +362,7 @@
             [(2, HALF, LANES), (EXT, LANES), (EXT, LANES), (ROWS, D)],
             [
                 ((BLOCKS, PATCH, LANES), BF16),
-                ((HALF, D), F32),
+                ((PATCH, D), F32),
                 ((PATCH, D), BF16),
                 ((PATCH, LANES), BF16),
                 ((PATCH, LANES), BF16),
@@ -384,7 +373,7 @@
             ],
             ln_gain,
             late=(o_near, o_far, near, far, w_mir, w_mir_far, w_turned, rest_far, shares),
-            semaphores=((2, 2), 16, 4), megabytes=56,
+            semaphores=(3, 16, 4), megabytes=56,
         )
         halos = [lax.ppermute(kv, AXES, links) for kv, links in zip(kvs, (inner, outer))]
         parts = None

time: 129 us -> 127 us (0.984)
  Pallas kernels: 32.4 us -> 26.1 us
  waiting for transfers between devices: 22.6 us -> 28.2 us
    pallas_call x7, Pallas kernels: 32.4 us -> 26.1 us  [call(): pl.pallas_call(kernel, out_shape=[jax.ShapeDtypeStruct(shape, BF16) for s...]
    ppermute x1, waiting for transfers between devices: 0.24 us -> 5.79 us  [on_device(): w_mir = lax.ppermute(w_own, AXES, mirror)]
    all_to_all x2, waiting for transfers between devices: 5.09 us -> 2.2 us  [over_y(): return lax.all_to_all(copies, 'y', 0, 0, tiled=True)]
    ppermute x1, waiting for transfers between devices: 5.68 us -> 8.49 us  [on_device(): first_far = lax.ppermute(first, AXES, mirror)]
    unnamed x26 -> x28, local copies, waits for them, and re-layouts: 4.04 us -> 3.7 us
  transfers between devices with their start and end apart: 11 -> 11, of which waited for: 5 -> 5; matrix products, arithmetic and copies ran while one was open for 1% -> 0% of each run, Pallas kernels for 22% -> 18%
where the time goes in v7:
time: 127 us; the launch traced here: 126 us
  starting transfers between devices  56.2 us (44%)
  waiting for transfers between devices  28.2 us (22%)
  Pallas kernels  26.1 us (21%)
  blocking collectives  11.5 us (9%)
  local copies, waits for them, and re-layouts  3.8 us (3%)
    pallas_call x7, Pallas kernels, call(): pl.pallas_call(kernel, out_shape=[jax.ShapeDtypeStruct(shape, BF16) for s...  26.1 us
    ppermute x2, starting transfers between devices, on_device(): lax.ppermute(kv, AXES, links)  15.4 us
    ppermute x3, starting transfers between devices, swapped(): return lax.ppermute(array, AXES, other_core)  13.9 us
    all_to_all x1, blocking collectives, on_device(): parts = lax.all_to_all(parts, ('y', 'c'), 0, 0, tiled=True)  11.5 us
    all_to_all x2, starting transfers between devices, over_y(): return lax.all_to_all(copies, 'y', 0, 0, tiled=True)  8.8 us
    ppermute x1, waiting for transfers between devices, on_device(): first_far = lax.ppermute(first, AXES, mirror)  8.49 us
    ppermute x1, waiting for transfers between devices, on_device(): rest_far = lax.ppermute(rest, AXES, mirror)  7.93 us
    ppermute x1, waiting for transfers between devices, on_device(): w_mir = lax.ppermute(w_own, AXES, mirror)  5.79 us
  transfers between devices with their start and end apart: 11, of which 5 were waited for; matrix products, arithmetic and copies ran while one was open for 0% of the time, Pallas kernels for 18%

profile of v7, /device:TPU:1, one launch (start us, length us, event | category | flops | bytes accessed | tf_op | source)
XLA Modules:
  0.0 126.1 jit_solution(10717574426534860793)
XLA Ops:
  0.0 2.5 %shard_map.64 = bf16[4,1552,128]{2,1,0:T(8,128)(2,1)} custom-call(bf16[128,1024]{1,0:T(8,128)(2,1)} %points_at.1, s32[1,128]{1,0:T(1,128)} %order_at.1, s32[1,128]{1,0:T(1,128)} %bitcast.15, bf16[2,64,1024]{2,1,0:T(8,128)(2,1)} %w_at.1), custom_call_target="tpu_custom_call" | custom-call | flops 1320000000 | tf_op jit(solution)/shard_map/pallas_call | solution.py:270
  2.5 0.0 copy-start.10
  2.6 0.0 copy-start.1
  2.6 5.2 %all-to-all-start = ((bf16[4,1552,128]{2,1,0:T(8,128)(2,1)}), bf16[4,1552,128]{2,1,0:T(8,128)(2,1)S(1)}, u32[]{:S(2)}, u32[]{:S(2)}) async-start(bf16[4,1552,128]{2,1,0:T(8,128)(2,1)} %shard_map.64), calls=%async_computation | async-start | bytes 3178496 | tf_op jit(solution)/shard_map/all_to_all | solution.py:305
  7.7 0.0 copy-start.7
  7.8 0.1 slice_bitcast_fusion
  7.9 4.4 %collective-permute-start = (bf16[256,1024]{1,0:T(8,128)(2,1)S(1)}, bf16[256,1024]{1,0:T(8,128)(2,1)S(1)}, u32[]{:S(2)}, u32[]{:S(2)}) collective-permute-start(bf16[256,1024]{1,0:T(8,128)(2,1)S(1)} %pad_maximum_fusion), channel_id=1, source_target_pairs={{0,24},{1,25},{2,26},{3,27},{4,28},{5,29},{6,30},{7,31},{8,16},{9,... | collective-permute-start | bytes 1572872 | tf_op jit(solution)/shard_map/ppermute | solution.py:321
  12.3 8.5 %collective-permute-done.mirrored.rest = bf16[256,1024]{1,0:T(8,128)(2,1)S(1)} collective-permute-done((bf16[256,1024]{1,0:T(8,128)(2,1)S(1)}, bf16[256,1024]{1,0:T(8,128)(2,1)S(1)}, u32[]{:S(2)}, u32[]{:S(2)}) %collective-permute-start) | collective-permute-done | bytes 524320 | tf_op jit(solution)/shard_map/ppermute | solution.py:321
  20.7 2.2 %all-to-all-done.near = bf16[4,1552,128]{2,1,0:T(8,128)(2,1)S(1)} async-done(((bf16[4,1552,128]{2,1,0:T(8,128)(2,1)}), bf16[4,1552,128]{2,1,0:T(8,128)(2,1)S(1)}, u32[]{:S(2)}, u32[]{:S(2)}) %all-to-all-start) | async-done | bytes 1589280 | tf_op jit(solution)/shard_map/all_to_all | solution.py:305
  22.9 8.5 %collective-permute-start.1 = (bf16[4,1552,128]{2,1,0:T(8,128)(2,1)S(1)}, bf16[4,1552,128]{2,1,0:T(8,128)(2,1)S(1)}, u32[]{:S(2)}, u32[]{:S(2)}) collective-permute-start(bf16[4,1552,128]{2,1,0:T(8,128)(2,1)S(1)} %all-to-all-done.near), channel_id=1, source_target_pairs={{0,1},{1,0},{2,3},{3,2},{4,5},{5,4},{6,7},{7,6},{8,9},{9,8},{10,11... | collective-permute-start | bytes 4767752 | tf_op jit(solution)/shard_map/ppermute | solution.py:308
  31.5 4.4 %collective-permute-start.2 = (bf16[4,8,64,128]{3,2,1,0:T(8,128)(2,1)S(1)}, bf16[4,8,64,128]{3,2,1,0:T(8,128)(2,1)S(1)}, u32[]{:S(2)}, u32[]{:S(2)}) collective-permute-start(bf16[4,8,64,128]{3,2,1,0:T(8,128)(2,1)S(1)} %bitcast.14), channel_id=1, source_target_pairs={{0,24},{1,25},{2,26},{3,27},{4,28},{5,29},{6,30},{7,31},{8,16},{9,... | collective-permute-start | bytes 1572872 | tf_op jit(solution)/shard_map/ppermute | solution.py:330
  35.9 6.4 %shard_map.65 = bf16[4,1024,128]{2,1,0:T(8,128)(2,1)} custom-call(f32[2,1024]{1,0:T(2,128)S(1)} %copy-done.7, bf16[4,1552,128]{2,1,0:T(8,128)(2,1)S(1)} %all-to-all-done.near, bf16[4,1552,128]{2,1,0:T(8,128)(2,1)S(1)} %collective-permute-done.1.far, bf16[2,192,1024]{2,1,0:T(8,128)(2,1)S(1)} %bitcast.13, bf16[256,1024]{1,0:T(8,128)(2,1)S(1)} %collective-permute-done.mirrored.rest), custom_call_target="tpu_custom_call" | custom-call | flops 8800000000 | tf_op jit(solution)/shard_map/pallas_call | solution.py:270
  42.4 5.8 %collective-permute-done.2.w_mir = bf16[4,8,64,128]{3,2,1,0:T(8,128)(2,1)S(1)} collective-permute-done((bf16[4,8,64,128]{3,2,1,0:T(8,128)(2,1)S(1)}, bf16[4,8,64,128]{3,2,1,0:T(8,128)(2,1)S(1)}, u32[]{:S(2)}, u32[]{:S(2)}) %collective-permute-start.2) | collective-permute-done | bytes 524320 | tf_op jit(solution)/shard_map/ppermute | solution.py:330
  48.2 0.8 copy-done.11
  49.0 3.6 %all-to-all-start.1 = ((bf16[4,1024,128]{2,1,0:T(8,128)(2,1)}), bf16[4,1024,128]{2,1,0:T(8,128)(2,1)S(1)}, u32[]{:S(2)}, u32[]{:S(2)}) async-start(bf16[4,1024,128]{2,1,0:T(8,128)(2,1)} %shard_map.65), calls=%async_computation.1 | async-start | bytes 2097152 | tf_op jit(solution)/shard_map/all_to_all | solution.py:305
  52.6 2.7 %collective-permute-start.3 = (bf16[4,8,64,128]{3,2,1,0:T(8,128)(2,1)S(1)}, bf16[4,8,64,128]{3,2,1,0:T(8,128)(2,1)S(1)}, u32[]{:S(2)}, u32[]{:S(2)}) collective-permute-start(bf16[4,8,64,128]{3,2,1,0:T(8,128)(2,1)S(1)} %copy-done.12), channel_id=1, source_target_pairs={{0,1},{1,0},{2,3},{3,2},{4,5},{5,4},{6,7},{7,6},{8,9},{9,8},{10,11... | collective-permute-start | bytes 1572872 | tf_op jit(solution)/shard_map/ppermute | solution.py:308
  55.4 4.4 %collective-permute-start.4 = (bf16[192,1024]{1,0:T(8,128)(2,1)S(1)}, bf16[192,1024]{1,0:T(8,128)(2,1)S(1)}, u32[]{:S(2)}, u32[]{:S(2)}) collective-permute-start(bf16[192,1024]{1,0:T(8,128)(2,1)S(1)} %get-tuple-element.26), channel_id=1, source_target_pairs={{0,24},{1,25},{2,26},{3,27},{4,28},{5,29},{6,30},{7,31},{8,16},{9,... | collective-permute-start | bytes 1179656 | tf_op jit(solution)/shard_map/ppermute | solution.py:348
  59.8 1.5 %shard_map.66.ready = bf16[8,128,1024]{2,1,0:T(8,128)(2,1)} custom-call(bf16[64,1024]{1,0:T(8,128)(2,1)S(1)} %slice_bitcast_fusion.2.own, bf16[256,1024]{1,0:T(8,128)(2,1)S(1)} %collective-permute-done.mirrored.rest, bf16[4,8,64,128]{3,2,1,0:T(8,128)(2,1)S(1)} %collective-permute-done.3.ready.w_mir_far), custom_call_target="tpu_custom_call" | custom-call | flops 1100000000 | tf_op jit(solution)/shard_map/pallas_call | solution.py:270
  61.3 7.9 %collective-permute-done.4.mirrored_at = bf16[192,1024]{1,0:T(8,128)(2,1)S(1)} collective-permute-done((bf16[192,1024]{1,0:T(8,128)(2,1)S(1)}, bf16[192,1024]{1,0:T(8,128)(2,1)S(1)}, u32[]{:S(2)}, u32[]{:S(2)}) %collective-permute-start.4) | collective-permute-done | bytes 393248 | tf_op jit(solution)/shard_map/ppermute | solution.py:348
  69.2 2.7 %collective-permute-start.5 = (bf16[4,1024,128]{2,1,0:T(8,128)(2,1)S(1)}, bf16[4,1024,128]{2,1,0:T(8,128)(2,1)}, u32[]{:S(2)}, u32[]{:S(2)}) collective-permute-start(bf16[4,1024,128]{2,1,0:T(8,128)(2,1)S(1)} %all-to-all-done.1.o_near), channel_id=1, source_target_pairs={{0,1},{1,0},{2,3},{3,2},{4,5},{5,4},{6,7},{7,6},{8,9},{9,8},{10,11... | collective-permute-start | bytes 3145736 | tf_op jit(solution)/shard_map/ppermute | solution.py:308
  71.9 4.9 %all-to-all-start.2 = ((bf16[8,128,1024]{2,1,0:T(8,128)(2,1)}), bf16[8,128,1024]{2,1,0:T(8,128)(2,1)S(1)}, u32[]{:S(2)}, u32[]{:S(2)}) async-start(bf16[8,128,1024]{2,1,0:T(8,128)(2,1)} %shard_map.66.ready), calls=%async_computation.2 | async-start | bytes 4194304 | tf_op jit(solution)/shard_map/all_to_all | solution.py:358
  76.8 10.1 %shard_map.67 = (bf16[2,512,128]{2,1,0:T(8,128)(2,1)}, bf16[1040,128]{1,0:T(8,128)(2,1)}, bf16[1040,128]{1,0:T(8,128)(2,1)}, bf16[128,1024]{1,0:T(8,128)(2,1)}) custom-call(f32[2,1024]{1,0:T(2,128)} %gain.3, bf16[4,1024,128]{2,1,0:T(8,128)(2,1)} %copy-done.9, bf16[4,1024,128]{2,1,0:T(8,128)(2,1)} %collective-permute-done.5.o_far, ...), custom_call_target="tpu_custom_call" | custom-call | flops 8800000000 | tf_op jit(solution)/shard_map/pallas_call | solution.py:270
  86.9 2.3 %collective-permute-start.7 = (bf16[1040,128]{1,0:T(8,128)(2,1)}, bf16[1040,128]{1,0:T(8,128)(2,1)S(1)}, u32[]{:S(2)}, u32[]{:S(2)}) collective-permute-start(bf16[1040,128]{1,0:T(8,128)(2,1)} %get-tuple-element.33.refs_1_), channel_id=1, source_target_pairs={{0,8},{1,9},{2,10},{3,11},{4,12},{5,13},{6,14},{7,15},{8,0},{9,1},... | collective-permute-start | bytes 798728 | tf_op jit(solution)/shard_map/ppermute | solution.py:378
  89.2 13.2 %collective-permute-start.6 = (bf16[1040,128]{1,0:T(8,128)(2,1)}, bf16[1040,128]{1,0:T(8,128)(2,1)S(1)}, u32[]{:S(2)}, u32[]{:S(2)}) collective-permute-start(bf16[1040,128]{1,0:T(8,128)(2,1)} %get-tuple-element.32.refs_1_), channel_id=1, source_target_pairs={{0,504},{1,505},{2,506},{3,507},{4,508},{5,509},{6,510},{7,511},{8... | collective-permute-start | bytes 798728 | tf_op jit(solution)/shard_map/ppermute | solution.py:378
  102.4 0.9 copy-done.2
  103.4 0.9 copy-done.3
  104.3 2.2 %shard_map.68.refs_3_ = bf16[4,128,128]{2,1,0:T(8,128)(2,1)S(1)} custom-call(bf16[2,512,128]{2,1,0:T(8,128)(2,1)S(1)} %copy-done.3, bf16[1040,128]{1,0:T(8,128)(2,1)S(1)} %copy-done.2, bf16[1040,128]{1,0:T(8,128)(2,1)S(1)} %collective-permute-done.7.refs_2_), custom_call_target="tpu_custom_call" | custom-call | tf_op jit(solution)/shard_map/pallas_call | solution.py:270
  106.5 3.7 %collective-permute-done.6.refs_2_ = bf16[1040,128]{1,0:T(8,128)(2,1)S(1)} collective-permute-done((bf16[1040,128]{1,0:T(8,128)(2,1)}, bf16[1040,128]{1,0:T(8,128)(2,1)S(1)}, u32[]{:S(2)}, u32[]{:S(2)}) %collective-permute-start.6) | collective-permute-done | bytes 266272 | tf_op jit(solution)/shard_map/ppermute | solution.py:378
  110.2 0.9 copy-done.6
  111.2 2.2 %shard_map.69 = bf16[8,128,128]{2,1,0:T(8,128)(2,1)S(1)} custom-call(bf16[2,512,128]{2,1,0:T(8,128)(2,1)S(1)} %copy-done.3, bf16[1040,128]{1,0:T(8,128)(2,1)S(1)} %copy-done.6, bf16[1040,128]{1,0:T(8,128)(2,1)S(1)} %collective-permute-done.6.refs_2_, bf16[4,128,128]{2,1,0:T(8,128)(2,1)S(1)} %shard_map.68.refs_3_), custom_call_target="tpu_custom_call" | custom-call | flops 3300000000 | tf_op jit(solution)/shard_map/pallas_call | solution.py:270
  113.4 11.5 %all_to_all.20.parts = bf16[8,128,128]{2,1,0:T(8,128)(2,1)S(1)} all-to-all(bf16[8,128,128]{2,1,0:T(8,128)(2,1)S(1)} %shard_map.69), channel_id=1, replica_groups=mesh['z'=16,'xl'=2,'xh'=2,'y'=4,'c'=2] {'y','c'}, dimensions={0} | all-to-all | bytes 524288 | tf_op jit(solution)/shard_map/all_to_all | solution.py:395
  124.9 1.2 shard_map.70
  (30 shorter events, 0.1 us)
Async XLA Ops:
  2.5 5.2 %copy-start.10 = (bf16[2,64,1024]{2,1,0:T(8,128)(2,1)S(1)}, bf16[2,64,1024]{2,1,0:T(8,128)(2,1)}, u32[]{:S(2)}) copy-start(bf16[2,64,1024]{2,1,0:T(8,128)(2,1)} %w_at.1) | copy-start | bytes 786436
  2.6 5.2 %copy-start.1 = (bf16[2,1024,192]{1,2,0:T(8,128)(2,1)S(1)}, bf16[2,1024,192]{1,2,0:T(8,128)(2,1)}, u32[]{:S(2)}) copy-start(bf16[2,1024,192]{1,2,0:T(8,128)(2,1)} %param.10) | copy-start | bytes 2359300
  2.6 20.4 %all-to-all-start = ((bf16[4,1552,128]{2,1,0:T(8,128)(2,1)}), bf16[4,1552,128]{2,1,0:T(8,128)(2,1)S(1)}, u32[]{:S(2)}, u32[]{:S(2)}) async-start(bf16[4,1552,128]{2,1,0:T(8,128)(2,1)} %shard_map.64), calls=%async_computation | async-start | bytes 3178496 | tf_op jit(solution)/shard_map/all_to_all | solution.py:305
  7.7 28.2 %copy-start.7 = (f32[2,1024]{1,0:T(2,128)S(1)}, f32[2,1024]{1,0:T(2,128)}, u32[]{:S(2)}) copy-start(f32[2,1024]{1,0:T(2,128)} %gain.3) | copy-start | bytes 24580
  7.9 12.9 %collective-permute-start = (bf16[256,1024]{1,0:T(8,128)(2,1)S(1)}, bf16[256,1024]{1,0:T(8,128)(2,1)S(1)}, u32[]{:S(2)}, u32[]{:S(2)}) collective-permute-start(bf16[256,1024]{1,0:T(8,128)(2,1)S(1)} %pad_maximum_fusion), channel_id=1, source_target_pairs={{0,24},{1,25},{2,26},{3,27},{4,28},{5,29},{6,30},{7,31},{8,16},{9,... | collective-permute-start | bytes 1572872 | tf_op jit(solution)/shard_map/ppermute | solution.py:321
  22.9 19.4 %copy-start = (bf16[4,1552,128]{2,1,0:T(8,128)(2,1)}, bf16[4,1552,128]{2,1,0:T(8,128)(2,1)S(1)}, u32[]{:S(2)}) copy-start(bf16[4,1552,128]{2,1,0:T(8,128)(2,1)S(1)} %all-to-all-done.near) | copy-start | bytes 4767748
  22.9 13.0 %collective-permute-start.1 = (bf16[4,1552,128]{2,1,0:T(8,128)(2,1)S(1)}, bf16[4,1552,128]{2,1,0:T(8,128)(2,1)S(1)}, u32[]{:S(2)}, u32[]{:S(2)}) collective-permute-start(bf16[4,1552,128]{2,1,0:T(8,128)(2,1)S(1)} %all-to-all-done.near), channel_id=1, source_target_pairs={{0,1},{1,0},{2,3},{3,2},{4,5},{5,4},{6,7},{7,6},{8,9},{9,8},{10,11... | collective-permute-start | bytes 4767752 | tf_op jit(solution)/shard_map/ppermute | solution.py:308
  31.5 16.6 %collective-permute-start.2 = (bf16[4,8,64,128]{3,2,1,0:T(8,128)(2,1)S(1)}, bf16[4,8,64,128]{3,2,1,0:T(8,128)(2,1)S(1)}, u32[]{:S(2)}, u32[]{:S(2)}) collective-permute-start(bf16[4,8,64,128]{3,2,1,0:T(8,128)(2,1)S(1)} %bitcast.14), channel_id=1, source_target_pairs={{0,24},{1,25},{2,26},{3,27},{4,28},{5,29},{6,30},{7,31},{8,16},{9,... | collective-permute-start | bytes 1572872 | tf_op jit(solution)/shard_map/ppermute | solution.py:330
  35.9 6.4 %copy-start.4 = (bf16[4,1552,128]{2,1,0:T(8,128)(2,1)}, bf16[4,1552,128]{2,1,0:T(8,128)(2,1)S(1)}, u32[]{:S(2)}) copy-start(bf16[4,1552,128]{2,1,0:T(8,128)(2,1)S(1)} %collective-permute-done.1.far) | copy-start | bytes 4767748
  48.2 0.8 copy-start.11
  49.0 3.7 %copy-start.12 = (bf16[4,8,64,128]{3,2,1,0:T(8,128)(2,1)S(1)}, bf16[4,8,64,128]{3,2,1,0:T(8,128)(2,1)}, u32[]{:S(2)}) copy-start(bf16[4,8,64,128]{3,2,1,0:T(8,128)(2,1)} %copy-done.11) | copy-start | bytes 1572868
  49.0 20.2 %all-to-all-start.1 = ((bf16[4,1024,128]{2,1,0:T(8,128)(2,1)}), bf16[4,1024,128]{2,1,0:T(8,128)(2,1)S(1)}, u32[]{:S(2)}, u32[]{:S(2)}) async-start(bf16[4,1024,128]{2,1,0:T(8,128)(2,1)} %shard_map.65), calls=%async_computation.1 | async-start | bytes 2097152 | tf_op jit(solution)/shard_map/all_to_all | solution.py:305
  52.6 7.1 %collective-permute-start.3 = (bf16[4,8,64,128]{3,2,1,0:T(8,128)(2,1)S(1)}, bf16[4,8,64,128]{3,2,1,0:T(8,128)(2,1)S(1)}, u32[]{:S(2)}, u32[]{:S(2)}) collective-permute-start(bf16[4,8,64,128]{3,2,1,0:T(8,128)(2,1)S(1)} %copy-done.12), channel_id=1, source_target_pairs={{0,1},{1,0},{2,3},{3,2},{4,5},{5,4},{6,7},{7,6},{8,9},{9,8},{10,11... | collective-permute-start | bytes 1572872 | tf_op jit(solution)/shard_map/ppermute | solution.py:308
  55.4 13.8 %collective-permute-start.4 = (bf16[192,1024]{1,0:T(8,128)(2,1)S(1)}, bf16[192,1024]{1,0:T(8,128)(2,1)S(1)}, u32[]{:S(2)}, u32[]{:S(2)}) collective-permute-start(bf16[192,1024]{1,0:T(8,128)(2,1)S(1)} %get-tuple-element.26), channel_id=1, source_target_pairs={{0,24},{1,25},{2,26},{3,27},{4,28},{5,29},{6,30},{7,31},{8,16},{9,... | collective-permute-start | bytes 1179656 | tf_op jit(solution)/shard_map/ppermute | solution.py:348
  59.8 1.5 %copy-start.5 = (bf16[4,8,64,128]{3,2,1,0:T(8,128)(2,1)}, bf16[4,8,64,128]{3,2,1,0:T(8,128)(2,1)S(1)}, u32[]{:S(2)}) copy-start(bf16[4,8,64,128]{3,2,1,0:T(8,128)(2,1)S(1)} %collective-permute-done.3.ready.w_mir_far) | copy-start | bytes 1572868
  69.2 2.7 %copy-start.13 = (bf16[192,1024]{1,0:T(8,128)(2,1)}, bf16[192,1024]{1,0:T(8,128)(2,1)S(1)}, u32[]{:S(2)}) copy-start(bf16[192,1024]{1,0:T(8,128)(2,1)S(1)} %collective-permute-done.4.mirrored_at) | copy-start | bytes 1179652
  69.2 2.7 %copy-start.9 = (bf16[4,1024,128]{2,1,0:T(8,128)(2,1)}, bf16[4,1024,128]{2,1,0:T(8,128)(2,1)S(1)}, u32[]{:S(2)}) copy-start(bf16[4,1024,128]{2,1,0:T(8,128)(2,1)S(1)} %all-to-all-done.1.o_near) | copy-start | bytes 3145732
  69.2 7.6 %collective-permute-start.5 = (bf16[4,1024,128]{2,1,0:T(8,128)(2,1)S(1)}, bf16[4,1024,128]{2,1,0:T(8,128)(2,1)}, u32[]{:S(2)}, u32[]{:S(2)}) collective-permute-start(bf16[4,1024,128]{2,1,0:T(8,128)(2,1)S(1)} %all-to-all-done.1.o_near), channel_id=1, source_target_pairs={{0,1},{1,0},{2,3},{3,2},{4,5},{5,4},{6,7},{7,6},{8,9},{9,8},{10,11... | collective-permute-start | bytes 3145736 | tf_op jit(solution)/shard_map/ppermute | solution.py:308
  71.9 41.5 %all-to-all-start.2 = ((bf16[8,128,1024]{2,1,0:T(8,128)(2,1)}), bf16[8,128,1024]{2,1,0:T(8,128)(2,1)S(1)}, u32[]{:S(2)}, u32[]{:S(2)}) async-start(bf16[8,128,1024]{2,1,0:T(8,128)(2,1)} %shard_map.66.ready), calls=%async_computation.2 | async-start | bytes 4194304 | tf_op jit(solution)/shard_map/all_to_all | solution.py:358
  86.9 15.5 %collective-permute-start.7 = (bf16[1040,128]{1,0:T(8,128)(2,1)}, bf16[1040,128]{1,0:T(8,128)(2,1)S(1)}, u32[]{:S(2)}, u32[]{:S(2)}) collective-permute-start(bf16[1040,128]{1,0:T(8,128)(2,1)} %get-tuple-element.33.refs_1_), channel_id=1, source_target_pairs={{0,8},{1,9},{2,10},{3,11},{4,12},{5,13},{6,14},{7,15},{8,0},{9,1},... | collective-permute-start | bytes 798728 | tf_op jit(solution)/shard_map/ppermute | solution.py:378
  89.2 21.0 %collective-permute-start.6 = (bf16[1040,128]{1,0:T(8,128)(2,1)}, bf16[1040,128]{1,0:T(8,128)(2,1)S(1)}, u32[]{:S(2)}, u32[]{:S(2)}) collective-permute-start(bf16[1040,128]{1,0:T(8,128)(2,1)} %get-tuple-element.32.refs_1_), channel_id=1, source_target_pairs={{0,504},{1,505},{2,506},{3,507},{4,508},{5,509},{6,510},{7,511},{8... | collective-permute-start | bytes 798728 | tf_op jit(solution)/shard_map/ppermute | solution.py:378
  102.4 1.0 copy-start.2
  103.4 0.9 copy-start.3
  110.2 1.0 copy-start.6
  111.2 13.7 %copy-start.8 = (bf16[128,1024]{1,0:T(8,128)(2,1)S(1)}, bf16[128,1024]{1,0:T(8,128)(2,1)}, u32[]{:S(2)}) copy-start(bf16[128,1024]{1,0:T(8,128)(2,1)} %get-tuple-element.36.stream) | copy-start | bytes 786436

commit v8 on v7

--- a/solution.py
+++ b/solution.py
@@ -320,14 +320,14 @@
         first = jnp.concatenate([w_turned[0], w_out[1]], axis=0)
         first_far = lax.ppermute(first, AXES, mirror)
         near = over_y(copies)
-        near, first_far = lax.optimization_barrier((near, first_far))
+        near, first_far, rest = lax.optimization_barrier((near, first_far, w_turned[1]))
+        rest_far = lax.ppermute(rest, AXES, mirror)
         far = swapped(near)
 
         def out_weights(array):
             return array[:, EXT:].reshape(4, BLOCKS, HEAD_DIM, LANES)
 
         w_own = out_weights(near)
-        w_mir = lax.ppermute(w_own, AXES, mirror)
         projection = [((3 * HEAD_DIM, D), BF16)] * 2
         (o_copies,) = call(
             first_kernel,
@@ -343,13 +343,12 @@
             ],
             ln_gain, near, far, w_turned, first_far, megabytes=16,
         )
-        o_copies, w_mir = lax.optimization_barrier((o_copies, w_mir))
-        o_copies, rest = lax.optimization_barrier((o_copies, w_turned[1]))
-        rest_far = lax.ppermute(rest, AXES, mirror)
+        o_copies, rest_far, w_own = lax.optimization_barrier((o_copies, rest_far, w_own))
+        w_mir = lax.ppermute(w_own, AXES, mirror)
         w_mir_far = swapped(w_mir)
         o_near = over_y(o_copies)
         (shares,) = call(
-            relay_kernel, 1, [(8, ROWS, D)], [], w_out[1], first_far, late=(w_mir_far,), megabytes=4
+            relay_kernel, 1, [(8, ROWS, D)], [], w_out[1], first_far, late=(rest_far,), megabytes=4
         )
         o_near, w_mir_far, rest_far, shares = lax.optimization_barrier(
             (o_near, w_mir_far, rest_far, shares)

time: 127 us -> 124 us (0.976)
  waiting for transfers between devices: 28.2 us -> 25.1 us
    ppermute x1, waiting for transfers between devices: 7.93 us -> 2.98 us  [on_device(): rest_far = lax.ppermute(rest, AXES, mirror)]
    ppermute x1, waiting for transfers between devices: 5.79 us -> 8.04 us  [on_device(): w_mir = lax.ppermute(w_own, AXES, mirror)]
    ppermute x3, starting transfers between devices: 13.9 us -> 16 us  [swapped(): return lax.ppermute(array, AXES, other_core)]
    ppermute x2, starting transfers between devices: 15.4 us -> 14.1 us  [on_device(): lax.ppermute(kv, AXES, links)]
    all_to_all x1, starting transfers between devices: 4.87 us -> 3.56 us  [on_device(): w_last = lax.all_to_all(shares, ('y', 'c'), 0, 0, tiled=True).reshape(D, D)]
  transfers between devices with their start and end apart: 11 -> 11, of which waited for: 5 -> 6; matrix products, arithmetic and copies ran while one was open for 0% -> 1% of each run, Pallas kernels for 18% -> 18%
where the time goes in v8:
time: 124 us; the launch traced here: 123 us
  starting transfers between devices  55.6 us (45%)
  Pallas kernels  26.1 us (21%)
  waiting for transfers between devices  25.1 us (20%)
  blocking collectives  11.9 us (10%)
  local copies, waits for them, and re-layouts  4.55 us (4%)
    pallas_call x7, Pallas kernels, call(): pl.pallas_call(kernel, out_shape=[jax.ShapeDtypeStruct(shape, BF16) for s...  26.1 us
    ppermute x3, starting transfers between devices, swapped(): return lax.ppermute(array, AXES, other_core)  16 us
    ppermute x2, starting transfers between devices, on_device(): lax.ppermute(kv, AXES, links)  14.1 us
    all_to_all x1, blocking collectives, on_device(): parts = lax.all_to_all(parts, ('y', 'c'), 0, 0, tiled=True)  11.9 us
    all_to_all x2, starting transfers between devices, over_y(): return lax.all_to_all(copies, 'y', 0, 0, tiled=True)  8.68 us
    ppermute x1, waiting for transfers between devices, on_device(): first_far = lax.ppermute(first, AXES, mirror)  8.49 us
    ppermute x1, waiting for transfers between devices, on_device(): w_mir = lax.ppermute(w_own, AXES, mirror)  8.04 us
    ppermute x1, starting transfers between devices, on_device(): w_mir = lax.ppermute(w_own, AXES, mirror)  4.51 us
  transfers between devices with their start and end apart: 11, of which 6 were waited for; matrix products, arithmetic and copies ran while one was open for 1% of the time, Pallas kernels for 18%

profile of v8, /device:TPU:1, one launch (start us, length us, event | category | flops | bytes accessed | tf_op | source)
XLA Modules:
  0.0 123.5 jit_solution(13849539350441854962)
XLA Ops:
  0.0 2.5 %shard_map.64 = bf16[4,1552,128]{2,1,0:T(8,128)(2,1)} custom-call(bf16[128,1024]{1,0:T(8,128)(2,1)} %points_at.1, s32[1,128]{1,0:T(1,128)} %order_at.1, s32[1,128]{1,0:T(1,128)} %bitcast.14, bf16[2,64,1024]{2,1,0:T(8,128)(2,1)} %w_at.1), custom_call_target="tpu_custom_call" | custom-call | flops 1320000000 | tf_op jit(solution)/shard_map/pallas_call | solution.py:270
  2.6 5.2 %all-to-all-start = ((bf16[4,1552,128]{2,1,0:T(8,128)(2,1)}), bf16[4,1552,128]{2,1,0:T(8,128)(2,1)S(1)}, u32[]{:S(2)}, u32[]{:S(2)}) async-start(bf16[4,1552,128]{2,1,0:T(8,128)(2,1)} %shard_map.64), calls=%async_computation | async-start | bytes 3178496 | tf_op jit(solution)/shard_map/all_to_all | solution.py:305
  7.7 0.0 copy-start.8
  7.8 0.1 slice_bitcast_fusion
  7.9 4.4 %collective-permute-start = (bf16[256,1024]{1,0:T(8,128)(2,1)S(1)}, bf16[256,1024]{1,0:T(8,128)(2,1)S(1)}, u32[]{:S(2)}, u32[]{:S(2)}) collective-permute-start(bf16[256,1024]{1,0:T(8,128)(2,1)S(1)} %pad_maximum_fusion), channel_id=1, source_target_pairs={{0,24},{1,25},{2,26},{3,27},{4,28},{5,29},{6,30},{7,31},{8,16},{9,... | collective-permute-start | bytes 1572872 | tf_op jit(solution)/shard_map/ppermute | solution.py:321
  12.3 8.5 %collective-permute-done.mirrored.rest = bf16[256,1024]{1,0:T(8,128)(2,1)S(1)} collective-permute-done((bf16[256,1024]{1,0:T(8,128)(2,1)S(1)}, bf16[256,1024]{1,0:T(8,128)(2,1)S(1)}, u32[]{:S(2)}, u32[]{:S(2)}) %collective-permute-start) | collective-permute-done | bytes 524320 | tf_op jit(solution)/shard_map/ppermute | solution.py:321
  20.7 2.2 %all-to-all-done.near = bf16[4,1552,128]{2,1,0:T(8,128)(2,1)S(1)} async-done(((bf16[4,1552,128]{2,1,0:T(8,128)(2,1)}), bf16[4,1552,128]{2,1,0:T(8,128)(2,1)S(1)}, u32[]{:S(2)}, u32[]{:S(2)}) %all-to-all-start) | async-done | bytes 1589280 | tf_op jit(solution)/shard_map/all_to_all | solution.py:305
  22.9 8.5 %collective-permute-start.1 = (bf16[4,1552,128]{2,1,0:T(8,128)(2,1)S(1)}, bf16[4,1552,128]{2,1,0:T(8,128)(2,1)S(1)}, u32[]{:S(2)}, u32[]{:S(2)}) collective-permute-start(bf16[4,1552,128]{2,1,0:T(8,128)(2,1)S(1)} %all-to-all-done.near), channel_id=1, source_target_pairs={{0,1},{1,0},{2,3},{3,2},{4,5},{5,4},{6,7},{7,6},{8,9},{9,8},{10,11... | collective-permute-start | bytes 4767752 | tf_op jit(solution)/shard_map/ppermute | solution.py:308
  31.5 0.9 slice.16
  32.3 4.4 %collective-permute-start.2 = (bf16[192,1024]{1,0:T(8,128)(2,1)S(1)}, bf16[192,1024]{1,0:T(8,128)(2,1)S(1)}, u32[]{:S(2)}, u32[]{:S(2)}) collective-permute-start(bf16[192,1024]{1,0:T(8,128)(2,1)S(1)} %get-tuple-element.23), channel_id=1, source_target_pairs={{0,24},{1,25},{2,26},{3,27},{4,28},{5,29},{6,30},{7,31},{8,16},{9,... | collective-permute-start | bytes 1179656 | tf_op jit(solution)/shard_map/ppermute | solution.py:324
  36.7 6.4 %shard_map.65 = bf16[4,1024,128]{2,1,0:T(8,128)(2,1)} custom-call(f32[2,1024]{1,0:T(2,128)S(1)} %copy-done.8, bf16[4,1552,128]{2,1,0:T(8,128)(2,1)S(1)} %all-to-all-done.near, bf16[4,1552,128]{2,1,0:T(8,128)(2,1)S(1)} %collective-permute-done.1.far, bf16[2,192,1024]{2,1,0:T(8,128)(2,1)S(1)} %bitcast.13, bf16[256,1024]{1,0:T(8,128)(2,1)S(1)} %collective-permute-done.mirrored.rest), custom_call_target="tpu_custom_call" | custom-call | flops 8800000000 | tf_op jit(solution)/shard_map/pallas_call | solution.py:270
  43.2 3.0 %collective-permute-done.2.ready.mirrored_at = bf16[192,1024]{1,0:T(8,128)(2,1)S(1)} collective-permute-done((bf16[192,1024]{1,0:T(8,128)(2,1)S(1)}, bf16[192,1024]{1,0:T(8,128)(2,1)S(1)}, u32[]{:S(2)}, u32[]{:S(2)}) %collective-permute-start.2) | collective-permute-done | bytes 393248 | tf_op jit(solution)/shard_map/ppermute | solution.py:324
  46.2 0.7 copy-done.5
  46.9 4.5 %collective-permute-start.3 = (bf16[4,8,64,128]{3,2,1,0:T(8,128)(2,1)}, bf16[4,8,64,128]{3,2,1,0:T(8,128)(2,1)S(1)}, u32[]{:S(2)}, u32[]{:S(2)}) collective-permute-start(bf16[4,8,64,128]{3,2,1,0:T(8,128)(2,1)} %bitcast.5), channel_id=1, source_target_pairs={{0,24},{1,25},{2,26},{3,27},{4,28},{5,29},{6,30},{7,31},{8,16},{9,... | collective-permute-start | bytes 1572872 | tf_op jit(solution)/shard_map/ppermute | solution.py:347
  51.4 3.5 %all-to-all-start.1 = ((bf16[4,1024,128]{2,1,0:T(8,128)(2,1)}), bf16[4,1024,128]{2,1,0:T(8,128)(2,1)S(1)}, u32[]{:S(2)}, u32[]{:S(2)}) async-start(bf16[4,1024,128]{2,1,0:T(8,128)(2,1)} %shard_map.65), calls=%async_computation.1 | async-start | bytes 2097152 | tf_op jit(solution)/shard_map/all_to_all | solution.py:305
  54.9 8.0 %collective-permute-done.3.w_mir = bf16[4,8,64,128]{3,2,1,0:T(8,128)(2,1)S(1)} collective-permute-done((bf16[4,8,64,128]{3,2,1,0:T(8,128)(2,1)}, bf16[4,8,64,128]{3,2,1,0:T(8,128)(2,1)S(1)}, u32[]{:S(2)}, u32[]{:S(2)}) %collective-permute-start.3) | collective-permute-done | bytes 524320 | tf_op jit(solution)/shard_map/ppermute | solution.py:347
  63.0 3.6 %collective-permute-start.4 = (bf16[4,8,64,128]{3,2,1,0:T(8,128)(2,1)S(1)}, bf16[4,8,64,128]{3,2,1,0:T(8,128)(2,1)S(1)}, u32[]{:S(2)}, u32[]{:S(2)}) collective-permute-start(bf16[4,8,64,128]{3,2,1,0:T(8,128)(2,1)S(1)} %collective-permute-done.3.w_mir), channel_id=1, source_target_pairs={{0,1},{1,0},{2,3},{3,2},{4,5},{5,4},{6,7},{7,6},{8,9},{9,8},{10,11... | collective-permute-start | bytes 1572872 | tf_op jit(solution)/shard_map/ppermute | solution.py:308
  66.6 1.5 %shard_map.66.ready = bf16[8,128,1024]{2,1,0:T(8,128)(2,1)} custom-call(bf16[64,1024]{1,0:T(8,128)(2,1)S(1)} %slice_bitcast_fusion.2.own, bf16[256,1024]{1,0:T(8,128)(2,1)S(1)} %collective-permute-done.mirrored.rest, bf16[192,1024]{1,0:T(8,128)(2,1)S(1)} %copy-done.6), custom_call_target="tpu_custom_call" | custom-call | flops 1100000000 | tf_op jit(solution)/shard_map/pallas_call | solution.py:270
  68.1 0.9 all-to-all-done.1.o_near
  69.0 3.9 %collective-permute-start.5 = (bf16[4,1024,128]{2,1,0:T(8,128)(2,1)S(1)}, bf16[4,1024,128]{2,1,0:T(8,128)(2,1)}, u32[]{:S(2)}, u32[]{:S(2)}) collective-permute-start(bf16[4,1024,128]{2,1,0:T(8,128)(2,1)S(1)} %all-to-all-done.1.o_near), channel_id=1, source_target_pairs={{0,1},{1,0},{2,3},{3,2},{4,5},{5,4},{6,7},{7,6},{8,9},{9,8},{10,11... | collective-permute-start | bytes 3145736 | tf_op jit(solution)/shard_map/ppermute | solution.py:308
  72.9 3.6 %all-to-all-start.2 = ((bf16[8,128,1024]{2,1,0:T(8,128)(2,1)}), bf16[8,128,1024]{2,1,0:T(8,128)(2,1)S(1)}, u32[]{:S(2)}, u32[]{:S(2)}) async-start(bf16[8,128,1024]{2,1,0:T(8,128)(2,1)} %shard_map.66.ready), calls=%async_computation.2 | async-start | bytes 4194304 | tf_op jit(solution)/shard_map/all_to_all | solution.py:357
  76.5 10.1 %shard_map.67 = (bf16[2,512,128]{2,1,0:T(8,128)(2,1)}, bf16[1040,128]{1,0:T(8,128)(2,1)}, bf16[1040,128]{1,0:T(8,128)(2,1)}, bf16[128,1024]{1,0:T(8,128)(2,1)}) custom-call(f32[2,1024]{1,0:T(2,128)} %gain.3, bf16[4,1024,128]{2,1,0:T(8,128)(2,1)} %copy-done.10, bf16[4,1024,128]{2,1,0:T(8,128)(2,1)} %collective-permute-done.5.o_far, ...), custom_call_target="tpu_custom_call" | custom-call | flops 8800000000 | tf_op jit(solution)/shard_map/pallas_call | solution.py:270
  86.6 1.9 %collective-permute-start.7 = (bf16[1040,128]{1,0:T(8,128)(2,1)}, bf16[1040,128]{1,0:T(8,128)(2,1)S(1)}, u32[]{:S(2)}, u32[]{:S(2)}) collective-permute-start(bf16[1040,128]{1,0:T(8,128)(2,1)} %get-tuple-element.33.refs_1_), channel_id=1, source_target_pairs={{0,8},{1,9},{2,10},{3,11},{4,12},{5,13},{6,14},{7,15},{8,0},{9,1},... | collective-permute-start | bytes 798728 | tf_op jit(solution)/shard_map/ppermute | solution.py:377
  88.6 12.1 %collective-permute-start.6 = (bf16[1040,128]{1,0:T(8,128)(2,1)}, bf16[1040,128]{1,0:T(8,128)(2,1)S(1)}, u32[]{:S(2)}, u32[]{:S(2)}) collective-permute-start(bf16[1040,128]{1,0:T(8,128)(2,1)} %get-tuple-element.32.refs_1_), channel_id=1, source_target_pairs={{0,504},{1,505},{2,506},{3,507},{4,508},{5,509},{6,510},{7,511},{8... | collective-permute-start | bytes 798728 | tf_op jit(solution)/shard_map/ppermute | solution.py:377
  100.7 0.9 copy-done.2
  101.7 0.9 copy-done.3
  102.6 2.2 %shard_map.68.refs_3_ = bf16[4,128,128]{2,1,0:T(8,128)(2,1)S(1)} custom-call(bf16[2,512,128]{2,1,0:T(8,128)(2,1)S(1)} %copy-done.3, bf16[1040,128]{1,0:T(8,128)(2,1)S(1)} %copy-done.2, bf16[1040,128]{1,0:T(8,128)(2,1)S(1)} %collective-permute-done.7.refs_2_), custom_call_target="tpu_custom_call" | custom-call | tf_op jit(solution)/shard_map/pallas_call | solution.py:270
  104.8 2.5 %collective-permute-done.6.refs_2_ = bf16[1040,128]{1,0:T(8,128)(2,1)S(1)} collective-permute-done((bf16[1040,128]{1,0:T(8,128)(2,1)}, bf16[1040,128]{1,0:T(8,128)(2,1)S(1)}, u32[]{:S(2)}, u32[]{:S(2)}) %collective-permute-start.6) | collective-permute-done | bytes 266272 | tf_op jit(solution)/shard_map/ppermute | solution.py:377
  107.3 0.9 copy-done.7
  108.2 2.2 %shard_map.69 = bf16[8,128,128]{2,1,0:T(8,128)(2,1)S(1)} custom-call(bf16[2,512,128]{2,1,0:T(8,128)(2,1)S(1)} %copy-done.3, bf16[1040,128]{1,0:T(8,128)(2,1)S(1)} %copy-done.7, bf16[1040,128]{1,0:T(8,128)(2,1)S(1)} %collective-permute-done.6.refs_2_, bf16[4,128,128]{2,1,0:T(8,128)(2,1)S(1)} %shard_map.68.refs_3_), custom_call_target="tpu_custom_call" | custom-call | flops 3300000000 | tf_op jit(solution)/shard_map/pallas_call | solution.py:270
  110.4 11.9 %all_to_all.20.parts = bf16[8,128,128]{2,1,0:T(8,128)(2,1)S(1)} all-to-all(bf16[8,128,128]{2,1,0:T(8,128)(2,1)S(1)} %shard_map.69), channel_id=1, replica_groups=mesh['z'=16,'xl'=2,'xh'=2,'y'=4,'c'=2] {'y','c'}, dimensions={0} | all-to-all | bytes 524288 | tf_op jit(solution)/shard_map/all_to_all | solution.py:394
  122.3 1.2 shard_map.70
  (30 shorter events, 0.1 us)
Async XLA Ops:
  2.5 5.2 %copy-start.11 = (bf16[2,64,1024]{2,1,0:T(8,128)(2,1)S(1)}, bf16[2,64,1024]{2,1,0:T(8,128)(2,1)}, u32[]{:S(2)}) copy-start(bf16[2,64,1024]{2,1,0:T(8,128)(2,1)} %w_at.1) | copy-start | bytes 786436
  2.6 5.2 %copy-start.1 = (bf16[2,1024,192]{1,2,0:T(8,128)(2,1)S(1)}, bf16[2,1024,192]{1,2,0:T(8,128)(2,1)}, u32[]{:S(2)}) copy-start(bf16[2,1024,192]{1,2,0:T(8,128)(2,1)} %param.10) | copy-start | bytes 2359300
  2.6 20.4 %all-to-all-start = ((bf16[4,1552,128]{2,1,0:T(8,128)(2,1)}), bf16[4,1552,128]{2,1,0:T(8,128)(2,1)S(1)}, u32[]{:S(2)}, u32[]{:S(2)}) async-start(bf16[4,1552,128]{2,1,0:T(8,128)(2,1)} %shard_map.64), calls=%async_computation | async-start | bytes 3178496 | tf_op jit(solution)/shard_map/all_to_all | solution.py:305
  7.7 29.0 %copy-start.8 = (f32[2,1024]{1,0:T(2,128)S(1)}, f32[2,1024]{1,0:T(2,128)}, u32[]{:S(2)}) copy-start(f32[2,1024]{1,0:T(2,128)} %gain.3) | copy-start | bytes 24580
  7.9 12.9 %collective-permute-start = (bf16[256,1024]{1,0:T(8,128)(2,1)S(1)}, bf16[256,1024]{1,0:T(8,128)(2,1)S(1)}, u32[]{:S(2)}, u32[]{:S(2)}) collective-permute-start(bf16[256,1024]{1,0:T(8,128)(2,1)S(1)} %pad_maximum_fusion), channel_id=1, source_target_pairs={{0,24},{1,25},{2,26},{3,27},{4,28},{5,29},{6,30},{7,31},{8,16},{9,... | collective-permute-start | bytes 1572872 | tf_op jit(solution)/shard_map/ppermute | solution.py:321
  22.9 20.2 %copy-start = (bf16[4,1552,128]{2,1,0:T(8,128)(2,1)}, bf16[4,1552,128]{2,1,0:T(8,128)(2,1)S(1)}, u32[]{:S(2)}) copy-start(bf16[4,1552,128]{2,1,0:T(8,128)(2,1)S(1)} %all-to-all-done.near) | copy-start | bytes 4767748
  22.9 13.8 %collective-permute-start.1 = (bf16[4,1552,128]{2,1,0:T(8,128)(2,1)S(1)}, bf16[4,1552,128]{2,1,0:T(8,128)(2,1)S(1)}, u32[]{:S(2)}, u32[]{:S(2)}) collective-permute-start(bf16[4,1552,128]{2,1,0:T(8,128)(2,1)S(1)} %all-to-all-done.near), channel_id=1, source_target_pairs={{0,1},{1,0},{2,3},{3,2},{4,5},{5,4},{6,7},{7,6},{8,9},{9,8},{10,11... | collective-permute-start | bytes 4767752 | tf_op jit(solution)/shard_map/ppermute | solution.py:308
  32.3 13.8 %collective-permute-start.2 = (bf16[192,1024]{1,0:T(8,128)(2,1)S(1)}, bf16[192,1024]{1,0:T(8,128)(2,1)S(1)}, u32[]{:S(2)}, u32[]{:S(2)}) collective-permute-start(bf16[192,1024]{1,0:T(8,128)(2,1)S(1)} %get-tuple-element.23), channel_id=1, source_target_pairs={{0,24},{1,25},{2,26},{3,27},{4,28},{5,29},{6,30},{7,31},{8,16},{9,... | collective-permute-start | bytes 1179656 | tf_op jit(solution)/shard_map/ppermute | solution.py:324
  36.7 6.4 %copy-start.4 = (bf16[4,1552,128]{2,1,0:T(8,128)(2,1)}, bf16[4,1552,128]{2,1,0:T(8,128)(2,1)S(1)}, u32[]{:S(2)}) copy-start(bf16[4,1552,128]{2,1,0:T(8,128)(2,1)S(1)} %collective-permute-done.1.far) | copy-start | bytes 4767748
  46.2 0.7 copy-start.5
  46.9 19.7 %copy-start.6 = (bf16[192,1024]{1,0:T(8,128)(2,1)S(1)}, bf16[192,1024]{1,0:T(8,128)(2,1)}, u32[]{:S(2)}) copy-start(bf16[192,1024]{1,0:T(8,128)(2,1)} %copy-done.5) | copy-start | bytes 1179652
  46.9 16.1 %collective-permute-start.3 = (bf16[4,8,64,128]{3,2,1,0:T(8,128)(2,1)}, bf16[4,8,64,128]{3,2,1,0:T(8,128)(2,1)S(1)}, u32[]{:S(2)}, u32[]{:S(2)}) collective-permute-start(bf16[4,8,64,128]{3,2,1,0:T(8,128)(2,1)} %bitcast.5), channel_id=1, source_target_pairs={{0,24},{1,25},{2,26},{3,27},{4,28},{5,29},{6,30},{7,31},{8,16},{9,... | collective-permute-start | bytes 1572872 | tf_op jit(solution)/shard_map/ppermute | solution.py:347
  51.4 17.6 %all-to-all-start.1 = ((bf16[4,1024,128]{2,1,0:T(8,128)(2,1)}), bf16[4,1024,128]{2,1,0:T(8,128)(2,1)S(1)}, u32[]{:S(2)}, u32[]{:S(2)}) async-start(bf16[4,1024,128]{2,1,0:T(8,128)(2,1)} %shard_map.65), calls=%async_computation.1 | async-start | bytes 2097152 | tf_op jit(solution)/shard_map/all_to_all | solution.py:305
  63.0 5.1 %copy-start.12 = (bf16[4,8,64,128]{3,2,1,0:T(8,128)(2,1)}, bf16[4,8,64,128]{3,2,1,0:T(8,128)(2,1)S(1)}, u32[]{:S(2)}) copy-start(bf16[4,8,64,128]{3,2,1,0:T(8,128)(2,1)S(1)} %collective-permute-done.3.w_mir) | copy-start | bytes 1572868
  63.0 6.0 %collective-permute-start.4 = (bf16[4,8,64,128]{3,2,1,0:T(8,128)(2,1)S(1)}, bf16[4,8,64,128]{3,2,1,0:T(8,128)(2,1)S(1)}, u32[]{:S(2)}, u32[]{:S(2)}) collective-permute-start(bf16[4,8,64,128]{3,2,1,0:T(8,128)(2,1)S(1)} %collective-permute-done.3.w_mir), channel_id=1, source_target_pairs={{0,1},{1,0},{2,3},{3,2},{4,5},{5,4},{6,7},{7,6},{8,9},{9,8},{10,11... | collective-permute-start | bytes 1572872 | tf_op jit(solution)/shard_map/ppermute | solution.py:308
  69.0 3.9 %copy-start.10 = (bf16[4,1024,128]{2,1,0:T(8,128)(2,1)}, bf16[4,1024,128]{2,1,0:T(8,128)(2,1)S(1)}, u32[]{:S(2)}) copy-start(bf16[4,1024,128]{2,1,0:T(8,128)(2,1)S(1)} %all-to-all-done.1.o_near) | copy-start | bytes 3145732
  69.0 3.9 %copy-start.13 = (bf16[4,8,64,128]{3,2,1,0:T(8,128)(2,1)}, bf16[4,8,64,128]{3,2,1,0:T(8,128)(2,1)S(1)}, u32[]{:S(2)}) copy-start(bf16[4,8,64,128]{3,2,1,0:T(8,128)(2,1)S(1)} %collective-permute-done.4.w_mir_far) | copy-start | bytes 1572868
  69.0 7.5 %collective-permute-start.5 = (bf16[4,1024,128]{2,1,0:T(8,128)(2,1)S(1)}, bf16[4,1024,128]{2,1,0:T(8,128)(2,1)}, u32[]{:S(2)}, u32[]{:S(2)}) collective-permute-start(bf16[4,1024,128]{2,1,0:T(8,128)(2,1)S(1)} %all-to-all-done.1.o_near), channel_id=1, source_target_pairs={{0,1},{1,0},{2,3},{3,2},{4,5},{5,4},{6,7},{7,6},{8,9},{9,8},{10,11... | collective-permute-start | bytes 3145736 | tf_op jit(solution)/shard_map/ppermute | solution.py:308
  72.9 37.5 %all-to-all-start.2 = ((bf16[8,128,1024]{2,1,0:T(8,128)(2,1)}), bf16[8,128,1024]{2,1,0:T(8,128)(2,1)S(1)}, u32[]{:S(2)}, u32[]{:S(2)}) async-start(bf16[8,128,1024]{2,1,0:T(8,128)(2,1)} %shard_map.66.ready), calls=%async_computation.2 | async-start | bytes 4194304 | tf_op jit(solution)/shard_map/all_to_all | solution.py:357
  86.6 14.1 %collective-permute-start.7 = (bf16[1040,128]{1,0:T(8,128)(2,1)}, bf16[1040,128]{1,0:T(8,128)(2,1)S(1)}, u32[]{:S(2)}, u32[]{:S(2)}) collective-permute-start(bf16[1040,128]{1,0:T(8,128)(2,1)} %get-tuple-element.33.refs_1_), channel_id=1, source_target_pairs={{0,8},{1,9},{2,10},{3,11},{4,12},{5,13},{6,14},{7,15},{8,0},{9,1},... | collective-permute-start | bytes 798728 | tf_op jit(solution)/shard_map/ppermute | solution.py:377
  88.6 18.7 %collective-permute-start.6 = (bf16[1040,128]{1,0:T(8,128)(2,1)}, bf16[1040,128]{1,0:T(8,128)(2,1)S(1)}, u32[]{:S(2)}, u32[]{:S(2)}) collective-permute-start(bf16[1040,128]{1,0:T(8,128)(2,1)} %get-tuple-element.32.refs_1_), channel_id=1, source_target_pairs={{0,504},{1,505},{2,506},{3,507},{4,508},{5,509},{6,510},{7,511},{8... | collective-permute-start | bytes 798728 | tf_op jit(solution)/shard_map/ppermute | solution.py:377
  100.7 1.0 copy-start.2
  101.7 0.9 copy-start.3
  107.3 1.0 copy-start.7
  108.2 14.1 %copy-start.9 = (bf16[128,1024]{1,0:T(8,128)(2,1)S(1)}, bf16[128,1024]{1,0:T(8,128)(2,1)}, u32[]{:S(2)}) copy-start(bf16[128,1024]{1,0:T(8,128)(2,1)} %get-tuple-element.36.stream) | copy-start | bytes 786436

commit v9 on v8

--- a/solution.py
+++ b/solution.py
@@ -17,6 +17,8 @@
 LANES = 128
 BLOCKS = D // LANES
 EXT = D + 16
+QKV_PART = 3 * HEAD_DIM // 2
+OUT_PART = HEAD_DIM // 2
 FULL = EXT + BLOCKS * HEAD_DIM
 EPSILON = 1e-05
 FAR = -1e30
@@ -122,7 +124,7 @@
 
 
 def first_kernel(
-    gain, near, far, own, mirrored, out, normed, queries, keys, turned, values, hots
+    gain, near, far, own, mirrored, out, w_own, normed, queries, keys, turned, values, hots
 ):
     rows = []
     for block in range(8):
@@ -131,6 +133,9 @@
             side_by_side(ref, y).astype(F32), gain[0:1, :]
         )
         rows.append(ref[y, D:EXT, :].astype(F32)[:1])
+    for y in range(4):
+        for b in range(BLOCKS):
+            w_own[y, b] = near[y, EXT + b * HEAD_DIM : EXT + (b + 1) * HEAD_DIM, :]
     columns = tag_columns(rows)
     project(normed[...], own.at[0], mirrored, queries, keys.at[:, :LANES], turned)
     put_values(values, slice(0, PATCH), turned, False)
@@ -153,7 +158,7 @@
 
 
 def middle_kernel(
-    gain, o_near, o_far, near, far, w_mir, w_mir_far, own_at, mirrored_at, ready,
+    gain, o_near, o_far, near, far, w_mir, w_mir_far, own_at, mine_at, other_at, ready,
     q_out, kv_p, kv_q, st_out,
     heads, update, normed, queries, keys, turned, w, points, own, mirrored,
     o_sems, w_sems, sems,
@@ -170,7 +175,15 @@
             targets.append(w.at[:, row : row + HEAD_DIM, :])
     w_copies = fetch(sources, targets, w_sems)
 
-    late = fetch((own_at.at[1], mirrored_at), (own, mirrored), sems.at[2:4])
+    xl = lax.axis_index("xl")
+    at_mine, at_other = [
+        pl.ds(pl.multiple_of(k * QKV_PART, QKV_PART), QKV_PART) for k in (xl, 1 - xl)
+    ]
+    late = fetch(
+        (own_at.at[1], mine_at.at[:QKV_PART], other_at.at[:QKV_PART]),
+        (own, mirrored.at[at_mine, :], mirrored.at[at_other, :]),
+        sems.at[2:5],
+    )
     top, end = slice(0, HALF), slice(HALF, PATCH)
     o_copies = fetch(
         (o_near, o_far.at[:, end, :], o_far.at[:, top, :]),
@@ -259,10 +272,15 @@
     out[...] = (stream[...].astype(F32) + update).astype(BF16)
 
 
-def relay_kernel(own, rest, ready, out):
+def relay_kernel(own, mine, other, out):
+    xl = lax.axis_index("xl")
+    at_mine, at_other = [
+        pl.ds(pl.multiple_of(HEAD_DIM + k * OUT_PART, OUT_PART), OUT_PART) for k in (xl, 1 - xl)
+    ]
     for copy in range(out.shape[0]):
         out[copy, :HEAD_DIM] = own[...]
-        out[copy, HEAD_DIM:] = rest[3 * HEAD_DIM :]
+        out[copy, at_mine, :] = mine[QKV_PART:]
+        out[copy, at_other, :] = other[QKV_PART:]
 
 
 def call(kernel, micros, outs, scratch, *args, late=(), semaphores=(), megabytes=16):
@@ -317,22 +335,25 @@
             ],
             late=(points, order, scan_ids.reshape(1, ROWS), w_out), semaphores=(4,), megabytes=56,
         )
-        first = jnp.concatenate([w_turned[0], w_out[1]], axis=0)
+        share = 1 - lax.axis_index("xl")
+        first = jnp.concatenate(
+            [
+                w_turned[0],
+                lax.dynamic_slice_in_dim(w_turned[1], share * QKV_PART, QKV_PART, 0),
+                lax.dynamic_slice_in_dim(w_out[1], share * OUT_PART, OUT_PART, 0),
+            ],
+            axis=0,
+        )
         first_far = lax.ppermute(first, AXES, mirror)
         near = over_y(copies)
-        near, first_far, rest = lax.optimization_barrier((near, first_far, w_turned[1]))
-        rest_far = lax.ppermute(rest, AXES, mirror)
+        near, first_far = lax.optimization_barrier((near, first_far))
         far = swapped(near)
 
-        def out_weights(array):
-            return array[:, EXT:].reshape(4, BLOCKS, HEAD_DIM, LANES)
-
-        w_own = out_weights(near)
         projection = [((3 * HEAD_DIM, D), BF16)] * 2
-        (o_copies,) = call(
+        o_copies, w_own = call(
             first_kernel,
             8,
-            [(4, PATCH, LANES)],
+            [(4, PATCH, LANES), (4, BLOCKS, HEAD_DIM, LANES)],
             [
                 ((PATCH, D), BF16),
                 ((PATCH, LANES), BF16),
@@ -343,12 +364,15 @@
             ],
             ln_gain, near, far, w_turned, first_far, megabytes=16,
         )
-        o_copies, rest_far, w_own = lax.optimization_barrier((o_copies, rest_far, w_own))
+        share_far = first_far[3 * HEAD_DIM :]
+        o_copies, w_own, share_far = lax.optimization_barrier((o_copies, w_own, share_far))
+        rest_far = lax.ppermute(share_far, AXES, beside)
         w_mir = lax.ppermute(w_own, AXES, mirror)
+        w_mir, rest_far = lax.optimization_barrier((w_mir, rest_far))
         w_mir_far = swapped(w_mir)
         o_near = over_y(o_copies)
         (shares,) = call(
-            relay_kernel, 1, [(8, ROWS, D)], [], w_out[1], first_far, late=(rest_far,), megabytes=4
+            relay_kernel, 1, [(8, ROWS, D)], [], w_out[1], share_far, rest_far, megabytes=4
         )
         o_near, w_mir_far, rest_far, shares = lax.optimization_barrier(
             (o_near, w_mir_far, rest_far, shares)
@@ -371,8 +395,8 @@
                 *projection,
             ],
             ln_gain,
-            late=(o_near, o_far, near, far, w_mir, w_mir_far, w_turned, rest_far, shares),
-            semaphores=(3, 16, 4), megabytes=56,
+            late=(o_near, o_far, near, far, w_mir, w_mir_far, w_turned, share_far, rest_far, shares),
+            semaphores=(3, 16, 5), megabytes=56,
         )
         halos = [lax.ppermute(kv, AXES, links) for kv, links in zip(kvs, (inner, outer))]
         parts = None

time: 124 us -> 126 us (1.016)
  Pallas kernels: 26.1 us -> 27.8 us
    ppermute x1, waiting for transfers between devices: 8.04 us -> 3.06 us  [on_device(): w_mir = lax.ppermute(w_own, AXES, mirror)]
    ppermute x1, waiting for transfers between devices: 8.49 us -> 11.3 us  [on_device(): first_far = lax.ppermute(first, AXES, mirror)]
    ppermute x2, starting transfers between devices: 14.1 us -> 16.8 us  [on_device(): lax.ppermute(kv, AXES, links)]
    ppermute x1, starting transfers between devices: 4.37 us -> 1.92 us  [on_device(): rest_far = lax.ppermute(share_far, AXES, beside)]
    ppermute x3, waiting for transfers between devices: 0.01 us -> 2.06 us  [swapped(): return lax.ppermute(array, AXES, other_core)]
    pallas_call x7, Pallas kernels: 26.1 us -> 27.8 us  [call(): pl.pallas_call(kernel, out_shape=[jax.ShapeDtypeStruct(shape, BF16) for s...]
    ppermute x3, starting transfers between devices: 16 us -> 14.5 us  [swapped(): return lax.ppermute(array, AXES, other_core)]
    unnamed x28 -> x26, local copies, waits for them, and re-layouts: 3.64 us -> 3.84 us
  transfers between devices with their start and end apart: 11 -> 11, of which waited for: 6 -> 6; matrix products, arithmetic and copies ran while one was open for 1% -> 1% of each run, Pallas kernels for 18% -> 13%
where the time goes in v9:
time: 126 us; the launch traced here: 125 us
  starting transfers between devices  54.9 us (44%)
  Pallas kernels  27.8 us (22%)
  waiting for transfers between devices  25.6 us (20%)
  blocking collectives  11.6 us (9%)
  local copies, waits for them, and re-layouts  4.92 us (4%)
    pallas_call x7, Pallas kernels, call(): pl.pallas_call(kernel, out_shape=[jax.ShapeDtypeStruct(shape, BF16) for s...  27.8 us
    ppermute x2, starting transfers between devices, on_device(): lax.ppermute(kv, AXES, links)  16.8 us
    ppermute x3, starting transfers between devices, swapped(): return lax.ppermute(array, AXES, other_core)  14.5 us
    all_to_all x1, blocking collectives, on_device(): parts = lax.all_to_all(parts, ('y', 'c'), 0, 0, tiled=True)  11.6 us
    ppermute x1, waiting for transfers between devices, on_device(): first_far = lax.ppermute(first, AXES, mirror)  11.3 us
    all_to_all x2, starting transfers between devices, over_y(): return lax.all_to_all(copies, 'y', 0, 0, tiled=True)  9.44 us
    ppermute x1, starting transfers between devices, on_device(): first_far = lax.ppermute(first, AXES, mirror)  4.39 us
    ppermute x1, starting transfers between devices, on_device(): w_mir = lax.ppermute(w_own, AXES, mirror)  4.38 us
  transfers between devices with their start and end apart: 11, of which 6 were waited for; matrix products, arithmetic and copies ran while one was open for 1% of the time, Pallas kernels for 13%

profile of v9, /device:TPU:1, one launch (start us, length us, event | category | flops | bytes accessed | tf_op | source)
XLA Modules:
  0.0 125.2 jit_solution(2423883699375621503)
XLA Ops:
  0.0 2.5 %shard_map.64 = bf16[4,1552,128]{2,1,0:T(8,128)(2,1)} custom-call(bf16[128,1024]{1,0:T(8,128)(2,1)} %points_at.1, s32[1,128]{1,0:T(1,128)} %order_at.1, s32[1,128]{1,0:T(1,128)} %bitcast.15, bf16[2,64,1024]{2,1,0:T(8,128)(2,1)} %w_at.1), custom_call_target="tpu_custom_call" | custom-call | flops 1320000000 | tf_op jit(solution)/shard_map/pallas_call | solution.py:288
  2.5 0.0 copy-start.10
  2.6 5.2 %all-to-all-start = ((bf16[4,1552,128]{2,1,0:T(8,128)(2,1)}), bf16[4,1552,128]{2,1,0:T(8,128)(2,1)S(1)}, u32[]{:S(2)}, u32[]{:S(2)}) async-start(bf16[4,1552,128]{2,1,0:T(8,128)(2,1)} %shard_map.64), calls=%async_computation | async-start | bytes 3178496 | tf_op jit(solution)/shard_map/all_to_all | solution.py:323
  7.8 0.1 slice_bitcast_fusion
  7.9 4.4 %collective-permute-start = (bf16[320,1024]{1,0:T(8,128)(2,1)S(1)}, bf16[320,1024]{1,0:T(8,128)(2,1)}, u32[]{:S(2)}, u32[]{:S(2)}) collective-permute-start(bf16[320,1024]{1,0:T(8,128)(2,1)S(1)} %pad_maximum_fusion), channel_id=1, source_target_pairs={{0,24},{1,25},{2,26},{3,27},{4,28},{5,29},{6,30},{7,31},{8,16},{9,... | collective-permute-start | bytes 1966088 | tf_op jit(solution)/shard_map/ppermute | solution.py:347
  12.3 11.3 %collective-permute-done.mirrored = bf16[320,1024]{1,0:T(8,128)(2,1)} collective-permute-done((bf16[320,1024]{1,0:T(8,128)(2,1)S(1)}, bf16[320,1024]{1,0:T(8,128)(2,1)}, u32[]{:S(2)}, u32[]{:S(2)}) %collective-permute-start) | collective-permute-done | bytes 655392 | tf_op jit(solution)/shard_map/ppermute | solution.py:347
  23.6 7.8 %collective-permute-start.1 = (bf16[4,1552,128]{2,1,0:T(8,128)(2,1)S(1)}, bf16[4,1552,128]{2,1,0:T(8,128)(2,1)S(1)}, u32[]{:S(2)}, u32[]{:S(2)}) collective-permute-start(bf16[4,1552,128]{2,1,0:T(8,128)(2,1)S(1)} %all-to-all-done.near), channel_id=1, source_target_pairs={{0,1},{1,0},{2,3},{3,2},{4,5},{5,4},{6,7},{7,6},{8,9},{9,8},{10,11... | collective-permute-start | bytes 4767752 | tf_op jit(solution)/shard_map/ppermute | solution.py:326
  31.5 1.0 slice.16.mine.mine_at
  32.5 2.1 %collective-permute-done.1.far = bf16[4,1552,128]{2,1,0:T(8,128)(2,1)S(1)} collective-permute-done((bf16[4,1552,128]{2,1,0:T(8,128)(2,1)S(1)}, bf16[4,1552,128]{2,1,0:T(8,128)(2,1)S(1)}, u32[]{:S(2)}, u32[]{:S(2)}) %collective-permute-start.1) | collective-permute-done | bytes 1589280 | tf_op jit(solution)/shard_map/ppermute | solution.py:326
  34.5 8.1 %shard_map.65 = (bf16[4,1024,128]{2,1,0:T(8,128)(2,1)}, bf16[4,8,64,128]{3,2,1,0:T(8,128)(2,1)}) custom-call(f32[2,1024]{1,0:T(2,128)S(1)} %copy-done.8, bf16[4,1552,128]{2,1,0:T(8,128)(2,1)S(1)} %all-to-all-done.near, bf16[4,1552,128]{2,1,0:T(8,128)(2,1)S(1)} %collective-permute-done.1.far, bf16[2,192,1024]{2,1,0:T(8,128)(2,1)S(1)} %bitcast.14, ...), custom_call_target="tpu_custom_call" | custom-call | flops 8800000000 | tf_op jit(solution)/shard_map/pallas_call | solution.py:288
  42.6 4.4 %collective-permute-start.2 = (bf16[4,8,64,128]{3,2,1,0:T(8,128)(2,1)}, bf16[4,8,64,128]{3,2,1,0:T(8,128)(2,1)S(1)}, u32[]{:S(2)}, u32[]{:S(2)}) collective-permute-start(bf16[4,8,64,128]{3,2,1,0:T(8,128)(2,1)} %get-tuple-element.29), channel_id=1, source_target_pairs={{0,24},{1,25},{2,26},{3,27},{4,28},{5,29},{6,30},{7,31},{8,16},{9,... | collective-permute-start | bytes 1572872 | tf_op jit(solution)/shard_map/ppermute | solution.py:370
  47.0 1.9 %collective-permute-start.3 = (bf16[128,1024]{1,0:T(8,128)(2,1)S(1)}, bf16[128,1024]{1,0:T(8,128)(2,1)S(1)}, u32[]{:S(2)}, u32[]{:S(2)}) collective-permute-start(bf16[128,1024]{1,0:T(8,128)(2,1)S(1)} %slice.16.mine.mine_at), channel_id=1, source_target_pairs={{0,16},{1,17},{2,18},{3,19},{4,20},{5,21},{6,22},{7,23},{8,24},{9,... | collective-permute-start | bytes 786440 | tf_op jit(solution)/shard_map/ppermute | solution.py:369
  48.9 4.3 %all-to-all-start.1 = ((bf16[4,1024,128]{2,1,0:T(8,128)(2,1)}), bf16[4,1024,128]{2,1,0:T(8,128)(2,1)}, u32[]{:S(2)}, u32[]{:S(2)}) async-start(bf16[4,1024,128]{2,1,0:T(8,128)(2,1)} %get-tuple-element.28), calls=%async_computation.1 | async-start | bytes 2097152 | tf_op jit(solution)/shard_map/all_to_all | solution.py:323
  53.2 2.9 %collective-permute-done.3.other.other_at = bf16[128,1024]{1,0:T(8,128)(2,1)S(1)} collective-permute-done((bf16[128,1024]{1,0:T(8,128)(2,1)S(1)}, bf16[128,1024]{1,0:T(8,128)(2,1)S(1)}, u32[]{:S(2)}, u32[]{:S(2)}) %collective-permute-start.3) | collective-permute-done | bytes 262176 | tf_op jit(solution)/shard_map/ppermute | solution.py:369
  56.1 3.1 %collective-permute-done.2.w_mir = bf16[4,8,64,128]{3,2,1,0:T(8,128)(2,1)S(1)} collective-permute-done((bf16[4,8,64,128]{3,2,1,0:T(8,128)(2,1)}, bf16[4,8,64,128]{3,2,1,0:T(8,128)(2,1)S(1)}, u32[]{:S(2)}, u32[]{:S(2)}) %collective-permute-start.2) | collective-permute-done | bytes 524320 | tf_op jit(solution)/shard_map/ppermute | solution.py:370
  59.1 3.0 %collective-permute-start.4 = (bf16[4,8,64,128]{3,2,1,0:T(8,128)(2,1)S(1)}, bf16[4,8,64,128]{3,2,1,0:T(8,128)(2,1)}, u32[]{:S(2)}, u32[]{:S(2)}) collective-permute-start(bf16[4,8,64,128]{3,2,1,0:T(8,128)(2,1)S(1)} %collective-permute-done.2.w_mir), channel_id=1, source_target_pairs={{0,1},{1,0},{2,3},{3,2},{4,5},{5,4},{6,7},{7,6},{8,9},{9,8},{10,11... | collective-permute-start | bytes 1572872 | tf_op jit(solution)/shard_map/ppermute | solution.py:326
  62.1 1.5 %shard_map.66.ready = bf16[8,128,1024]{2,1,0:T(8,128)(2,1)} custom-call(bf16[64,1024]{1,0:T(8,128)(2,1)S(1)} %get-tuple-element.45.own, bf16[128,1024]{1,0:T(8,128)(2,1)S(1)} %slice.16.mine.mine_at, bf16[128,1024]{1,0:T(8,128)(2,1)S(1)} %collective-permute-done.3.other.other_at), custom_call_target="tpu_custom_call" | custom-call | flops 1100000000 | tf_op jit(solution)/shard_map/pallas_call | solution.py:288
  63.6 3.9 %all-to-all-done.1.o_near = bf16[4,1024,128]{2,1,0:T(8,128)(2,1)} async-done(((bf16[4,1024,128]{2,1,0:T(8,128)(2,1)}), bf16[4,1024,128]{2,1,0:T(8,128)(2,1)}, u32[]{:S(2)}, u32[]{:S(2)}) %all-to-all-start.1) | async-done | bytes 1048608 | tf_op jit(solution)/shard_map/all_to_all | solution.py:323
  67.5 3.7 %collective-permute-start.5 = (bf16[4,1024,128]{2,1,0:T(8,128)(2,1)}, bf16[4,1024,128]{2,1,0:T(8,128)(2,1)S(1)}, u32[]{:S(2)}, u32[]{:S(2)}) collective-permute-start(bf16[4,1024,128]{2,1,0:T(8,128)(2,1)} %all-to-all-done.1.o_near), channel_id=1, source_target_pairs={{0,1},{1,0},{2,3},{3,2},{4,5},{5,4},{6,7},{7,6},{8,9},{9,8},{10,11... | collective-permute-start | bytes 3145736 | tf_op jit(solution)/shard_map/ppermute | solution.py:326
  71.2 3.6 %all-to-all-start.2 = ((bf16[8,128,1024]{2,1,0:T(8,128)(2,1)}), bf16[8,128,1024]{2,1,0:T(8,128)(2,1)S(1)}, u32[]{:S(2)}, u32[]{:S(2)}) async-start(bf16[8,128,1024]{2,1,0:T(8,128)(2,1)} %shard_map.66.ready), calls=%async_computation.2 | async-start | bytes 4194304 | tf_op jit(solution)/shard_map/all_to_all | solution.py:381
  74.8 1.0 copy-done.11
  75.8 10.2 %shard_map.67 = (bf16[2,512,128]{2,1,0:T(8,128)(2,1)}, bf16[1040,128]{1,0:T(8,128)(2,1)}, bf16[1040,128]{1,0:T(8,128)(2,1)}, bf16[128,1024]{1,0:T(8,128)(2,1)}) custom-call(f32[2,1024]{1,0:T(2,128)} %gain.3, bf16[4,1024,128]{2,1,0:T(8,128)(2,1)} %all-to-all-done.1.o_near, bf16[4,1024,128]{2,1,0:T(8,128)(2,1)} %copy-done.11, bf16[4,1552,128]{2,1,0:T(8,128)(2,1)} %copy-done, ...), custom_call_target="tpu_custom_call" | custom-call | flops 8800000000 | tf_op jit(solution)/shard_map/pallas_call | solution.py:288
  86.0 3.3 %collective-permute-start.7 = (bf16[1040,128]{1,0:T(8,128)(2,1)}, bf16[1040,128]{1,0:T(8,128)(2,1)S(1)}, u32[]{:S(2)}, u32[]{:S(2)}) collective-permute-start(bf16[1040,128]{1,0:T(8,128)(2,1)} %get-tuple-element.39.refs_1_), channel_id=1, source_target_pairs={{0,8},{1,9},{2,10},{3,11},{4,12},{5,13},{6,14},{7,15},{8,0},{9,1},... | collective-permute-start | bytes 798728 | tf_op jit(solution)/shard_map/ppermute | solution.py:401
  89.3 13.5 %collective-permute-start.6 = (bf16[1040,128]{1,0:T(8,128)(2,1)}, bf16[1040,128]{1,0:T(8,128)(2,1)S(1)}, u32[]{:S(2)}, u32[]{:S(2)}) collective-permute-start(bf16[1040,128]{1,0:T(8,128)(2,1)} %get-tuple-element.38.refs_1_), channel_id=1, source_target_pairs={{0,504},{1,505},{2,506},{3,507},{4,508},{5,509},{6,510},{7,511},{8... | collective-permute-start | bytes 798728 | tf_op jit(solution)/shard_map/ppermute | solution.py:401
  102.8 0.9 copy-done.2
  103.7 0.9 copy-done.3
  104.7 2.2 %shard_map.68.refs_3_ = bf16[4,128,128]{2,1,0:T(8,128)(2,1)S(1)} custom-call(bf16[2,512,128]{2,1,0:T(8,128)(2,1)S(1)} %copy-done.3, bf16[1040,128]{1,0:T(8,128)(2,1)S(1)} %copy-done.2, bf16[1040,128]{1,0:T(8,128)(2,1)S(1)} %collective-permute-done.7.refs_2_), custom_call_target="tpu_custom_call" | custom-call | tf_op jit(solution)/shard_map/pallas_call | solution.py:288
  106.8 2.4 %collective-permute-done.6.refs_2_ = bf16[1040,128]{1,0:T(8,128)(2,1)S(1)} collective-permute-done((bf16[1040,128]{1,0:T(8,128)(2,1)}, bf16[1040,128]{1,0:T(8,128)(2,1)S(1)}, u32[]{:S(2)}, u32[]{:S(2)}) %collective-permute-start.6) | collective-permute-done | bytes 266272 | tf_op jit(solution)/shard_map/ppermute | solution.py:401
  109.3 0.9 copy-done.6
  110.2 2.2 %shard_map.69 = bf16[8,128,128]{2,1,0:T(8,128)(2,1)S(1)} custom-call(bf16[2,512,128]{2,1,0:T(8,128)(2,1)S(1)} %copy-done.3, bf16[1040,128]{1,0:T(8,128)(2,1)S(1)} %copy-done.6, bf16[1040,128]{1,0:T(8,128)(2,1)S(1)} %collective-permute-done.6.refs_2_, bf16[4,128,128]{2,1,0:T(8,128)(2,1)S(1)} %shard_map.68.refs_3_), custom_call_target="tpu_custom_call" | custom-call | flops 3300000000 | tf_op jit(solution)/shard_map/pallas_call | solution.py:288
  112.4 11.6 %all_to_all.20.parts = bf16[8,128,128]{2,1,0:T(8,128)(2,1)S(1)} all-to-all(bf16[8,128,128]{2,1,0:T(8,128)(2,1)S(1)} %shard_map.69), channel_id=1, replica_groups=mesh['z'=16,'xl'=2,'xh'=2,'y'=4,'c'=2] {'y','c'}, dimensions={0} | all-to-all | bytes 524288 | tf_op jit(solution)/shard_map/all_to_all | solution.py:418
  124.0 1.2 shard_map.70
  (30 shorter events, 0.2 us)
Async XLA Ops:
  2.5 5.2 %copy-start.10 = (bf16[2,64,1024]{2,1,0:T(8,128)(2,1)S(1)}, bf16[2,64,1024]{2,1,0:T(8,128)(2,1)}, u32[]{:S(2)}) copy-start(bf16[2,64,1024]{2,1,0:T(8,128)(2,1)} %w_at.1) | copy-start | bytes 786436
  2.5 5.2 %copy-start.1 = (bf16[2,1024,192]{1,2,0:T(8,128)(2,1)S(1)}, bf16[2,1024,192]{1,2,0:T(8,128)(2,1)}, u32[]{:S(2)}) copy-start(bf16[2,1024,192]{1,2,0:T(8,128)(2,1)} %param.10) | copy-start | bytes 2359300
  2.6 21.1 %all-to-all-start = ((bf16[4,1552,128]{2,1,0:T(8,128)(2,1)}), bf16[4,1552,128]{2,1,0:T(8,128)(2,1)S(1)}, u32[]{:S(2)}, u32[]{:S(2)}) async-start(bf16[4,1552,128]{2,1,0:T(8,128)(2,1)} %shard_map.64), calls=%async_computation | async-start | bytes 3178496 | tf_op jit(solution)/shard_map/all_to_all | solution.py:323
  7.8 26.7 %copy-start.8 = (f32[2,1024]{1,0:T(2,128)S(1)}, f32[2,1024]{1,0:T(2,128)}, u32[]{:S(2)}) copy-start(f32[2,1024]{1,0:T(2,128)} %gain.3) | copy-start | bytes 24580
  7.9 15.7 %collective-permute-start = (bf16[320,1024]{1,0:T(8,128)(2,1)S(1)}, bf16[320,1024]{1,0:T(8,128)(2,1)}, u32[]{:S(2)}, u32[]{:S(2)}) collective-permute-start(bf16[320,1024]{1,0:T(8,128)(2,1)S(1)} %pad_maximum_fusion), channel_id=1, source_target_pairs={{0,24},{1,25},{2,26},{3,27},{4,28},{5,29},{6,30},{7,31},{8,16},{9,... | collective-permute-start | bytes 1966088 | tf_op jit(solution)/shard_map/ppermute | solution.py:347
  23.6 18.9 %copy-start = (bf16[4,1552,128]{2,1,0:T(8,128)(2,1)}, bf16[4,1552,128]{2,1,0:T(8,128)(2,1)S(1)}, u32[]{:S(2)}) copy-start(bf16[4,1552,128]{2,1,0:T(8,128)(2,1)S(1)} %all-to-all-done.near) | copy-start | bytes 4767748
  23.6 10.9 %collective-permute-start.1 = (bf16[4,1552,128]{2,1,0:T(8,128)(2,1)S(1)}, bf16[4,1552,128]{2,1,0:T(8,128)(2,1)S(1)}, u32[]{:S(2)}, u32[]{:S(2)}) collective-permute-start(bf16[4,1552,128]{2,1,0:T(8,128)(2,1)S(1)} %all-to-all-done.near), channel_id=1, source_target_pairs={{0,1},{1,0},{2,3},{3,2},{4,5},{5,4},{6,7},{7,6},{8,9},{9,8},{10,11... | collective-permute-start | bytes 4767752 | tf_op jit(solution)/shard_map/ppermute | solution.py:326
  32.4 29.7 %copy-start.4 = (bf16[128,1024]{1,0:T(8,128)(2,1)}, bf16[128,1024]{1,0:T(8,128)(2,1)S(1)}, u32[]{:S(2)}) copy-start(bf16[128,1024]{1,0:T(8,128)(2,1)S(1)} %slice.16.mine.mine_at) | copy-start | bytes 786436
  34.5 8.1 %copy-start.5 = (bf16[4,1552,128]{2,1,0:T(8,128)(2,1)}, bf16[4,1552,128]{2,1,0:T(8,128)(2,1)S(1)}, u32[]{:S(2)}) copy-start(bf16[4,1552,128]{2,1,0:T(8,128)(2,1)S(1)} %collective-permute-done.1.far) | copy-start | bytes 4767748
  42.6 16.5 %collective-permute-start.2 = (bf16[4,8,64,128]{3,2,1,0:T(8,128)(2,1)}, bf16[4,8,64,128]{3,2,1,0:T(8,128)(2,1)S(1)}, u32[]{:S(2)}, u32[]{:S(2)}) collective-permute-start(bf16[4,8,64,128]{3,2,1,0:T(8,128)(2,1)} %get-tuple-element.29), channel_id=1, source_target_pairs={{0,24},{1,25},{2,26},{3,27},{4,28},{5,29},{6,30},{7,31},{8,16},{9,... | collective-permute-start | bytes 1572872 | tf_op jit(solution)/shard_map/ppermute | solution.py:370
  47.0 9.1 %collective-permute-start.3 = (bf16[128,1024]{1,0:T(8,128)(2,1)S(1)}, bf16[128,1024]{1,0:T(8,128)(2,1)S(1)}, u32[]{:S(2)}, u32[]{:S(2)}) collective-permute-start(bf16[128,1024]{1,0:T(8,128)(2,1)S(1)} %slice.16.mine.mine_at), channel_id=1, source_target_pairs={{0,16},{1,17},{2,18},{3,19},{4,20},{5,21},{6,22},{7,23},{8,24},{9,... | collective-permute-start | bytes 786440 | tf_op jit(solution)/shard_map/ppermute | solution.py:369
  48.9 18.6 %all-to-all-start.1 = ((bf16[4,1024,128]{2,1,0:T(8,128)(2,1)}), bf16[4,1024,128]{2,1,0:T(8,128)(2,1)}, u32[]{:S(2)}, u32[]{:S(2)}) async-start(bf16[4,1024,128]{2,1,0:T(8,128)(2,1)} %get-tuple-element.28), calls=%async_computation.1 | async-start | bytes 2097152 | tf_op jit(solution)/shard_map/all_to_all | solution.py:323
  56.1 7.6 %copy-start.7 = (bf16[128,1024]{1,0:T(8,128)(2,1)}, bf16[128,1024]{1,0:T(8,128)(2,1)S(1)}, u32[]{:S(2)}) copy-start(bf16[128,1024]{1,0:T(8,128)(2,1)S(1)} %collective-permute-done.3.other.other_at) | copy-start | bytes 786436
  59.1 4.5 %copy-start.12 = (bf16[4,8,64,128]{3,2,1,0:T(8,128)(2,1)}, bf16[4,8,64,128]{3,2,1,0:T(8,128)(2,1)S(1)}, u32[]{:S(2)}) copy-start(bf16[4,8,64,128]{3,2,1,0:T(8,128)(2,1)S(1)} %collective-permute-done.2.w_mir) | copy-start | bytes 1572868
  59.1 8.4 %collective-permute-start.4 = (bf16[4,8,64,128]{3,2,1,0:T(8,128)(2,1)S(1)}, bf16[4,8,64,128]{3,2,1,0:T(8,128)(2,1)}, u32[]{:S(2)}, u32[]{:S(2)}) collective-permute-start(bf16[4,8,64,128]{3,2,1,0:T(8,128)(2,1)S(1)} %collective-permute-done.2.w_mir), channel_id=1, source_target_pairs={{0,1},{1,0},{2,3},{3,2},{4,5},{5,4},{6,7},{7,6},{8,9},{9,8},{10,11... | collective-permute-start | bytes 1572872 | tf_op jit(solution)/shard_map/ppermute | solution.py:326
  67.5 7.2 %collective-permute-start.5 = (bf16[4,1024,128]{2,1,0:T(8,128)(2,1)}, bf16[4,1024,128]{2,1,0:T(8,128)(2,1)S(1)}, u32[]{:S(2)}, u32[]{:S(2)}) collective-permute-start(bf16[4,1024,128]{2,1,0:T(8,128)(2,1)} %all-to-all-done.1.o_near), channel_id=1, source_target_pairs={{0,1},{1,0},{2,3},{3,2},{4,5},{5,4},{6,7},{7,6},{8,9},{9,8},{10,11... | collective-permute-start | bytes 3145736 | tf_op jit(solution)/shard_map/ppermute | solution.py:326
  71.2 41.2 %all-to-all-start.2 = ((bf16[8,128,1024]{2,1,0:T(8,128)(2,1)}), bf16[8,128,1024]{2,1,0:T(8,128)(2,1)S(1)}, u32[]{:S(2)}, u32[]{:S(2)}) async-start(bf16[8,128,1024]{2,1,0:T(8,128)(2,1)} %shard_map.66.ready), calls=%async_computation.2 | async-start | bytes 4194304 | tf_op jit(solution)/shard_map/all_to_all | solution.py:381
  74.8 1.0 copy-start.11
  86.0 16.8 %collective-permute-start.7 = (bf16[1040,128]{1,0:T(8,128)(2,1)}, bf16[1040,128]{1,0:T(8,128)(2,1)S(1)}, u32[]{:S(2)}, u32[]{:S(2)}) collective-permute-start(bf16[1040,128]{1,0:T(8,128)(2,1)} %get-tuple-element.39.refs_1_), channel_id=1, source_target_pairs={{0,8},{1,9},{2,10},{3,11},{4,12},{5,13},{6,14},{7,15},{8,0},{9,1},... | collective-permute-start | bytes 798728 | tf_op jit(solution)/shard_map/ppermute | solution.py:401
  89.3 20.0 %collective-permute-start.6 = (bf16[1040,128]{1,0:T(8,128)(2,1)}, bf16[1040,128]{1,0:T(8,128)(2,1)S(1)}, u32[]{:S(2)}, u32[]{:S(2)}) collective-permute-start(bf16[1040,128]{1,0:T(8,128)(2,1)} %get-tuple-element.38.refs_1_), channel_id=1, source_target_pairs={{0,504},{1,505},{2,506},{3,507},{4,508},{5,509},{6,510},{7,511},{8... | collective-permute-start | bytes 798728 | tf_op jit(solution)/shard_map/ppermute | solution.py:401
  102.8 1.0 copy-start.2
  103.7 0.9 copy-start.3
  109.3 1.0 copy-start.6
  110.2 13.8 %copy-start.9 = (bf16[128,1024]{1,0:T(8,128)(2,1)S(1)}, bf16[128,1024]{1,0:T(8,128)(2,1)}, u32[]{:S(2)}) copy-start(bf16[128,1024]{1,0:T(8,128)(2,1)} %get-tuple-element.42.stream) | copy-start | bytes 786436

commit v10 on v9

--- a/solution.py
+++ b/solution.py
@@ -124,7 +124,7 @@
 
 
 def first_kernel(
-    gain, near, far, own, mirrored, out, w_own, normed, queries, keys, turned, values, hots
+    gain, near, far, own, mirrored, out, normed, queries, keys, turned, values, hots
 ):
     rows = []
     for block in range(8):
@@ -133,9 +133,6 @@
             side_by_side(ref, y).astype(F32), gain[0:1, :]
         )
         rows.append(ref[y, D:EXT, :].astype(F32)[:1])
-    for y in range(4):
-        for b in range(BLOCKS):
-            w_own[y, b] = near[y, EXT + b * HEAD_DIM : EXT + (b + 1) * HEAD_DIM, :]
     columns = tag_columns(rows)
     project(normed[...], own.at[0], mirrored, queries, keys.at[:, :LANES], turned)
     put_values(values, slice(0, PATCH), turned, False)
@@ -350,10 +347,10 @@
         far = swapped(near)
 
         projection = [((3 * HEAD_DIM, D), BF16)] * 2
-        o_copies, w_own = call(
+        (o_copies,) = call(
             first_kernel,
             8,
-            [(4, PATCH, LANES), (4, BLOCKS, HEAD_DIM, LANES)],
+            [(4, PATCH, LANES)],
             [
                 ((PATCH, D), BF16),
                 ((PATCH, LANES), BF16),
@@ -364,20 +361,19 @@
             ],
             ln_gain, near, far, w_turned, first_far, megabytes=16,
         )
+        w_own = near[:, EXT:].reshape(4, BLOCKS, HEAD_DIM, LANES)
         share_far = first_far[3 * HEAD_DIM :]
         o_copies, w_own, share_far = lax.optimization_barrier((o_copies, w_own, share_far))
         rest_far = lax.ppermute(share_far, AXES, beside)
         w_mir = lax.ppermute(w_own, AXES, mirror)
-        w_mir, rest_far = lax.optimization_barrier((w_mir, rest_far))
-        w_mir_far = swapped(w_mir)
-        o_near = over_y(o_copies)
         (shares,) = call(
             relay_kernel, 1, [(8, ROWS, D)], [], w_out[1], share_far, rest_far, megabytes=4
         )
-        o_near, w_mir_far, rest_far, shares = lax.optimization_barrier(
-            (o_near, w_mir_far, rest_far, shares)
+        o_near, w_mir, rest_far, shares = lax.optimization_barrier(
+            (over_y(o_copies), w_mir, rest_far, shares)
         )
         o_far = swapped(o_near)
+        w_mir_far = swapped(w_mir)
         w_last = lax.all_to_all(shares, ("y", "c"), 0, 0, tiled=True).reshape(D, D)
         queries, *kvs, stream = call(
             middle_kernel,
@@ -396,7 +392,7 @@
             ],
             ln_gain,
             late=(o_near, o_far, near, far, w_mir, w_mir_far, w_turned, share_far, rest_far, shares),
-            semaphores=(3, 16, 5), megabytes=56,
+            semaphores=(3, 16, 5), megabytes=52,
         )
         halos = [lax.ppermute(kv, AXES, links) for kv, links in zip(kvs, (inner, outer))]
         parts = None

time: 126 us -> 121 us (0.960)
  local copies, waits for them, and re-layouts: 4.92 us -> 1.98 us
  Pallas kernels: 27.8 us -> 26.1 us
  starting transfers between devices: 54.9 us -> 53.3 us
    ppermute x1, waiting for transfers between devices: 2.87 us -> 7.26 us  [on_device(): rest_far = lax.ppermute(share_far, AXES, beside)]
    all_to_all x2, waiting for transfers between devices: 3.89 us -> 0.01 us  [over_y(): return lax.all_to_all(copies, 'y', 0, 0, tiled=True)]
    unnamed x26 -> x10, local copies, waits for them, and re-layouts: 3.84 us -> 0.03 us
    ppermute x2, waiting for transfers between devices: 2.43 us -> 5.14 us  [on_device(): lax.ppermute(kv, AXES, links)]
    pallas_call x7, Pallas kernels: 27.8 us -> 26.1 us  [call(): pl.pallas_call(kernel, out_shape=[jax.ShapeDtypeStruct(shape, BF16) for s...]
    ppermute x3, starting transfers between devices: 14.5 us -> 12.8 us  [swapped(): return lax.ppermute(array, AXES, other_core)]
    ppermute x1, waiting for transfers between devices: 3.06 us -> 1.51 us  [on_device(): w_mir = lax.ppermute(w_own, AXES, mirror)]
    all_to_all x1, starting transfers between devices: 3.56 us -> 4.97 us  [on_device(): w_last = lax.all_to_all(shares, ('y', 'c'), 0, 0, tiled=True).reshape(D, D)]
  transfers between devices with their start and end apart: 11 -> 11, of which waited for: 6 -> 5; matrix products, arithmetic and copies ran while one was open for 1% -> 2% of each run, Pallas kernels for 13% -> 12%
where the time goes in v10:
time: 121 us; the launch traced here: 120 us
  starting transfers between devices  53.3 us (44%)
  waiting for transfers between devices  26.4 us (22%)
  Pallas kernels  26.1 us (22%)
  blocking collectives  11.7 us (10%)
  local copies, waits for them, and re-layouts  1.98 us (2%)
    pallas_call x7, Pallas kernels, call(): pl.pallas_call(kernel, out_shape=[jax.ShapeDtypeStruct(shape, BF16) for s...  26.1 us
    ppermute x2, starting transfers between devices, on_device(): lax.ppermute(kv, AXES, links)  15.4 us
    ppermute x3, starting transfers between devices, swapped(): return lax.ppermute(array, AXES, other_core)  12.8 us
    all_to_all x1, blocking collectives, on_device(): parts = lax.all_to_all(parts, ('y', 'c'), 0, 0, tiled=True)  11.7 us
    ppermute x1, waiting for transfers between devices, on_device(): first_far = lax.ppermute(first, AXES, mirror)  11.3 us
    all_to_all x2, starting transfers between devices, over_y(): return lax.all_to_all(copies, 'y', 0, 0, tiled=True)  9.4 us
    ppermute x1, waiting for transfers between devices, on_device(): rest_far = lax.ppermute(share_far, AXES, beside)  7.26 us
    ppermute x2, waiting for transfers between devices, on_device(): lax.ppermute(kv, AXES, links)  5.14 us
  transfers between devices with their start and end apart: 11, of which 5 were waited for; matrix products, arithmetic and copies ran while one was open for 2% of the time, Pallas kernels for 12%

profile of v10, /device:TPU:1, one launch (start us, length us, event | category | flops | bytes accessed | tf_op | source)
XLA Modules:
  0.0 119.8 jit_solution(4753421246397847384)
XLA Ops:
  0.0 2.5 %shard_map.64 = bf16[4,1552,128]{2,1,0:T(8,128)(2,1)} custom-call(bf16[128,1024]{1,0:T(8,128)(2,1)} %points_at.1, s32[1,128]{1,0:T(1,128)} %order_at.1, s32[1,128]{1,0:T(1,128)} %bitcast.16, bf16[2,64,1024]{2,1,0:T(8,128)(2,1)} %w_at.1), custom_call_target="tpu_custom_call" | custom-call | flops 1320000000 | tf_op jit(solution)/shard_map/pallas_call | solution.py:285
  2.5 0.0 copy-start.4
  2.5 0.0 copy-start.1
  2.5 5.2 %all-to-all-start = ((bf16[4,1552,128]{2,1,0:T(8,128)(2,1)}), bf16[4,1552,128]{2,1,0:T(8,128)(2,1)S(1)}, u32[]{:S(2)}, u32[]{:S(2)}) async-start(bf16[4,1552,128]{2,1,0:T(8,128)(2,1)} %shard_map.64), calls=%async_computation | async-start | bytes 3178496 | tf_op jit(solution)/shard_map/all_to_all | solution.py:320
  7.8 0.1 slice_bitcast_fusion
  7.8 0.0 copy-start.3
  7.9 4.4 %collective-permute-start = (bf16[320,1024]{1,0:T(8,128)(2,1)S(1)}, bf16[320,1024]{1,0:T(8,128)(2,1)}, u32[]{:S(2)}, u32[]{:S(2)}) collective-permute-start(bf16[320,1024]{1,0:T(8,128)(2,1)S(1)} %pad_maximum_fusion), channel_id=1, source_target_pairs={{0,24},{1,25},{2,26},{3,27},{4,28},{5,29},{6,30},{7,31},{8,16},{9,... | collective-permute-start | bytes 1966088 | tf_op jit(solution)/shard_map/ppermute | solution.py:344
  12.3 11.3 %collective-permute-done.mirrored = bf16[320,1024]{1,0:T(8,128)(2,1)} collective-permute-done((bf16[320,1024]{1,0:T(8,128)(2,1)S(1)}, bf16[320,1024]{1,0:T(8,128)(2,1)}, u32[]{:S(2)}, u32[]{:S(2)}) %collective-permute-start) | collective-permute-done | bytes 655392 | tf_op jit(solution)/shard_map/ppermute | solution.py:344
  23.6 0.0 all-to-all-done.near
  23.6 7.8 %collective-permute-start.1 = (bf16[4,1552,128]{2,1,0:T(8,128)(2,1)S(1)}, bf16[4,1552,128]{2,1,0:T(8,128)(2,1)S(1)}, u32[]{:S(2)}, u32[]{:S(2)}) collective-permute-start(bf16[4,1552,128]{2,1,0:T(8,128)(2,1)S(1)} %all-to-all-done.near), channel_id=1, source_target_pairs={{0,1},{1,0},{2,3},{3,2},{4,5},{5,4},{6,7},{7,6},{8,9},{9,8},{10,11... | collective-permute-start | bytes 4767752 | tf_op jit(solution)/shard_map/ppermute | solution.py:323
  31.4 0.9 slice.19
  32.3 1.0 slice.20.mine.mine_at
  33.3 1.2 collective-permute-done.1.far
  34.5 8.0 %shard_map.65 = bf16[4,1024,128]{2,1,0:T(8,128)(2,1)} custom-call(f32[2,1024]{1,0:T(2,128)S(1)} %copy-done.3, bf16[4,1552,128]{2,1,0:T(8,128)(2,1)S(1)} %all-to-all-done.near, bf16[4,1552,128]{2,1,0:T(8,128)(2,1)S(1)} %collective-permute-done.1.far, bf16[2,192,1024]{2,1,0:T(8,128)(2,1)S(1)} %bitcast.15, bf16[320,1024]{1,0:T(8,128)(2,1)} %collective-permute-done.mirrored), custom_call_target="tpu_custom_call" | custom-call | flops 8800000000 | tf_op jit(solution)/shard_map/pallas_call | solution.py:285
  42.5 4.2 %all-to-all-start.1 = ((bf16[4,1024,128]{2,1,0:T(8,128)(2,1)}), bf16[4,1024,128]{2,1,0:T(8,128)(2,1)}, u32[]{:S(2)}, u32[]{:S(2)}) async-start(bf16[4,1024,128]{2,1,0:T(8,128)(2,1)} %shard_map.65), calls=%async_computation.1 | async-start | bytes 2097152 | tf_op jit(solution)/shard_map/all_to_all | solution.py:320
  46.7 4.4 %collective-permute-start.2 = (bf16[4,8,64,128]{3,2,1,0:T(8,128)(2,1)}, bf16[4,8,64,128]{3,2,1,0:T(8,128)(2,1)}, u32[]{:S(2)}, u32[]{:S(2)}) collective-permute-start(bf16[4,8,64,128]{3,2,1,0:T(8,128)(2,1)} %bitcast.5), channel_id=1, source_target_pairs={{0,24},{1,25},{2,26},{3,27},{4,28},{5,29},{6,30},{7,31},{8,16},{9,... | collective-permute-start | bytes 1572872 | tf_op jit(solution)/shard_map/ppermute | solution.py:368
  51.1 1.9 %collective-permute-start.3 = (bf16[128,1024]{1,0:T(8,128)(2,1)S(1)}, bf16[128,1024]{1,0:T(8,128)(2,1)S(1)}, u32[]{:S(2)}, u32[]{:S(2)}) collective-permute-start(bf16[128,1024]{1,0:T(8,128)(2,1)S(1)} %slice.20.mine.mine_at), channel_id=1, source_target_pairs={{0,16},{1,17},{2,18},{3,19},{4,20},{5,21},{6,22},{7,23},{8,24},{9,... | collective-permute-start | bytes 786440 | tf_op jit(solution)/shard_map/ppermute | solution.py:367
  53.0 7.3 %collective-permute-done.3.other.other_at = bf16[128,1024]{1,0:T(8,128)(2,1)S(1)} collective-permute-done((bf16[128,1024]{1,0:T(8,128)(2,1)S(1)}, bf16[128,1024]{1,0:T(8,128)(2,1)S(1)}, u32[]{:S(2)}, u32[]{:S(2)}) %collective-permute-start.3) | collective-permute-done | bytes 262176 | tf_op jit(solution)/shard_map/ppermute | solution.py:367
  60.3 1.5 %shard_map.66.ready = bf16[8,128,1024]{2,1,0:T(8,128)(2,1)} custom-call(bf16[64,1024]{1,0:T(8,128)(2,1)S(1)} %get-tuple-element.37.own, bf16[128,1024]{1,0:T(8,128)(2,1)S(1)} %slice.20.mine.mine_at, bf16[128,1024]{1,0:T(8,128)(2,1)S(1)} %collective-permute-done.3.other.other_at), custom_call_target="tpu_custom_call" | custom-call | flops 1100000000 | tf_op jit(solution)/shard_map/pallas_call | solution.py:285
  61.7 1.5 %collective-permute-done.2.w_mir = bf16[4,8,64,128]{3,2,1,0:T(8,128)(2,1)} collective-permute-done((bf16[4,8,64,128]{3,2,1,0:T(8,128)(2,1)}, bf16[4,8,64,128]{3,2,1,0:T(8,128)(2,1)}, u32[]{:S(2)}, u32[]{:S(2)}) %collective-permute-start.2) | collective-permute-done | bytes 524320 | tf_op jit(solution)/shard_map/ppermute | solution.py:368
  63.3 3.1 %collective-permute-start.4 = (bf16[4,1024,128]{2,1,0:T(8,128)(2,1)}, bf16[4,1024,128]{2,1,0:T(8,128)(2,1)}, u32[]{:S(2)}, u32[]{:S(2)}) collective-permute-start(bf16[4,1024,128]{2,1,0:T(8,128)(2,1)} %all-to-all-done.1.o_near), channel_id=1, source_target_pairs={{0,1},{1,0},{2,3},{3,2},{4,5},{5,4},{6,7},{7,6},{8,9},{9,8},{10,11... | collective-permute-start | bytes 3145736 | tf_op jit(solution)/shard_map/ppermute | solution.py:323
  66.4 1.9 %collective-permute-start.5 = (bf16[4,8,64,128]{3,2,1,0:T(8,128)(2,1)}, bf16[4,8,64,128]{3,2,1,0:T(8,128)(2,1)}, u32[]{:S(2)}, u32[]{:S(2)}) collective-permute-start(bf16[4,8,64,128]{3,2,1,0:T(8,128)(2,1)} %collective-permute-done.2.w_mir), channel_id=1, source_target_pairs={{0,1},{1,0},{2,3},{3,2},{4,5},{5,4},{6,7},{7,6},{8,9},{9,8},{10,11... | collective-permute-start | bytes 1572872 | tf_op jit(solution)/shard_map/ppermute | solution.py:323
  68.3 5.0 %all-to-all-start.2 = ((bf16[8,128,1024]{2,1,0:T(8,128)(2,1)}), bf16[8,128,1024]{2,1,0:T(8,128)(2,1)S(1)}, u32[]{:S(2)}, u32[]{:S(2)}) async-start(bf16[8,128,1024]{2,1,0:T(8,128)(2,1)} %shard_map.66.ready), calls=%async_computation.2 | async-start | bytes 4194304 | tf_op jit(solution)/shard_map/all_to_all | solution.py:377
  73.3 8.7 %shard_map.67 = (bf16[2,512,128]{2,1,0:T(8,128)(2,1)S(1)}, bf16[1040,128]{1,0:T(8,128)(2,1)S(1)}, bf16[1040,128]{1,0:T(8,128)(2,1)S(1)}, bf16[128,1024]{1,0:T(8,128)(2,1)S(1)}) custom-call(f32[2,1024]{1,0:T(2,128)S(1)} %copy-done.3, bf16[4,1024,128]{2,1,0:T(8,128)(2,1)} %all-to-all-done.1.o_near, bf16[4,1024,128]{2,1,0:T(8,128)(2,1)} %collective-permute-done.4.o_far, ...), custom_call_target="tpu_custom_call" | custom-call | flops 8800000000 | tf_op jit(solution)/shard_map/pallas_call | solution.py:285
  81.9 3.5 %collective-permute-start.7 = (bf16[1040,128]{1,0:T(8,128)(2,1)S(1)}, bf16[1040,128]{1,0:T(8,128)(2,1)S(1)}, u32[]{:S(2)}, u32[]{:S(2)}) collective-permute-start(bf16[1040,128]{1,0:T(8,128)(2,1)S(1)} %get-tuple-element.31.refs_1_), channel_id=1, source_target_pairs={{0,8},{1,9},{2,10},{3,11},{4,12},{5,13},{6,14},{7,15},{8,0},{9,1},... | collective-permute-start | bytes 798728 | tf_op jit(solution)/shard_map/ppermute | solution.py:397
  85.4 12.0 %collective-permute-start.6 = (bf16[1040,128]{1,0:T(8,128)(2,1)S(1)}, bf16[1040,128]{1,0:T(8,128)(2,1)S(1)}, u32[]{:S(2)}, u32[]{:S(2)}) collective-permute-start(bf16[1040,128]{1,0:T(8,128)(2,1)S(1)} %get-tuple-element.30.refs_1_), channel_id=1, source_target_pairs={{0,504},{1,505},{2,506},{3,507},{4,508},{5,509},{6,510},{7,511},{8... | collective-permute-start | bytes 798728 | tf_op jit(solution)/shard_map/ppermute | solution.py:397
  97.4 0.0 collective-permute-done.7.refs_2_
  97.4 2.2 %shard_map.68.refs_3_ = bf16[4,128,128]{2,1,0:T(8,128)(2,1)S(1)} custom-call(bf16[2,512,128]{2,1,0:T(8,128)(2,1)S(1)} %get-tuple-element.29.refs_0_, bf16[1040,128]{1,0:T(8,128)(2,1)S(1)} %get-tuple-element.31.refs_1_, bf16[1040,128]{1,0:T(8,128)(2,1)S(1)} %collective-permute-done.7.refs_2_), custom_call_target="tpu_custom_call" | custom-call | tf_op jit(solution)/shard_map/pallas_call | solution.py:285
  99.6 5.1 %collective-permute-done.6.refs_2_ = bf16[1040,128]{1,0:T(8,128)(2,1)S(1)} collective-permute-done((bf16[1040,128]{1,0:T(8,128)(2,1)S(1)}, bf16[1040,128]{1,0:T(8,128)(2,1)S(1)}, u32[]{:S(2)}, u32[]{:S(2)}) %collective-permute-start.6) | collective-permute-done | bytes 266272 | tf_op jit(solution)/shard_map/ppermute | solution.py:397
  104.7 2.2 %shard_map.69 = bf16[8,128,128]{2,1,0:T(8,128)(2,1)S(1)} custom-call(bf16[2,512,128]{2,1,0:T(8,128)(2,1)S(1)} %get-tuple-element.29.refs_0_, bf16[1040,128]{1,0:T(8,128)(2,1)S(1)} %get-tuple-element.30.refs_1_, bf16[1040,128]{1,0:T(8,128)(2,1)S(1)} %collective-permute-done.6.refs_2_, bf16[4,128,128]{2,1,0:T(8,128)(2,1)S(1)} %shard_map.68.refs_3_), custom_call_target="tpu_custom_call" | custom-call | flops 3300000000 | tf_op jit(solution)/shard_map/pallas_call | solution.py:285
  106.9 11.7 %all_to_all.20.parts = bf16[8,128,128]{2,1,0:T(8,128)(2,1)S(1)} all-to-all(bf16[8,128,128]{2,1,0:T(8,128)(2,1)S(1)} %shard_map.69), channel_id=1, replica_groups=mesh['z'=16,'xl'=2,'xh'=2,'y'=4,'c'=2] {'y','c'}, dimensions={0} | all-to-all | bytes 524288 | tf_op jit(solution)/shard_map/all_to_all | solution.py:414
  118.7 1.2 shard_map.70
  (15 shorter events, 0.1 us)
Async XLA Ops:
  2.5 5.2 %copy-start.4 = (bf16[2,64,1024]{2,1,0:T(8,128)(2,1)S(1)}, bf16[2,64,1024]{2,1,0:T(8,128)(2,1)}, u32[]{:S(2)}) copy-start(bf16[2,64,1024]{2,1,0:T(8,128)(2,1)} %w_at.1) | copy-start | bytes 786436
  2.5 5.2 %copy-start.1 = (bf16[2,1024,192]{1,2,0:T(8,128)(2,1)S(1)}, bf16[2,1024,192]{1,2,0:T(8,128)(2,1)}, u32[]{:S(2)}) copy-start(bf16[2,1024,192]{1,2,0:T(8,128)(2,1)} %param.10) | copy-start | bytes 2359300
  2.5 21.1 %all-to-all-start = ((bf16[4,1552,128]{2,1,0:T(8,128)(2,1)}), bf16[4,1552,128]{2,1,0:T(8,128)(2,1)S(1)}, u32[]{:S(2)}, u32[]{:S(2)}) async-start(bf16[4,1552,128]{2,1,0:T(8,128)(2,1)} %shard_map.64), calls=%async_computation | async-start | bytes 3178496 | tf_op jit(solution)/shard_map/all_to_all | solution.py:320
  7.8 26.7 %copy-start.3 = (f32[2,1024]{1,0:T(2,128)S(1)}, f32[2,1024]{1,0:T(2,128)}, u32[]{:S(2)}) copy-start(f32[2,1024]{1,0:T(2,128)} %gain.3) | copy-start | bytes 24580
  7.9 15.7 %collective-permute-start = (bf16[320,1024]{1,0:T(8,128)(2,1)S(1)}, bf16[320,1024]{1,0:T(8,128)(2,1)}, u32[]{:S(2)}, u32[]{:S(2)}) collective-permute-start(bf16[320,1024]{1,0:T(8,128)(2,1)S(1)} %pad_maximum_fusion), channel_id=1, source_target_pairs={{0,24},{1,25},{2,26},{3,27},{4,28},{5,29},{6,30},{7,31},{8,16},{9,... | collective-permute-start | bytes 1966088 | tf_op jit(solution)/shard_map/ppermute | solution.py:344
  23.6 18.8 %copy-start = (bf16[4,1552,128]{2,1,0:T(8,128)(2,1)}, bf16[4,1552,128]{2,1,0:T(8,128)(2,1)S(1)}, u32[]{:S(2)}) copy-start(bf16[4,1552,128]{2,1,0:T(8,128)(2,1)S(1)} %all-to-all-done.near) | copy-start | bytes 4767748
  23.6 10.9 %collective-permute-start.1 = (bf16[4,1552,128]{2,1,0:T(8,128)(2,1)S(1)}, bf16[4,1552,128]{2,1,0:T(8,128)(2,1)S(1)}, u32[]{:S(2)}, u32[]{:S(2)}) collective-permute-start(bf16[4,1552,128]{2,1,0:T(8,128)(2,1)S(1)} %all-to-all-done.near), channel_id=1, source_target_pairs={{0,1},{1,0},{2,3},{3,2},{4,5},{5,4},{6,7},{7,6},{8,9},{9,8},{10,11... | collective-permute-start | bytes 4767752 | tf_op jit(solution)/shard_map/ppermute | solution.py:323
  34.5 8.0 %copy-start.2 = (bf16[4,1552,128]{2,1,0:T(8,128)(2,1)}, bf16[4,1552,128]{2,1,0:T(8,128)(2,1)S(1)}, u32[]{:S(2)}) copy-start(bf16[4,1552,128]{2,1,0:T(8,128)(2,1)S(1)} %collective-permute-done.1.far) | copy-start | bytes 4767748
  42.5 20.8 %all-to-all-start.1 = ((bf16[4,1024,128]{2,1,0:T(8,128)(2,1)}), bf16[4,1024,128]{2,1,0:T(8,128)(2,1)}, u32[]{:S(2)}, u32[]{:S(2)}) async-start(bf16[4,1024,128]{2,1,0:T(8,128)(2,1)} %shard_map.65), calls=%async_computation.1 | async-start | bytes 2097152 | tf_op jit(solution)/shard_map/all_to_all | solution.py:320
  46.7 16.6 %collective-permute-start.2 = (bf16[4,8,64,128]{3,2,1,0:T(8,128)(2,1)}, bf16[4,8,64,128]{3,2,1,0:T(8,128)(2,1)}, u32[]{:S(2)}, u32[]{:S(2)}) collective-permute-start(bf16[4,8,64,128]{3,2,1,0:T(8,128)(2,1)} %bitcast.5), channel_id=1, source_target_pairs={{0,24},{1,25},{2,26},{3,27},{4,28},{5,29},{6,30},{7,31},{8,16},{9,... | collective-permute-start | bytes 1572872 | tf_op jit(solution)/shard_map/ppermute | solution.py:368
  51.1 9.2 %collective-permute-start.3 = (bf16[128,1024]{1,0:T(8,128)(2,1)S(1)}, bf16[128,1024]{1,0:T(8,128)(2,1)S(1)}, u32[]{:S(2)}, u32[]{:S(2)}) collective-permute-start(bf16[128,1024]{1,0:T(8,128)(2,1)S(1)} %slice.20.mine.mine_at), channel_id=1, source_target_pairs={{0,16},{1,17},{2,18},{3,19},{4,20},{5,21},{6,22},{7,23},{8,24},{9,... | collective-permute-start | bytes 786440 | tf_op jit(solution)/shard_map/ppermute | solution.py:367
  63.3 10.0 %collective-permute-start.4 = (bf16[4,1024,128]{2,1,0:T(8,128)(2,1)}, bf16[4,1024,128]{2,1,0:T(8,128)(2,1)}, u32[]{:S(2)}, u32[]{:S(2)}) collective-permute-start(bf16[4,1024,128]{2,1,0:T(8,128)(2,1)} %all-to-all-done.1.o_near), channel_id=1, source_target_pairs={{0,1},{1,0},{2,3},{3,2},{4,5},{5,4},{6,7},{7,6},{8,9},{9,8},{10,11... | collective-permute-start | bytes 3145736 | tf_op jit(solution)/shard_map/ppermute | solution.py:323
  66.4 6.9 %collective-permute-start.5 = (bf16[4,8,64,128]{3,2,1,0:T(8,128)(2,1)}, bf16[4,8,64,128]{3,2,1,0:T(8,128)(2,1)}, u32[]{:S(2)}, u32[]{:S(2)}) collective-permute-start(bf16[4,8,64,128]{3,2,1,0:T(8,128)(2,1)} %collective-permute-done.2.w_mir), channel_id=1, source_target_pairs={{0,1},{1,0},{2,3},{3,2},{4,5},{5,4},{6,7},{7,6},{8,9},{9,8},{10,11... | collective-permute-start | bytes 1572872 | tf_op jit(solution)/shard_map/ppermute | solution.py:323
  68.3 38.6 %all-to-all-start.2 = ((bf16[8,128,1024]{2,1,0:T(8,128)(2,1)}), bf16[8,128,1024]{2,1,0:T(8,128)(2,1)S(1)}, u32[]{:S(2)}, u32[]{:S(2)}) async-start(bf16[8,128,1024]{2,1,0:T(8,128)(2,1)} %shard_map.66.ready), calls=%async_computation.2 | async-start | bytes 4194304 | tf_op jit(solution)/shard_map/all_to_all | solution.py:377
  81.9 15.5 %collective-permute-start.7 = (bf16[1040,128]{1,0:T(8,128)(2,1)S(1)}, bf16[1040,128]{1,0:T(8,128)(2,1)S(1)}, u32[]{:S(2)}, u32[]{:S(2)}) collective-permute-start(bf16[1040,128]{1,0:T(8,128)(2,1)S(1)} %get-tuple-element.31.refs_1_), channel_id=1, source_target_pairs={{0,8},{1,9},{2,10},{3,11},{4,12},{5,13},{6,14},{7,15},{8,0},{9,1},... | collective-permute-start | bytes 798728 | tf_op jit(solution)/shard_map/ppermute | solution.py:397
  85.4 19.3 %collective-permute-start.6 = (bf16[1040,128]{1,0:T(8,128)(2,1)S(1)}, bf16[1040,128]{1,0:T(8,128)(2,1)S(1)}, u32[]{:S(2)}, u32[]{:S(2)}) collective-permute-start(bf16[1040,128]{1,0:T(8,128)(2,1)S(1)} %get-tuple-element.30.refs_1_), channel_id=1, source_target_pairs={{0,504},{1,505},{2,506},{3,507},{4,508},{5,509},{6,510},{7,511},{8... | collective-permute-start | bytes 798728 | tf_op jit(solution)/shard_map/ppermute | solution.py:397

commit v11 on v10

--- a/solution.py
+++ b/solution.py
@@ -124,8 +124,10 @@
 
 
 def first_kernel(
-    gain, near, far, own, mirrored, out, normed, queries, keys, turned, values, hots
+    gain, near, far, own, mirrored_at, out,
+    normed, queries, keys, turned, values, hots, mirrored, sems,
 ):
+    (copy,) = fetch((mirrored_at.at[: 3 * HEAD_DIM],), (mirrored,), sems)
     rows = []
     for block in range(8):
         ref, y = (near, far)[block // 4], block % 4
@@ -134,6 +136,7 @@
         )
         rows.append(ref[y, D:EXT, :].astype(F32)[:1])
     columns = tag_columns(rows)
+    copy.wait()
     project(normed[...], own.at[0], mirrored, queries, keys.at[:, :LANES], turned)
     put_values(values, slice(0, PATCH), turned, False)
     values[:, HEAD_DIM:, :] = jnp.ones((2, 16, PATCH), BF16)
@@ -176,11 +179,6 @@
     at_mine, at_other = [
         pl.ds(pl.multiple_of(k * QKV_PART, QKV_PART), QKV_PART) for k in (xl, 1 - xl)
     ]
-    late = fetch(
-        (own_at.at[1], mine_at.at[:QKV_PART], other_at.at[:QKV_PART]),
-        (own, mirrored.at[at_mine, :], mirrored.at[at_other, :]),
-        sems.at[2:5],
-    )
     top, end = slice(0, HALF), slice(HALF, PATCH)
     o_copies = fetch(
         (o_near, o_far.at[:, end, :], o_far.at[:, top, :]),
@@ -188,6 +186,11 @@
         o_sems,
     )
     x_copies = fetch((near.at[:, :EXT, :], far.at[:, :EXT, :]), (points.at[0], points.at[1]), sems)
+    late = fetch(
+        (own_at.at[1], mine_at.at[:QKV_PART], other_at.at[:QKV_PART]),
+        (own, mirrored.at[at_mine, :], mirrored.at[at_other, :]),
+        sems.at[2:5],
+    )
     for copy in w_copies + o_copies:
         copy.wait()
     left = jnp.concatenate([heads[g] for g in range(BLOCKS)], axis=1)
@@ -358,8 +361,9 @@
                 ((LANES, PATCH), BF16),
                 ((2, HEAD_DIM + 16, PATCH), BF16),
                 ((PATCH, LANES), BF16),
+                ((3 * HEAD_DIM, D), BF16),
             ],
-            ln_gain, near, far, w_turned, first_far, megabytes=16,
+            ln_gain, near, far, w_turned, late=(first_far,), semaphores=(1,), megabytes=16,
         )
         w_own = near[:, EXT:].reshape(4, BLOCKS, HEAD_DIM, LANES)
         share_far = first_far[3 * HEAD_DIM :]

time: 121 us -> 120 us (level)
  no operation moved by 1% of the time
where the time goes in v11:
time: 120 us; the launch traced here: 119 us
  starting transfers between devices  53.4 us (44%)
  waiting for transfers between devices  26.4 us (22%)
  Pallas kernels  25.4 us (21%)
  blocking collectives  11.7 us (10%)
  local copies, waits for them, and re-layouts  1.98 us (2%)
    pallas_call x7, Pallas kernels, call(): pl.pallas_call(kernel, out_shape=[jax.ShapeDtypeStruct(shape, BF16) for s...  25.4 us
    ppermute x2, starting transfers between devices, on_device(): lax.ppermute(kv, AXES, links)  15.4 us
    ppermute x3, starting transfers between devices, swapped(): return lax.ppermute(array, AXES, other_core)  12.8 us
    all_to_all x1, blocking collectives, on_device(): parts = lax.all_to_all(parts, ('y', 'c'), 0, 0, tiled=True)  11.7 us
    ppermute x1, waiting for transfers between devices, on_device(): first_far = lax.ppermute(first, AXES, mirror)  11.3 us
    all_to_all x2, starting transfers between devices, over_y(): return lax.all_to_all(copies, 'y', 0, 0, tiled=True)  9.41 us
    ppermute x1, waiting for transfers between devices, on_device(): rest_far = lax.ppermute(share_far, AXES, beside)  7.27 us
    ppermute x2, waiting for transfers between devices, on_device(): lax.ppermute(kv, AXES, links)  5.14 us
  transfers between devices with their start and end apart: 11, of which 5 were waited for; matrix products, arithmetic and copies ran while one was open for 2% of the time, Pallas kernels for 12%

profile of v11, /device:TPU:1, one launch (start us, length us, event | category | flops | bytes accessed | tf_op | source)
XLA Modules:
  0.0 119.2 jit_solution(2353301879080871633)
XLA Ops:
  0.0 2.5 %shard_map.64 = bf16[4,1552,128]{2,1,0:T(8,128)(2,1)} custom-call(bf16[128,1024]{1,0:T(8,128)(2,1)} %points_at.1, s32[1,128]{1,0:T(1,128)} %order_at.1, s32[1,128]{1,0:T(1,128)} %bitcast.16, bf16[2,64,1024]{2,1,0:T(8,128)(2,1)} %w_at.1), custom_call_target="tpu_custom_call" | custom-call | flops 1320000000 | tf_op jit(solution)/shard_map/pallas_call | solution.py:288
  2.5 0.0 copy-start.4
  2.5 0.0 copy-start.1
  2.5 5.2 %all-to-all-start = ((bf16[4,1552,128]{2,1,0:T(8,128)(2,1)}), bf16[4,1552,128]{2,1,0:T(8,128)(2,1)S(1)}, u32[]{:S(2)}, u32[]{:S(2)}) async-start(bf16[4,1552,128]{2,1,0:T(8,128)(2,1)} %shard_map.64), calls=%async_computation | async-start | bytes 3178496 | tf_op jit(solution)/shard_map/all_to_all | solution.py:323
  7.8 0.1 slice_bitcast_fusion
  7.8 0.0 copy-start.3
  7.9 4.4 %collective-permute-start = (bf16[320,1024]{1,0:T(8,128)(2,1)S(1)}, bf16[320,1024]{1,0:T(8,128)(2,1)}, u32[]{:S(2)}, u32[]{:S(2)}) collective-permute-start(bf16[320,1024]{1,0:T(8,128)(2,1)S(1)} %pad_maximum_fusion), channel_id=1, source_target_pairs={{0,24},{1,25},{2,26},{3,27},{4,28},{5,29},{6,30},{7,31},{8,16},{9,... | collective-permute-start | bytes 1966088 | tf_op jit(solution)/shard_map/ppermute | solution.py:347
  12.3 11.3 %collective-permute-done.mirrored_at = bf16[320,1024]{1,0:T(8,128)(2,1)} collective-permute-done((bf16[320,1024]{1,0:T(8,128)(2,1)S(1)}, bf16[320,1024]{1,0:T(8,128)(2,1)}, u32[]{:S(2)}, u32[]{:S(2)}) %collective-permute-start) | collective-permute-done | bytes 655392 | tf_op jit(solution)/shard_map/ppermute | solution.py:347
  23.6 0.0 all-to-all-done.near
  23.6 7.8 %collective-permute-start.1 = (bf16[4,1552,128]{2,1,0:T(8,128)(2,1)S(1)}, bf16[4,1552,128]{2,1,0:T(8,128)(2,1)S(1)}, u32[]{:S(2)}, u32[]{:S(2)}) collective-permute-start(bf16[4,1552,128]{2,1,0:T(8,128)(2,1)S(1)} %all-to-all-done.near), channel_id=1, source_target_pairs={{0,1},{1,0},{2,3},{3,2},{4,5},{5,4},{6,7},{7,6},{8,9},{9,8},{10,11... | collective-permute-start | bytes 4767752 | tf_op jit(solution)/shard_map/ppermute | solution.py:326
  31.4 0.9 slice.19
  32.3 1.0 slice.20.mine.mine_at
  33.3 1.2 collective-permute-done.1.far
  34.5 7.2 %shard_map.65 = bf16[4,1024,128]{2,1,0:T(8,128)(2,1)} custom-call(f32[2,1024]{1,0:T(2,128)S(1)} %copy-done.3, bf16[4,1552,128]{2,1,0:T(8,128)(2,1)S(1)} %all-to-all-done.near, bf16[4,1552,128]{2,1,0:T(8,128)(2,1)S(1)} %collective-permute-done.1.far, bf16[2,192,1024]{2,1,0:T(8,128)(2,1)S(1)} %bitcast.15, bf16[320,1024]{1,0:T(8,128)(2,1)} %collective-permute-done.mirrored_at), custom_call_target="tpu_custom_call" | custom-call | flops 8800000000 | tf_op jit(solution)/shard_map/pallas_call | solution.py:288
  41.7 4.3 %all-to-all-start.1 = ((bf16[4,1024,128]{2,1,0:T(8,128)(2,1)}), bf16[4,1024,128]{2,1,0:T(8,128)(2,1)}, u32[]{:S(2)}, u32[]{:S(2)}) async-start(bf16[4,1024,128]{2,1,0:T(8,128)(2,1)} %shard_map.65), calls=%async_computation.1 | async-start | bytes 2097152 | tf_op jit(solution)/shard_map/all_to_all | solution.py:323
  46.0 4.4 %collective-permute-start.2 = (bf16[4,8,64,128]{3,2,1,0:T(8,128)(2,1)}, bf16[4,8,64,128]{3,2,1,0:T(8,128)(2,1)}, u32[]{:S(2)}, u32[]{:S(2)}) collective-permute-start(bf16[4,8,64,128]{3,2,1,0:T(8,128)(2,1)} %bitcast.5), channel_id=1, source_target_pairs={{0,24},{1,25},{2,26},{3,27},{4,28},{5,29},{6,30},{7,31},{8,16},{9,... | collective-permute-start | bytes 1572872 | tf_op jit(solution)/shard_map/ppermute | solution.py:372
  50.4 1.9 %collective-permute-start.3 = (bf16[128,1024]{1,0:T(8,128)(2,1)S(1)}, bf16[128,1024]{1,0:T(8,128)(2,1)S(1)}, u32[]{:S(2)}, u32[]{:S(2)}) collective-permute-start(bf16[128,1024]{1,0:T(8,128)(2,1)S(1)} %slice.20.mine.mine_at), channel_id=1, source_target_pairs={{0,16},{1,17},{2,18},{3,19},{4,20},{5,21},{6,22},{7,23},{8,24},{9,... | collective-permute-start | bytes 786440 | tf_op jit(solution)/shard_map/ppermute | solution.py:371
  52.3 7.3 %collective-permute-done.3.other.other_at = bf16[128,1024]{1,0:T(8,128)(2,1)S(1)} collective-permute-done((bf16[128,1024]{1,0:T(8,128)(2,1)S(1)}, bf16[128,1024]{1,0:T(8,128)(2,1)S(1)}, u32[]{:S(2)}, u32[]{:S(2)}) %collective-permute-start.3) | collective-permute-done | bytes 262176 | tf_op jit(solution)/shard_map/ppermute | solution.py:371
  59.6 1.5 %shard_map.66.ready = bf16[8,128,1024]{2,1,0:T(8,128)(2,1)} custom-call(bf16[64,1024]{1,0:T(8,128)(2,1)S(1)} %get-tuple-element.37.own, bf16[128,1024]{1,0:T(8,128)(2,1)S(1)} %slice.20.mine.mine_at, bf16[128,1024]{1,0:T(8,128)(2,1)S(1)} %collective-permute-done.3.other.other_at), custom_call_target="tpu_custom_call" | custom-call | flops 1100000000 | tf_op jit(solution)/shard_map/pallas_call | solution.py:288
  61.0 1.5 %collective-permute-done.2.w_mir = bf16[4,8,64,128]{3,2,1,0:T(8,128)(2,1)} collective-permute-done((bf16[4,8,64,128]{3,2,1,0:T(8,128)(2,1)}, bf16[4,8,64,128]{3,2,1,0:T(8,128)(2,1)}, u32[]{:S(2)}, u32[]{:S(2)}) %collective-permute-start.2) | collective-permute-done | bytes 524320 | tf_op jit(solution)/shard_map/ppermute | solution.py:372
  62.5 3.1 %collective-permute-start.4 = (bf16[4,1024,128]{2,1,0:T(8,128)(2,1)}, bf16[4,1024,128]{2,1,0:T(8,128)(2,1)}, u32[]{:S(2)}, u32[]{:S(2)}) collective-permute-start(bf16[4,1024,128]{2,1,0:T(8,128)(2,1)} %all-to-all-done.1.o_near), channel_id=1, source_target_pairs={{0,1},{1,0},{2,3},{3,2},{4,5},{5,4},{6,7},{7,6},{8,9},{9,8},{10,11... | collective-permute-start | bytes 3145736 | tf_op jit(solution)/shard_map/ppermute | solution.py:326
  65.6 1.9 %collective-permute-start.5 = (bf16[4,8,64,128]{3,2,1,0:T(8,128)(2,1)}, bf16[4,8,64,128]{3,2,1,0:T(8,128)(2,1)}, u32[]{:S(2)}, u32[]{:S(2)}) collective-permute-start(bf16[4,8,64,128]{3,2,1,0:T(8,128)(2,1)} %collective-permute-done.2.w_mir), channel_id=1, source_target_pairs={{0,1},{1,0},{2,3},{3,2},{4,5},{5,4},{6,7},{7,6},{8,9},{9,8},{10,11... | collective-permute-start | bytes 1572872 | tf_op jit(solution)/shard_map/ppermute | solution.py:326
  67.6 5.0 %all-to-all-start.2 = ((bf16[8,128,1024]{2,1,0:T(8,128)(2,1)}), bf16[8,128,1024]{2,1,0:T(8,128)(2,1)S(1)}, u32[]{:S(2)}, u32[]{:S(2)}) async-start(bf16[8,128,1024]{2,1,0:T(8,128)(2,1)} %shard_map.66.ready), calls=%async_computation.2 | async-start | bytes 4194304 | tf_op jit(solution)/shard_map/all_to_all | solution.py:381
  72.5 0.0 collective-permute-done.5.w_mir_far
  72.6 8.7 %shard_map.67 = (bf16[2,512,128]{2,1,0:T(8,128)(2,1)S(1)}, bf16[1040,128]{1,0:T(8,128)(2,1)S(1)}, bf16[1040,128]{1,0:T(8,128)(2,1)S(1)}, bf16[128,1024]{1,0:T(8,128)(2,1)S(1)}) custom-call(f32[2,1024]{1,0:T(2,128)S(1)} %copy-done.3, bf16[4,1024,128]{2,1,0:T(8,128)(2,1)} %all-to-all-done.1.o_near, bf16[4,1024,128]{2,1,0:T(8,128)(2,1)} %collective-permute-done.4.o_far, ...), custom_call_target="tpu_custom_call" | custom-call | flops 8800000000 | tf_op jit(solution)/shard_map/pallas_call | solution.py:288
  81.3 3.5 %collective-permute-start.7 = (bf16[1040,128]{1,0:T(8,128)(2,1)S(1)}, bf16[1040,128]{1,0:T(8,128)(2,1)S(1)}, u32[]{:S(2)}, u32[]{:S(2)}) collective-permute-start(bf16[1040,128]{1,0:T(8,128)(2,1)S(1)} %get-tuple-element.31.refs_1_), channel_id=1, source_target_pairs={{0,8},{1,9},{2,10},{3,11},{4,12},{5,13},{6,14},{7,15},{8,0},{9,1},... | collective-permute-start | bytes 798728 | tf_op jit(solution)/shard_map/ppermute | solution.py:401
  84.8 12.0 %collective-permute-start.6 = (bf16[1040,128]{1,0:T(8,128)(2,1)S(1)}, bf16[1040,128]{1,0:T(8,128)(2,1)S(1)}, u32[]{:S(2)}, u32[]{:S(2)}) collective-permute-start(bf16[1040,128]{1,0:T(8,128)(2,1)S(1)} %get-tuple-element.30.refs_1_), channel_id=1, source_target_pairs={{0,504},{1,505},{2,506},{3,507},{4,508},{5,509},{6,510},{7,511},{8... | collective-permute-start | bytes 798728 | tf_op jit(solution)/shard_map/ppermute | solution.py:401
  96.8 2.2 %shard_map.68.refs_3_ = bf16[4,128,128]{2,1,0:T(8,128)(2,1)S(1)} custom-call(bf16[2,512,128]{2,1,0:T(8,128)(2,1)S(1)} %get-tuple-element.29.refs_0_, bf16[1040,128]{1,0:T(8,128)(2,1)S(1)} %get-tuple-element.31.refs_1_, bf16[1040,128]{1,0:T(8,128)(2,1)S(1)} %collective-permute-done.7.refs_2_), custom_call_target="tpu_custom_call" | custom-call | tf_op jit(solution)/shard_map/pallas_call | solution.py:288
  98.9 5.1 %collective-permute-done.6.refs_2_ = bf16[1040,128]{1,0:T(8,128)(2,1)S(1)} collective-permute-done((bf16[1040,128]{1,0:T(8,128)(2,1)S(1)}, bf16[1040,128]{1,0:T(8,128)(2,1)S(1)}, u32[]{:S(2)}, u32[]{:S(2)}) %collective-permute-start.6) | collective-permute-done | bytes 266272 | tf_op jit(solution)/shard_map/ppermute | solution.py:401
  104.1 2.2 %shard_map.69 = bf16[8,128,128]{2,1,0:T(8,128)(2,1)S(1)} custom-call(bf16[2,512,128]{2,1,0:T(8,128)(2,1)S(1)} %get-tuple-element.29.refs_0_, bf16[1040,128]{1,0:T(8,128)(2,1)S(1)} %get-tuple-element.30.refs_1_, bf16[1040,128]{1,0:T(8,128)(2,1)S(1)} %collective-permute-done.6.refs_2_, bf16[4,128,128]{2,1,0:T(8,128)(2,1)S(1)} %shard_map.68.refs_3_), custom_call_target="tpu_custom_call" | custom-call | flops 3300000000 | tf_op jit(solution)/shard_map/pallas_call | solution.py:288
  106.3 11.7 %all_to_all.20.parts = bf16[8,128,128]{2,1,0:T(8,128)(2,1)S(1)} all-to-all(bf16[8,128,128]{2,1,0:T(8,128)(2,1)S(1)} %shard_map.69), channel_id=1, replica_groups=mesh['z'=16,'xl'=2,'xh'=2,'y'=4,'c'=2] {'y','c'}, dimensions={0} | all-to-all | bytes 524288 | tf_op jit(solution)/shard_map/all_to_all | solution.py:418
  118.0 1.2 shard_map.70
  (15 shorter events, 0.1 us)
Async XLA Ops:
  2.5 5.2 %copy-start.4 = (bf16[2,64,1024]{2,1,0:T(8,128)(2,1)S(1)}, bf16[2,64,1024]{2,1,0:T(8,128)(2,1)}, u32[]{:S(2)}) copy-start(bf16[2,64,1024]{2,1,0:T(8,128)(2,1)} %w_at.1) | copy-start | bytes 786436
  2.5 5.2 %copy-start.1 = (bf16[2,1024,192]{1,2,0:T(8,128)(2,1)S(1)}, bf16[2,1024,192]{1,2,0:T(8,128)(2,1)}, u32[]{:S(2)}) copy-start(bf16[2,1024,192]{1,2,0:T(8,128)(2,1)} %param.10) | copy-start | bytes 2359300
  2.5 21.1 %all-to-all-start = ((bf16[4,1552,128]{2,1,0:T(8,128)(2,1)}), bf16[4,1552,128]{2,1,0:T(8,128)(2,1)S(1)}, u32[]{:S(2)}, u32[]{:S(2)}) async-start(bf16[4,1552,128]{2,1,0:T(8,128)(2,1)} %shard_map.64), calls=%async_computation | async-start | bytes 3178496 | tf_op jit(solution)/shard_map/all_to_all | solution.py:323
  7.8 26.7 %copy-start.3 = (f32[2,1024]{1,0:T(2,128)S(1)}, f32[2,1024]{1,0:T(2,128)}, u32[]{:S(2)}) copy-start(f32[2,1024]{1,0:T(2,128)} %gain.3) | copy-start | bytes 24580
  7.9 15.7 %collective-permute-start = (bf16[320,1024]{1,0:T(8,128)(2,1)S(1)}, bf16[320,1024]{1,0:T(8,128)(2,1)}, u32[]{:S(2)}, u32[]{:S(2)}) collective-permute-start(bf16[320,1024]{1,0:T(8,128)(2,1)S(1)} %pad_maximum_fusion), channel_id=1, source_target_pairs={{0,24},{1,25},{2,26},{3,27},{4,28},{5,29},{6,30},{7,31},{8,16},{9,... | collective-permute-start | bytes 1966088 | tf_op jit(solution)/shard_map/ppermute | solution.py:347
  23.6 18.1 %copy-start = (bf16[4,1552,128]{2,1,0:T(8,128)(2,1)}, bf16[4,1552,128]{2,1,0:T(8,128)(2,1)S(1)}, u32[]{:S(2)}) copy-start(bf16[4,1552,128]{2,1,0:T(8,128)(2,1)S(1)} %all-to-all-done.near) | copy-start | bytes 4767748
  23.6 10.9 %collective-permute-start.1 = (bf16[4,1552,128]{2,1,0:T(8,128)(2,1)S(1)}, bf16[4,1552,128]{2,1,0:T(8,128)(2,1)S(1)}, u32[]{:S(2)}, u32[]{:S(2)}) collective-permute-start(bf16[4,1552,128]{2,1,0:T(8,128)(2,1)S(1)} %all-to-all-done.near), channel_id=1, source_target_pairs={{0,1},{1,0},{2,3},{3,2},{4,5},{5,4},{6,7},{7,6},{8,9},{9,8},{10,11... | collective-permute-start | bytes 4767752 | tf_op jit(solution)/shard_map/ppermute | solution.py:326
  34.5 7.2 %copy-start.2 = (bf16[4,1552,128]{2,1,0:T(8,128)(2,1)}, bf16[4,1552,128]{2,1,0:T(8,128)(2,1)S(1)}, u32[]{:S(2)}) copy-start(bf16[4,1552,128]{2,1,0:T(8,128)(2,1)S(1)} %collective-permute-done.1.far) | copy-start | bytes 4767748
  41.7 20.8 %all-to-all-start.1 = ((bf16[4,1024,128]{2,1,0:T(8,128)(2,1)}), bf16[4,1024,128]{2,1,0:T(8,128)(2,1)}, u32[]{:S(2)}, u32[]{:S(2)}) async-start(bf16[4,1024,128]{2,1,0:T(8,128)(2,1)} %shard_map.65), calls=%async_computation.1 | async-start | bytes 2097152 | tf_op jit(solution)/shard_map/all_to_all | solution.py:323
  46.0 16.6 %collective-permute-start.2 = (bf16[4,8,64,128]{3,2,1,0:T(8,128)(2,1)}, bf16[4,8,64,128]{3,2,1,0:T(8,128)(2,1)}, u32[]{:S(2)}, u32[]{:S(2)}) collective-permute-start(bf16[4,8,64,128]{3,2,1,0:T(8,128)(2,1)} %bitcast.5), channel_id=1, source_target_pairs={{0,24},{1,25},{2,26},{3,27},{4,28},{5,29},{6,30},{7,31},{8,16},{9,... | collective-permute-start | bytes 1572872 | tf_op jit(solution)/shard_map/ppermute | solution.py:372
  50.4 9.2 %collective-permute-start.3 = (bf16[128,1024]{1,0:T(8,128)(2,1)S(1)}, bf16[128,1024]{1,0:T(8,128)(2,1)S(1)}, u32[]{:S(2)}, u32[]{:S(2)}) collective-permute-start(bf16[128,1024]{1,0:T(8,128)(2,1)S(1)} %slice.20.mine.mine_at), channel_id=1, source_target_pairs={{0,16},{1,17},{2,18},{3,19},{4,20},{5,21},{6,22},{7,23},{8,24},{9,... | collective-permute-start | bytes 786440 | tf_op jit(solution)/shard_map/ppermute | solution.py:371
  62.5 10.0 %collective-permute-start.4 = (bf16[4,1024,128]{2,1,0:T(8,128)(2,1)}, bf16[4,1024,128]{2,1,0:T(8,128)(2,1)}, u32[]{:S(2)}, u32[]{:S(2)}) collective-permute-start(bf16[4,1024,128]{2,1,0:T(8,128)(2,1)} %all-to-all-done.1.o_near), channel_id=1, source_target_pairs={{0,1},{1,0},{2,3},{3,2},{4,5},{5,4},{6,7},{7,6},{8,9},{9,8},{10,11... | collective-permute-start | bytes 3145736 | tf_op jit(solution)/shard_map/ppermute | solution.py:326
  65.6 6.9 %collective-permute-start.5 = (bf16[4,8,64,128]{3,2,1,0:T(8,128)(2,1)}, bf16[4,8,64,128]{3,2,1,0:T(8,128)(2,1)}, u32[]{:S(2)}, u32[]{:S(2)}) collective-permute-start(bf16[4,8,64,128]{3,2,1,0:T(8,128)(2,1)} %collective-permute-done.2.w_mir), channel_id=1, source_target_pairs={{0,1},{1,0},{2,3},{3,2},{4,5},{5,4},{6,7},{7,6},{8,9},{9,8},{10,11... | collective-permute-start | bytes 1572872 | tf_op jit(solution)/shard_map/ppermute | solution.py:326
  67.6 38.7 %all-to-all-start.2 = ((bf16[8,128,1024]{2,1,0:T(8,128)(2,1)}), bf16[8,128,1024]{2,1,0:T(8,128)(2,1)S(1)}, u32[]{:S(2)}, u32[]{:S(2)}) async-start(bf16[8,128,1024]{2,1,0:T(8,128)(2,1)} %shard_map.66.ready), calls=%async_computation.2 | async-start | bytes 4194304 | tf_op jit(solution)/shard_map/all_to_all | solution.py:381
  81.3 15.5 %collective-permute-start.7 = (bf16[1040,128]{1,0:T(8,128)(2,1)S(1)}, bf16[1040,128]{1,0:T(8,128)(2,1)S(1)}, u32[]{:S(2)}, u32[]{:S(2)}) collective-permute-start(bf16[1040,128]{1,0:T(8,128)(2,1)S(1)} %get-tuple-element.31.refs_1_), channel_id=1, source_target_pairs={{0,8},{1,9},{2,10},{3,11},{4,12},{5,13},{6,14},{7,15},{8,0},{9,1},... | collective-permute-start | bytes 798728 | tf_op jit(solution)/shard_map/ppermute | solution.py:401
  84.8 19.3 %collective-permute-start.6 = (bf16[1040,128]{1,0:T(8,128)(2,1)S(1)}, bf16[1040,128]{1,0:T(8,128)(2,1)S(1)}, u32[]{:S(2)}, u32[]{:S(2)}) collective-permute-start(bf16[1040,128]{1,0:T(8,128)(2,1)S(1)} %get-tuple-element.30.refs_1_), channel_id=1, source_target_pairs={{0,504},{1,505},{2,506},{3,507},{4,508},{5,509},{6,510},{7,511},{8... | collective-permute-start | bytes 798728 | tf_op jit(solution)/shard_map/ppermute | solution.py:401

commit v12 on v11

--- a/solution.py
+++ b/solution.py
@@ -367,15 +367,13 @@
         )
         w_own = near[:, EXT:].reshape(4, BLOCKS, HEAD_DIM, LANES)
         share_far = first_far[3 * HEAD_DIM :]
-        o_copies, w_own, share_far = lax.optimization_barrier((o_copies, w_own, share_far))
         rest_far = lax.ppermute(share_far, AXES, beside)
+        o_copies, w_own, rest_far = lax.optimization_barrier((o_copies, w_own, rest_far))
         w_mir = lax.ppermute(w_own, AXES, mirror)
         (shares,) = call(
             relay_kernel, 1, [(8, ROWS, D)], [], w_out[1], share_far, rest_far, megabytes=4
         )
-        o_near, w_mir, rest_far, shares = lax.optimization_barrier(
-            (over_y(o_copies), w_mir, rest_far, shares)
-        )
+        o_near, shares = lax.optimization_barrier((over_y(o_copies), shares))
         o_far = swapped(o_near)
         w_mir_far = swapped(w_mir)
         w_last = lax.all_to_all(shares, ("y", "c"), 0, 0, tiled=True).reshape(D, D)

time: 120 us -> 119 us (level)
    all_to_all x2, waiting for transfers between devices: 0.01 us -> 9.73 us  [over_y(): return lax.all_to_all(copies, 'y', 0, 0, tiled=True)]
    ppermute x1, waiting for transfers between devices: 7.27 us -> 0.01 us  [on_device(): rest_far = lax.ppermute(share_far, AXES, beside)]
    ppermute x1, waiting for transfers between devices: 1.49 us -> 0.01 us  [on_device(): w_mir = lax.ppermute(w_own, AXES, mirror)]
    ppermute x1, starting transfers between devices: 1.92 us -> 3.12 us  [on_device(): rest_far = lax.ppermute(share_far, AXES, beside)]
  transfers between devices with their start and end apart: 11 -> 11, of which waited for: 5 -> 3; matrix products, arithmetic and copies ran while one was open for 2% -> 2% of each run, Pallas kernels for 12% -> 18%
where the time goes in v12:
time: 119 us; the launch traced here: 118 us
  starting transfers between devices  53.4 us (45%)
  Pallas kernels  25.4 us (21%)
  waiting for transfers between devices  25.2 us (21%)
  blocking collectives  11.9 us (10%)
  local copies, waits for them, and re-layouts  1.92 us (2%)
    pallas_call x7, Pallas kernels, call(): pl.pallas_call(kernel, out_shape=[jax.ShapeDtypeStruct(shape, BF16) for s...  25.4 us
    ppermute x2, starting transfers between devices, on_device(): lax.ppermute(kv, AXES, links)  15.7 us
    ppermute x3, starting transfers between devices, swapped(): return lax.ppermute(array, AXES, other_core)  12.7 us
    all_to_all x1, blocking collectives, on_device(): parts = lax.all_to_all(parts, ('y', 'c'), 0, 0, tiled=True)  11.9 us
    ppermute x1, waiting for transfers between devices, on_device(): first_far = lax.ppermute(first, AXES, mirror)  11.3 us
    all_to_all x2, waiting for transfers between devices, over_y(): return lax.all_to_all(copies, 'y', 0, 0, tiled=True)  9.73 us
    all_to_all x2, starting transfers between devices, over_y(): return lax.all_to_all(copies, 'y', 0, 0, tiled=True)  9.41 us
    ppermute x1, starting transfers between devices, on_device(): first_far = lax.ppermute(first, AXES, mirror)  4.39 us
  transfers between devices with their start and end apart: 11, of which 3 were waited for; matrix products, arithmetic and copies ran while one was open for 2% of the time, Pallas kernels for 18%

profile of v12, /device:TPU:1, one launch (start us, length us, event | category | flops | bytes accessed | tf_op | source)
XLA Modules:
  0.0 118.2 jit_solution(15465049089921208595)
XLA Ops:
  0.0 2.5 %shard_map.64 = bf16[4,1552,128]{2,1,0:T(8,128)(2,1)} custom-call(bf16[128,1024]{1,0:T(8,128)(2,1)} %points_at.1, s32[1,128]{1,0:T(1,128)} %order_at.1, s32[1,128]{1,0:T(1,128)} %bitcast.16, bf16[2,64,1024]{2,1,0:T(8,128)(2,1)} %w_at.1), custom_call_target="tpu_custom_call" | custom-call | flops 1320000000 | tf_op jit(solution)/shard_map/pallas_call | solution.py:288
  2.5 0.0 copy-start.4
  2.5 0.0 copy-start.1
  2.5 5.2 %all-to-all-start = ((bf16[4,1552,128]{2,1,0:T(8,128)(2,1)}), bf16[4,1552,128]{2,1,0:T(8,128)(2,1)S(1)}, u32[]{:S(2)}, u32[]{:S(2)}) async-start(bf16[4,1552,128]{2,1,0:T(8,128)(2,1)} %shard_map.64), calls=%async_computation | async-start | bytes 3178496 | tf_op jit(solution)/shard_map/all_to_all | solution.py:323
  7.8 0.1 slice_bitcast_fusion
  7.8 0.0 copy-start.3
  7.9 4.4 %collective-permute-start = (bf16[320,1024]{1,0:T(8,128)(2,1)S(1)}, bf16[320,1024]{1,0:T(8,128)(2,1)}, u32[]{:S(2)}, u32[]{:S(2)}) collective-permute-start(bf16[320,1024]{1,0:T(8,128)(2,1)S(1)} %pad_maximum_fusion), channel_id=1, source_target_pairs={{0,24},{1,25},{2,26},{3,27},{4,28},{5,29},{6,30},{7,31},{8,16},{9,... | collective-permute-start | bytes 1966088 | tf_op jit(solution)/shard_map/ppermute | solution.py:347
  12.3 11.3 %collective-permute-done.mirrored_at = bf16[320,1024]{1,0:T(8,128)(2,1)} collective-permute-done((bf16[320,1024]{1,0:T(8,128)(2,1)S(1)}, bf16[320,1024]{1,0:T(8,128)(2,1)}, u32[]{:S(2)}, u32[]{:S(2)}) %collective-permute-start) | collective-permute-done | bytes 655392 | tf_op jit(solution)/shard_map/ppermute | solution.py:347
  23.6 0.0 all-to-all-done.near
  23.6 7.8 %collective-permute-start.1 = (bf16[4,1552,128]{2,1,0:T(8,128)(2,1)S(1)}, bf16[4,1552,128]{2,1,0:T(8,128)(2,1)S(1)}, u32[]{:S(2)}, u32[]{:S(2)}) collective-permute-start(bf16[4,1552,128]{2,1,0:T(8,128)(2,1)S(1)} %all-to-all-done.near), channel_id=1, source_target_pairs={{0,1},{1,0},{2,3},{3,2},{4,5},{5,4},{6,7},{7,6},{8,9},{9,8},{10,11... | collective-permute-start | bytes 4767752 | tf_op jit(solution)/shard_map/ppermute | solution.py:326
  31.4 0.8 slice.19
  32.3 1.0 slice.20.mine.mine_at
  33.2 3.1 %collective-permute-start.2 = (bf16[128,1024]{1,0:T(8,128)(2,1)S(1)}, bf16[128,1024]{1,0:T(8,128)(2,1)S(1)}, u32[]{:S(2)}, u32[]{:S(2)}) collective-permute-start(bf16[128,1024]{1,0:T(8,128)(2,1)S(1)} %slice.20.mine.mine_at), channel_id=1, source_target_pairs={{0,16},{1,17},{2,18},{3,19},{4,20},{5,21},{6,22},{7,23},{8,24},{9,... | collective-permute-start | bytes 786440 | tf_op jit(solution)/shard_map/ppermute | solution.py:370
  36.4 0.0 collective-permute-done.1.far
  36.4 7.2 %shard_map.65 = bf16[4,1024,128]{2,1,0:T(8,128)(2,1)} custom-call(f32[2,1024]{1,0:T(2,128)S(1)} %copy-done.3, bf16[4,1552,128]{2,1,0:T(8,128)(2,1)S(1)} %all-to-all-done.near, bf16[4,1552,128]{2,1,0:T(8,128)(2,1)S(1)} %collective-permute-done.1.far, bf16[2,192,1024]{2,1,0:T(8,128)(2,1)S(1)} %bitcast.15, bf16[320,1024]{1,0:T(8,128)(2,1)} %collective-permute-done.mirrored_at), custom_call_target="tpu_custom_call" | custom-call | flops 8800000000 | tf_op jit(solution)/shard_map/pallas_call | solution.py:288
  43.6 0.0 collective-permute-done.2.other.other_at
  43.6 4.3 %all-to-all-start.1 = ((bf16[4,1024,128]{2,1,0:T(8,128)(2,1)}), bf16[4,1024,128]{2,1,0:T(8,128)(2,1)}, u32[]{:S(2)}, u32[]{:S(2)}) async-start(bf16[4,1024,128]{2,1,0:T(8,128)(2,1)} %shard_map.65), calls=%async_computation.1 | async-start | bytes 2097152 | tf_op jit(solution)/shard_map/all_to_all | solution.py:323
  47.9 3.8 %collective-permute-start.4 = (bf16[4,8,64,128]{3,2,1,0:T(8,128)(2,1)}, bf16[4,8,64,128]{3,2,1,0:T(8,128)(2,1)}, u32[]{:S(2)}, u32[]{:S(2)}) collective-permute-start(bf16[4,8,64,128]{3,2,1,0:T(8,128)(2,1)} %bitcast.5), channel_id=1, source_target_pairs={{0,24},{1,25},{2,26},{3,27},{4,28},{5,29},{6,30},{7,31},{8,16},{9,... | collective-permute-start | bytes 1572872 | tf_op jit(solution)/shard_map/ppermute | solution.py:372
  51.7 1.5 %shard_map.66.ready = bf16[8,128,1024]{2,1,0:T(8,128)(2,1)} custom-call(bf16[64,1024]{1,0:T(8,128)(2,1)S(1)} %get-tuple-element.33.own, bf16[128,1024]{1,0:T(8,128)(2,1)S(1)} %slice.20.mine.mine_at, bf16[128,1024]{1,0:T(8,128)(2,1)S(1)} %collective-permute-done.2.other.other_at), custom_call_target="tpu_custom_call" | custom-call | flops 1100000000 | tf_op jit(solution)/shard_map/pallas_call | solution.py:288
  53.2 9.7 %all-to-all-done.1.o_near = bf16[4,1024,128]{2,1,0:T(8,128)(2,1)} async-done(((bf16[4,1024,128]{2,1,0:T(8,128)(2,1)}), bf16[4,1024,128]{2,1,0:T(8,128)(2,1)}, u32[]{:S(2)}, u32[]{:S(2)}) %all-to-all-start.1) | async-done | bytes 1048608 | tf_op jit(solution)/shard_map/all_to_all | solution.py:323
  62.9 3.0 %collective-permute-start.3 = (bf16[4,1024,128]{2,1,0:T(8,128)(2,1)}, bf16[4,1024,128]{2,1,0:T(8,128)(2,1)}, u32[]{:S(2)}, u32[]{:S(2)}) collective-permute-start(bf16[4,1024,128]{2,1,0:T(8,128)(2,1)} %all-to-all-done.1.o_near), channel_id=1, source_target_pairs={{0,1},{1,0},{2,3},{3,2},{4,5},{5,4},{6,7},{7,6},{8,9},{9,8},{10,11... | collective-permute-start | bytes 3145736 | tf_op jit(solution)/shard_map/ppermute | solution.py:326
  65.9 1.9 %collective-permute-start.5 = (bf16[4,8,64,128]{3,2,1,0:T(8,128)(2,1)}, bf16[4,8,64,128]{3,2,1,0:T(8,128)(2,1)}, u32[]{:S(2)}, u32[]{:S(2)}) collective-permute-start(bf16[4,8,64,128]{3,2,1,0:T(8,128)(2,1)} %collective-permute-done.4.w_mir), channel_id=1, source_target_pairs={{0,1},{1,0},{2,3},{3,2},{4,5},{5,4},{6,7},{7,6},{8,9},{9,8},{10,11... | collective-permute-start | bytes 1572872 | tf_op jit(solution)/shard_map/ppermute | solution.py:326
  67.8 4.3 %all-to-all-start.2 = ((bf16[8,128,1024]{2,1,0:T(8,128)(2,1)}), bf16[8,128,1024]{2,1,0:T(8,128)(2,1)S(1)}, u32[]{:S(2)}, u32[]{:S(2)}) async-start(bf16[8,128,1024]{2,1,0:T(8,128)(2,1)} %shard_map.66.ready), calls=%async_computation.2 | async-start | bytes 4194304 | tf_op jit(solution)/shard_map/all_to_all | solution.py:379
  72.1 0.0 collective-permute-done.3.o_far
  72.2 8.7 %shard_map.67 = (bf16[2,512,128]{2,1,0:T(8,128)(2,1)S(1)}, bf16[1040,128]{1,0:T(8,128)(2,1)S(1)}, bf16[1040,128]{1,0:T(8,128)(2,1)S(1)}, bf16[128,1024]{1,0:T(8,128)(2,1)S(1)}) custom-call(f32[2,1024]{1,0:T(2,128)S(1)} %copy-done.3, bf16[4,1024,128]{2,1,0:T(8,128)(2,1)} %all-to-all-done.1.o_near, bf16[4,1024,128]{2,1,0:T(8,128)(2,1)} %collective-permute-done.3.o_far, ...), custom_call_target="tpu_custom_call" | custom-call | flops 8800000000 | tf_op jit(solution)/shard_map/pallas_call | solution.py:288
  80.9 4.1 %collective-permute-start.7 = (bf16[1040,128]{1,0:T(8,128)(2,1)S(1)}, bf16[1040,128]{1,0:T(8,128)(2,1)S(1)}, u32[]{:S(2)}, u32[]{:S(2)}) collective-permute-start(bf16[1040,128]{1,0:T(8,128)(2,1)S(1)} %get-tuple-element.27.refs_1_), channel_id=1, source_target_pairs={{0,8},{1,9},{2,10},{3,11},{4,12},{5,13},{6,14},{7,15},{8,0},{9,1},... | collective-permute-start | bytes 798728 | tf_op jit(solution)/shard_map/ppermute | solution.py:399
  85.0 11.6 %collective-permute-start.6 = (bf16[1040,128]{1,0:T(8,128)(2,1)S(1)}, bf16[1040,128]{1,0:T(8,128)(2,1)S(1)}, u32[]{:S(2)}, u32[]{:S(2)}) collective-permute-start(bf16[1040,128]{1,0:T(8,128)(2,1)S(1)} %get-tuple-element.26.refs_1_), channel_id=1, source_target_pairs={{0,504},{1,505},{2,506},{3,507},{4,508},{5,509},{6,510},{7,511},{8... | collective-permute-start | bytes 798728 | tf_op jit(solution)/shard_map/ppermute | solution.py:399
  96.6 2.2 %shard_map.68.refs_3_ = bf16[4,128,128]{2,1,0:T(8,128)(2,1)S(1)} custom-call(bf16[2,512,128]{2,1,0:T(8,128)(2,1)S(1)} %get-tuple-element.25.refs_0_, bf16[1040,128]{1,0:T(8,128)(2,1)S(1)} %get-tuple-element.27.refs_1_, bf16[1040,128]{1,0:T(8,128)(2,1)S(1)} %collective-permute-done.7.refs_2_), custom_call_target="tpu_custom_call" | custom-call | tf_op jit(solution)/shard_map/pallas_call | solution.py:288
  98.8 4.2 %collective-permute-done.6.refs_2_ = bf16[1040,128]{1,0:T(8,128)(2,1)S(1)} collective-permute-done((bf16[1040,128]{1,0:T(8,128)(2,1)S(1)}, bf16[1040,128]{1,0:T(8,128)(2,1)S(1)}, u32[]{:S(2)}, u32[]{:S(2)}) %collective-permute-start.6) | collective-permute-done | bytes 266272 | tf_op jit(solution)/shard_map/ppermute | solution.py:399
  102.9 2.2 %shard_map.69 = bf16[8,128,128]{2,1,0:T(8,128)(2,1)S(1)} custom-call(bf16[2,512,128]{2,1,0:T(8,128)(2,1)S(1)} %get-tuple-element.25.refs_0_, bf16[1040,128]{1,0:T(8,128)(2,1)S(1)} %get-tuple-element.26.refs_1_, bf16[1040,128]{1,0:T(8,128)(2,1)S(1)} %collective-permute-done.6.refs_2_, bf16[4,128,128]{2,1,0:T(8,128)(2,1)S(1)} %shard_map.68.refs_3_), custom_call_target="tpu_custom_call" | custom-call | flops 3300000000 | tf_op jit(solution)/shard_map/pallas_call | solution.py:288
  105.1 11.9 %all_to_all.20.parts = bf16[8,128,128]{2,1,0:T(8,128)(2,1)S(1)} all-to-all(bf16[8,128,128]{2,1,0:T(8,128)(2,1)S(1)} %shard_map.69), channel_id=1, replica_groups=mesh['z'=16,'xl'=2,'xh'=2,'y'=4,'c'=2] {'y','c'}, dimensions={0} | all-to-all | bytes 524288 | tf_op jit(solution)/shard_map/all_to_all | solution.py:416
  117.0 1.2 shard_map.70
  (15 shorter events, 0.1 us)
Async XLA Ops:
  2.5 5.2 %copy-start.4 = (bf16[2,64,1024]{2,1,0:T(8,128)(2,1)S(1)}, bf16[2,64,1024]{2,1,0:T(8,128)(2,1)}, u32[]{:S(2)}) copy-start(bf16[2,64,1024]{2,1,0:T(8,128)(2,1)} %w_at.1) | copy-start | bytes 786436
  2.5 5.2 %copy-start.1 = (bf16[2,1024,192]{1,2,0:T(8,128)(2,1)S(1)}, bf16[2,1024,192]{1,2,0:T(8,128)(2,1)}, u32[]{:S(2)}) copy-start(bf16[2,1024,192]{1,2,0:T(8,128)(2,1)} %param.10) | copy-start | bytes 2359300
  2.5 21.1 %all-to-all-start = ((bf16[4,1552,128]{2,1,0:T(8,128)(2,1)}), bf16[4,1552,128]{2,1,0:T(8,128)(2,1)S(1)}, u32[]{:S(2)}, u32[]{:S(2)}) async-start(bf16[4,1552,128]{2,1,0:T(8,128)(2,1)} %shard_map.64), calls=%async_computation | async-start | bytes 3178496 | tf_op jit(solution)/shard_map/all_to_all | solution.py:323
  7.8 28.6 %copy-start.3 = (f32[2,1024]{1,0:T(2,128)S(1)}, f32[2,1024]{1,0:T(2,128)}, u32[]{:S(2)}) copy-start(f32[2,1024]{1,0:T(2,128)} %gain.3) | copy-start | bytes 24580
  7.9 15.7 %collective-permute-start = (bf16[320,1024]{1,0:T(8,128)(2,1)S(1)}, bf16[320,1024]{1,0:T(8,128)(2,1)}, u32[]{:S(2)}, u32[]{:S(2)}) collective-permute-start(bf16[320,1024]{1,0:T(8,128)(2,1)S(1)} %pad_maximum_fusion), channel_id=1, source_target_pairs={{0,24},{1,25},{2,26},{3,27},{4,28},{5,29},{6,30},{7,31},{8,16},{9,... | collective-permute-start | bytes 1966088 | tf_op jit(solution)/shard_map/ppermute | solution.py:347
  23.6 20.0 %copy-start = (bf16[4,1552,128]{2,1,0:T(8,128)(2,1)}, bf16[4,1552,128]{2,1,0:T(8,128)(2,1)S(1)}, u32[]{:S(2)}) copy-start(bf16[4,1552,128]{2,1,0:T(8,128)(2,1)S(1)} %all-to-all-done.near) | copy-start | bytes 4767748
  23.6 12.7 %collective-permute-start.1 = (bf16[4,1552,128]{2,1,0:T(8,128)(2,1)S(1)}, bf16[4,1552,128]{2,1,0:T(8,128)(2,1)S(1)}, u32[]{:S(2)}, u32[]{:S(2)}) collective-permute-start(bf16[4,1552,128]{2,1,0:T(8,128)(2,1)S(1)} %all-to-all-done.near), channel_id=1, source_target_pairs={{0,1},{1,0},{2,3},{3,2},{4,5},{5,4},{6,7},{7,6},{8,9},{9,8},{10,11... | collective-permute-start | bytes 4767752 | tf_op jit(solution)/shard_map/ppermute | solution.py:326
  33.2 10.4 %collective-permute-start.2 = (bf16[128,1024]{1,0:T(8,128)(2,1)S(1)}, bf16[128,1024]{1,0:T(8,128)(2,1)S(1)}, u32[]{:S(2)}, u32[]{:S(2)}) collective-permute-start(bf16[128,1024]{1,0:T(8,128)(2,1)S(1)} %slice.20.mine.mine_at), channel_id=1, source_target_pairs={{0,16},{1,17},{2,18},{3,19},{4,20},{5,21},{6,22},{7,23},{8,24},{9,... | collective-permute-start | bytes 786440 | tf_op jit(solution)/shard_map/ppermute | solution.py:370
  36.4 7.2 %copy-start.2 = (bf16[4,1552,128]{2,1,0:T(8,128)(2,1)}, bf16[4,1552,128]{2,1,0:T(8,128)(2,1)S(1)}, u32[]{:S(2)}) copy-start(bf16[4,1552,128]{2,1,0:T(8,128)(2,1)S(1)} %collective-permute-done.1.far) | copy-start | bytes 4767748
  43.6 19.3 %all-to-all-start.1 = ((bf16[4,1024,128]{2,1,0:T(8,128)(2,1)}), bf16[4,1024,128]{2,1,0:T(8,128)(2,1)}, u32[]{:S(2)}, u32[]{:S(2)}) async-start(bf16[4,1024,128]{2,1,0:T(8,128)(2,1)} %shard_map.65), calls=%async_computation.1 | async-start | bytes 2097152 | tf_op jit(solution)/shard_map/all_to_all | solution.py:323
  47.9 18.0 %collective-permute-start.4 = (bf16[4,8,64,128]{3,2,1,0:T(8,128)(2,1)}, bf16[4,8,64,128]{3,2,1,0:T(8,128)(2,1)}, u32[]{:S(2)}, u32[]{:S(2)}) collective-permute-start(bf16[4,8,64,128]{3,2,1,0:T(8,128)(2,1)} %bitcast.5), channel_id=1, source_target_pairs={{0,24},{1,25},{2,26},{3,27},{4,28},{5,29},{6,30},{7,31},{8,16},{9,... | collective-permute-start | bytes 1572872 | tf_op jit(solution)/shard_map/ppermute | solution.py:372
  62.9 9.3 %collective-permute-start.3 = (bf16[4,1024,128]{2,1,0:T(8,128)(2,1)}, bf16[4,1024,128]{2,1,0:T(8,128)(2,1)}, u32[]{:S(2)}, u32[]{:S(2)}) collective-permute-start(bf16[4,1024,128]{2,1,0:T(8,128)(2,1)} %all-to-all-done.1.o_near), channel_id=1, source_target_pairs={{0,1},{1,0},{2,3},{3,2},{4,5},{5,4},{6,7},{7,6},{8,9},{9,8},{10,11... | collective-permute-start | bytes 3145736 | tf_op jit(solution)/shard_map/ppermute | solution.py:326
  65.9 6.2 %collective-permute-start.5 = (bf16[4,8,64,128]{3,2,1,0:T(8,128)(2,1)}, bf16[4,8,64,128]{3,2,1,0:T(8,128)(2,1)}, u32[]{:S(2)}, u32[]{:S(2)}) collective-permute-start(bf16[4,8,64,128]{3,2,1,0:T(8,128)(2,1)} %collective-permute-done.4.w_mir), channel_id=1, source_target_pairs={{0,1},{1,0},{2,3},{3,2},{4,5},{5,4},{6,7},{7,6},{8,9},{9,8},{10,11... | collective-permute-start | bytes 1572872 | tf_op jit(solution)/shard_map/ppermute | solution.py:326
  67.8 37.3 %all-to-all-start.2 = ((bf16[8,128,1024]{2,1,0:T(8,128)(2,1)}), bf16[8,128,1024]{2,1,0:T(8,128)(2,1)S(1)}, u32[]{:S(2)}, u32[]{:S(2)}) async-start(bf16[8,128,1024]{2,1,0:T(8,128)(2,1)} %shard_map.66.ready), calls=%async_computation.2 | async-start | bytes 4194304 | tf_op jit(solution)/shard_map/all_to_all | solution.py:379
  80.9 15.7 %collective-permute-start.7 = (bf16[1040,128]{1,0:T(8,128)(2,1)S(1)}, bf16[1040,128]{1,0:T(8,128)(2,1)S(1)}, u32[]{:S(2)}, u32[]{:S(2)}) collective-permute-start(bf16[1040,128]{1,0:T(8,128)(2,1)S(1)} %get-tuple-element.27.refs_1_), channel_id=1, source_target_pairs={{0,8},{1,9},{2,10},{3,11},{4,12},{5,13},{6,14},{7,15},{8,0},{9,1},... | collective-permute-start | bytes 798728 | tf_op jit(solution)/shard_map/ppermute | solution.py:399
  85.0 18.0 %collective-permute-start.6 = (bf16[1040,128]{1,0:T(8,128)(2,1)S(1)}, bf16[1040,128]{1,0:T(8,128)(2,1)S(1)}, u32[]{:S(2)}, u32[]{:S(2)}) collective-permute-start(bf16[1040,128]{1,0:T(8,128)(2,1)S(1)} %get-tuple-element.26.refs_1_), channel_id=1, source_target_pairs={{0,504},{1,505},{2,506},{3,507},{4,508},{5,509},{6,510},{7,511},{8... | collective-permute-start | bytes 798728 | tf_op jit(solution)/shard_map/ppermute | solution.py:399

commit v13 on v12

--- a/solution.py
+++ b/solution.py
@@ -173,17 +173,18 @@
             else:
                 sources.append(ref.at[g, EXT:FULL, :].reshape(BLOCKS, HEAD_DIM, LANES))
             targets.append(w.at[:, row : row + HEAD_DIM, :])
-    w_copies = fetch(sources, targets, w_sems)
-
+    w_copies = fetch(sources[:8], targets[:8], w_sems.at[:8])
+    o_copies = fetch((o_near,), (heads.at[:4],), o_sems.at[:1])
+    w_copies += fetch(sources[8:], targets[8:], w_sems.at[8:])
     xl = lax.axis_index("xl")
     at_mine, at_other = [
         pl.ds(pl.multiple_of(k * QKV_PART, QKV_PART), QKV_PART) for k in (xl, 1 - xl)
     ]
     top, end = slice(0, HALF), slice(HALF, PATCH)
-    o_copies = fetch(
-        (o_near, o_far.at[:, end, :], o_far.at[:, top, :]),
-        (heads.at[:4], heads.at[4:, top, :], heads.at[4:, end, :]),
-        o_sems,
+    o_copies += fetch(
+        (o_far.at[:, end, :], o_far.at[:, top, :]),
+        (heads.at[4:, top, :], heads.at[4:, end, :]),
+        o_sems.at[1:],
     )
     x_copies = fetch((near.at[:, :EXT, :], far.at[:, :EXT, :]), (points.at[0], points.at[1]), sems)
     late = fetch(
@@ -191,12 +192,16 @@
         (own, mirrored.at[at_mine, :], mirrored.at[at_other, :]),
         sems.at[2:5],
     )
-    for copy in w_copies + o_copies:
-        copy.wait()
-    left = jnp.concatenate([heads[g] for g in range(BLOCKS)], axis=1)
-    for j in range(2):
-        both = jnp.concatenate([w[4 * j + i] for i in range(4)], axis=1)
-        update[:, j * 512 : (j + 1) * 512] = dot(left, both)
+    for side in range(2):
+        for copy in w_copies[side * 8 : (side + 1) * 8] + (o_copies[1:] if side else o_copies[:1]):
+            copy.wait()
+        depth = slice(side * HALF, (side + 1) * HALF)
+        left = jnp.concatenate([heads[side * 4 + g] for g in range(4)], axis=1)
+        for j in range(2):
+            both = jnp.concatenate([w[4 * j + i, depth, :] for i in range(4)], axis=1)
+            cut = slice(j * HALF, (j + 1) * HALF)
+            product = dot(left, both)
+            update[:, cut] = update[:, cut] + product if side else product
     rows = []
     for s in range(2):
         x_copies[s].wait()

time: 119 us -> 118 us (level)
  no operation moved by 1% of the time
where the time goes in v13:
time: 118 us; the launch traced here: 117 us
  starting transfers between devices  53.2 us (45%)
  waiting for transfers between devices  25.3 us (21%)
  Pallas kernels  24.8 us (21%)
  blocking collectives  12 us (10%)
  local copies, waits for them, and re-layouts  1.92 us (2%)
    pallas_call x7, Pallas kernels, call(): pl.pallas_call(kernel, out_shape=[jax.ShapeDtypeStruct(shape, BF16) for s...  24.8 us
    ppermute x2, starting transfers between devices, on_device(): lax.ppermute(kv, AXES, links)  15.5 us
    ppermute x3, starting transfers between devices, swapped(): return lax.ppermute(array, AXES, other_core)  12.7 us
    all_to_all x1, blocking collectives, on_device(): parts = lax.all_to_all(parts, ('y', 'c'), 0, 0, tiled=True)  12 us
    ppermute x1, waiting for transfers between devices, on_device(): first_far = lax.ppermute(first, AXES, mirror)  11.3 us
    all_to_all x2, waiting for transfers between devices, over_y(): return lax.all_to_all(copies, 'y', 0, 0, tiled=True)  9.73 us
    all_to_all x2, starting transfers between devices, over_y(): return lax.all_to_all(copies, 'y', 0, 0, tiled=True)  9.41 us
    ppermute x1, starting transfers between devices, on_device(): first_far = lax.ppermute(first, AXES, mirror)  4.39 us
  transfers between devices with their start and end apart: 11, of which 3 were waited for; matrix products, arithmetic and copies ran while one was open for 2% of the time, Pallas kernels for 18%

profile of v13, /device:TPU:1, one launch (start us, length us, event | category | flops | bytes accessed | tf_op | source)
XLA Modules:
  0.0 117.5 jit_solution(1202673228291823658)
XLA Ops:
  0.0 2.5 %shard_map.64 = bf16[4,1552,128]{2,1,0:T(8,128)(2,1)} custom-call(bf16[128,1024]{1,0:T(8,128)(2,1)} %points_at.1, s32[1,128]{1,0:T(1,128)} %order_at.1, s32[1,128]{1,0:T(1,128)} %bitcast.16, bf16[2,64,1024]{2,1,0:T(8,128)(2,1)} %w_at.1), custom_call_target="tpu_custom_call" | custom-call | flops 1320000000 | tf_op jit(solution)/shard_map/pallas_call | solution.py:293
  2.5 0.0 copy-start.4
  2.5 0.0 copy-start.1
  2.5 5.2 %all-to-all-start = ((bf16[4,1552,128]{2,1,0:T(8,128)(2,1)}), bf16[4,1552,128]{2,1,0:T(8,128)(2,1)S(1)}, u32[]{:S(2)}, u32[]{:S(2)}) async-start(bf16[4,1552,128]{2,1,0:T(8,128)(2,1)} %shard_map.64), calls=%async_computation | async-start | bytes 3178496 | tf_op jit(solution)/shard_map/all_to_all | solution.py:328
  7.8 0.1 slice_bitcast_fusion
  7.8 0.0 copy-start.3
  7.9 4.4 %collective-permute-start = (bf16[320,1024]{1,0:T(8,128)(2,1)S(1)}, bf16[320,1024]{1,0:T(8,128)(2,1)}, u32[]{:S(2)}, u32[]{:S(2)}) collective-permute-start(bf16[320,1024]{1,0:T(8,128)(2,1)S(1)} %pad_maximum_fusion), channel_id=1, source_target_pairs={{0,24},{1,25},{2,26},{3,27},{4,28},{5,29},{6,30},{7,31},{8,16},{9,... | collective-permute-start | bytes 1966088 | tf_op jit(solution)/shard_map/ppermute | solution.py:352
  12.3 11.3 %collective-permute-done.mirrored_at = bf16[320,1024]{1,0:T(8,128)(2,1)} collective-permute-done((bf16[320,1024]{1,0:T(8,128)(2,1)S(1)}, bf16[320,1024]{1,0:T(8,128)(2,1)}, u32[]{:S(2)}, u32[]{:S(2)}) %collective-permute-start) | collective-permute-done | bytes 655392 | tf_op jit(solution)/shard_map/ppermute | solution.py:352
  23.6 0.0 all-to-all-done.near
  23.6 7.8 %collective-permute-start.1 = (bf16[4,1552,128]{2,1,0:T(8,128)(2,1)S(1)}, bf16[4,1552,128]{2,1,0:T(8,128)(2,1)S(1)}, u32[]{:S(2)}, u32[]{:S(2)}) collective-permute-start(bf16[4,1552,128]{2,1,0:T(8,128)(2,1)S(1)} %all-to-all-done.near), channel_id=1, source_target_pairs={{0,1},{1,0},{2,3},{3,2},{4,5},{5,4},{6,7},{7,6},{8,9},{9,8},{10,11... | collective-permute-start | bytes 4767752 | tf_op jit(solution)/shard_map/ppermute | solution.py:331
  31.4 0.8 slice.19
  32.3 1.0 slice.20.mine.mine_at
  33.2 3.1 %collective-permute-start.2 = (bf16[128,1024]{1,0:T(8,128)(2,1)S(1)}, bf16[128,1024]{1,0:T(8,128)(2,1)S(1)}, u32[]{:S(2)}, u32[]{:S(2)}) collective-permute-start(bf16[128,1024]{1,0:T(8,128)(2,1)S(1)} %slice.20.mine.mine_at), channel_id=1, source_target_pairs={{0,16},{1,17},{2,18},{3,19},{4,20},{5,21},{6,22},{7,23},{8,24},{9,... | collective-permute-start | bytes 786440 | tf_op jit(solution)/shard_map/ppermute | solution.py:375
  36.4 0.0 collective-permute-done.1.far
  36.4 7.2 %shard_map.65 = bf16[4,1024,128]{2,1,0:T(8,128)(2,1)} custom-call(f32[2,1024]{1,0:T(2,128)S(1)} %copy-done.3, bf16[4,1552,128]{2,1,0:T(8,128)(2,1)S(1)} %all-to-all-done.near, bf16[4,1552,128]{2,1,0:T(8,128)(2,1)S(1)} %collective-permute-done.1.far, bf16[2,192,1024]{2,1,0:T(8,128)(2,1)S(1)} %bitcast.15, bf16[320,1024]{1,0:T(8,128)(2,1)} %collective-permute-done.mirrored_at), custom_call_target="tpu_custom_call" | custom-call | flops 8800000000 | tf_op jit(solution)/shard_map/pallas_call | solution.py:293
  43.6 0.0 collective-permute-done.2.other.other_at
  43.6 4.3 %all-to-all-start.1 = ((bf16[4,1024,128]{2,1,0:T(8,128)(2,1)}), bf16[4,1024,128]{2,1,0:T(8,128)(2,1)}, u32[]{:S(2)}, u32[]{:S(2)}) async-start(bf16[4,1024,128]{2,1,0:T(8,128)(2,1)} %shard_map.65), calls=%async_computation.1 | async-start | bytes 2097152 | tf_op jit(solution)/shard_map/all_to_all | solution.py:328
  47.9 3.8 %collective-permute-start.4 = (bf16[4,8,64,128]{3,2,1,0:T(8,128)(2,1)}, bf16[4,8,64,128]{3,2,1,0:T(8,128)(2,1)}, u32[]{:S(2)}, u32[]{:S(2)}) collective-permute-start(bf16[4,8,64,128]{3,2,1,0:T(8,128)(2,1)} %bitcast.5), channel_id=1, source_target_pairs={{0,24},{1,25},{2,26},{3,27},{4,28},{5,29},{6,30},{7,31},{8,16},{9,... | collective-permute-start | bytes 1572872 | tf_op jit(solution)/shard_map/ppermute | solution.py:377
  51.7 1.5 %shard_map.66.ready = bf16[8,128,1024]{2,1,0:T(8,128)(2,1)} custom-call(bf16[64,1024]{1,0:T(8,128)(2,1)S(1)} %get-tuple-element.33.own, bf16[128,1024]{1,0:T(8,128)(2,1)S(1)} %slice.20.mine.mine_at, bf16[128,1024]{1,0:T(8,128)(2,1)S(1)} %collective-permute-done.2.other.other_at), custom_call_target="tpu_custom_call" | custom-call | flops 1100000000 | tf_op jit(solution)/shard_map/pallas_call | solution.py:293
  53.2 9.7 %all-to-all-done.1.o_near = bf16[4,1024,128]{2,1,0:T(8,128)(2,1)} async-done(((bf16[4,1024,128]{2,1,0:T(8,128)(2,1)}), bf16[4,1024,128]{2,1,0:T(8,128)(2,1)}, u32[]{:S(2)}, u32[]{:S(2)}) %all-to-all-start.1) | async-done | bytes 1048608 | tf_op jit(solution)/shard_map/all_to_all | solution.py:328
  62.9 3.0 %collective-permute-start.3 = (bf16[4,1024,128]{2,1,0:T(8,128)(2,1)}, bf16[4,1024,128]{2,1,0:T(8,128)(2,1)}, u32[]{:S(2)}, u32[]{:S(2)}) collective-permute-start(bf16[4,1024,128]{2,1,0:T(8,128)(2,1)} %all-to-all-done.1.o_near), channel_id=1, source_target_pairs={{0,1},{1,0},{2,3},{3,2},{4,5},{5,4},{6,7},{7,6},{8,9},{9,8},{10,11... | collective-permute-start | bytes 3145736 | tf_op jit(solution)/shard_map/ppermute | solution.py:331
  65.9 1.9 %collective-permute-start.5 = (bf16[4,8,64,128]{3,2,1,0:T(8,128)(2,1)}, bf16[4,8,64,128]{3,2,1,0:T(8,128)(2,1)}, u32[]{:S(2)}, u32[]{:S(2)}) collective-permute-start(bf16[4,8,64,128]{3,2,1,0:T(8,128)(2,1)} %collective-permute-done.4.w_mir), channel_id=1, source_target_pairs={{0,1},{1,0},{2,3},{3,2},{4,5},{5,4},{6,7},{7,6},{8,9},{9,8},{10,11... | collective-permute-start | bytes 1572872 | tf_op jit(solution)/shard_map/ppermute | solution.py:331
  67.8 4.3 %all-to-all-start.2 = ((bf16[8,128,1024]{2,1,0:T(8,128)(2,1)}), bf16[8,128,1024]{2,1,0:T(8,128)(2,1)S(1)}, u32[]{:S(2)}, u32[]{:S(2)}) async-start(bf16[8,128,1024]{2,1,0:T(8,128)(2,1)} %shard_map.66.ready), calls=%async_computation.2 | async-start | bytes 4194304 | tf_op jit(solution)/shard_map/all_to_all | solution.py:384
  72.1 0.0 collective-permute-done.3.o_far
  72.2 8.1 %shard_map.67 = (bf16[2,512,128]{2,1,0:T(8,128)(2,1)S(1)}, bf16[1040,128]{1,0:T(8,128)(2,1)S(1)}, bf16[1040,128]{1,0:T(8,128)(2,1)S(1)}, bf16[128,1024]{1,0:T(8,128)(2,1)S(1)}) custom-call(f32[2,1024]{1,0:T(2,128)S(1)} %copy-done.3, bf16[4,1024,128]{2,1,0:T(8,128)(2,1)} %all-to-all-done.1.o_near, bf16[4,1024,128]{2,1,0:T(8,128)(2,1)} %collective-permute-done.3.o_far, ...), custom_call_target="tpu_custom_call" | custom-call | flops 8800000000 | tf_op jit(solution)/shard_map/pallas_call | solution.py:293
  80.2 4.1 %collective-permute-start.7 = (bf16[1040,128]{1,0:T(8,128)(2,1)S(1)}, bf16[1040,128]{1,0:T(8,128)(2,1)S(1)}, u32[]{:S(2)}, u32[]{:S(2)}) collective-permute-start(bf16[1040,128]{1,0:T(8,128)(2,1)S(1)} %get-tuple-element.27.refs_1_), channel_id=1, source_target_pairs={{0,8},{1,9},{2,10},{3,11},{4,12},{5,13},{6,14},{7,15},{8,0},{9,1},... | collective-permute-start | bytes 798728 | tf_op jit(solution)/shard_map/ppermute | solution.py:404
  84.3 11.4 %collective-permute-start.6 = (bf16[1040,128]{1,0:T(8,128)(2,1)S(1)}, bf16[1040,128]{1,0:T(8,128)(2,1)S(1)}, u32[]{:S(2)}, u32[]{:S(2)}) collective-permute-start(bf16[1040,128]{1,0:T(8,128)(2,1)S(1)} %get-tuple-element.26.refs_1_), channel_id=1, source_target_pairs={{0,504},{1,505},{2,506},{3,507},{4,508},{5,509},{6,510},{7,511},{8... | collective-permute-start | bytes 798728 | tf_op jit(solution)/shard_map/ppermute | solution.py:404
  95.7 2.2 %shard_map.68.refs_3_ = bf16[4,128,128]{2,1,0:T(8,128)(2,1)S(1)} custom-call(bf16[2,512,128]{2,1,0:T(8,128)(2,1)S(1)} %get-tuple-element.25.refs_0_, bf16[1040,128]{1,0:T(8,128)(2,1)S(1)} %get-tuple-element.27.refs_1_, bf16[1040,128]{1,0:T(8,128)(2,1)S(1)} %collective-permute-done.7.refs_2_), custom_call_target="tpu_custom_call" | custom-call | tf_op jit(solution)/shard_map/pallas_call | solution.py:293
  97.9 4.2 %collective-permute-done.6.refs_2_ = bf16[1040,128]{1,0:T(8,128)(2,1)S(1)} collective-permute-done((bf16[1040,128]{1,0:T(8,128)(2,1)S(1)}, bf16[1040,128]{1,0:T(8,128)(2,1)S(1)}, u32[]{:S(2)}, u32[]{:S(2)}) %collective-permute-start.6) | collective-permute-done | bytes 266272 | tf_op jit(solution)/shard_map/ppermute | solution.py:404
  102.1 2.2 %shard_map.69 = bf16[8,128,128]{2,1,0:T(8,128)(2,1)S(1)} custom-call(bf16[2,512,128]{2,1,0:T(8,128)(2,1)S(1)} %get-tuple-element.25.refs_0_, bf16[1040,128]{1,0:T(8,128)(2,1)S(1)} %get-tuple-element.26.refs_1_, bf16[1040,128]{1,0:T(8,128)(2,1)S(1)} %collective-permute-done.6.refs_2_, bf16[4,128,128]{2,1,0:T(8,128)(2,1)S(1)} %shard_map.68.refs_3_), custom_call_target="tpu_custom_call" | custom-call | flops 3300000000 | tf_op jit(solution)/shard_map/pallas_call | solution.py:293
  104.3 12.0 %all_to_all.20.parts = bf16[8,128,128]{2,1,0:T(8,128)(2,1)S(1)} all-to-all(bf16[8,128,128]{2,1,0:T(8,128)(2,1)S(1)} %shard_map.69), channel_id=1, replica_groups=mesh['z'=16,'xl'=2,'xh'=2,'y'=4,'c'=2] {'y','c'}, dimensions={0} | all-to-all | bytes 524288 | tf_op jit(solution)/shard_map/all_to_all | solution.py:421
  116.3 1.2 shard_map.70
  (15 shorter events, 0.1 us)
Async XLA Ops:
  2.5 5.2 %copy-start.4 = (bf16[2,64,1024]{2,1,0:T(8,128)(2,1)S(1)}, bf16[2,64,1024]{2,1,0:T(8,128)(2,1)}, u32[]{:S(2)}) copy-start(bf16[2,64,1024]{2,1,0:T(8,128)(2,1)} %w_at.1) | copy-start | bytes 786436
  2.5 5.2 %copy-start.1 = (bf16[2,1024,192]{1,2,0:T(8,128)(2,1)S(1)}, bf16[2,1024,192]{1,2,0:T(8,128)(2,1)}, u32[]{:S(2)}) copy-start(bf16[2,1024,192]{1,2,0:T(8,128)(2,1)} %param.10) | copy-start | bytes 2359300
  2.5 21.1 %all-to-all-start = ((bf16[4,1552,128]{2,1,0:T(8,128)(2,1)}), bf16[4,1552,128]{2,1,0:T(8,128)(2,1)S(1)}, u32[]{:S(2)}, u32[]{:S(2)}) async-start(bf16[4,1552,128]{2,1,0:T(8,128)(2,1)} %shard_map.64), calls=%async_computation | async-start | bytes 3178496 | tf_op jit(solution)/shard_map/all_to_all | solution.py:328
  7.8 28.6 %copy-start.3 = (f32[2,1024]{1,0:T(2,128)S(1)}, f32[2,1024]{1,0:T(2,128)}, u32[]{:S(2)}) copy-start(f32[2,1024]{1,0:T(2,128)} %gain.3) | copy-start | bytes 24580
  7.9 15.7 %collective-permute-start = (bf16[320,1024]{1,0:T(8,128)(2,1)S(1)}, bf16[320,1024]{1,0:T(8,128)(2,1)}, u32[]{:S(2)}, u32[]{:S(2)}) collective-permute-start(bf16[320,1024]{1,0:T(8,128)(2,1)S(1)} %pad_maximum_fusion), channel_id=1, source_target_pairs={{0,24},{1,25},{2,26},{3,27},{4,28},{5,29},{6,30},{7,31},{8,16},{9,... | collective-permute-start | bytes 1966088 | tf_op jit(solution)/shard_map/ppermute | solution.py:352
  23.6 20.0 %copy-start = (bf16[4,1552,128]{2,1,0:T(8,128)(2,1)}, bf16[4,1552,128]{2,1,0:T(8,128)(2,1)S(1)}, u32[]{:S(2)}) copy-start(bf16[4,1552,128]{2,1,0:T(8,128)(2,1)S(1)} %all-to-all-done.near) | copy-start | bytes 4767748
  23.6 12.7 %collective-permute-start.1 = (bf16[4,1552,128]{2,1,0:T(8,128)(2,1)S(1)}, bf16[4,1552,128]{2,1,0:T(8,128)(2,1)S(1)}, u32[]{:S(2)}, u32[]{:S(2)}) collective-permute-start(bf16[4,1552,128]{2,1,0:T(8,128)(2,1)S(1)} %all-to-all-done.near), channel_id=1, source_target_pairs={{0,1},{1,0},{2,3},{3,2},{4,5},{5,4},{6,7},{7,6},{8,9},{9,8},{10,11... | collective-permute-start | bytes 4767752 | tf_op jit(solution)/shard_map/ppermute | solution.py:331
  33.2 10.4 %collective-permute-start.2 = (bf16[128,1024]{1,0:T(8,128)(2,1)S(1)}, bf16[128,1024]{1,0:T(8,128)(2,1)S(1)}, u32[]{:S(2)}, u32[]{:S(2)}) collective-permute-start(bf16[128,1024]{1,0:T(8,128)(2,1)S(1)} %slice.20.mine.mine_at), channel_id=1, source_target_pairs={{0,16},{1,17},{2,18},{3,19},{4,20},{5,21},{6,22},{7,23},{8,24},{9,... | collective-permute-start | bytes 786440 | tf_op jit(solution)/shard_map/ppermute | solution.py:375
  36.4 7.2 %copy-start.2 = (bf16[4,1552,128]{2,1,0:T(8,128)(2,1)}, bf16[4,1552,128]{2,1,0:T(8,128)(2,1)S(1)}, u32[]{:S(2)}) copy-start(bf16[4,1552,128]{2,1,0:T(8,128)(2,1)S(1)} %collective-permute-done.1.far) | copy-start | bytes 4767748
  43.6 19.3 %all-to-all-start.1 = ((bf16[4,1024,128]{2,1,0:T(8,128)(2,1)}), bf16[4,1024,128]{2,1,0:T(8,128)(2,1)}, u32[]{:S(2)}, u32[]{:S(2)}) async-start(bf16[4,1024,128]{2,1,0:T(8,128)(2,1)} %shard_map.65), calls=%async_computation.1 | async-start | bytes 2097152 | tf_op jit(solution)/shard_map/all_to_all | solution.py:328
  47.9 18.0 %collective-permute-start.4 = (bf16[4,8,64,128]{3,2,1,0:T(8,128)(2,1)}, bf16[4,8,64,128]{3,2,1,0:T(8,128)(2,1)}, u32[]{:S(2)}, u32[]{:S(2)}) collective-permute-start(bf16[4,8,64,128]{3,2,1,0:T(8,128)(2,1)} %bitcast.5), channel_id=1, source_target_pairs={{0,24},{1,25},{2,26},{3,27},{4,28},{5,29},{6,30},{7,31},{8,16},{9,... | collective-permute-start | bytes 1572872 | tf_op jit(solution)/shard_map/ppermute | solution.py:377
  62.9 9.3 %collective-permute-start.3 = (bf16[4,1024,128]{2,1,0:T(8,128)(2,1)}, bf16[4,1024,128]{2,1,0:T(8,128)(2,1)}, u32[]{:S(2)}, u32[]{:S(2)}) collective-permute-start(bf16[4,1024,128]{2,1,0:T(8,128)(2,1)} %all-to-all-done.1.o_near), channel_id=1, source_target_pairs={{0,1},{1,0},{2,3},{3,2},{4,5},{5,4},{6,7},{7,6},{8,9},{9,8},{10,11... | collective-permute-start | bytes 3145736 | tf_op jit(solution)/shard_map/ppermute | solution.py:331
  65.9 6.2 %collective-permute-start.5 = (bf16[4,8,64,128]{3,2,1,0:T(8,128)(2,1)}, bf16[4,8,64,128]{3,2,1,0:T(8,128)(2,1)}, u32[]{:S(2)}, u32[]{:S(2)}) collective-permute-start(bf16[4,8,64,128]{3,2,1,0:T(8,128)(2,1)} %collective-permute-done.4.w_mir), channel_id=1, source_target_pairs={{0,1},{1,0},{2,3},{3,2},{4,5},{5,4},{6,7},{7,6},{8,9},{9,8},{10,11... | collective-permute-start | bytes 1572872 | tf_op jit(solution)/shard_map/ppermute | solution.py:331
  67.8 36.5 %all-to-all-start.2 = ((bf16[8,128,1024]{2,1,0:T(8,128)(2,1)}), bf16[8,128,1024]{2,1,0:T(8,128)(2,1)S(1)}, u32[]{:S(2)}, u32[]{:S(2)}) async-start(bf16[8,128,1024]{2,1,0:T(8,128)(2,1)} %shard_map.66.ready), calls=%async_computation.2 | async-start | bytes 4194304 | tf_op jit(solution)/shard_map/all_to_all | solution.py:384
  80.2 15.5 %collective-permute-start.7 = (bf16[1040,128]{1,0:T(8,128)(2,1)S(1)}, bf16[1040,128]{1,0:T(8,128)(2,1)S(1)}, u32[]{:S(2)}, u32[]{:S(2)}) collective-permute-start(bf16[1040,128]{1,0:T(8,128)(2,1)S(1)} %get-tuple-element.27.refs_1_), channel_id=1, source_target_pairs={{0,8},{1,9},{2,10},{3,11},{4,12},{5,13},{6,14},{7,15},{8,0},{9,1},... | collective-permute-start | bytes 798728 | tf_op jit(solution)/shard_map/ppermute | solution.py:404
  84.3 17.8 %collective-permute-start.6 = (bf16[1040,128]{1,0:T(8,128)(2,1)S(1)}, bf16[1040,128]{1,0:T(8,128)(2,1)S(1)}, u32[]{:S(2)}, u32[]{:S(2)}) collective-permute-start(bf16[1040,128]{1,0:T(8,128)(2,1)S(1)} %get-tuple-element.26.refs_1_), channel_id=1, source_target_pairs={{0,504},{1,505},{2,506},{3,507},{4,508},{5,509},{6,510},{7,511},{8... | collective-permute-start | bytes 798728 | tf_op jit(solution)/shard_map/ppermute | solution.py:404
